TPU v7x, 32 devices: a whole 2x2x4 slice. The times are simulated.
32 devices in a mesh: dp: 8 (over z, x), mp: 4 (over y, core).
Axes of the slice: x: 2, y: 2, z: 4, core: 2. Of those that a mesh axis runs over, the one named last changes fastest.
Arguments:
- query_states: bfloat16 [1024, 8192], P('dp', 'mp'), may hold values from -35.35534 to 35.35534
- key_states: bfloat16 [1024, 1024], P('dp', 'mp'), may hold values from -3 to 3
- value_states: bfloat16 [1024, 1024], P('dp', 'mp'), may hold values from -6 to 6
- grad_context: bfloat16 [1024, 8192], P('dp', 'mp'), may hold values from -6 to 6
- inputs_normed: bfloat16 [1024, 4096], P('dp'), may hold values from -6 to 6
- projections: bfloat16 [2, 4096, 1024], P(None, None, 'mp'), may hold values from -0.09375 to 0.09375
Outputs:
- grad_query: bfloat16 [1024, 8192], P('dp', 'mp')
- grad_input: bfloat16 [1024, 4096], P('dp', 'mp')
- grad_weights: float32 [4096, 1024], P('dp', 'mp')
All inputs are finite; a program needn't handle non-finite values.
Results may differ from a plain program's by a relative error of at most 0.013.
Values may be sent and summed in bfloat16 or wider, within the bound.
No kernel may reach another device: no remote copies, remote signals or barrier semaphores. Data moves between devices by JAX's collectives and lax.ppermute only.
A program may use at most 64 MiB of HBM per device.

v0:
```python
import math

import jax
import jax.numpy as jnp
from jax import lax
from jax.sharding import PartitionSpec as P

HEAD_SIZE = 128


def attention_grads(query_states, key_states, value_states, grad_context):
    length = query_states.shape[0]
    kv_heads = key_states.shape[1] // HEAD_SIZE
    per_group = query_states.shape[1] // key_states.shape[1]
    scale = 1.0 / math.sqrt(HEAD_SIZE)
    query_per_head = query_states.reshape(length, kv_heads, per_group, HEAD_SIZE)
    key_per_head = key_states.reshape(length, kv_heads, HEAD_SIZE)
    value_per_head = value_states.reshape(length, kv_heads, HEAD_SIZE)
    gradient_per_head = grad_context.reshape(length, kv_heads, per_group, HEAD_SIZE)
    scores = (
        jnp.einsum(
            "ikgd,jkd->kgij", query_per_head, key_per_head, preferred_element_type=jnp.float32
        )
        * scale
    )
    positions = lax.broadcasted_iota(jnp.int32, (length, length), 0)
    targets = lax.broadcasted_iota(jnp.int32, (length, length), 1)
    allowed = targets <= positions
    masked = jnp.where(allowed, scores, -1e30)
    row_max = jnp.max(masked, axis=-1, keepdims=True)
    raw_weights = jnp.where(allowed, jnp.exp(masked - row_max), 0.0)
    probs = raw_weights / jnp.sum(raw_weights, axis=-1, keepdims=True)
    probs_b = probs.astype(jnp.bfloat16)
    grad_value = jnp.einsum(
        "kgij,ikgd->jkd", probs_b, gradient_per_head, preferred_element_type=jnp.float32
    ).astype(jnp.bfloat16)
    grad_probs = jnp.einsum(
        "ikgd,jkd->kgij", gradient_per_head, value_per_head, preferred_element_type=jnp.float32
    )
    delta = jnp.sum(probs * grad_probs, axis=-1, keepdims=True)
    grad_scores = (probs * (grad_probs - delta)).astype(jnp.bfloat16)
    grad_query = (
        jnp.einsum("kgij,jkd->ikgd", grad_scores, key_per_head, preferred_element_type=jnp.float32)
        * scale
    ).astype(jnp.bfloat16)
    grad_key = (
        jnp.einsum(
            "kgij,ikgd->jkd", grad_scores, query_per_head, preferred_element_type=jnp.float32
        )
        * scale
    ).astype(jnp.bfloat16)
    return (
        grad_query.reshape(length, query_states.shape[1]),
        grad_key.reshape(length, key_states.shape[1]),
        grad_value.reshape(length, key_states.shape[1]),
    )


def body(query_states, key_states, value_states, grad_context, inputs_normed, projections):
    grad_query, grad_key, grad_value = attention_grads(
        query_states, key_states, value_states, grad_context
    )
    both_grads = jnp.stack([grad_key, grad_value])
    weight_terms = jnp.einsum(
        "sd,sc->dc", inputs_normed, grad_key, preferred_element_type=jnp.float32
    )
    summed = lax.psum_scatter(weight_terms, "dp", scatter_dimension=0, tiled=True)
    grad_weights = summed / lax.axis_size("dp")
    feature_rows = lax.all_to_all(projections, "mp", split_axis=1, concat_axis=2, tiled=True)
    all_heads = lax.all_gather(both_grads, "mp", axis=2, tiled=True)
    groups = lax.axis_size("mp")
    width = all_heads.shape[2] // groups
    head_blocks = all_heads.reshape(2, all_heads.shape[1], groups, width)
    row_blocks = feature_rows.reshape(2, feature_rows.shape[1], groups, width)
    block_partial = jnp.einsum(
        "tsmc,tdmc->msd", head_blocks, row_blocks, preferred_element_type=jnp.float32
    ).astype(jnp.bfloat16)
    grad_input = jnp.sum(block_partial.astype(jnp.float32), axis=0).astype(jnp.bfloat16)
    return (grad_query, grad_input, grad_weights)


def solution(mesh):
    placed = (
        P("dp", "mp"),
        P("dp", "mp"),
        P("dp", "mp"),
        P("dp", "mp"),
        P("dp", None),
        P(None, None, "mp"),
    )
    return jax.shard_map(
        body,
        mesh=mesh,
        in_specs=placed,
        out_specs=(P("dp", "mp"), P("dp", "mp"), P("dp", "mp")),
        check_vma=False,
    )
```

profile of v0, /device:TPU:0, one launch (start us, length us, event | category | flops | bytes accessed | tf_op | source)
XLA Modules:
  0.0 116.2 jit_solution(17225142510682557195)
XLA Ops:
  7.2 0.0 copy-start
  7.2 0.0 reduce-scatter.2.cloned.1.call-start
  7.2 0.9 reshape.32
  8.2 0.1 copy.53
  8.3 1.3 %copy.65 = bf16[128,2048]{0,1:T(8,128)(2,1)S(1)} copy(bf16[128,2048]{1,0:T(8,128)(2,1)} %param.6) | data formatting | bytes 1048576 | tf_op jit(solution)/shard_map/reshape | solution.py:16
  9.6 1.3 %copy.66 = bf16[128,2048]{0,1:T(8,128)(2,1)S(1)} copy(bf16[128,2048]{1,0:T(8,128)(2,1)} %param.9) | data formatting | bytes 1048576 | tf_op jit(solution)/shard_map/reshape | solution.py:19
  11.0 0.9 reshape.34
  11.9 0.6 fusion.16
  12.4 0.3 multiply_reduce_fusion
  12.8 0.2 multiply_convert_fusion
  13.0 0.3 fusion.9
  13.3 2.6 %convolution_bitcast_fusion = f32[4096,256]{0,1:T(8,128)} fusion(bf16[128,256]{0,1:T(8,128)(2,1)S(1)} %bitcast.67, bf16[128,4096]{1,0:T(8,128)(2,1)S(1)} %copy-done), kind=kOutput, calls=%fused_computation.1 | convolution fusion | flops 268435456 | bytes 5308416 | tf_op jit(solution)/shard_map/sd,sc->dc/dot_general | solution.py:64
  15.9 0.0 reduce-scatter.2.cloned.1.call-update
  15.9 10.1 %copy.45 = bf16[2,4096,256]{2,0,1:T(2,128)(2,1)} copy(bf16[2,4096,256]{2,1,0:T(8,128)(2,1)} %param.11) | data formatting | bytes 8388608 | tf_op args[5]
  26.0 4.8 %all-to-all-start = ((bf16[2,4096,256]{2,0,1:T(2,128)(2,1)}), bf16[2,4096,256]{2,0,1:T(2,128)(2,1)}, u32[]{:S(2)}, u32[]{:S(2)}) async-start(bf16[2,4096,256]{2,0,1:T(2,128)(2,1)} %copy.45), calls=%async_computation | async-start | bytes 8388608 | tf_op jit(solution)/shard_map/all_to_all | solution.py:69
  30.9 0.3 fusion.6
  31.2 1.0 copy.48
  32.2 1.3 %fusion.10 = bf16[2,128,128]{1,2,0:T(8,128)(2,1)S(1)} fusion(bf16[128,2,8,128]{0,3,2,1:T(8,128)(2,1)} %bitcast.70, f32[2,8,128,128]{2,3,1,0:T(8,128)S(1)} %get-tuple-element.13, f32[2,8,128]{2,1,0:T(8,128)S(1)} %get-tuple-element.12), kind=kOutput, calls=%fused_computation.17 | convolution fusion | flops 67665920 | bytes 1646592 | tf_op jit(solution)/shard_map/kgij,ikgd->jkd/dot_general | solution.py:34
  33.6 49.7 %all_gather.3 = bf16[2,128,1024]{1,2,0:T(8,128)(2,1)S(1)} all-gather(bf16[2,128,256]{1,2,0:T(8,128)(2,1)S(1)} %pad_maximum_fusion), channel_id=1, replica_groups=mesh['dp'=8,'mp'=4] {'mp'}, dimensions={2}, use_global_device_ids=true | all-gather | bytes 655360 | tf_op jit(solution)/shard_map/all_gather | solution.py:70
  83.3 2.7 %copy.46 = bf16[2,4096,256]{2,1,0:T(8,128)(2,1)S(1)} copy(bf16[2,4096,256]{2,0,1:T(2,128)(2,1)} %all-to-all-done) | data formatting | bytes 8388608 | tf_op jit(solution)/shard_map/all_to_all | solution.py:69
  86.0 2.3 %fusion.7 = bf16[128,1024]{1,0:T(8,128)(2,1)} fusion(bf16[2,128,4,256]{1,3,2,0:T(8,128)(2,1)S(1)} %bitcast.63, bf16[2,1024,4,256]{3,1,2,0:T(8,128)(2,1)S(1)} %bitcast.62), kind=kOutput, calls=%fused_computation.12 | convolution fusion | flops 537788416 | bytes 4980736 | tf_op jit(solution)/shard_map/tsmc,tdmc->msd/dot_general | solution.py:75
  88.3 19.0 %reduce-scatter.2.cloned.1.call-done = f32[512,256]{0,1:T(8,128)} async-done(((f32[4096,256]{0,1:T(8,128)}), f32[512,256]{0,1:T(8,128)}) %reduce-scatter.2.cloned.1.call-update) | async-done | bytes 524304 | tf_op jit(solution)/shard_map/reduce_scatter | solution.py:67
  107.3 1.1 broadcast_multiply_fusion
  108.3 1.0 copy.49
  (6 shorter events, 0.0 us)
Async XLA Ops:
  7.2 6.1 %copy-start = (bf16[128,4096]{1,0:T(8,128)(2,1)S(1)}, bf16[128,4096]{1,0:T(8,128)(2,1)}, u32[]{:S(2)}) copy-start(bf16[128,4096]{1,0:T(8,128)(2,1)} %param.10) | copy-start | bytes 3145732
  7.2 100.1 %reduce-scatter.2.cloned.1.call-start = ((), (), s32[]{:S(2)}) async-start(), calls=%async_computation.2 | async-start | bytes 4718592 | tf_op jit(solution)/shard_map/reduce_scatter | solution.py:67
  11.0 1.8 %copy-start.1 = (bf16[128,2048]{0,1:T(8,128)(2,1)}, bf16[128,2048]{0,1:T(8,128)(2,1)S(1)}, u32[]{:S(2)}) copy-start(bf16[128,2048]{0,1:T(8,128)(2,1)S(1)} %copy.66) | copy-start | bytes 1572868
  26.0 57.3 %all-to-all-start = ((bf16[2,4096,256]{2,0,1:T(2,128)(2,1)}), bf16[2,4096,256]{2,0,1:T(2,128)(2,1)}, u32[]{:S(2)}, u32[]{:S(2)}) async-start(bf16[2,4096,256]{2,0,1:T(2,128)(2,1)} %copy.45), calls=%async_computation | async-start | bytes 8388608 | tf_op jit(solution)/shard_map/all_to_all | solution.py:69
Sparse Core Ops, SparseCore 0:
  16.0 91.1 reduce-scatter.1
where the time goes:
time: 117 us; the launch traced here: 116 us
  blocking collectives  49.7 us (42%)
  local copies, waits for them, and re-layouts  19.5 us (17%)
  waiting for transfers between devices  19 us (16%)
  between operations  14.1 us (12%)
  matrix products  7.66 us (7%)
  starting transfers between devices  4.88 us (4%)
  other arithmetic  1.32 us (1%)
    all_gather x1, blocking collectives, body(): all_heads = lax.all_gather(both_grads, 'mp', axis=2, tiled=True)  49.7 us
    reduce_scatter x1, waiting for transfers between devices, body(): lax.psum_scatter(weight_terms, 'dp', scatter_dimension=0, tiled=True)  19 us
    unnamed x7, local copies, waits for them, and re-layouts  12.1 us
    all_to_all x1, starting transfers between devices, body(): lax.all_to_all(projections, 'mp', split_axis=1, concat_axis=2, tiled=True)  4.84 us
    all_to_all x1, local copies, waits for them, and re-layouts, body(): lax.all_to_all(projections, 'mp', split_axis=1, concat_axis=2, tiled=True)  2.73 us
    dot_general x1, matrix products, body(): jnp.einsum('sd,sc->dc', inputs_normed, grad_key, preferred_element_type=j...  2.62 us
  transfers between devices with their start and end apart: 2, of which 1 were waited for; matrix products, arithmetic and copies ran while one was open for 15% of the time, Pallas kernels for 0%

commit v1 on v0

v1 whole, which is shorter than its diff:
```python
import functools
import math

import jax
import jax.numpy as jnp
from jax import lax
from jax.experimental import pallas as pl
from jax.experimental.pallas import tpu as pltpu
from jax.sharding import PartitionSpec as P

HEAD_SIZE = 128
F32 = jnp.float32
BF16 = jnp.bfloat16
NT = (((1,), (1,)), ((), ()))
TN = (((0,), (0,)), ((), ()))
VMEM_LIMIT = 32 * 1024 * 1024


def dot(a, b, dims=(((1,), (0,)), ((), ()))):
    return lax.dot_general(a, b, dims, preferred_element_type=F32)


def attention_kernel(q_ref, k_ref, v_ref, do_ref, gk_ref, gv_ref, ds_ref):
    length = q_ref.shape[0]
    kv_heads = k_ref.shape[1] // HEAD_SIZE
    per_group = q_ref.shape[1] // k_ref.shape[1]
    scale = 1.0 / math.sqrt(HEAD_SIZE)
    targets = lax.broadcasted_iota(jnp.int32, (length, length), 0)
    positions = lax.broadcasted_iota(jnp.int32, (length, length), 1)
    allowed = targets <= positions
    for g in range(kv_heads):
        cols = slice(g * HEAD_SIZE, (g + 1) * HEAD_SIZE)
        key, value = k_ref[:, cols], v_ref[:, cols]
        acc_k = jnp.zeros((length, HEAD_SIZE), F32)
        acc_v = jnp.zeros((length, HEAD_SIZE), F32)
        for h in range(per_group):
            at = (g * per_group + h) * HEAD_SIZE
            query, grad = q_ref[:, at : at + HEAD_SIZE], do_ref[:, at : at + HEAD_SIZE]
            scores = jnp.where(allowed, dot(key, query, NT) * scale, -1e30)
            raw = jnp.exp(scores - jnp.max(scores, axis=0, keepdims=True))
            raw = jnp.where(allowed, raw, 0.0)
            probs = raw * (1.0 / jnp.sum(raw, axis=0, keepdims=True))
            grad_probs = dot(value, grad, NT)
            delta = jnp.sum(probs * grad_probs, axis=0, keepdims=True)
            grad_scores = (probs * (grad_probs - delta)).astype(BF16)
            ds_ref[:, at : at + length] = grad_scores
            acc_v += dot(probs.astype(BF16), grad)
            acc_k += dot(grad_scores, query)
        gk_ref[:, cols] = (acc_k * scale).astype(BF16)
        gv_ref[:, cols] = acc_v.astype(BF16)


def query_kernel(ds_ref, k_ref, gq_ref):
    kv_heads = k_ref.shape[1] // HEAD_SIZE
    per_group = gq_ref.shape[1] // k_ref.shape[1]
    scale = 1.0 / math.sqrt(HEAD_SIZE)
    for g in range(kv_heads):
        key = k_ref[:, g * HEAD_SIZE : (g + 1) * HEAD_SIZE]
        for h in range(per_group):
            at = (g * per_group + h) * HEAD_SIZE
            grad = dot(ds_ref[:, at : at + HEAD_SIZE], key, TN) * scale
            gq_ref[:, at : at + HEAD_SIZE] = grad.astype(BF16)


def partial_kernel(order_ref, gk_ref, gv_ref, p_ref, out_ref):
    del order_ref
    total = dot(gk_ref[...], p_ref[0], NT) + dot(gv_ref[...], p_ref[1], NT)
    out_ref[0] = total.astype(BF16)


def partials(order, grad_key, grad_value, projections, blocks):
    rows, width = grad_key.shape
    features = projections.shape[1] // blocks
    count = order.shape[0]
    return pl.pallas_call(
        partial_kernel,
        grid_spec=pltpu.PrefetchScalarGridSpec(
            num_scalar_prefetch=1,
            grid=(count,),
            in_specs=[
                pl.BlockSpec((rows, width), lambda t, order: (0, 0)),
                pl.BlockSpec((rows, width), lambda t, order: (0, 0)),
                pl.BlockSpec((2, features, width), lambda t, order: (0, order[t], 0)),
            ],
            out_specs=pl.BlockSpec((1, rows, features), lambda t, order: (t, 0, 0)),
        ),
        out_shape=jax.ShapeDtypeStruct((count, rows, features), BF16),
        compiler_params=pltpu.CompilerParams(vmem_limit_bytes=VMEM_LIMIT),
        cost_estimate=pl.CostEstimate(
            flops=4 * rows * width * features * count,
            bytes_accessed=count * features * (4 * width + 2 * rows),
            transcendentals=0,
        ),
    )(order, grad_key, grad_value, projections)


def split_kernel(core_ref, x_ref, out_ref):
    del core_ref
    width = out_ref.shape[2]
    for b in range(out_ref.shape[0]):
        out_ref[b] = x_ref[:, b * width : (b + 1) * width]


def column_blocks(core, inputs, parts):
    half = inputs.shape[0] // 2
    width = inputs.shape[1] // parts
    if width % 128:
        mine = lax.dynamic_slice_in_dim(inputs, core * half, half, 0)
        return mine.reshape(half, parts, width).transpose(1, 0, 2)
    return pl.pallas_call(
        split_kernel,
        grid_spec=pltpu.PrefetchScalarGridSpec(
            num_scalar_prefetch=1,
            grid=(1,),
            in_specs=[pl.BlockSpec((half, inputs.shape[1]), lambda t, core: (core[0], 0))],
            out_specs=pl.BlockSpec((parts, half, width), lambda t, core: (0, 0, 0)),
        ),
        out_shape=jax.ShapeDtypeStruct((parts, half, width), inputs.dtype),
    )(core.reshape(1), inputs)


def weights_kernel(core_ref, mine_ref, other_ref, keys_ref, out_ref):
    parts, half, width = mine_ref.shape
    columns = keys_ref.shape[2]
    core = core_ref[0]
    own = keys_ref[:, pl.ds(core * half, half), :].reshape(parts * half, columns)
    rest = keys_ref[:, pl.ds((1 - core) * half, half), :].reshape(parts * half, columns)
    total = dot(mine_ref[...].reshape(parts * half, width), own, TN)
    total += dot(other_ref[...].reshape(parts * half, width), rest, TN)
    out_ref[...] = total * (1.0 / parts)


def body(query_states, key_states, value_states, grad_context, inputs_normed, projections):
    parts = lax.axis_size("dp")
    groups = lax.axis_size("mp")
    chips = groups // 2
    place = lax.axis_index("mp")
    core, chip = lax.rem(place, 2), lax.div(place, 2)
    to_other_core = [(i, i ^ 1) for i in range(groups)]
    rows, width = key_states.shape
    query_width = query_states.shape[1]
    features = projections.shape[1] // groups
    half = rows // 2

    blocks = column_blocks(core, inputs_normed, parts)
    mine = lax.all_to_all(blocks, "dp", split_axis=0, concat_axis=0, tiled=True)
    other = lax.ppermute(mine, "mp", to_other_core)

    grad_key, grad_value, grad_scores = pl.pallas_call(
        attention_kernel,
        out_shape=(
            jax.ShapeDtypeStruct((rows, width), BF16),
            jax.ShapeDtypeStruct((rows, width), BF16),
            jax.ShapeDtypeStruct((rows, query_width), BF16),
        ),
        compiler_params=pltpu.CompilerParams(vmem_limit_bytes=VMEM_LIMIT),
        cost_estimate=pl.CostEstimate(
            flops=8 * rows * rows * query_width,
            bytes_accessed=6 * rows * query_width,
            transcendentals=rows * query_width,
        ),
    )(query_states, key_states, value_states, grad_context)

    all_keys = lax.all_gather(grad_key, "dp", axis=0)

    chip_order = [lax.rem(chip + k, chips) for k in range(1, chips + 1)]
    for_other = jnp.stack([2 * c + 1 - core for c in chip_order]).astype(jnp.int32)
    for_own = jnp.stack([2 * c + core for c in chip_order]).astype(jnp.int32)
    sent = partials(for_other, grad_key, grad_value, projections, groups)
    kept = partials(for_own, grad_key, grad_value, projections, groups)
    came = lax.ppermute(sent, "mp", to_other_core)
    pair = kept.astype(F32) + came.astype(F32)
    grad_input = pair[chips - 1]
    for k in range(1, chips):
        shift = [(i, (i + 2 * k) % groups) for i in range(groups)]
        grad_input += lax.ppermute(pair[k - 1].astype(BF16), "mp", shift).astype(F32)
    grad_input = grad_input.astype(BF16)

    grad_query = pl.pallas_call(
        query_kernel,
        out_shape=jax.ShapeDtypeStruct((rows, query_width), BF16),
        compiler_params=pltpu.CompilerParams(vmem_limit_bytes=VMEM_LIMIT),
        cost_estimate=pl.CostEstimate(
            flops=2 * rows * rows * query_width,
            bytes_accessed=4 * rows * query_width,
            transcendentals=0,
        ),
    )(grad_scores, key_states)

    spec = pl.BlockSpec(memory_space=pltpu.VMEM)
    grad_weights = pl.pallas_call(
        weights_kernel,
        in_specs=[pl.BlockSpec(memory_space=pltpu.SMEM), spec, spec, spec],
        out_specs=spec,
        out_shape=jax.ShapeDtypeStruct((inputs_normed.shape[1] // parts, width), F32),
        compiler_params=pltpu.CompilerParams(vmem_limit_bytes=VMEM_LIMIT),
        cost_estimate=pl.CostEstimate(
            flops=2 * rows * inputs_normed.shape[1] * width,
            bytes_accessed=4 * half * inputs_normed.shape[1],
            transcendentals=0,
        ),
    )(core.reshape(1), mine, other, all_keys)
    return (grad_query, grad_input, grad_weights)


def solution(mesh):
    placed = (
        P("dp", "mp"),
        P("dp", "mp"),
        P("dp", "mp"),
        P("dp", "mp"),
        P("dp", None),
        P(None, None, "mp"),
    )
    return jax.shard_map(
        body,
        mesh=mesh,
        in_specs=placed,
        out_specs=(P("dp", "mp"), P("dp", "mp"), P("dp", "mp")),
        check_vma=False,
    )
```

time: 117 us -> 62.9 us (0.54)
  waiting for transfers between devices: 19 us -> 0.01 us
  blocking collectives: 49.7 us -> 31.9 us
  between operations: 14.1 us -> 0.72 us
  local copies, waits for them, and re-layouts: 19.5 us -> 8.17 us
  Pallas kernels: 0 us -> 11.1 us
  matrix products: 7.66 us -> 0 us
  starting transfers between devices: 4.88 us -> 9.46 us
    reduce_scatter x1 -> x0, waiting for transfers between devices: 19 us -> none  [body(): lax.psum_scatter(weight_terms, 'dp', scatter_dimension=0, tiled=True)]
    all_gather x1, blocking collectives: 49.7 us -> 31.9 us  [body(): all_keys = lax.all_gather(grad_key, 'dp', axis=0)]
    pallas_call x0 -> x6, Pallas kernels: none -> 11.1 us  [the longest x1 3.4 us: body(): pl.pallas_call(attention_kernel, out_shape=(jax.ShapeDtypeStruct((rows, w...]
    dot_general x6 -> x0, matrix products: 7.1 us -> none  [the longest x1 2.62 us: body(): jnp.einsum('sd,sc->dc', inputs_normed, grad_key, preferred_element_type=j...]
    reshape x5 -> x0, local copies, waits for them, and re-layouts: 4.6 us -> none  [the longest x1 1.32 us: attention_grads(): query_states.reshape(length, kv_heads, per_group, HEAD_SIZE)]
    unnamed x7 -> x14, local copies, waits for them, and re-layouts: 12.1 us -> 8.14 us
    all_to_all x1 -> x0, local copies, waits for them, and re-layouts: 2.73 us -> none  [body(): lax.all_to_all(projections, 'mp', split_axis=1, concat_axis=2, tiled=True)]
    all_to_all x1, starting transfers between devices: 4.84 us -> 7.25 us  [body(): mine = lax.all_to_all(blocks, 'dp', split_axis=0, concat_axis=0, tiled=True)]
  transfers between devices with their start and end apart: 2 -> 4, of which waited for: 1 -> 0; matrix products, arithmetic and copies ran while one was open for 15% -> 2% of each run, Pallas kernels for 0% -> 13%
where the time goes in v1:
time: 62.9 us; the launch traced here: 62.4 us
  blocking collectives  31.9 us (51%)
  Pallas kernels  11.1 us (18%)
  starting transfers between devices  9.46 us (15%)
  local copies, waits for them, and re-layouts  8.17 us (13%)
  other arithmetic  1.09 us (2%)
  between operations  0.72 us (1%)
    all_gather x1, blocking collectives, body(): all_keys = lax.all_gather(grad_key, 'dp', axis=0)  31.9 us
    unnamed x14, local copies, waits for them, and re-layouts  8.14 us
    all_to_all x1, starting transfers between devices, body(): mine = lax.all_to_all(blocks, 'dp', split_axis=0, concat_axis=0, tiled=True)  7.25 us
    pallas_call x1, Pallas kernels, body(): pl.pallas_call(attention_kernel, out_shape=(jax.ShapeDtypeStruct((rows, w...  3.4 us
    pallas_call x2, Pallas kernels, partials(): pl.pallas_call(partial_kernel, grid_spec=pltpu.PrefetchScalarGridSpec(num...  3.38 us
    pallas_call x1, Pallas kernels, column_blocks(): pl.pallas_call(split_kernel, grid_spec=pltpu.PrefetchScalarGridSpec(num_s...  1.87 us
    ppermute x1, starting transfers between devices, body(): lax.ppermute(pair[k - 1].astype(BF16), 'mp', shift).astype(F32)  1.58 us
    pallas_call x1, Pallas kernels, body(): pl.pallas_call(weights_kernel, in_specs=[pl.BlockSpec(memory_space=pltpu....  1.28 us
  transfers between devices with their start and end apart: 4, of which 0 were waited for; matrix products, arithmetic and copies ran while one was open for 2% of the time, Pallas kernels for 13%

profile of v1, /device:TPU:0, one launch (start us, length us, event | category | flops | bytes accessed | tf_op | source)
XLA Modules:
  0.0 62.4 jit_solution(3703098623946325189)
XLA Ops:
  0.6 1.9 %shard_map.89 = bf16[8,64,512]{2,1,0:T(8,128)(2,1)} custom-call(s32[1]{0:T(128)} %bitcast.6.core_ref, bf16[128,4096]{1,0:T(8,128)(2,1)} %x_ref.1), custom_call_target="tpu_custom_call" | custom-call | tf_op jit(solution)/shard_map/pallas_call | solution.py:110
  2.5 7.3 %all-to-all-start = ((bf16[8,64,512]{2,1,0:T(8,128)(2,1)}), bf16[8,64,512]{2,1,0:T(8,128)(2,1)S(1)}, u32[]{:S(2)}, u32[]{:S(2)}) async-start(bf16[8,64,512]{2,1,0:T(8,128)(2,1)} %shard_map.89), calls=%async_computation | async-start | bytes 1048576 | tf_op jit(solution)/shard_map/all_to_all | solution.py:146
  9.8 1.0 %copy-done.2 = bf16[128,2048]{1,0:T(8,128)(2,1)S(1)} copy-done((bf16[128,2048]{1,0:T(8,128)(2,1)S(1)}, bf16[128,2048]{1,0:T(8,128)(2,1)}, u32[]{:S(2)}) %copy-start.2) | copy-done | bytes 524312
  10.8 1.0 %copy-done.3 = bf16[128,2048]{1,0:T(8,128)(2,1)S(1)} copy-done((bf16[128,2048]{1,0:T(8,128)(2,1)S(1)}, bf16[128,2048]{1,0:T(8,128)(2,1)}, u32[]{:S(2)}) %copy-start.3) | copy-done | bytes 524312
  11.8 0.8 %copy-done.4 = bf16[128,256]{1,0:T(8,128)(2,1)S(1)} copy-done((bf16[128,256]{1,0:T(8,128)(2,1)S(1)}, bf16[128,256]{1,0:T(8,128)(2,1)}, u32[]{:S(2)}) %copy-start.4) | copy-done | bytes 65560
  12.7 0.8 %copy-done.6 = bf16[128,256]{1,0:T(8,128)(2,1)S(1)} copy-done((bf16[128,256]{1,0:T(8,128)(2,1)S(1)}, bf16[128,256]{1,0:T(8,128)(2,1)}, u32[]{:S(2)}) %copy-start.6) | copy-done | bytes 65560
  13.5 3.4 %shard_map.85 = (bf16[128,256]{1,0:T(8,128)(2,1)S(1)}, bf16[128,256]{1,0:T(8,128)(2,1)S(1)}, bf16[128,2048]{1,0:T(8,128)(2,1)S(1)}) custom-call(bf16[128,2048]{1,0:T(8,128)(2,1)S(1)} %copy-done.2, bf16[128,256]{1,0:T(8,128)(2,1)S(1)} %copy-done.4, bf16[128,256]{1,0:T(8,128)(2,1)S(1)} %copy-done.6, bf16[128,2048]{1,0:T(8,128)(2,1)S(1)} %copy-done.3), custom_call_target="tpu_custom_call" | custom-call | flops 268435456 | bytes 1572864 | tf_op jit(solution)/shard_map/pallas_call | solution.py:149
  16.9 0.1 pad_add_fusion.1.order_ref
  17.0 2.2 %copy-done = bf16[2,4096,256]{2,1,0:T(8,128)(2,1)S(1)} copy-done((bf16[2,4096,256]{2,1,0:T(8,128)(2,1)S(1)}, bf16[2,4096,256]{2,1,0:T(8,128)(2,1)}, u32[]{:S(2)}) %copy-start) | copy-done | bytes 4194328
  19.2 1.7 %shard_map.88 = bf16[2,128,1024]{2,1,0:T(8,128)(2,1)S(1)} custom-call(s32[2]{0:T(128)S(1)} %pad_add_fusion.1.order_ref, bf16[128,256]{1,0:T(8,128)(2,1)S(1)} %get-tuple-element.7.gk_ref, bf16[128,256]{1,0:T(8,128)(2,1)S(1)} %get-tuple-element.8.gv_ref, bf16[2,4096,256]{2,1,0:T(8,128)(2,1)S(1)} %copy-done), custom_call_target="tpu_custom_call" | custom-call | flops 268435456 | bytes 2621440 | tf_op jit(solution)/shard_map/pallas_call | solution.py:75
  20.9 0.1 collective-permute-start
  21.0 0.1 pad_add_fusion.order_ref
  21.1 2.2 %copy-done.1 = bf16[2,4096,256]{2,1,0:T(8,128)(2,1)S(1)} copy-done((bf16[2,4096,256]{2,1,0:T(8,128)(2,1)S(1)}, bf16[2,4096,256]{2,1,0:T(8,128)(2,1)}, u32[]{:S(2)}) %copy-start.1) | copy-done | bytes 4194328
  23.3 1.7 %shard_map.87 = bf16[2,128,1024]{2,1,0:T(8,128)(2,1)S(1)} custom-call(s32[2]{0:T(128)S(1)} %pad_add_fusion.order_ref, bf16[128,256]{1,0:T(8,128)(2,1)S(1)} %get-tuple-element.7.gk_ref, bf16[128,256]{1,0:T(8,128)(2,1)S(1)} %get-tuple-element.8.gv_ref, bf16[2,4096,256]{2,1,0:T(8,128)(2,1)S(1)} %copy-done.1), custom_call_target="tpu_custom_call" | custom-call | flops 268435456 | bytes 2621440 | tf_op jit(solution)/shard_map/pallas_call | solution.py:75
  25.0 0.0 collective-permute-done
  25.0 0.2 convert_add_fusion
  25.1 0.0 all-to-all-done.mine_ref
  25.1 0.6 collective-permute-start.2
  25.7 1.6 %collective-permute-start.1 = (bf16[128,1024]{1,0:T(8,128)(2,1)S(1)}, bf16[128,1024]{1,0:T(8,128)(2,1)S(1)}, u32[]{:S(2)}, u32[]{:S(2)}) collective-permute-start(bf16[128,1024]{1,0:T(8,128)(2,1)S(1)} %fusion.2), channel_id=1, source_target_pairs={{0,2},{1,3},{2,0},{3,1},{4,6},{5,7},{6,4},{7,5},{8,10},{9,11},{10,... | collective-permute-start | bytes 786440 | tf_op jit(solution)/shard_map/ppermute | solution.py:176
  27.3 1.1 %shard_map.86 = bf16[128,2048]{1,0:T(8,128)(2,1)} custom-call(bf16[128,2048]{1,0:T(8,128)(2,1)S(1)} %get-tuple-element.6.ds_ref, bf16[128,256]{1,0:T(8,128)(2,1)S(1)} %copy-done.5), custom_call_target="tpu_custom_call" | custom-call | flops 67108864 | bytes 1048576 | tf_op jit(solution)/shard_map/pallas_call | solution.py:179
  28.5 31.9 %all-gather = bf16[1024,256]{1,0:T(8,128)(2,1)S(1)} all-gather(bf16[128,256]{1,0:T(8,128)(2,1)S(1)} %get-tuple-element.7.gk_ref), channel_id=2, replica_groups=mesh['dp'=8,'mp'=4] {'dp'}, dimensions={0}, use_global_device_ids=true | all-gather | bytes 589824 | tf_op jit(solution)/shard_map/all_gather | solution.py:164
  60.4 0.0 collective-permute-done.1
  60.4 0.8 %fusion.1 = bf16[128,1024]{1,0:T(8,128)(2,1)} fusion(f32[2,128,1024]{2,1,0:T(8,128)S(1)} %convert_add_fusion, bf16[128,1024]{1,0:T(8,128)(2,1)S(1)} %collective-permute-done.1), kind=kLoop, calls=%fused_computation.4 | loop fusion | flops 393216 | bytes 1048576 | tf_op jit(solution)/shard_map/convert_element_type | solution.py:177
  61.1 1.3 %shard_map.90 = f32[512,256]{1,0:T(8,128)} custom-call(s32[1]{0:T(128)} %bitcast.6.core_ref, bf16[8,64,512]{2,1,0:T(8,128)(2,1)S(1)} %all-to-all-done.mine_ref, bf16[8,64,512]{2,1,0:T(8,128)(2,1)S(1)} %collective-permute-done.2.other_ref, bf16[8,128,256]{2,1,0:T(8,128)(2,1)S(1)} %bitcast.14), custom_call_target="tpu_custom_call" | custom-call | flops 268435456 | bytes 1048576 | tf_op jit(solution)/shard_map/pallas_call | solution.py:191
  (10 shorter events, 0.0 us)
Async XLA Ops:
  2.5 22.6 %all-to-all-start = ((bf16[8,64,512]{2,1,0:T(8,128)(2,1)}), bf16[8,64,512]{2,1,0:T(8,128)(2,1)S(1)}, u32[]{:S(2)}, u32[]{:S(2)}) async-start(bf16[8,64,512]{2,1,0:T(8,128)(2,1)} %shard_map.89), calls=%async_computation | async-start | bytes 1048576 | tf_op jit(solution)/shard_map/all_to_all | solution.py:146
  9.8 1.0 %copy-start.2 = (bf16[128,2048]{1,0:T(8,128)(2,1)S(1)}, bf16[128,2048]{1,0:T(8,128)(2,1)}, u32[]{:S(2)}) copy-start(bf16[128,2048]{1,0:T(8,128)(2,1)} %q_ref.1) | copy-start | bytes 1572868
  10.8 1.0 %copy-start.3 = (bf16[128,2048]{1,0:T(8,128)(2,1)S(1)}, bf16[128,2048]{1,0:T(8,128)(2,1)}, u32[]{:S(2)}) copy-start(bf16[128,2048]{1,0:T(8,128)(2,1)} %do_ref.1) | copy-start | bytes 1572868
  11.8 0.8 %copy-start.4 = (bf16[128,256]{1,0:T(8,128)(2,1)S(1)}, bf16[128,256]{1,0:T(8,128)(2,1)}, u32[]{:S(2)}) copy-start(bf16[128,256]{1,0:T(8,128)(2,1)} %k_ref.3) | copy-start | bytes 196612
  12.7 0.8 %copy-start.6 = (bf16[128,256]{1,0:T(8,128)(2,1)S(1)}, bf16[128,256]{1,0:T(8,128)(2,1)}, u32[]{:S(2)}) copy-start(bf16[128,256]{1,0:T(8,128)(2,1)} %v_ref.1) | copy-start | bytes 196612
  17.0 2.2 %copy-start = (bf16[2,4096,256]{2,1,0:T(8,128)(2,1)S(1)}, bf16[2,4096,256]{2,1,0:T(8,128)(2,1)}, u32[]{:S(2)}) copy-start(bf16[2,4096,256]{2,1,0:T(8,128)(2,1)} %p_ref.3) | copy-start | bytes 12582916
  19.2 8.1 %copy-start.5 = (bf16[128,256]{1,0:T(8,128)(2,1)S(1)}, bf16[128,256]{1,0:T(8,128)(2,1)}, u32[]{:S(2)}) copy-start(bf16[128,256]{1,0:T(8,128)(2,1)} %k_ref.3) | copy-start | bytes 196612
  20.9 4.1 %collective-permute-start = (bf16[2,128,1024]{2,1,0:T(8,128)(2,1)S(1)}, bf16[2,128,1024]{2,1,0:T(8,128)(2,1)S(1)}, u32[]{:S(2)}, u32[]{:S(2)}) collective-permute-start(bf16[2,128,1024]{2,1,0:T(8,128)(2,1)S(1)} %shard_map.88), channel_id=1, source_target_pairs={{0,1},{1,0},{2,3},{3,2},{4,5},{5,4},{6,7},{7,6},{8,9},{9,8},{10,11... | collective-permute-start | bytes 1572872 | tf_op jit(solution)/shard_map/ppermute | solution.py:171
  21.1 2.2 %copy-start.1 = (bf16[2,4096,256]{2,1,0:T(8,128)(2,1)S(1)}, bf16[2,4096,256]{2,1,0:T(8,128)(2,1)}, u32[]{:S(2)}) copy-start(bf16[2,4096,256]{2,1,0:T(8,128)(2,1)} %p_ref.3) | copy-start | bytes 12582916
  25.1 36.0 %collective-permute-start.2 = (bf16[8,64,512]{2,1,0:T(8,128)(2,1)S(1)}, bf16[8,64,512]{2,1,0:T(8,128)(2,1)S(1)}, u32[]{:S(2)}, u32[]{:S(2)}) collective-permute-start(bf16[8,64,512]{2,1,0:T(8,128)(2,1)S(1)} %all-to-all-done.mine_ref), channel_id=1, source_target_pairs={{0,1},{1,0},{2,3},{3,2},{4,5},{5,4},{6,7},{7,6},{8,9},{9,8},{10,11... | collective-permute-start | bytes 1572872 | tf_op jit(solution)/shard_map/ppermute | solution.py:147
  25.7 34.6 %collective-permute-start.1 = (bf16[128,1024]{1,0:T(8,128)(2,1)S(1)}, bf16[128,1024]{1,0:T(8,128)(2,1)S(1)}, u32[]{:S(2)}, u32[]{:S(2)}) collective-permute-start(bf16[128,1024]{1,0:T(8,128)(2,1)S(1)} %fusion.2), channel_id=1, source_target_pairs={{0,2},{1,3},{2,0},{3,1},{4,6},{5,7},{6,4},{7,5},{8,10},{9,11},{10,... | collective-permute-start | bytes 786440 | tf_op jit(solution)/shard_map/ppermute | solution.py:176

commit v2 on v0

v2 whole, which is shorter than its diff:
```python
import functools
import math

import jax
import jax.numpy as jnp
from jax import lax
from jax.experimental import pallas as pl
from jax.experimental.pallas import tpu as pltpu
from jax.sharding import PartitionSpec as P

HEAD_SIZE = 128
F32 = jnp.float32
BF16 = jnp.bfloat16
NN = (((1,), (0,)), ((), ()))
NT = (((1,), (1,)), ((), ()))
TN = (((0,), (0,)), ((), ()))
IN_HBM = pl.BlockSpec(memory_space=pltpu.HBM)
ANYWHERE = pl.BlockSpec(memory_space=pl.ANY)
IN_VMEM = pl.BlockSpec(memory_space=pltpu.VMEM)
IN_SMEM = pl.BlockSpec(memory_space=pltpu.SMEM)
CHUNK = 512
PARAMS = pltpu.CompilerParams(vmem_limit_bytes=24 * 1024 * 1024)
WHOLE = pltpu.CompilerParams()


def dot(a, b, dims=NN):
    return lax.dot_general(a, b, dims, preferred_element_type=F32)


def cost(flops, moved, transcendentals=0):
    return pl.CostEstimate(flops=flops, bytes_accessed=moved, transcendentals=transcendentals)


def attention_group(g, q, k, v, do, gk_ref, gv_ref, ds_ref):
    length = q.shape[0]
    per_group = q.shape[1] // k.shape[1]
    scale = 1.0 / math.sqrt(HEAD_SIZE)
    targets = lax.broadcasted_iota(jnp.int32, (length, length), 0)
    positions = lax.broadcasted_iota(jnp.int32, (length, length), 1)
    allowed = targets <= positions
    cols = slice(g * HEAD_SIZE, (g + 1) * HEAD_SIZE)
    key, value = k[:, cols], v[:, cols]
    acc_k = jnp.zeros((length, HEAD_SIZE), F32)
    acc_v = jnp.zeros((length, HEAD_SIZE), F32)
    for h in range(per_group):
        at = (g * per_group + h) * HEAD_SIZE
        query, grad = q[:, at : at + HEAD_SIZE], do[:, at : at + HEAD_SIZE]
        scores = jnp.where(allowed, dot(key, query, NT) * scale, -1e30)
        raw = jnp.exp(scores - jnp.max(scores, axis=0, keepdims=True))
        raw = jnp.where(allowed, raw, 0.0)
        probs = raw * (1.0 / jnp.sum(raw, axis=0, keepdims=True))
        grad_probs = dot(value, grad, NT)
        delta = jnp.sum(probs * grad_probs, axis=0, keepdims=True)
        grad_scores = (probs * (grad_probs - delta)).astype(BF16)
        ds_ref[:, at : at + length] = grad_scores
        acc_v += dot(probs.astype(BF16), grad)
        acc_k += dot(grad_scores, query)
    gk_ref[:, cols] = (acc_k * scale).astype(BF16)
    gv_ref[:, cols] = acc_v.astype(BF16)


def block_partials(p, gk, gv, out_ref):
    features = p.shape[2]
    step = min(CHUNK, features)
    for b in range(p.shape[0]):
        for at in range(0, features, step):
            rows = slice(at, at + step)
            total = dot(p[b, 0, rows, :], gk, NT) + dot(p[b, 1, rows, :], gv, NT)
            out_ref[b, rows, :] = total.astype(BF16)


def projection_copies(place_ref, p_hbm, p, sems, own):
    chips, features = p.shape[0], p.shape[2]
    chip, core = lax.div(place_ref[1], 2), lax.rem(place_ref[1], 2)
    column = core if own else 1 - core
    copies = []
    for b in range(chips):
        start = (2 * lax.rem(chip + b + 1, chips) + column) * features
        rows = pl.ds(pl.multiple_of(start, features), features)
        copies.append(pltpu.make_async_copy(p_hbm.at[:, rows, :], p.at[b], sems.at[b]))
    return copies


def attention_kernel(
    place_ref, q_hbm, k_hbm, v_hbm, do_hbm, p_hbm,
    gk_ref, gv_ref, ds_ref, sent_ref,
    q, k, v, do, p, sems, p_sems,
):
    kv_heads = k.shape[1] // HEAD_SIZE
    group = q.shape[1] // kv_heads
    small = [
        pltpu.make_async_copy(k_hbm, k, sems.at[0]),
        pltpu.make_async_copy(v_hbm, v, sems.at[1]),
    ]
    large = []
    for g in range(kv_heads):
        cols = pl.ds(g * group, group)
        large.append((
            pltpu.make_async_copy(q_hbm.at[:, cols], q.at[:, cols], sems.at[2 + 2 * g]),
            pltpu.make_async_copy(do_hbm.at[:, cols], do.at[:, cols], sems.at[3 + 2 * g]),
        ))
    blocks = projection_copies(place_ref, p_hbm, p, p_sems, own=False)
    for copy in small:
        copy.start()
    for pair in large:
        for copy in pair:
            copy.start()
    for copy in blocks:
        copy.start()
    for copy in small:
        copy.wait()
    for g in range(kv_heads):
        for copy in large[g]:
            copy.wait()
        attention_group(g, q, k, v, do, gk_ref, gv_ref, ds_ref)
    for copy in blocks:
        copy.wait()
    block_partials(p, gk_ref[...], gv_ref[...], sent_ref)


def own_partials_kernel(place_ref, gk_ref, gv_ref, p_hbm, kept_ref, p, p_sems):
    blocks = projection_copies(place_ref, p_hbm, p, p_sems, own=True)
    for copy in blocks:
        copy.start()
    for copy in blocks:
        copy.wait()
    block_partials(p, gk_ref[...], gv_ref[...], kept_ref)


def query_kernel(ds_ref, k_ref, gq_ref):
    kv_heads = k_ref.shape[1] // HEAD_SIZE
    per_group = gq_ref.shape[1] // k_ref.shape[1]
    scale = 1.0 / math.sqrt(HEAD_SIZE)
    for g in range(kv_heads):
        key = k_ref[:, g * HEAD_SIZE : (g + 1) * HEAD_SIZE]
        for h in range(per_group):
            at = (g * per_group + h) * HEAD_SIZE
            grad = dot(ds_ref[:, at : at + HEAD_SIZE], key, TN) * scale
            gq_ref[:, at : at + HEAD_SIZE] = grad.astype(BF16)


def input_kernel(kept_ref, came_ref, *refs):
    out_ref = refs[-1]
    total = kept_ref[len(refs) - 1].astype(F32) + came_ref[len(refs) - 1].astype(F32)
    for ref in refs[:-1]:
        total += ref[...].astype(F32)
    out_ref[...] = total.T.astype(BF16)


def column_blocks_kernel(index_ref, x_hbm, *refs):
    outs, sems = refs[:-1], refs[-1]
    width = outs[0].shape[1]
    copies = []
    for j, out in enumerate(outs):
        cols = pl.ds(pl.multiple_of(index_ref[j] * width, width), width)
        copies.append(pltpu.make_async_copy(x_hbm.at[:, cols], out, sems.at[j]))
    for copy in copies:
        copy.start()
    for copy in copies:
        copy.wait()


def weights_kernel(count, slot_ref, *refs):
    inputs, keys, out_ref, x, gk = refs[:count], refs[count : 2 * count], *refs[2 * count :]
    rows = inputs[0].shape[0]
    for j in range(count):
        x[pl.ds(pl.multiple_of(slot_ref[j] * rows, rows), rows), :] = inputs[j][...]
        gk[j * rows : (j + 1) * rows, :] = keys[j][...]
    out_ref[...] = dot(x[...], gk[...], TN) * (1.0 / count)


def outgoing_blocks(inputs, place, parts, groups):
    far = parts // 2
    part, member = place[0], place[1]
    core = lax.rem(member, 2)
    rows = inputs.shape[0]
    width = inputs.shape[1] // parts
    targets = [part ^ (far + member)] + [part ^ (k + core) for k in range(2, far, 2)]
    targets += [part ^ 1, part]
    return pl.pallas_call(
        column_blocks_kernel,
        in_specs=[IN_SMEM, IN_HBM],
        out_specs=[ANYWHERE] * len(targets),
        out_shape=[jax.ShapeDtypeStruct((rows, width), inputs.dtype)] * len(targets),
        scratch_shapes=[pltpu.SemaphoreType.DMA((len(targets),))],
        compiler_params=WHOLE,
        cost_estimate=cost(0, 4 * len(targets) * rows * width),
    )(jnp.stack(targets).astype(jnp.int32), inputs)


def exchanged_weights(inputs, blocks, grad_key, place, parts, groups):
    far = parts // 2
    part, member = place[0], place[1]
    core = lax.rem(member, 2)
    rows = inputs.shape[0]
    width = inputs.shape[1] // parts

    def along_dp(array, partner):
        pairs = [
            (i * groups + m, (i ^ partner(m)) * groups + m)
            for i in range(parts)
            for m in range(groups)
        ]
        return lax.ppermute(array, ("dp", "mp"), pairs)

    def along_mp(array, bit):
        return lax.ppermute(array, "mp", [(m, m ^ bit) for m in range(groups)])

    near = list(range(2, far, 2))
    slots, pieces = [jnp.int32(0)], [blocks[-1]]
    slots.append(jnp.int32(1))
    shared = {0: along_dp(blocks[0], lambda m: far + m)}
    for k, block in zip(near, blocks[1:]):
        first = along_dp(block, lambda m, k=k: k + m % 2)
        pieces += [first, along_mp(first, 1)]
        slots += [k + core, k + (core ^ 1)]
    pieces.insert(1, along_dp(blocks[-2], lambda m: 1))
    bit = groups // 2
    while bit:
        for j in list(shared):
            shared[j ^ bit] = along_mp(shared[j], bit)
        bit //= 2
    for j, piece in shared.items():
        pieces.append(piece)
        slots.append(far + (member ^ j))

    keys = {0: grad_key}
    for k in sorted(range(2, parts, 2), reverse=True):
        keys[k] = along_dp(grad_key, lambda m, k=k: k)
    for k in range(0, parts, 2):
        keys[k + 1] = along_dp(keys[k], lambda m: 1)

    columns = grad_key.shape[1]
    return pl.pallas_call(
        functools.partial(weights_kernel, parts),
        in_specs=[IN_SMEM] + [IN_VMEM] * (2 * parts),
        out_specs=IN_VMEM,
        out_shape=jax.ShapeDtypeStruct((width, columns), F32),
        scratch_shapes=[
            pltpu.VMEM((parts * rows, width), inputs.dtype),
            pltpu.VMEM((parts * rows, columns), BF16),
        ],
        compiler_params=PARAMS,
        cost_estimate=cost(
            2 * parts * rows * width * columns, 2 * parts * rows * (width + columns)
        ),
    )(jnp.stack(slots).astype(jnp.int32), *pieces, *[keys[k] for k in range(parts)])


def gathered_weights(inputs, grad_key, parts):
    rows = inputs.shape[0]
    width = inputs.shape[1] // parts
    blocks = inputs.reshape(rows, parts, width).transpose(1, 0, 2)
    mine = lax.all_to_all(blocks, "dp", split_axis=0, concat_axis=0, tiled=True)
    keys = lax.all_gather(grad_key, "dp", axis=0)
    return jnp.einsum("psd,psc->dc", mine, keys, preferred_element_type=F32) / parts


def body(query_states, key_states, value_states, grad_context, inputs_normed, projections):
    parts = lax.axis_size("dp")
    groups = lax.axis_size("mp")
    chips = groups // 2
    place = jnp.stack([lax.axis_index("dp"), lax.axis_index("mp")]).astype(jnp.int32)
    rows, width = key_states.shape
    query_width = query_states.shape[1]
    features = projections.shape[1] // groups
    kv_heads = width // HEAD_SIZE
    blocks = jax.ShapeDtypeStruct((chips, features, rows), BF16)
    p_scratch = [
        pltpu.VMEM((chips, 2, features, width), BF16),
        pltpu.SemaphoreType.DMA((chips,)),
    ]

    exchange = parts == 2 * groups
    if exchange:
        outgoing = outgoing_blocks(inputs_normed, place, parts, groups)
        place, outgoing = lax.optimization_barrier((place, outgoing))

    grad_key, grad_value, grad_scores, sent = pl.pallas_call(
        attention_kernel,
        in_specs=[IN_SMEM] + [IN_HBM] * 5,
        out_specs=[IN_VMEM] * 4,
        out_shape=(
            jax.ShapeDtypeStruct((rows, width), BF16),
            jax.ShapeDtypeStruct((rows, width), BF16),
            jax.ShapeDtypeStruct((rows, query_width), BF16),
            blocks,
        ),
        scratch_shapes=[
            pltpu.VMEM((rows, query_width), BF16),
            pltpu.VMEM((rows, width), BF16),
            pltpu.VMEM((rows, width), BF16),
            pltpu.VMEM((rows, query_width), BF16),
            p_scratch[0],
            pltpu.SemaphoreType.DMA((2 + 2 * kv_heads,)),
            p_scratch[1],
        ],
        compiler_params=WHOLE,
        cost_estimate=cost(
            8 * rows * rows * query_width + 4 * rows * width * features * chips,
            6 * rows * query_width + 4 * width * features * chips,
            rows * query_width,
        ),
    )(place, query_states, key_states, value_states, grad_context, projections)

    if exchange:
        grad_weights = exchanged_weights(
            inputs_normed, outgoing, grad_key, place, parts, groups
        )
    else:
        grad_weights = gathered_weights(inputs_normed, grad_key, parts)

    came = lax.ppermute(sent, "mp", [(m, m ^ 1) for m in range(groups)])
    kept = pl.pallas_call(
        own_partials_kernel,
        in_specs=[IN_SMEM, IN_VMEM, IN_VMEM, IN_HBM],
        out_specs=IN_VMEM,
        out_shape=blocks,
        scratch_shapes=p_scratch,
        compiler_params=WHOLE,
        cost_estimate=cost(
            4 * rows * width * features * chips, 4 * width * features * chips
        ),
    )(place, grad_key, grad_value, projections)
    arrived = []
    for b in range(chips - 1):
        pair = (kept[b].astype(F32) + came[b].astype(F32)).astype(BF16)
        shift = [(m, (m + 2 * (b + 1)) % groups) for m in range(groups)]
        arrived.append(lax.ppermute(pair, "mp", shift))
    grad_input = pl.pallas_call(
        input_kernel,
        in_specs=[IN_VMEM] * (2 + len(arrived)),
        out_specs=IN_VMEM,
        out_shape=jax.ShapeDtypeStruct((rows, features), BF16),
        compiler_params=PARAMS,
        cost_estimate=cost(rows * features, 8 * rows * features),
    )(kept, came, *arrived)

    grad_query = pl.pallas_call(
        query_kernel,
        out_shape=jax.ShapeDtypeStruct((rows, query_width), BF16),
        compiler_params=PARAMS,
        cost_estimate=cost(2 * rows * rows * query_width, 4 * rows * query_width),
    )(grad_scores, key_states)
    return (grad_query, grad_input, grad_weights)


def solution(mesh):
    placed = (
        P("dp", "mp"),
        P("dp", "mp"),
        P("dp", "mp"),
        P("dp", "mp"),
        P("dp", None),
        P(None, None, "mp"),
    )
    return jax.shard_map(
        body,
        mesh=mesh,
        in_specs=placed,
        out_specs=(P("dp", "mp"), P("dp", "mp"), P("dp", "mp")),
        check_vma=False,
    )
```

time: 117 us -> 62.1 us (0.53)
  blocking collectives: 49.7 us -> 0 us
  Pallas kernels: 0 us -> 32.6 us
  local copies, waits for them, and re-layouts: 19.5 us -> 0.71 us
  waiting for transfers between devices: 19 us -> 2.96 us
  starting transfers between devices: 4.88 us -> 17 us
  between operations: 14.1 us -> 5.32 us
  matrix products: 7.66 us -> 0 us
  other arithmetic: 1.32 us -> 2.96 us
    all_gather x1 -> x0, blocking collectives: 49.7 us -> none  [body(): all_heads = lax.all_gather(both_grads, 'mp', axis=2, tiled=True)]
    pallas_call x0 -> x6, Pallas kernels: none -> 32.6 us  [the longest x1 17.7 us: outgoing_blocks(): pl.pallas_call(column_blocks_kernel, in_specs=[IN_SMEM, IN_HBM], out_spec...]
    reduce_scatter x1 -> x0, waiting for transfers between devices: 19 us -> none  [body(): lax.psum_scatter(weight_terms, 'dp', scatter_dimension=0, tiled=True)]
    ppermute x0 -> x16, starting transfers between devices: none -> 17 us  [the longest x10 14 us: along_dp(): return lax.ppermute(array, ('dp', 'mp'), pairs)]
    unnamed x7 -> x18, local copies, waits for them, and re-layouts: 12.1 us -> 0.04 us
    dot_general x6 -> x0, matrix products: 7.1 us -> none  [the longest x1 2.62 us: body(): jnp.einsum('sd,sc->dc', inputs_normed, grad_key, preferred_element_type=j...]
    all_to_all x1 -> x0, starting transfers between devices: 4.84 us -> none  [body(): lax.all_to_all(projections, 'mp', split_axis=1, concat_axis=2, tiled=True)]
    reshape x5 -> x0, local copies, waits for them, and re-layouts: 4.6 us -> none  [the longest x1 1.32 us: attention_grads(): query_states.reshape(length, kv_heads, per_group, HEAD_SIZE)]
  transfers between devices with their start and end apart: 2 -> 16, of which waited for: 1 -> 2; matrix products, arithmetic and copies ran while one was open for 15% -> 4% of each run, Pallas kernels for 0% -> 11%
where the time goes in v2:
time: 62.1 us; the launch traced here: 61.6 us
  Pallas kernels  32.6 us (52%)
  starting transfers between devices  17 us (27%)
  between operations  5.32 us (9%)
  other arithmetic  2.96 us (5%)
  waiting for transfers between devices  2.96 us (5%)
  local copies, waits for them, and re-layouts  0.71 us (1%)
    pallas_call x1, Pallas kernels, outgoing_blocks(): pl.pallas_call(column_blocks_kernel, in_specs=[IN_SMEM, IN_HBM], out_spec...  17.7 us
    ppermute x10, starting transfers between devices, along_dp(): return lax.ppermute(array, ('dp', 'mp'), pairs)  14 us
    pallas_call x1, Pallas kernels, body(): pl.pallas_call(attention_kernel, in_specs=[IN_SMEM] + [IN_HBM] * 5, out_s...  7.04 us
    pallas_call x1, Pallas kernels, body(): pl.pallas_call(own_partials_kernel, in_specs=[IN_SMEM, IN_VMEM, IN_VMEM,...  3.95 us
    ppermute x10, waiting for transfers between devices, along_dp(): return lax.ppermute(array, ('dp', 'mp'), pairs)  2.95 us
    ppermute x4, starting transfers between devices, along_mp(): return lax.ppermute(array, 'mp', [(m, m ^ bit) for m in range(groups)])  2.44 us
    pallas_call x1, Pallas kernels, exchanged_weights(): pl.pallas_call(functools.partial(weights_kernel, parts), in_specs=[IN_SME...  1.91 us
    convert_element_type x1, other arithmetic, body(): pair = (kept[b].astype(F32) + came[b].astype(F32)).astype(BF16)  1.72 us
  transfers between devices with their start and end apart: 16, of which 2 were waited for; matrix products, arithmetic and copies ran while one was open for 4% of the time, Pallas kernels for 11%

profile of v2, /device:TPU:0, one launch (start us, length us, event | category | flops | bytes accessed | tf_op | source)
XLA Modules:
  0.0 61.6 jit_solution(5868820946683388808)
XLA Ops:
  0.6 0.6 %pad_add_fusion.place_ref = s32[2]{0:T(128)} fusion(s32[1]{0:T(128)} %bitcast.1, s32[1]{0:T(128)} %bitcast), kind=kLoop, calls=%fused_computation.2 | loop fusion | flops 2 | bytes 16 | tf_op jit(solution)/shard_map/stack | solution.py:263
  1.3 0.6 pad_add_fusion.1.index_ref
  1.9 17.7 %shard_map.85 = (bf16[128,512]{1,0:T(8,128)(2,1)}, bf16[128,512]{1,0:T(8,128)(2,1)}, bf16[128,512]{1,0:T(8,128)(2,1)}, bf16[128,512]{1,0:T(8,128)(2,1)}) custom-call(s32[4]{0:T(128)} %pad_add_fusion.1.index_ref, bf16[128,4096]{1,0:T(8,128)(2,1)} %x_hbm.1), custom_call_target="tpu_custom_call" | custom-call | bytes 1048576 | tf_op jit(solution)/shard_map/pallas_call | solution.py:180
  19.6 7.0 %shard_map.86 = (bf16[128,256]{1,0:T(8,128)(2,1)}, bf16[128,256]{1,0:T(8,128)(2,1)}, bf16[128,2048]{1,0:T(8,128)(2,1)}, bf16[2,1024,128]{2,1,0:T(8,128)(2,1)}) custom-call(s32[2]{0:T(128)} %pad_add_fusion.place_ref, bf16[128,2048]{1,0:T(8,128)(2,1)} %q_hbm.1, bf16[128,256]{1,0:T(8,128)(2,1)} %k_ref.1, bf16[128,256]{1,0:T(8,128)(2,1)} %v_hbm.1, ...), custom_call_target="tpu_custom_call" | custom-call | flops 536870912 | bytes 3670016 | tf_op jit(solution)/shard_map/pallas_call | solution.py:279
  26.7 0.5 collective-permute-start
  27.2 3.7 %collective-permute-start.5 = (bf16[128,512]{1,0:T(8,128)(2,1)S(1)}, bf16[128,512]{1,0:T(8,128)(2,1)S(1)}, u32[]{:S(2)}, u32[]{:S(2)}) collective-permute-start(bf16[128,512]{1,0:T(8,128)(2,1)S(1)} %copy-done.8), channel_id=1, source_target_pairs={{0,16},{1,21},{2,26},{3,31},{4,20},{5,17},{6,30},{7,27},{8,24},{9,... | collective-permute-start | bytes 393224 | tf_op jit(solution)/shard_map/ppermute | solution.py:204
  30.9 1.5 %collective-permute-start.9 = (bf16[128,256]{1,0:T(8,128)(2,1)}, bf16[128,256]{1,0:T(8,128)(2,1)S(1)}, u32[]{:S(2)}, u32[]{:S(2)}) collective-permute-start(bf16[128,256]{1,0:T(8,128)(2,1)} %get-tuple-element.22.gk_ref.refs_8_), channel_id=1, source_target_pairs={{0,4},{1,5},{2,6},{3,7},{4,0},{5,1},{6,2},{7,3},{8,12},{9,13},{10,... | collective-permute-start | bytes 196616 | tf_op jit(solution)/shard_map/ppermute | solution.py:204
  32.4 1.6 %collective-permute-start.10 = (bf16[128,256]{1,0:T(8,128)(2,1)}, bf16[128,256]{1,0:T(8,128)(2,1)S(1)}, u32[]{:S(2)}, u32[]{:S(2)}) collective-permute-start(bf16[128,256]{1,0:T(8,128)(2,1)} %get-tuple-element.22.gk_ref.refs_8_), channel_id=1, source_target_pairs={{0,8},{1,9},{2,10},{3,11},{4,12},{5,13},{6,14},{7,15},{8,0},{9,1},... | collective-permute-start | bytes 196616 | tf_op jit(solution)/shard_map/ppermute | solution.py:204
  34.3 4.0 %shard_map.88.kept_ref = bf16[2,1024,128]{2,1,0:T(8,128)(2,1)} custom-call(s32[2]{0:T(128)} %pad_add_fusion.place_ref, bf16[128,256]{1,0:T(8,128)(2,1)} %get-tuple-element.22.gk_ref.refs_8_, bf16[128,256]{1,0:T(8,128)(2,1)} %get-tuple-element.23.gv_ref, bf16[2,4096,256]{2,1,0:T(8,128)(2,1)} %p_hbm.3), custom_call_target="tpu_custom_call" | custom-call | flops 268435456 | bytes 2097152 | tf_op jit(solution)/shard_map/pallas_call | solution.py:314
  38.3 2.5 %collective-permute-start.14 = (bf16[128,256]{1,0:T(8,128)(2,1)S(1)}, bf16[128,256]{1,0:T(8,128)(2,1)S(1)}, u32[]{:S(2)}, u32[]{:S(2)}) collective-permute-start(bf16[128,256]{1,0:T(8,128)(2,1)S(1)} %copy-done.3), channel_id=1, source_target_pairs={{0,24},{1,25},{2,26},{3,27},{4,28},{5,29},{6,30},{7,31},{8,16},{9,... | collective-permute-start | bytes 196616 | tf_op jit(solution)/shard_map/ppermute | solution.py:204
  40.8 0.5 collective-permute-start.2
  41.4 0.7 %collective-permute-start.3 = (bf16[128,512]{1,0:T(8,128)(2,1)S(1)}, bf16[128,512]{1,0:T(8,128)(2,1)S(1)}, u32[]{:S(2)}, u32[]{:S(2)}) collective-permute-start(bf16[128,512]{1,0:T(8,128)(2,1)S(1)} %copy-done.6), channel_id=1, source_target_pairs={{0,8},{1,13},{2,10},{3,15},{4,12},{5,9},{6,14},{7,11},{8,0},{9,5},... | collective-permute-start | bytes 393224 | tf_op jit(solution)/shard_map/ppermute | solution.py:204
  42.1 1.9 %collective-permute-start.6 = (bf16[128,512]{1,0:T(8,128)(2,1)S(1)}, bf16[128,512]{1,0:T(8,128)(2,1)S(1)}, u32[]{:S(2)}, u32[]{:S(2)}) collective-permute-start(bf16[128,512]{1,0:T(8,128)(2,1)S(1)} %collective-permute-done.5.refs_4_), channel_id=1, source_target_pairs={{0,2},{1,3},{2,0},{3,1},{4,6},{5,7},{6,4},{7,5},{8,10},{9,11},{10,... | collective-permute-start | bytes 393224 | tf_op jit(solution)/shard_map/ppermute | solution.py:207
  44.0 1.7 %fusion = bf16[1024,128]{1,0:T(8,128)(2,1)} fusion(bf16[2,1024,128]{2,1,0:T(8,128)(2,1)S(1)} %collective-permute-done.came_ref, bf16[2,1024,128]{2,1,0:T(8,128)(2,1)} %shard_map.88.kept_ref), kind=kLoop, calls=%fused_computation.1 | loop fusion | flops 524288 | bytes 786432 | tf_op jit(solution)/shard_map/convert_element_type | solution.py:327
  45.8 1.5 %collective-permute-start.11 = (bf16[128,256]{1,0:T(8,128)(2,1)S(1)}, bf16[128,256]{1,0:T(8,128)(2,1)S(1)}, u32[]{:S(2)}, u32[]{:S(2)}) collective-permute-start(bf16[128,256]{1,0:T(8,128)(2,1)S(1)} %collective-permute-done.10.refs_10_), channel_id=1, source_target_pairs={{0,4},{1,5},{2,6},{3,7},{4,0},{5,1},{6,2},{7,3},{8,12},{9,13},{10,... | collective-permute-start | bytes 196616 | tf_op jit(solution)/shard_map/ppermute | solution.py:204
  47.3 0.8 %collective-permute-start.13 = (bf16[128,256]{1,0:T(8,128)(2,1)S(1)}, bf16[128,256]{1,0:T(8,128)(2,1)S(1)}, u32[]{:S(2)}, u32[]{:S(2)}) collective-permute-start(bf16[128,256]{1,0:T(8,128)(2,1)S(1)} %collective-permute-done.12.refs_12_), channel_id=1, source_target_pairs={{0,4},{1,5},{2,6},{3,7},{4,0},{5,1},{6,2},{7,3},{8,12},{9,13},{10,... | collective-permute-start | bytes 196616 | tf_op jit(solution)/shard_map/ppermute | solution.py:204
  48.1 1.9 %collective-permute-done.11.refs_11_ = bf16[128,256]{1,0:T(8,128)(2,1)S(1)} collective-permute-done((bf16[128,256]{1,0:T(8,128)(2,1)S(1)}, bf16[128,256]{1,0:T(8,128)(2,1)S(1)}, u32[]{:S(2)}, u32[]{:S(2)}) %collective-permute-start.11) | collective-permute-done | bytes 65568 | tf_op jit(solution)/shard_map/ppermute | solution.py:204
  50.1 0.5 collective-permute-start.8
  50.6 1.0 %collective-permute-done.13.refs_13_ = bf16[128,256]{1,0:T(8,128)(2,1)S(1)} collective-permute-done((bf16[128,256]{1,0:T(8,128)(2,1)S(1)}, bf16[128,256]{1,0:T(8,128)(2,1)S(1)}, u32[]{:S(2)}, u32[]{:S(2)}) %collective-permute-start.13) | collective-permute-done | bytes 65568 | tf_op jit(solution)/shard_map/ppermute | solution.py:204
  51.6 0.8 %collective-permute-start.15 = (bf16[128,256]{1,0:T(8,128)(2,1)S(1)}, bf16[128,256]{1,0:T(8,128)(2,1)S(1)}, u32[]{:S(2)}, u32[]{:S(2)}) collective-permute-start(bf16[128,256]{1,0:T(8,128)(2,1)S(1)} %collective-permute-done.14.refs_14_), channel_id=1, source_target_pairs={{0,4},{1,5},{2,6},{3,7},{4,0},{5,1},{6,2},{7,3},{8,12},{9,13},{10,... | collective-permute-start | bytes 196616 | tf_op jit(solution)/shard_map/ppermute | solution.py:204
  52.4 0.6 slice.11
  57.6 1.1 %shard_map.87 = bf16[128,2048]{1,0:T(8,128)(2,1)} custom-call(bf16[128,2048]{1,0:T(8,128)(2,1)S(1)} %copy-done.1, bf16[128,256]{1,0:T(8,128)(2,1)S(1)} %copy-done.2), custom_call_target="tpu_custom_call" | custom-call | flops 67108864 | bytes 1048576 | tf_op jit(solution)/shard_map/pallas_call | solution.py:339
  58.8 1.9 %shard_map.90 = f32[512,256]{1,0:T(8,128)} custom-call(s32[8]{0:T(128)S(1)} %stack.55.slot_ref, bf16[128,512]{1,0:T(8,128)(2,1)S(1)} %copy-done.4, bf16[128,512]{1,0:T(8,128)(2,1)S(1)} %collective-permute-done.2.refs_1_, bf16[128,512]{1,0:T(8,128)(2,1)S(1)} %collective-permute-done.3.refs_2_, bf16[128,512]{1,0:T(8,128)(2,1)S(1)} %collective-permute-done.4.refs_3_, ...), custom_call_target="tpu_custom_call" | custom-call | flops 268435456 | bytes 1572864 | tf_op jit(solution)/shard_map/pallas_call | solution.py:234
  60.7 0.9 %shard_map.89 = bf16[128,1024]{1,0:T(8,128)(2,1)} custom-call(bf16[2,1024,128]{2,1,0:T(8,128)(2,1)S(1)} %copy-done, bf16[2,1024,128]{2,1,0:T(8,128)(2,1)S(1)} %collective-permute-done.came_ref, bf16[1024,128]{1,0:T(8,128)(2,1)S(1)} %collective-permute-done.1.refs_0_), custom_call_target="tpu_custom_call" | custom-call | flops 131072 | bytes 1048576 | tf_op jit(solution)/shard_map/pallas_call | solution.py:330
  (37 shorter events, 0.6 us)
Async XLA Ops:
  19.6 21.3 %copy-start.7 = (bf16[128,512]{1,0:T(8,128)(2,1)S(1)}, bf16[128,512]{1,0:T(8,128)(2,1)}, u32[]{:S(2)}) copy-start(bf16[128,512]{1,0:T(8,128)(2,1)} %get-tuple-element.26) | copy-start | bytes 393220
  19.6 21.8 %copy-start.6 = (bf16[128,512]{1,0:T(8,128)(2,1)S(1)}, bf16[128,512]{1,0:T(8,128)(2,1)}, u32[]{:S(2)}) copy-start(bf16[128,512]{1,0:T(8,128)(2,1)} %get-tuple-element.27) | copy-start | bytes 393220
  19.6 32.8 %copy-start.5 = (s32[2]{0:T(128)S(1)}, s32[2]{0:T(128)}, u32[]{:S(2)}) copy-start(s32[2]{0:T(128)} %pad_add_fusion.place_ref) | copy-start | bytes 28
  19.6 38.0 %copy-start.2 = (bf16[128,256]{1,0:T(8,128)(2,1)S(1)}, bf16[128,256]{1,0:T(8,128)(2,1)}, u32[]{:S(2)}) copy-start(bf16[128,256]{1,0:T(8,128)(2,1)} %k_ref.1) | copy-start | bytes 196612
  26.7 11.6 %copy-start.3 = (bf16[128,256]{1,0:T(8,128)(2,1)S(1)}, bf16[128,256]{1,0:T(8,128)(2,1)}, u32[]{:S(2)}) copy-start(bf16[128,256]{1,0:T(8,128)(2,1)} %get-tuple-element.22.gk_ref.refs_8_) | copy-start | bytes 196612
  26.7 30.9 %copy-start.1 = (bf16[128,2048]{1,0:T(8,128)(2,1)S(1)}, bf16[128,2048]{1,0:T(8,128)(2,1)}, u32[]{:S(2)}) copy-start(bf16[128,2048]{1,0:T(8,128)(2,1)} %get-tuple-element.21.ds_ref) | copy-start | bytes 1572868
  26.7 32.1 %copy-start.4 = (bf16[128,512]{1,0:T(8,128)(2,1)S(1)}, bf16[128,512]{1,0:T(8,128)(2,1)}, u32[]{:S(2)}) copy-start(bf16[128,512]{1,0:T(8,128)(2,1)} %get-tuple-element.25.refs_0_) | copy-start | bytes 393220
  26.7 15.4 %collective-permute-start = (bf16[2,1024,128]{2,1,0:T(8,128)(2,1)}, bf16[2,1024,128]{2,1,0:T(8,128)(2,1)S(1)}, u32[]{:S(2)}, u32[]{:S(2)}) collective-permute-start(bf16[2,1024,128]{2,1,0:T(8,128)(2,1)} %get-tuple-element.24), channel_id=1, source_target_pairs={{0,1},{1,0},{2,3},{3,2},{4,5},{5,4},{6,7},{7,6},{8,9},{9,8},{10,11... | collective-permute-start | bytes 1572872 | tf_op jit(solution)/shard_map/ppermute | solution.py:313
  27.2 14.2 %collective-permute-start.5 = (bf16[128,512]{1,0:T(8,128)(2,1)S(1)}, bf16[128,512]{1,0:T(8,128)(2,1)S(1)}, u32[]{:S(2)}, u32[]{:S(2)}) collective-permute-start(bf16[128,512]{1,0:T(8,128)(2,1)S(1)} %copy-done.8), channel_id=1, source_target_pairs={{0,16},{1,21},{2,26},{3,31},{4,20},{5,17},{6,30},{7,27},{8,24},{9,... | collective-permute-start | bytes 393224 | tf_op jit(solution)/shard_map/ppermute | solution.py:204
  30.9 7.4 %collective-permute-start.9 = (bf16[128,256]{1,0:T(8,128)(2,1)}, bf16[128,256]{1,0:T(8,128)(2,1)S(1)}, u32[]{:S(2)}, u32[]{:S(2)}) collective-permute-start(bf16[128,256]{1,0:T(8,128)(2,1)} %get-tuple-element.22.gk_ref.refs_8_), channel_id=1, source_target_pairs={{0,4},{1,5},{2,6},{3,7},{4,0},{5,1},{6,2},{7,3},{8,12},{9,13},{10,... | collective-permute-start | bytes 196616 | tf_op jit(solution)/shard_map/ppermute | solution.py:204
  32.4 8.4 %collective-permute-start.10 = (bf16[128,256]{1,0:T(8,128)(2,1)}, bf16[128,256]{1,0:T(8,128)(2,1)S(1)}, u32[]{:S(2)}, u32[]{:S(2)}) collective-permute-start(bf16[128,256]{1,0:T(8,128)(2,1)} %get-tuple-element.22.gk_ref.refs_8_), channel_id=1, source_target_pairs={{0,8},{1,9},{2,10},{3,11},{4,12},{5,13},{6,14},{7,15},{8,0},{9,1},... | collective-permute-start | bytes 196616 | tf_op jit(solution)/shard_map/ppermute | solution.py:204
  34.0 11.7 %collective-permute-start.12 = (bf16[128,256]{1,0:T(8,128)(2,1)}, bf16[128,256]{1,0:T(8,128)(2,1)S(1)}, u32[]{:S(2)}, u32[]{:S(2)}) collective-permute-start(bf16[128,256]{1,0:T(8,128)(2,1)} %get-tuple-element.22.gk_ref.refs_8_), channel_id=1, source_target_pairs={{0,16},{1,17},{2,18},{3,19},{4,20},{5,21},{6,22},{7,23},{8,24},{9,... | collective-permute-start | bytes 196616 | tf_op jit(solution)/shard_map/ppermute | solution.py:204
  38.3 22.4 %copy-start = (bf16[2,1024,128]{2,1,0:T(8,128)(2,1)S(1)}, bf16[2,1024,128]{2,1,0:T(8,128)(2,1)}, u32[]{:S(2)}) copy-start(bf16[2,1024,128]{2,1,0:T(8,128)(2,1)} %shard_map.88.kept_ref) | copy-start | bytes 1572868
  38.3 7.5 %collective-permute-start.14 = (bf16[128,256]{1,0:T(8,128)(2,1)S(1)}, bf16[128,256]{1,0:T(8,128)(2,1)S(1)}, u32[]{:S(2)}, u32[]{:S(2)}) collective-permute-start(bf16[128,256]{1,0:T(8,128)(2,1)S(1)} %copy-done.3), channel_id=1, source_target_pairs={{0,24},{1,25},{2,26},{3,27},{4,28},{5,29},{6,30},{7,31},{8,16},{9,... | collective-permute-start | bytes 196616 | tf_op jit(solution)/shard_map/ppermute | solution.py:204
  40.8 6.5 %collective-permute-start.2 = (bf16[128,512]{1,0:T(8,128)(2,1)S(1)}, bf16[128,512]{1,0:T(8,128)(2,1)S(1)}, u32[]{:S(2)}, u32[]{:S(2)}) collective-permute-start(bf16[128,512]{1,0:T(8,128)(2,1)S(1)} %copy-done.7), channel_id=1, source_target_pairs={{0,4},{1,5},{2,6},{3,7},{4,0},{5,1},{6,2},{7,3},{8,12},{9,13},{10,... | collective-permute-start | bytes 393224 | tf_op jit(solution)/shard_map/ppermute | solution.py:204
  41.4 6.8 %collective-permute-start.3 = (bf16[128,512]{1,0:T(8,128)(2,1)S(1)}, bf16[128,512]{1,0:T(8,128)(2,1)S(1)}, u32[]{:S(2)}, u32[]{:S(2)}) collective-permute-start(bf16[128,512]{1,0:T(8,128)(2,1)S(1)} %copy-done.6), channel_id=1, source_target_pairs={{0,8},{1,13},{2,10},{3,15},{4,12},{5,9},{6,14},{7,11},{8,0},{9,5},... | collective-permute-start | bytes 393224 | tf_op jit(solution)/shard_map/ppermute | solution.py:204
  42.1 8.0 %collective-permute-start.6 = (bf16[128,512]{1,0:T(8,128)(2,1)S(1)}, bf16[128,512]{1,0:T(8,128)(2,1)S(1)}, u32[]{:S(2)}, u32[]{:S(2)}) collective-permute-start(bf16[128,512]{1,0:T(8,128)(2,1)S(1)} %collective-permute-done.5.refs_4_), channel_id=1, source_target_pairs={{0,2},{1,3},{2,0},{3,1},{4,6},{5,7},{6,4},{7,5},{8,10},{9,11},{10,... | collective-permute-start | bytes 393224 | tf_op jit(solution)/shard_map/ppermute | solution.py:207
  45.7 15.0 %collective-permute-start.1 = (bf16[1024,128]{1,0:T(8,128)(2,1)}, bf16[1024,128]{1,0:T(8,128)(2,1)S(1)}, u32[]{:S(2)}, u32[]{:S(2)}) collective-permute-start(bf16[1024,128]{1,0:T(8,128)(2,1)} %fusion), channel_id=1, source_target_pairs={{0,2},{1,3},{2,0},{3,1},{4,6},{5,7},{6,4},{7,5},{8,10},{9,11},{10,... | collective-permute-start | bytes 786440 | tf_op jit(solution)/shard_map/ppermute | solution.py:329
  45.8 4.3 %collective-permute-start.11 = (bf16[128,256]{1,0:T(8,128)(2,1)S(1)}, bf16[128,256]{1,0:T(8,128)(2,1)S(1)}, u32[]{:S(2)}, u32[]{:S(2)}) collective-permute-start(bf16[128,256]{1,0:T(8,128)(2,1)S(1)} %collective-permute-done.10.refs_10_), channel_id=1, source_target_pairs={{0,4},{1,5},{2,6},{3,7},{4,0},{5,1},{6,2},{7,3},{8,12},{9,13},{10,... | collective-permute-start | bytes 196616 | tf_op jit(solution)/shard_map/ppermute | solution.py:204
  47.3 4.3 %collective-permute-start.13 = (bf16[128,256]{1,0:T(8,128)(2,1)S(1)}, bf16[128,256]{1,0:T(8,128)(2,1)S(1)}, u32[]{:S(2)}, u32[]{:S(2)}) collective-permute-start(bf16[128,256]{1,0:T(8,128)(2,1)S(1)} %collective-permute-done.12.refs_12_), channel_id=1, source_target_pairs={{0,4},{1,5},{2,6},{3,7},{4,0},{5,1},{6,2},{7,3},{8,12},{9,13},{10,... | collective-permute-start | bytes 196616 | tf_op jit(solution)/shard_map/ppermute | solution.py:204
  48.1 10.6 %collective-permute-start.7 = (bf16[128,512]{1,0:T(8,128)(2,1)S(1)}, bf16[128,512]{1,0:T(8,128)(2,1)S(1)}, u32[]{:S(2)}, u32[]{:S(2)}) collective-permute-start(bf16[128,512]{1,0:T(8,128)(2,1)S(1)} %collective-permute-done.5.refs_4_), channel_id=1, source_target_pairs={{0,1},{1,0},{2,3},{3,2},{4,5},{5,4},{6,7},{7,6},{8,9},{9,8},{10,11... | collective-permute-start | bytes 393224 | tf_op jit(solution)/shard_map/ppermute | solution.py:207
  50.1 8.7 %collective-permute-start.4 = (bf16[128,512]{1,0:T(8,128)(2,1)S(1)}, bf16[128,512]{1,0:T(8,128)(2,1)S(1)}, u32[]{:S(2)}, u32[]{:S(2)}) collective-permute-start(bf16[128,512]{1,0:T(8,128)(2,1)S(1)} %collective-permute-done.3.refs_2_), channel_id=1, source_target_pairs={{0,1},{1,0},{2,3},{3,2},{4,5},{5,4},{6,7},{7,6},{8,9},{9,8},{10,11... | collective-permute-start | bytes 393224 | tf_op jit(solution)/shard_map/ppermute | solution.py:207
  50.1 8.7 %collective-permute-start.8 = (bf16[128,512]{1,0:T(8,128)(2,1)S(1)}, bf16[128,512]{1,0:T(8,128)(2,1)S(1)}, u32[]{:S(2)}, u32[]{:S(2)}) collective-permute-start(bf16[128,512]{1,0:T(8,128)(2,1)S(1)} %collective-permute-done.6.refs_5_), channel_id=1, source_target_pairs={{0,1},{1,0},{2,3},{3,2},{4,5},{5,4},{6,7},{7,6},{8,9},{9,8},{10,11... | collective-permute-start | bytes 393224 | tf_op jit(solution)/shard_map/ppermute | solution.py:207
  51.6 7.2 %collective-permute-start.15 = (bf16[128,256]{1,0:T(8,128)(2,1)S(1)}, bf16[128,256]{1,0:T(8,128)(2,1)S(1)}, u32[]{:S(2)}, u32[]{:S(2)}) collective-permute-start(bf16[128,256]{1,0:T(8,128)(2,1)S(1)} %collective-permute-done.14.refs_14_), channel_id=1, source_target_pairs={{0,4},{1,5},{2,6},{3,7},{4,0},{5,1},{6,2},{7,3},{8,12},{9,13},{10,... | collective-permute-start | bytes 196616 | tf_op jit(solution)/shard_map/ppermute | solution.py:204
  (1 other events, 7.7 us)

commit v3 on v2

v3 whole, which is shorter than its diff:
```python
import math

import jax
import jax.numpy as jnp
from jax import lax
from jax.experimental import pallas as pl
from jax.experimental.pallas import tpu as pltpu
from jax.sharding import PartitionSpec as P

HEAD_SIZE = 128
F32 = jnp.float32
BF16 = jnp.bfloat16
NN = (((1,), (0,)), ((), ()))
NT = (((1,), (1,)), ((), ()))
TN = (((0,), (0,)), ((), ()))
IN_HBM = pl.BlockSpec(memory_space=pltpu.HBM)
ANYWHERE = pl.BlockSpec(memory_space=pl.ANY)
IN_VMEM = pl.BlockSpec(memory_space=pltpu.VMEM)
CHUNK = 512
PARAMS = pltpu.CompilerParams(vmem_limit_bytes=24 * 1024 * 1024)
WHOLE = pltpu.CompilerParams()


def dot(a, b, dims=NN):
    return lax.dot_general(a, b, dims, preferred_element_type=F32)


def cost(flops, moved, transcendentals=0):
    return pl.CostEstimate(flops=flops, bytes_accessed=moved, transcendentals=transcendentals)


def attention_group(g, q, k, v, do, gk_ref, ds):
    length = q.shape[0]
    per_group = q.shape[1] // k.shape[1]
    together = 2 - per_group % 2
    wide = together * length
    scale = 1.0 / math.sqrt(HEAD_SIZE)
    targets = lax.broadcasted_iota(jnp.int32, (length, wide), 0)
    positions = lax.rem(lax.broadcasted_iota(jnp.int32, (length, wide), 1), length)
    allowed = targets <= positions
    cols = slice(g * HEAD_SIZE, (g + 1) * HEAD_SIZE)
    key, value = k[:, cols], v[:, cols]
    acc_k = jnp.zeros((length, HEAD_SIZE), F32)
    acc_v = jnp.zeros((length, HEAD_SIZE), F32)
    for h in range(0, per_group, together):
        at = [(g * per_group + h + e) * HEAD_SIZE for e in range(together)]
        query = jnp.concatenate([q[:, s : s + HEAD_SIZE] for s in at], axis=0)
        grad = jnp.concatenate([do[:, s : s + HEAD_SIZE] for s in at], axis=0)
        scores = jnp.where(allowed, dot(key, query, NT), -1e30)
        raw = jnp.exp((scores - jnp.max(scores, axis=0, keepdims=True)) * scale)
        probs = raw * (1.0 / jnp.sum(raw, axis=0, keepdims=True))
        grad_probs = dot(value, grad, NT)
        delta = jnp.sum(probs * grad_probs, axis=0, keepdims=True)
        grad_scores = (probs * (grad_probs - delta)).astype(BF16)
        ds[:, at[0] : at[0] + wide] = grad_scores
        acc_v += dot(probs.astype(BF16), grad)
        acc_k += dot(grad_scores, query)
    gk_ref[:, cols] = (acc_k * scale).astype(BF16)
    return acc_v.astype(BF16)


def attention_kernel(
    q_hbm, k_hbm, v_hbm, do_hbm, p_hbm,
    gk_ref, ds_hbm, sent_hbm, kept_hbm,
    q, k, v, do, p, ds, partial, sems, p_sems, out_sems,
):
    kv_heads = k.shape[1] // HEAD_SIZE
    group = q.shape[1] // kv_heads
    groups, features = p.shape[0], p.shape[2]
    chips = groups // 2
    member = lax.axis_index("mp")
    chip, core = lax.div(member, 2), lax.rem(member, 2)
    small = [
        pltpu.make_async_copy(k_hbm, k, sems.at[0]),
        pltpu.make_async_copy(v_hbm, v, sems.at[1]),
    ]
    large, stored = [], []
    for g in range(kv_heads):
        cols = pl.ds(g * group, group)
        large.append((
            pltpu.make_async_copy(q_hbm.at[:, cols], q.at[:, cols], sems.at[2 + 2 * g]),
            pltpu.make_async_copy(do_hbm.at[:, cols], do.at[:, cols], sems.at[3 + 2 * g]),
        ))
        stored.append(pltpu.make_async_copy(ds.at[:, cols], ds_hbm.at[:, cols], out_sems.at[g]))
    blocks = []
    for b in range(groups):
        column = core if b >= chips else 1 - core
        start = (2 * lax.rem(chip + b + 1, chips) + column) * features
        rows = pl.ds(pl.multiple_of(start, features), features)
        blocks.append(pltpu.make_async_copy(p_hbm.at[:, rows, :], p.at[b], p_sems.at[b]))
    for copy in small:
        copy.start()
    for pair in large:
        for copy in pair:
            copy.start()
    for copy in blocks:
        copy.start()
    for copy in small:
        copy.wait()
    values = []
    for g in range(kv_heads):
        for copy in large[g]:
            copy.wait()
        values.append(attention_group(g, q, k, v, do, gk_ref, ds))
        stored[g].start()
    gk = gk_ref[...]
    gv = jnp.concatenate(values, axis=1)
    step = min(CHUNK, features)
    for b in range(groups):
        blocks[b].wait()
        for at in range(0, features, step):
            rows = slice(at, at + step)
            total = dot(p[b, 0, rows, :], gk, NT) + dot(p[b, 1, rows, :], gv, NT)
            partial[b, rows, :] = total.astype(BF16)
        target = sent_hbm.at[b] if b < chips else kept_hbm.at[b - chips]
        stored.append(pltpu.make_async_copy(partial.at[b], target, out_sems.at[kv_heads + b]))
        stored[-1].start()
    for copy in stored:
        copy.wait()


def query_kernel(ds_ref, k_ref, gq_ref):
    kv_heads = k_ref.shape[1] // HEAD_SIZE
    per_group = gq_ref.shape[1] // k_ref.shape[1]
    scale = 1.0 / math.sqrt(HEAD_SIZE)
    for g in range(kv_heads):
        key = k_ref[:, g * HEAD_SIZE : (g + 1) * HEAD_SIZE]
        for h in range(per_group):
            at = (g * per_group + h) * HEAD_SIZE
            grad = dot(ds_ref[:, at : at + HEAD_SIZE], key, TN) * scale
            gq_ref[:, at : at + HEAD_SIZE] = grad.astype(BF16)


def input_kernel(kept_ref, came_ref, *refs):
    out_ref = refs[-1]
    total = kept_ref[len(refs) - 1].astype(F32) + came_ref[len(refs) - 1].astype(F32)
    for ref in refs[:-1]:
        total += ref[...].astype(F32)
    out_ref[...] = total.T.astype(BF16)


def turned_kernel(mine_ref, theirs_ref, next_ref, x_hbm, out_ref, own, sem):
    rows, width = next_ref.shape
    parts = out_ref.shape[1] // rows
    far, groups = parts // 2, parts // 2
    part, member = lax.axis_index("dp"), lax.axis_index("mp")
    cols = pl.ds(pl.multiple_of(part * width, width), width)
    copy = pltpu.make_async_copy(x_hbm.at[:, cols], own, sem)
    copy.start()

    def put(k, piece):
        place = 2 * lax.rem(k, far) + lax.div(k, far)
        out_ref[:, pl.ds(pl.multiple_of(place * rows, rows), rows)] = piece.T

    partners = [lambda m, j=j: far + (m ^ j) for j in range(0, groups, 2)]
    partners += [lambda m, k=k: k + lax.rem(m, 2) for k in range(2, far, 2)]
    for at, partner in enumerate(partners):
        put(partner(member), mine_ref[at * rows : (at + 1) * rows, :])
        put(partner(member ^ 1), theirs_ref[at * rows : (at + 1) * rows, :])
    put(jnp.int32(1), next_ref[...])
    copy.wait()
    put(jnp.int32(0), own[...])


def weights_kernel(x_ref, *refs):
    keys, out_ref = refs[:-1], refs[-1]
    rows = keys[0].shape[0]
    total = dot(x_ref[:, :rows], keys[0][...])
    for j in range(1, len(keys)):
        total += dot(x_ref[:, j * rows : (j + 1) * rows], keys[j][...])
    out_ref[...] = total * (1.0 / (2 * len(keys)))


def along_dp(array, partner, parts, groups):
    pairs = [
        (i * groups + m, (i ^ partner(m)) * groups + m)
        for i in range(parts)
        for m in range(groups)
    ]
    return lax.ppermute(array, ("dp", "mp"), pairs)


def along_mp(array, bit, groups):
    return lax.ppermute(array, "mp", [(m, m ^ bit) for m in range(groups)])


def sent_inputs(inputs, parts, groups):
    far = parts // 2
    part, member = lax.axis_index("dp"), lax.axis_index("mp")
    rows, width = inputs.shape[0], inputs.shape[1] // parts

    def block(k):
        return lax.dynamic_slice(inputs, (0, (part ^ k) * width), (rows, width))

    arrived = [along_dp(block(far + member), lambda m: far + m, parts, groups)]
    for k in range(2, far, 2):
        block_k = block(k + lax.rem(member, 2))
        arrived.append(along_dp(block_k, lambda m, k=k: k + m % 2, parts, groups))
    return arrived, block(1)


def exchanged_weights(inputs, arrived, next_block, grad_key, parts, groups):
    far = parts // 2
    rows, columns = grad_key.shape
    width = inputs.shape[1] // parts

    keys = [jnp.concatenate([grad_key, along_dp(grad_key, lambda m: far, parts, groups)])]
    next_inputs = along_dp(next_block, lambda m: 1, parts, groups)
    shared = {0: arrived[0]}
    bit = groups // 2
    while bit > 1:
        for j in list(shared):
            shared[j ^ bit] = along_mp(shared[j], bit, groups)
        bit //= 2
    mine = jnp.concatenate([shared[j] for j in range(0, groups, 2)] + arrived[1:])
    theirs = along_mp(mine, 1, groups)
    by_k = {0: keys[0]}
    bit = far // 2
    while bit:
        for k in list(by_k):
            by_k[k ^ bit] = along_dp(by_k[k], lambda m, bit=bit: bit, parts, groups)
        bit //= 2

    turned = pl.pallas_call(
        turned_kernel,
        in_specs=[IN_VMEM, IN_VMEM, IN_VMEM, IN_HBM],
        out_specs=IN_VMEM,
        out_shape=jax.ShapeDtypeStruct((width, parts * rows), inputs.dtype),
        scratch_shapes=[pltpu.VMEM((rows, width), inputs.dtype), pltpu.SemaphoreType.DMA],
        compiler_params=PARAMS,
        cost_estimate=cost(0, 4 * parts * rows * width),
    )(mine, theirs, next_inputs, inputs)
    return pl.pallas_call(
        weights_kernel,
        in_specs=[IN_VMEM] * (1 + far),
        out_specs=IN_VMEM,
        out_shape=jax.ShapeDtypeStruct((width, columns), F32),
        compiler_params=PARAMS,
        cost_estimate=cost(
            2 * parts * rows * width * columns, 2 * parts * rows * (width + columns)
        ),
    )(turned, *[by_k[k] for k in range(far)])


def gathered_weights(inputs, grad_key, parts):
    rows = inputs.shape[0]
    width = inputs.shape[1] // parts
    blocks = inputs.reshape(rows, parts, width).transpose(1, 0, 2)
    mine = lax.all_to_all(blocks, "dp", split_axis=0, concat_axis=0, tiled=True)
    keys = lax.all_gather(grad_key, "dp", axis=0)
    return jnp.einsum("psd,psc->dc", mine, keys, preferred_element_type=F32) / parts


def body(query_states, key_states, value_states, grad_context, inputs_normed, projections):
    parts = lax.axis_size("dp")
    groups = lax.axis_size("mp")
    chips = groups // 2
    rows, width = key_states.shape
    query_width = query_states.shape[1]
    features = projections.shape[1] // groups
    kv_heads = width // HEAD_SIZE
    blocks = jax.ShapeDtypeStruct((chips, features, rows), BF16)
    exchange = parts == 2 * groups and inputs_normed.shape[1] % (parts * 128) == 0
    if exchange:
        arrived, next_block = sent_inputs(inputs_normed, parts, groups)

    grad_key, grad_scores, sent, kept = pl.pallas_call(
        attention_kernel,
        in_specs=[IN_HBM] * 5,
        out_specs=[IN_VMEM, ANYWHERE, ANYWHERE, ANYWHERE],
        out_shape=(
            jax.ShapeDtypeStruct((rows, width), BF16),
            jax.ShapeDtypeStruct((rows, query_width), BF16),
            blocks,
            blocks,
        ),
        scratch_shapes=[
            pltpu.VMEM((rows, query_width), BF16),
            pltpu.VMEM((rows, width), BF16),
            pltpu.VMEM((rows, width), BF16),
            pltpu.VMEM((rows, query_width), BF16),
            pltpu.VMEM((groups, 2, features, width), BF16),
            pltpu.VMEM((rows, query_width), BF16),
            pltpu.VMEM((groups, features, rows), BF16),
            pltpu.SemaphoreType.DMA((2 + 2 * kv_heads,)),
            pltpu.SemaphoreType.DMA((groups,)),
            pltpu.SemaphoreType.DMA((kv_heads + groups,)),
        ],
        compiler_params=WHOLE,
        cost_estimate=cost(
            8 * rows * rows * query_width + 4 * rows * width * features * groups,
            6 * rows * query_width + 4 * width * features * groups,
            rows * query_width,
        ),
    )(query_states, key_states, value_states, grad_context, projections)

    if exchange:
        grad_weights = exchanged_weights(
            inputs_normed, arrived, next_block, grad_key, parts, groups
        )
    else:
        grad_weights = gathered_weights(inputs_normed, grad_key, parts)

    came = along_mp(sent, 1, groups)
    last = []
    for b in range(chips - 1):
        pair = (kept[b].astype(F32) + came[b].astype(F32)).astype(BF16)
        shift = [(m, (m + 2 * (b + 1)) % groups) for m in range(groups)]
        last.append(lax.ppermute(pair, "mp", shift))
    grad_input = pl.pallas_call(
        input_kernel,
        out_specs=IN_VMEM,
        out_shape=jax.ShapeDtypeStruct((rows, features), BF16),
        compiler_params=PARAMS,
        cost_estimate=cost(rows * features, 8 * rows * features),
    )(kept, came, *last)

    grad_query = pl.pallas_call(
        query_kernel,
        out_shape=jax.ShapeDtypeStruct((rows, query_width), BF16),
        compiler_params=PARAMS,
        cost_estimate=cost(2 * rows * rows * query_width, 4 * rows * query_width),
    )(grad_scores, key_states)
    return (grad_query, grad_input, grad_weights)


def solution(mesh):
    placed = (
        P("dp", "mp"),
        P("dp", "mp"),
        P("dp", "mp"),
        P("dp", "mp"),
        P("dp", None),
        P(None, None, "mp"),
    )
    return jax.shard_map(
        body,
        mesh=mesh,
        in_specs=placed,
        out_specs=(P("dp", "mp"), P("dp", "mp"), P("dp", "mp")),
        check_vma=False,
    )
```

time: 62.1 us -> 38.1 us (0.61)
  Pallas kernels: 32.6 us -> 10.2 us
  waiting for transfers between devices: 2.96 us -> 10.4 us
  starting transfers between devices: 17 us -> 12.4 us
  between operations: 5.32 us -> 0.77 us
  local copies, waits for them, and re-layouts: 0.71 us -> 3.04 us
  other arithmetic: 2.96 us -> 1.02 us
    pallas_call x5 -> x4, Pallas kernels: 31.5 us -> 9.02 us  [the longest x1 6.46 us: body(): pl.pallas_call(attention_kernel, in_specs=[IN_HBM] * 5, out_specs=[IN_VME...]
    ppermute x10 -> x7, waiting for transfers between devices: 2.95 us -> 10.4 us  [along_dp(): return lax.ppermute(array, ('dp', 'mp'), pairs)]
    ppermute x10 -> x7, starting transfers between devices: 14 us -> 8.78 us  [along_dp(): return lax.ppermute(array, ('dp', 'mp'), pairs)]
    unnamed x18 -> x11, local copies, waits for them, and re-layouts: 0.04 us -> 1.96 us
    another operation x2 -> x0, other arithmetic: 1.24 us -> none  [the longest x1 0.65 us: body(): jnp.stack([lax.axis_index('dp'), lax.axis_index('mp')]).astype(jnp.int32)]
    dynamic_slice x0 -> x1, local copies, waits for them, and re-layouts: none -> 1.07 us  [block(): return lax.dynamic_slice(inputs, (0, (part ^ k) * width), (rows, width))]
    ppermute x2 -> x1, starting transfers between devices: 0.62 us -> 1.62 us  [body(): last.append(lax.ppermute(pair, 'mp', shift))]
    convert_element_type x1, other arithmetic: 1.72 us -> 1.02 us  [body(): pair = (kept[b].astype(F32) + came[b].astype(F32)).astype(BF16)]
  transfers between devices with their start and end apart: 16 -> 11, of which waited for: 2 -> 5; matrix products, arithmetic and copies ran while one was open for 4% -> 5% of each run, Pallas kernels for 11% -> 25%
where the time goes in v3:
time: 38.1 us; the launch traced here: 37.8 us
  starting transfers between devices  12.4 us (33%)
  waiting for transfers between devices  10.4 us (27%)
  Pallas kernels  10.2 us (27%)
  local copies, waits for them, and re-layouts  3.04 us (8%)
  other arithmetic  1.02 us (3%)
  between operations  0.77 us (2%)
    ppermute x7, waiting for transfers between devices, along_dp(): return lax.ppermute(array, ('dp', 'mp'), pairs)  10.4 us
    ppermute x7, starting transfers between devices, along_dp(): return lax.ppermute(array, ('dp', 'mp'), pairs)  8.78 us
    pallas_call x1, Pallas kernels, body(): pl.pallas_call(attention_kernel, in_specs=[IN_HBM] * 5, out_specs=[IN_VME...  6.46 us
    ppermute x3, starting transfers between devices, along_mp(): return lax.ppermute(array, 'mp', [(m, m ^ bit) for m in range(groups)])  1.99 us
    unnamed x11, local copies, waits for them, and re-layouts  1.96 us
    ppermute x1, starting transfers between devices, body(): last.append(lax.ppermute(pair, 'mp', shift))  1.62 us
    pallas_call x1, Pallas kernels, exchanged_weights(): pl.pallas_call(weights_kernel, in_specs=[IN_VMEM] * (1 + far), out_specs=...  1.24 us
    pallas_call x1, Pallas kernels, body(): pl.pallas_call(query_kernel, out_shape=jax.ShapeDtypeStruct((rows, query_...  1.14 us
  transfers between devices with their start and end apart: 11, of which 5 were waited for; matrix products, arithmetic and copies ran while one was open for 5% of the time, Pallas kernels for 25%

profile of v3, /device:TPU:0, one launch (start us, length us, event | category | flops | bytes accessed | tf_op | source)
XLA Modules:
  0.0 37.8 jit_solution(10328996123429345467)
XLA Ops:
  0.7 1.1 %constant_dynamic-slice_fusion = (bf16[128,512]{1,0:T(8,128)(2,1)S(1)}, bf16[128,512]{1,0:T(8,128)(2,1)S(1)}, bf16[128,512]{1,0:T(8,128)(2,1)S(1)}) fusion(bf16[128,4096]{1,0:T(8,128)(2,1)} %x_hbm.1, s32[]{:T(128)S(6)} %select_n.11, s32[]{:T(128)S(6)} %select_n.10, s32[]{:T(128)S(6)} %select_n.9), kind=kLoop, calls=%fused_computation.7 | loop fusion | bytes 786444 | tf_op jit(solution)/shard_map/dynamic_slice | solution.py:193
  1.7 4.1 %collective-permute-start.2 = (bf16[128,512]{1,0:T(8,128)(2,1)S(1)}, bf16[128,512]{1,0:T(8,128)(2,1)S(1)}, u32[]{:S(2)}, u32[]{:S(2)}) collective-permute-start(bf16[128,512]{1,0:T(8,128)(2,1)S(1)} %get-tuple-element.13), channel_id=1, source_target_pairs={{0,16},{1,21},{2,26},{3,31},{4,20},{5,17},{6,30},{7,27},{8,24},{9,... | collective-permute-start | bytes 393224 | tf_op jit(solution)/shard_map/ppermute | solution.py:180
  5.8 6.5 %shard_map.85 = (bf16[128,256]{1,0:T(8,128)(2,1)}, bf16[128,2048]{1,0:T(8,128)(2,1)}, bf16[2,1024,128]{2,1,0:T(8,128)(2,1)}, bf16[2,1024,128]{2,1,0:T(8,128)(2,1)}) custom-call(bf16[128,2048]{1,0:T(8,128)(2,1)} %q_hbm.1, bf16[128,256]{1,0:T(8,128)(2,1)} %k_ref.1, bf16[128,256]{1,0:T(8,128)(2,1)} %v_hbm.1, bf16[128,2048]{1,0:T(8,128)(2,1)} %do_hbm.1, ...), custom_call_target="tpu_custom_call" | custom-call | flops 805306368 | bytes 5767168 | tf_op jit(solution)/shard_map/pallas_call | solution.py:267
  12.3 0.5 %collective-permute-start = (bf16[2,1024,128]{2,1,0:T(8,128)(2,1)}, bf16[2,1024,128]{2,1,0:T(8,128)(2,1)S(1)}, u32[]{:S(2)}, u32[]{:S(2)}) collective-permute-start(bf16[2,1024,128]{2,1,0:T(8,128)(2,1)} %get-tuple-element.9), channel_id=1, source_target_pairs={{0,1},{1,0},{2,3},{3,2},{4,5},{5,4},{6,7},{7,6},{8,9},{9,8},{10,11... | collective-permute-start | bytes 1572872 | tf_op jit(solution)/shard_map/ppermute | solution.py:184
  12.9 1.6 %collective-permute-start.4 = (bf16[128,512]{1,0:T(8,128)(2,1)S(1)}, bf16[128,512]{1,0:T(8,128)(2,1)S(1)}, u32[]{:S(2)}, u32[]{:S(2)}) collective-permute-start(bf16[128,512]{1,0:T(8,128)(2,1)S(1)} %get-tuple-element.12), channel_id=1, source_target_pairs={{0,8},{1,13},{2,10},{3,15},{4,12},{5,9},{6,14},{7,11},{8,0},{9,5},... | collective-permute-start | bytes 393224 | tf_op jit(solution)/shard_map/ppermute | solution.py:180
  14.4 0.3 collective-permute-start.7
  14.8 0.9 %constant_dynamic-update-slice_fusion.4 = bf16[256,256]{1,0:T(8,128)(2,1)S(1)} fusion(bf16[128,256]{1,0:T(8,128)(2,1)} %get-tuple-element.10), kind=kLoop, calls=%fused_computation.6 | loop fusion | bytes 131072
  15.7 1.4 %collective-permute-start.3 = (bf16[128,512]{1,0:T(8,128)(2,1)S(1)}, bf16[128,512]{1,0:T(8,128)(2,1)S(1)}, u32[]{:S(2)}, u32[]{:S(2)}) collective-permute-start(bf16[128,512]{1,0:T(8,128)(2,1)S(1)} %collective-permute-done.2), channel_id=1, source_target_pairs={{0,2},{1,3},{2,0},{3,1},{4,6},{5,7},{6,4},{7,5},{8,10},{9,11},{10,... | collective-permute-start | bytes 393224 | tf_op jit(solution)/shard_map/ppermute | solution.py:184
  17.0 4.6 %collective-permute-done.7 = bf16[128,256]{1,0:T(8,128)(2,1)S(1)} collective-permute-done((bf16[128,256]{1,0:T(8,128)(2,1)}, bf16[128,256]{1,0:T(8,128)(2,1)S(1)}, u32[]{:S(2)}, u32[]{:S(2)}) %collective-permute-start.7) | collective-permute-done | bytes 65568 | tf_op jit(solution)/shard_map/ppermute | solution.py:180
  21.7 0.1 collective-permute-start.5
  21.8 1.0 %fusion = bf16[1024,128]{1,0:T(8,128)(2,1)S(1)} fusion(bf16[2,1024,128]{2,1,0:T(8,128)(2,1)S(1)} %collective-permute-done.came_ref, bf16[2,1024,128]{2,1,0:T(8,128)(2,1)} %get-tuple-element.8.kept_ref), kind=kLoop, calls=%fused_computation.1 | loop fusion | flops 524288 | bytes 786432 | tf_op jit(solution)/shard_map/convert_element_type | solution.py:307
  22.8 1.6 %collective-permute-start.1 = (bf16[1024,128]{1,0:T(8,128)(2,1)S(1)}, bf16[1024,128]{1,0:T(8,128)(2,1)S(1)}, u32[]{:S(2)}, u32[]{:S(2)}) collective-permute-start(bf16[1024,128]{1,0:T(8,128)(2,1)S(1)} %fusion), channel_id=1, source_target_pairs={{0,2},{1,3},{2,0},{3,1},{4,6},{5,7},{6,4},{7,5},{8,10},{9,11},{10,... | collective-permute-start | bytes 786440 | tf_op jit(solution)/shard_map/ppermute | solution.py:309
  24.5 1.1 %collective-permute-start.6 = (bf16[128,512]{1,0:T(8,128)(2,1)S(1)}, bf16[128,512]{1,0:T(8,128)(2,1)S(1)}, u32[]{:S(2)}, u32[]{:S(2)}) collective-permute-start(bf16[128,512]{1,0:T(8,128)(2,1)S(1)} %get-tuple-element.11), channel_id=1, source_target_pairs={{0,4},{1,5},{2,6},{3,7},{4,0},{5,1},{6,2},{7,3},{8,12},{9,13},{10,... | collective-permute-start | bytes 393224 | tf_op jit(solution)/shard_map/ppermute | solution.py:180
  25.6 0.9 %collective-permute-start.8 = (bf16[256,256]{1,0:T(8,128)(2,1)S(1)}, bf16[256,256]{1,0:T(8,128)(2,1)S(1)}, u32[]{:S(2)}, u32[]{:S(2)}) collective-permute-start(bf16[256,256]{1,0:T(8,128)(2,1)S(1)} %constant_dynamic-update-slice_fusion.3.refs_0_), channel_id=1, source_target_pairs={{0,4},{1,5},{2,6},{3,7},{4,0},{5,1},{6,2},{7,3},{8,12},{9,13},{10,... | collective-permute-start | bytes 393224 | tf_op jit(solution)/shard_map/ppermute | solution.py:180
  26.5 0.4 %collective-permute-done.9.refs_2_ = bf16[256,256]{1,0:T(8,128)(2,1)S(1)} collective-permute-done((bf16[256,256]{1,0:T(8,128)(2,1)S(1)}, bf16[256,256]{1,0:T(8,128)(2,1)S(1)}, u32[]{:S(2)}, u32[]{:S(2)}) %collective-permute-start.9) | collective-permute-done | bytes 131104 | tf_op jit(solution)/shard_map/ppermute | solution.py:180
  26.9 0.7 %collective-permute-start.10 = (bf16[256,256]{1,0:T(8,128)(2,1)S(1)}, bf16[256,256]{1,0:T(8,128)(2,1)S(1)}, u32[]{:S(2)}, u32[]{:S(2)}) collective-permute-start(bf16[256,256]{1,0:T(8,128)(2,1)S(1)} %collective-permute-done.9.refs_2_), channel_id=1, source_target_pairs={{0,4},{1,5},{2,6},{3,7},{4,0},{5,1},{6,2},{7,3},{8,12},{9,13},{10,... | collective-permute-start | bytes 393224 | tf_op jit(solution)/shard_map/ppermute | solution.py:180
  27.6 1.0 %copy-done.2 = bf16[128,2048]{1,0:T(8,128)(2,1)S(1)} copy-done((bf16[128,2048]{1,0:T(8,128)(2,1)S(1)}, bf16[128,2048]{1,0:T(8,128)(2,1)}, u32[]{:S(2)}) %copy-start.2) | copy-done | bytes 524312
  28.7 1.1 %shard_map.86 = bf16[128,2048]{1,0:T(8,128)(2,1)} custom-call(bf16[128,2048]{1,0:T(8,128)(2,1)S(1)} %copy-done.2, bf16[128,256]{1,0:T(8,128)(2,1)S(1)} %copy-done.3), custom_call_target="tpu_custom_call" | custom-call | flops 67108864 | bytes 1048576 | tf_op jit(solution)/shard_map/pallas_call | solution.py:318
  29.8 1.0 %collective-permute-done.6.next_ref = bf16[128,512]{1,0:T(8,128)(2,1)S(1)} collective-permute-done((bf16[128,512]{1,0:T(8,128)(2,1)S(1)}, bf16[128,512]{1,0:T(8,128)(2,1)S(1)}, u32[]{:S(2)}, u32[]{:S(2)}) %collective-permute-start.6) | collective-permute-done | bytes 131104 | tf_op jit(solution)/shard_map/ppermute | solution.py:180
  30.8 0.5 %shard_map.88.x_ref = bf16[512,1024]{1,0:T(8,128)(2,1)S(1)} custom-call(bf16[384,512]{1,0:T(8,128)(2,1)S(1)} %constant_dynamic-update-slice_fusion.mine_ref, bf16[384,512]{1,0:T(8,128)(2,1)S(1)} %collective-permute-done.5.theirs_ref, bf16[128,512]{1,0:T(8,128)(2,1)S(1)} %collective-permute-done.6.next_ref, bf16[128,4096]{1,0:T(8,128)(2,1)S(1)} %copy-done), custom_call_target="tpu_custom_call" | custom-call | bytes 2097152 | tf_op jit(solution)/shard_map/pallas_call | solution.py:224
  31.3 2.3 %collective-permute-done.8.refs_1_ = bf16[256,256]{1,0:T(8,128)(2,1)S(1)} collective-permute-done((bf16[256,256]{1,0:T(8,128)(2,1)S(1)}, bf16[256,256]{1,0:T(8,128)(2,1)S(1)}, u32[]{:S(2)}, u32[]{:S(2)}) %collective-permute-start.8) | collective-permute-done | bytes 131104 | tf_op jit(solution)/shard_map/ppermute | solution.py:180
  33.6 2.1 %collective-permute-done.10.refs_3_ = bf16[256,256]{1,0:T(8,128)(2,1)S(1)} collective-permute-done((bf16[256,256]{1,0:T(8,128)(2,1)S(1)}, bf16[256,256]{1,0:T(8,128)(2,1)S(1)}, u32[]{:S(2)}, u32[]{:S(2)}) %collective-permute-start.10) | collective-permute-done | bytes 131104 | tf_op jit(solution)/shard_map/ppermute | solution.py:180
  35.7 1.2 %shard_map.89 = f32[512,256]{1,0:T(8,128)} custom-call(bf16[512,1024]{1,0:T(8,128)(2,1)S(1)} %shard_map.88.x_ref, bf16[256,256]{1,0:T(8,128)(2,1)S(1)} %constant_dynamic-update-slice_fusion.3.refs_0_, bf16[256,256]{1,0:T(8,128)(2,1)S(1)} %collective-permute-done.8.refs_1_, bf16[256,256]{1,0:T(8,128)(2,1)S(1)} %collective-permute-done.9.refs_2_, ...), custom_call_target="tpu_custom_call" | custom-call | flops 268435456 | bytes 1572864 | tf_op jit(solution)/shard_map/pallas_call | solution.py:233
  36.9 0.9 %shard_map.87 = bf16[128,1024]{1,0:T(8,128)(2,1)} custom-call(bf16[2,1024,128]{2,1,0:T(8,128)(2,1)S(1)} %copy-done.1, bf16[2,1024,128]{2,1,0:T(8,128)(2,1)S(1)} %collective-permute-done.came_ref, bf16[1024,128]{1,0:T(8,128)(2,1)S(1)} %collective-permute-done.1.refs_0_), custom_call_target="tpu_custom_call" | custom-call | flops 131072 | bytes 1048576 | tf_op jit(solution)/shard_map/pallas_call | solution.py:310
  (18 shorter events, 0.1 us)
Async XLA Ops:
  0.6 27.0 %copy-start.3 = (bf16[128,256]{1,0:T(8,128)(2,1)S(1)}, bf16[128,256]{1,0:T(8,128)(2,1)}, u32[]{:S(2)}) copy-start(bf16[128,256]{1,0:T(8,128)(2,1)} %k_ref.1) | copy-start | bytes 196612
  1.7 29.1 %copy-start = (bf16[128,4096]{1,0:T(8,128)(2,1)S(1)}, bf16[128,4096]{1,0:T(8,128)(2,1)}, u32[]{:S(2)}) copy-start(bf16[128,4096]{1,0:T(8,128)(2,1)} %x_hbm.1) | copy-start | bytes 3145732
  1.7 13.9 %collective-permute-start.2 = (bf16[128,512]{1,0:T(8,128)(2,1)S(1)}, bf16[128,512]{1,0:T(8,128)(2,1)S(1)}, u32[]{:S(2)}, u32[]{:S(2)}) collective-permute-start(bf16[128,512]{1,0:T(8,128)(2,1)S(1)} %get-tuple-element.13), channel_id=1, source_target_pairs={{0,16},{1,21},{2,26},{3,31},{4,20},{5,17},{6,30},{7,27},{8,24},{9,... | collective-permute-start | bytes 393224 | tf_op jit(solution)/shard_map/ppermute | solution.py:180
  12.3 24.6 %copy-start.1 = (bf16[2,1024,128]{2,1,0:T(8,128)(2,1)S(1)}, bf16[2,1024,128]{2,1,0:T(8,128)(2,1)}, u32[]{:S(2)}) copy-start(bf16[2,1024,128]{2,1,0:T(8,128)(2,1)} %get-tuple-element.8.kept_ref) | copy-start | bytes 1572868
  12.3 9.5 %collective-permute-start = (bf16[2,1024,128]{2,1,0:T(8,128)(2,1)}, bf16[2,1024,128]{2,1,0:T(8,128)(2,1)S(1)}, u32[]{:S(2)}, u32[]{:S(2)}) collective-permute-start(bf16[2,1024,128]{2,1,0:T(8,128)(2,1)} %get-tuple-element.9), channel_id=1, source_target_pairs={{0,1},{1,0},{2,3},{3,2},{4,5},{5,4},{6,7},{7,6},{8,9},{9,8},{10,11... | collective-permute-start | bytes 1572872 | tf_op jit(solution)/shard_map/ppermute | solution.py:184
  12.9 8.8 %collective-permute-start.4 = (bf16[128,512]{1,0:T(8,128)(2,1)S(1)}, bf16[128,512]{1,0:T(8,128)(2,1)S(1)}, u32[]{:S(2)}, u32[]{:S(2)}) collective-permute-start(bf16[128,512]{1,0:T(8,128)(2,1)S(1)} %get-tuple-element.12), channel_id=1, source_target_pairs={{0,8},{1,13},{2,10},{3,15},{4,12},{5,9},{6,14},{7,11},{8,0},{9,5},... | collective-permute-start | bytes 393224 | tf_op jit(solution)/shard_map/ppermute | solution.py:180
  14.4 7.2 %collective-permute-start.7 = (bf16[128,256]{1,0:T(8,128)(2,1)}, bf16[128,256]{1,0:T(8,128)(2,1)S(1)}, u32[]{:S(2)}, u32[]{:S(2)}) collective-permute-start(bf16[128,256]{1,0:T(8,128)(2,1)} %get-tuple-element.10), channel_id=1, source_target_pairs={{0,16},{1,17},{2,18},{3,19},{4,20},{5,21},{6,22},{7,23},{8,24},{9,... | collective-permute-start | bytes 196616 | tf_op jit(solution)/shard_map/ppermute | solution.py:180
  15.7 6.0 %collective-permute-start.3 = (bf16[128,512]{1,0:T(8,128)(2,1)S(1)}, bf16[128,512]{1,0:T(8,128)(2,1)S(1)}, u32[]{:S(2)}, u32[]{:S(2)}) collective-permute-start(bf16[128,512]{1,0:T(8,128)(2,1)S(1)} %collective-permute-done.2), channel_id=1, source_target_pairs={{0,2},{1,3},{2,0},{3,1},{4,6},{5,7},{6,4},{7,5},{8,10},{9,11},{10,... | collective-permute-start | bytes 393224 | tf_op jit(solution)/shard_map/ppermute | solution.py:184
  21.6 5.2 %collective-permute-start.9 = (bf16[256,256]{1,0:T(8,128)(2,1)S(1)}, bf16[256,256]{1,0:T(8,128)(2,1)S(1)}, u32[]{:S(2)}, u32[]{:S(2)}) collective-permute-start(bf16[256,256]{1,0:T(8,128)(2,1)S(1)} %constant_dynamic-update-slice_fusion.3.refs_0_), channel_id=1, source_target_pairs={{0,8},{1,9},{2,10},{3,11},{4,12},{5,13},{6,14},{7,15},{8,0},{9,1},... | collective-permute-start | bytes 393224 | tf_op jit(solution)/shard_map/ppermute | solution.py:180
  21.7 9.1 %collective-permute-start.5 = (bf16[384,512]{1,0:T(8,128)(2,1)S(1)}, bf16[384,512]{1,0:T(8,128)(2,1)S(1)}, u32[]{:S(2)}, u32[]{:S(2)}) collective-permute-start(bf16[384,512]{1,0:T(8,128)(2,1)S(1)} %constant_dynamic-update-slice_fusion.mine_ref), channel_id=1, source_target_pairs={{0,1},{1,0},{2,3},{3,2},{4,5},{5,4},{6,7},{7,6},{8,9},{9,8},{10,11... | collective-permute-start | bytes 1179656 | tf_op jit(solution)/shard_map/ppermute | solution.py:184
  22.8 14.1 %collective-permute-start.1 = (bf16[1024,128]{1,0:T(8,128)(2,1)S(1)}, bf16[1024,128]{1,0:T(8,128)(2,1)S(1)}, u32[]{:S(2)}, u32[]{:S(2)}) collective-permute-start(bf16[1024,128]{1,0:T(8,128)(2,1)S(1)} %fusion), channel_id=1, source_target_pairs={{0,2},{1,3},{2,0},{3,1},{4,6},{5,7},{6,4},{7,5},{8,10},{9,11},{10,... | collective-permute-start | bytes 786440 | tf_op jit(solution)/shard_map/ppermute | solution.py:309
  24.5 6.3 %collective-permute-start.6 = (bf16[128,512]{1,0:T(8,128)(2,1)S(1)}, bf16[128,512]{1,0:T(8,128)(2,1)S(1)}, u32[]{:S(2)}, u32[]{:S(2)}) collective-permute-start(bf16[128,512]{1,0:T(8,128)(2,1)S(1)} %get-tuple-element.11), channel_id=1, source_target_pairs={{0,4},{1,5},{2,6},{3,7},{4,0},{5,1},{6,2},{7,3},{8,12},{9,13},{10,... | collective-permute-start | bytes 393224 | tf_op jit(solution)/shard_map/ppermute | solution.py:180
  25.6 8.0 %collective-permute-start.8 = (bf16[256,256]{1,0:T(8,128)(2,1)S(1)}, bf16[256,256]{1,0:T(8,128)(2,1)S(1)}, u32[]{:S(2)}, u32[]{:S(2)}) collective-permute-start(bf16[256,256]{1,0:T(8,128)(2,1)S(1)} %constant_dynamic-update-slice_fusion.3.refs_0_), channel_id=1, source_target_pairs={{0,4},{1,5},{2,6},{3,7},{4,0},{5,1},{6,2},{7,3},{8,12},{9,13},{10,... | collective-permute-start | bytes 393224 | tf_op jit(solution)/shard_map/ppermute | solution.py:180
  26.9 8.8 %collective-permute-start.10 = (bf16[256,256]{1,0:T(8,128)(2,1)S(1)}, bf16[256,256]{1,0:T(8,128)(2,1)S(1)}, u32[]{:S(2)}, u32[]{:S(2)}) collective-permute-start(bf16[256,256]{1,0:T(8,128)(2,1)S(1)} %collective-permute-done.9.refs_2_), channel_id=1, source_target_pairs={{0,4},{1,5},{2,6},{3,7},{4,0},{5,1},{6,2},{7,3},{8,12},{9,13},{10,... | collective-permute-start | bytes 393224 | tf_op jit(solution)/shard_map/ppermute | solution.py:180
  27.6 1.0 %copy-start.2 = (bf16[128,2048]{1,0:T(8,128)(2,1)S(1)}, bf16[128,2048]{1,0:T(8,128)(2,1)}, u32[]{:S(2)}) copy-start(bf16[128,2048]{1,0:T(8,128)(2,1)} %get-tuple-element.7.ds_ref) | copy-start | bytes 1572868

commit v4 on v3

v4 whole, which is shorter than its diff:
```python
import math

import jax
import jax.numpy as jnp
from jax import lax
from jax.experimental import pallas as pl
from jax.experimental.pallas import tpu as pltpu
from jax.sharding import PartitionSpec as P

HEAD_SIZE = 128
F32 = jnp.float32
BF16 = jnp.bfloat16
NN = (((1,), (0,)), ((), ()))
NT = (((1,), (1,)), ((), ()))
TN = (((0,), (0,)), ((), ()))
IN_HBM = pl.BlockSpec(memory_space=pltpu.HBM)
ANYWHERE = pl.BlockSpec(memory_space=pl.ANY)
IN_VMEM = pl.BlockSpec(memory_space=pltpu.VMEM)
CHUNK = 512
PARAMS = pltpu.CompilerParams(vmem_limit_bytes=24 * 1024 * 1024)
WHOLE = pltpu.CompilerParams(vmem_limit_bytes=60 * 1024 * 1024)


def dot(a, b, dims=NN):
    return lax.dot_general(a, b, dims, preferred_element_type=F32)


def cost(flops, moved, transcendentals=0):
    return pl.CostEstimate(flops=flops, bytes_accessed=moved, transcendentals=transcendentals)


def attention_group(g, q, k, v, do, gk_ref, gv_ref, ds):
    length = q.shape[0]
    per_group = q.shape[1] // k.shape[1]
    together = 2 - per_group % 2
    wide = together * length
    scale = 1.0 / math.sqrt(HEAD_SIZE)
    targets = lax.broadcasted_iota(jnp.int32, (length, wide), 0)
    positions = lax.rem(lax.broadcasted_iota(jnp.int32, (length, wide), 1), length)
    allowed = targets <= positions
    cols = slice(g * HEAD_SIZE, (g + 1) * HEAD_SIZE)
    key, value = k[:, cols], v[:, cols]
    acc_k = jnp.zeros((length, HEAD_SIZE), F32)
    acc_v = jnp.zeros((length, HEAD_SIZE), F32)
    for h in range(0, per_group, together):
        at = [(g * per_group + h + e) * HEAD_SIZE for e in range(together)]
        query = jnp.concatenate([q[:, s : s + HEAD_SIZE] for s in at], axis=0)
        grad = jnp.concatenate([do[:, s : s + HEAD_SIZE] for s in at], axis=0)
        scores = jnp.where(allowed, dot(key, query, NT), -1e30)
        raw = jnp.exp((scores - jnp.max(scores, axis=0, keepdims=True)) * scale)
        probs = raw * (1.0 / jnp.sum(raw, axis=0, keepdims=True))
        grad_probs = dot(value, grad, NT)
        delta = jnp.sum(probs * grad_probs, axis=0, keepdims=True)
        grad_scores = (probs * (grad_probs - delta)).astype(BF16)
        ds[:, at[0] : at[0] + wide] = grad_scores
        acc_v += dot(probs.astype(BF16), grad)
        acc_k += dot(grad_scores, query)
    gk_ref[:, cols] = (acc_k * scale).astype(BF16)
    gv_ref[:, cols] = acc_v.astype(BF16)


def blocks_of_partial(p_hbm, p, sems, own):
    chips, features = p.shape[0], p.shape[2]
    member = lax.axis_index("mp")
    chip, core = lax.div(member, 2), lax.rem(member, 2)
    column = core if own else 1 - core
    copies = []
    for b in range(chips):
        start = (2 * lax.rem(chip + b + 1, chips) + column) * features
        rows = pl.ds(pl.multiple_of(start, features), features)
        copies.append(pltpu.make_async_copy(p_hbm.at[:, rows, :], p.at[b], sems.at[b]))
    return copies


def partials(copies, p, gk, gv, out_ref):
    features = p.shape[2]
    step = min(CHUNK, features)
    for b, copy in enumerate(copies):
        copy.wait()
        for at in range(0, features, step):
            rows = slice(at, at + step)
            total = dot(p[b, 0, rows, :], gk, NT) + dot(p[b, 1, rows, :], gv, NT)
            out_ref[b, rows, :] = total.astype(BF16)


def attention_kernel(
    q_hbm, k_hbm, v_hbm, do_hbm, p_hbm,
    gk_ref, gv_ref, sent_ref, ds_hbm,
    q, k, v, do, p, ds, sems, p_sems, out_sems,
):
    kv_heads = k.shape[1] // HEAD_SIZE
    group = q.shape[1] // kv_heads
    small = [
        pltpu.make_async_copy(k_hbm, k, sems.at[0]),
        pltpu.make_async_copy(v_hbm, v, sems.at[1]),
    ]
    large, stored = [], []
    for g in range(kv_heads):
        cols = pl.ds(g * group, group)
        large.append((
            pltpu.make_async_copy(q_hbm.at[:, cols], q.at[:, cols], sems.at[2 + 2 * g]),
            pltpu.make_async_copy(do_hbm.at[:, cols], do.at[:, cols], sems.at[3 + 2 * g]),
        ))
        stored.append(pltpu.make_async_copy(ds.at[:, cols], ds_hbm.at[:, cols], out_sems.at[g]))
    blocks = blocks_of_partial(p_hbm, p, p_sems, own=False)
    for copy in small:
        copy.start()
    for pair in large:
        for copy in pair:
            copy.start()
    for copy in blocks:
        copy.start()
    for copy in small:
        copy.wait()
    for g in range(kv_heads):
        for copy in large[g]:
            copy.wait()
        attention_group(g, q, k, v, do, gk_ref, gv_ref, ds)
        stored[g].start()
    partials(blocks, p, gk_ref[...], gv_ref[...], sent_ref)
    for copy in stored:
        copy.wait()


def kept_kernel(gk_ref, gv_ref, p_hbm, kept_ref, p, p_sems):
    blocks = blocks_of_partial(p_hbm, p, p_sems, own=True)
    for copy in blocks:
        copy.start()
    partials(blocks, p, gk_ref[...], gv_ref[...], kept_ref)


def query_kernel(ds_hbm, k_hbm, gq_hbm, ds, k, gq, sems, out_sems):
    kv_heads = k.shape[1] // HEAD_SIZE
    group = gq.shape[1] // kv_heads
    scale = 1.0 / math.sqrt(HEAD_SIZE)
    key_copy = pltpu.make_async_copy(k_hbm, k, sems.at[kv_heads])
    key_copy.start()
    loads, stores = [], []
    for g in range(kv_heads):
        cols = pl.ds(g * group, group)
        loads.append(pltpu.make_async_copy(ds_hbm.at[:, cols], ds.at[:, cols], sems.at[g]))
        stores.append(pltpu.make_async_copy(gq.at[:, cols], gq_hbm.at[:, cols], out_sems.at[g]))
        loads[-1].start()
    key_copy.wait()
    for g in range(kv_heads):
        loads[g].wait()
        key = k[:, g * HEAD_SIZE : (g + 1) * HEAD_SIZE]
        for at in range(g * group, (g + 1) * group, HEAD_SIZE):
            grad = dot(ds[:, at : at + HEAD_SIZE], key, TN) * scale
            gq[:, at : at + HEAD_SIZE] = grad.astype(BF16)
        stores[g].start()
    for copy in stores:
        copy.wait()


def input_kernel(kept_ref, came_ref, *refs):
    out_ref = refs[-1]
    total = kept_ref[len(refs) - 1].astype(F32) + came_ref[len(refs) - 1].astype(F32)
    for ref in refs[:-1]:
        total += ref[...].astype(F32)
    out_ref[...] = total.T.astype(BF16)


def turned_kernel(mine_ref, theirs_ref, out_ref):
    parts = 2 * lax.axis_size("mp")
    far = parts // 2
    rows = out_ref.shape[1] // parts
    member = lax.axis_index("mp")

    def put(k, piece):
        place = far * lax.rem(k, 2) + 2 * lax.div(lax.rem(k, far), 2) + lax.div(k, far)
        out_ref[:, pl.ds(pl.multiple_of(place * rows, rows), rows)] = piece.T

    for at in range(far):
        k = far * (at % 2) + (member ^ (at // 2 * 2))
        put(k, mine_ref[at * rows : (at + 1) * rows, :])
        put(k ^ 1, theirs_ref[at * rows : (at + 1) * rows, :])


def weights_kernel(x_ref, *refs):
    keys, out_ref = refs[:-1], refs[-1]
    rows = keys[0].shape[0]
    total = dot(x_ref[:, :rows], keys[0][...])
    for j in range(1, len(keys)):
        total += dot(x_ref[:, j * rows : (j + 1) * rows], keys[j][...])
    out_ref[...] = total * (1.0 / (2 * len(keys)))


def along_dp(array, partner, parts, groups):
    pairs = [
        (i * groups + m, (i ^ partner(m)) * groups + m)
        for i in range(parts)
        for m in range(groups)
    ]
    return lax.ppermute(array, ("dp", "mp"), pairs)


def along_mp(array, bit, groups):
    return lax.ppermute(array, "mp", [(m, m ^ bit) for m in range(groups)])


def sent_inputs(inputs, parts, groups):
    far = parts // 2
    part, member = lax.axis_index("dp"), lax.axis_index("mp")
    rows, width = inputs.shape[0], inputs.shape[1] // parts

    def sent(k):
        block = lax.dynamic_slice(inputs, (0, (part ^ (k + member)) * width), (rows, width))
        return along_dp(block, lambda m: k + m, parts, groups)

    return sent(0), sent(far)


def gathered_inputs(arrived, after, parts, groups):
    rows, width = arrived.shape[0] // 2, arrived.shape[1]
    pieces = [arrived]
    bit = 2
    while bit < groups:
        pieces += [along_mp(piece, bit, groups) for piece in pieces]
        bit *= 2
    pieces, _ = lax.optimization_barrier((pieces, after))
    mine = jnp.concatenate(pieces)
    theirs = along_mp(mine, 1, groups)
    return pl.pallas_call(
        turned_kernel,
        out_specs=IN_VMEM,
        out_shape=jax.ShapeDtypeStruct((width, parts * rows), arrived.dtype),
        compiler_params=PARAMS,
        cost_estimate=cost(0, 4 * parts * rows * width),
    )(mine, theirs)


def gathered_keys(first, parts, groups):
    far = parts // 2
    keys = {0: first}
    bit = far // 2
    while bit > 1:
        for k in list(keys):
            keys[k ^ bit] = along_dp(keys[k], lambda m, bit=bit: bit, parts, groups)
        bit //= 2
    return [keys[k] for k in range(0, far, 2)]


def summed_weights(turned, keys):
    width, columns = turned.shape[0], keys[0].shape[1]
    return pl.pallas_call(
        weights_kernel,
        out_specs=IN_VMEM,
        out_shape=jax.ShapeDtypeStruct((width, columns), F32),
        compiler_params=PARAMS,
        cost_estimate=cost(
            2 * turned.size * columns, 2 * turned.size + 4 * width * columns
        ),
    )(turned, *keys)


def gathered_weights(inputs, grad_key, parts):
    rows = inputs.shape[0]
    width = inputs.shape[1] // parts
    blocks = inputs.reshape(rows, parts, width).transpose(1, 0, 2)
    mine = lax.all_to_all(blocks, "dp", split_axis=0, concat_axis=0, tiled=True)
    keys = lax.all_gather(grad_key, "dp", axis=0)
    return jnp.einsum("psd,psc->dc", mine, keys, preferred_element_type=F32) / parts


def body(query_states, key_states, value_states, grad_context, inputs_normed, projections):
    parts = lax.axis_size("dp")
    groups = lax.axis_size("mp")
    chips = groups // 2
    rows, width = key_states.shape
    query_width = query_states.shape[1]
    features = projections.shape[1] // groups
    kv_heads = width // HEAD_SIZE
    partial = jax.ShapeDtypeStruct((chips, features, rows), BF16)
    exchange = parts == 2 * groups and inputs_normed.shape[1] % (parts * 128) == 0
    if exchange:
        near, distant = sent_inputs(inputs_normed, parts, groups)

    p_scratch = [
        pltpu.VMEM((chips, 2, features, width), BF16),
        pltpu.SemaphoreType.DMA((chips,)),
    ]
    whole = pltpu.VMEM((rows, query_width), BF16)
    narrow = pltpu.VMEM((rows, width), BF16)
    grad_key, grad_value, sent, grad_scores = pl.pallas_call(
        attention_kernel,
        in_specs=[IN_HBM] * 5,
        out_specs=[IN_VMEM, IN_VMEM, IN_VMEM, ANYWHERE],
        out_shape=(
            jax.ShapeDtypeStruct((rows, width), BF16),
            jax.ShapeDtypeStruct((rows, width), BF16),
            partial,
            jax.ShapeDtypeStruct((rows, query_width), BF16),
        ),
        scratch_shapes=[whole, narrow, narrow, whole, p_scratch[0], whole]
        + [pltpu.SemaphoreType.DMA((2 + 2 * kv_heads,)), p_scratch[1]]
        + [pltpu.SemaphoreType.DMA((kv_heads,))],
        compiler_params=WHOLE,
        cost_estimate=cost(
            8 * rows * rows * query_width + 4 * rows * width * features * chips,
            6 * rows * query_width + 4 * width * features * chips,
            rows * query_width,
        ),
    )(query_states, key_states, value_states, grad_context, projections)

    if exchange:
        ready, near = lax.optimization_barrier((grad_key, near))
        first = along_dp(ready, lambda m: parts // 2, parts, groups)
        arrived = jnp.concatenate([near, distant])
        grad_value, sent, arrived = lax.optimization_barrier((grad_value, sent, arrived))
    came = along_mp(sent, 1, groups)
    kept = pl.pallas_call(
        kept_kernel,
        in_specs=[IN_VMEM, IN_VMEM, IN_HBM],
        out_specs=IN_VMEM,
        out_shape=partial,
        scratch_shapes=p_scratch,
        compiler_params=WHOLE,
        cost_estimate=cost(
            4 * rows * width * features * chips, 4 * width * features * chips
        ),
    )(grad_key, grad_value, projections)
    if exchange:
        kept, first = lax.optimization_barrier((kept, first))
        keys = gathered_keys(jnp.concatenate([grad_key, first]), parts, groups)
        keys += [along_dp(key, lambda m: 1, parts, groups) for key in keys]
    last, pairs = [], []
    for b in range(chips - 1):
        pairs.append((kept[b].astype(F32) + came[b].astype(F32)).astype(BF16))
        shift = [(m, (m + 2 * (b + 1)) % groups) for m in range(groups)]
        last.append(lax.ppermute(pairs[b], "mp", shift))
    if exchange:
        turned = gathered_inputs(arrived, (keys[parts // 4 - 1], keys[parts // 4], pairs), parts, groups)
    grad_input = pl.pallas_call(
        input_kernel,
        out_specs=IN_VMEM,
        out_shape=jax.ShapeDtypeStruct((rows, features), BF16),
        compiler_params=PARAMS,
        cost_estimate=cost(rows * features, 8 * rows * features),
    )(kept, came, *last)

    grad_query = pl.pallas_call(
        query_kernel,
        in_specs=[IN_HBM, IN_HBM],
        out_specs=ANYWHERE,
        out_shape=jax.ShapeDtypeStruct((rows, query_width), BF16),
        scratch_shapes=[whole, narrow, whole]
        + [pltpu.SemaphoreType.DMA((1 + kv_heads,)), pltpu.SemaphoreType.DMA((kv_heads,))],
        compiler_params=WHOLE,
        cost_estimate=cost(2 * rows * rows * query_width, 4 * rows * query_width),
    )(grad_scores, key_states)

    if exchange:
        keys[-1], grad_input, grad_query = lax.optimization_barrier(
            (keys[-1], grad_input, grad_query)
        )
        grad_weights = summed_weights(turned, keys)
    else:
        grad_weights = gathered_weights(inputs_normed, grad_key, parts)
    return (grad_query, grad_input, grad_weights)


def solution(mesh):
    placed = (
        P("dp", "mp"),
        P("dp", "mp"),
        P("dp", "mp"),
        P("dp", "mp"),
        P("dp", None),
        P(None, None, "mp"),
    )
    return jax.shard_map(
        body,
        mesh=mesh,
        in_specs=placed,
        out_specs=(P("dp", "mp"), P("dp", "mp"), P("dp", "mp")),
        check_vma=False,
    )
```

time: 38.1 us -> 42.4 us (1.11)
  starting transfers between devices: 12.4 us -> 16.4 us
  Pallas kernels: 10.2 us -> 13.5 us
  waiting for transfers between devices: 10.4 us -> 7.37 us
    ppermute x7 -> x6, waiting for transfers between devices: 10.4 us -> 2.77 us  [along_dp(): return lax.ppermute(array, ('dp', 'mp'), pairs)]
    ppermute x3, starting transfers between devices: 1.99 us -> 8.42 us  [along_mp(): return lax.ppermute(array, 'mp', [(m, m ^ bit) for m in range(groups)])]
    pallas_call x3 -> x4, Pallas kernels: 2.83 us -> 7.65 us  [the longest x1 3.79 us: body(): pl.pallas_call(kept_kernel, in_specs=[IN_VMEM, IN_VMEM, IN_HBM], out_spec...]
    ppermute x1, waiting for transfers between devices: 0.01 us -> 4.6 us  [body(): last.append(lax.ppermute(pairs[b], 'mp', shift))]
    ppermute x7 -> x6, starting transfers between devices: 8.78 us -> 7.11 us  [along_dp(): return lax.ppermute(array, ('dp', 'mp'), pairs)]
    pallas_call x1, Pallas kernels: 6.46 us -> 4.98 us  [body(): pl.pallas_call(attention_kernel, in_specs=[IN_HBM] * 5, out_specs=[IN_VME...]
    ppermute x1, starting transfers between devices: 1.62 us -> 0.92 us  [body(): last.append(lax.ppermute(pairs[b], 'mp', shift))]
    unnamed x11 -> x4, local copies, waits for them, and re-layouts: 1.96 us -> 1.94 us
  transfers between devices with their start and end apart: 11 -> 10, of which waited for: 5 -> 3; matrix products, arithmetic and copies ran while one was open for 5% -> 5% of each run, Pallas kernels for 25% -> 28%
where the time goes in v4:
time: 42.4 us; the launch traced here: 42.1 us
  starting transfers between devices  16.4 us (39%)
  Pallas kernels  13.5 us (32%)
  waiting for transfers between devices  7.37 us (17%)
  local copies, waits for them, and re-layouts  2.96 us (7%)
  other arithmetic  1.04 us (2%)
  between operations  0.77 us (2%)
    ppermute x3, starting transfers between devices, along_mp(): return lax.ppermute(array, 'mp', [(m, m ^ bit) for m in range(groups)])  8.42 us
    ppermute x6, starting transfers between devices, along_dp(): return lax.ppermute(array, ('dp', 'mp'), pairs)  7.11 us
    pallas_call x1, Pallas kernels, body(): pl.pallas_call(attention_kernel, in_specs=[IN_HBM] * 5, out_specs=[IN_VME...  4.98 us
    ppermute x1, waiting for transfers between devices, body(): last.append(lax.ppermute(pairs[b], 'mp', shift))  4.6 us
    pallas_call x1, Pallas kernels, body(): pl.pallas_call(kept_kernel, in_specs=[IN_VMEM, IN_VMEM, IN_HBM], out_spec...  3.79 us
    ppermute x6, waiting for transfers between devices, along_dp(): return lax.ppermute(array, ('dp', 'mp'), pairs)  2.77 us
    pallas_call x1, Pallas kernels, body(): pl.pallas_call(query_kernel, in_specs=[IN_HBM, IN_HBM], out_specs=ANYWHER...  2.26 us
    unnamed x4, local copies, waits for them, and re-layouts  1.94 us
  transfers between devices with their start and end apart: 10, of which 3 were waited for; matrix products, arithmetic and copies ran while one was open for 5% of the time, Pallas kernels for 28%

profile of v4, /device:TPU:0, one launch (start us, length us, event | category | flops | bytes accessed | tf_op | source)
XLA Modules:
  0.0 42.1 jit_solution(10442240750380232891)
XLA Ops:
  0.6 1.0 %constant_dynamic-slice_fusion.1 = (bf16[128,512]{1,0:T(8,128)(2,1)S(1)}, bf16[128,512]{1,0:T(8,128)(2,1)S(1)}) fusion(bf16[128,4096]{1,0:T(8,128)(2,1)} %param.10, s32[]{:T(128)S(6)} %select_n.6, s32[]{:T(128)S(6)} %select_n.7), kind=kLoop, calls=%fused_computation.8 | loop fusion | bytes 524296 | tf_op jit(solution)/shard_map/dynamic_slice | solution.py:208
  1.6 0.7 %collective-permute-start = (bf16[128,512]{1,0:T(8,128)(2,1)S(1)}, bf16[128,512]{1,0:T(8,128)(2,1)S(1)}, u32[]{:S(2)}, u32[]{:S(2)}) collective-permute-start(bf16[128,512]{1,0:T(8,128)(2,1)S(1)} %get-tuple-element.35), channel_id=1, source_target_pairs={{0,0},{1,5},{2,10},{3,15},{4,4},{5,1},{6,14},{7,11},{8,8},{9,13},{... | collective-permute-start | bytes 393224 | tf_op jit(solution)/shard_map/ppermute | solution.py:195
  2.3 4.1 %collective-permute-start.1 = (bf16[128,512]{1,0:T(8,128)(2,1)S(1)}, bf16[128,512]{1,0:T(8,128)(2,1)S(1)}, u32[]{:S(2)}, u32[]{:S(2)}) collective-permute-start(bf16[128,512]{1,0:T(8,128)(2,1)S(1)} %get-tuple-element.36), channel_id=1, source_target_pairs={{0,16},{1,21},{2,26},{3,31},{4,20},{5,17},{6,30},{7,27},{8,24},{9,... | collective-permute-start | bytes 393224 | tf_op jit(solution)/shard_map/ppermute | solution.py:195
  6.4 5.0 %shard_map.85 = (bf16[128,256]{1,0:T(8,128)(2,1)}, bf16[128,256]{1,0:T(8,128)(2,1)}, bf16[2,1024,128]{2,1,0:T(8,128)(2,1)}, bf16[128,2048]{1,0:T(8,128)(2,1)}) custom-call(bf16[128,2048]{1,0:T(8,128)(2,1)} %q_hbm.1, bf16[128,256]{1,0:T(8,128)(2,1)} %k_hbm.3, bf16[128,256]{1,0:T(8,128)(2,1)} %v_hbm.1, bf16[128,2048]{1,0:T(8,128)(2,1)} %do_hbm.1, ...), custom_call_target="tpu_custom_call" | custom-call | flops 536870912 | bytes 3670016 | tf_op jit(solution)/shard_map/pallas_call | solution.py:285
  11.5 3.3 %collective-permute-start.5 = (bf16[2,1024,128]{2,1,0:T(8,128)(2,1)}, bf16[2,1024,128]{2,1,0:T(8,128)(2,1)S(1)}, u32[]{:S(2)}, u32[]{:S(2)}) collective-permute-start(bf16[2,1024,128]{2,1,0:T(8,128)(2,1)} %get-tuple-element.27), channel_id=1, source_target_pairs={{0,1},{1,0},{2,3},{3,2},{4,5},{5,4},{6,7},{7,6},{8,9},{9,8},{10,11... | collective-permute-start | bytes 1572872 | tf_op jit(solution)/shard_map/ppermute | solution.py:199
  14.7 0.0 collective-permute-start.2
  14.7 0.9 %constant_dynamic-update-slice_fusion.1 = bf16[256,256]{1,0:T(8,128)(2,1)S(1)} fusion(bf16[128,256]{1,0:T(8,128)(2,1)} %get-tuple-element.24.gk_ref), kind=kLoop, calls=%fused_computation.4 | loop fusion | bytes 131072
  15.6 5.1 %collective-permute-start.7 = (bf16[256,512]{1,0:T(8,128)(2,1)S(1)}, bf16[256,512]{1,0:T(8,128)(2,1)S(1)}, u32[]{:S(2)}, u32[]{:S(2)}) collective-permute-start(bf16[256,512]{1,0:T(8,128)(2,1)S(1)} %pad_maximum_fusion), channel_id=1, source_target_pairs={{0,2},{1,3},{2,0},{3,1},{4,6},{5,7},{6,4},{7,5},{8,10},{9,11},{10,... | collective-permute-start | bytes 786440 | tf_op jit(solution)/shard_map/ppermute | solution.py:199
  20.7 3.8 %shard_map.86.kept_ref = bf16[2,1024,128]{2,1,0:T(8,128)(2,1)} custom-call(bf16[128,256]{1,0:T(8,128)(2,1)} %get-tuple-element.24.gk_ref, bf16[128,256]{1,0:T(8,128)(2,1)} %get-tuple-element.23.gv_ref, bf16[2,4096,256]{2,1,0:T(8,128)(2,1)} %p_hbm.3), custom_call_target="tpu_custom_call" | custom-call | flops 268435456 | bytes 2097152 | tf_op jit(solution)/shard_map/pallas_call | solution.py:312
  24.5 0.0 collective-permute-done.2
  24.5 0.1 collective-permute-start.3
  24.6 1.3 %collective-permute-start.8 = (bf16[256,256]{1,0:T(8,128)(2,1)S(1)}, bf16[256,256]{1,0:T(8,128)(2,1)S(1)}, u32[]{:S(2)}, u32[]{:S(2)}) collective-permute-start(bf16[256,256]{1,0:T(8,128)(2,1)S(1)} %constant_dynamic-update-slice_fusion.refs_0_), channel_id=1, source_target_pairs={{0,4},{1,5},{2,6},{3,7},{4,0},{5,1},{6,2},{7,3},{8,12},{9,13},{10,... | collective-permute-start | bytes 393224 | tf_op jit(solution)/shard_map/ppermute | solution.py:195
  25.9 1.0 %fusion = bf16[1024,128]{1,0:T(8,128)(2,1)S(1)} fusion(bf16[2,1024,128]{2,1,0:T(8,128)(2,1)S(1)} %collective-permute-done.5.came_ref, bf16[2,1024,128]{2,1,0:T(8,128)(2,1)} %shard_map.86.kept_ref), kind=kLoop, calls=%fused_computation.1 | loop fusion | flops 524288 | bytes 786432 | tf_op jit(solution)/shard_map/convert_element_type | solution.py:329
  26.9 2.7 %collective-permute-done.3.refs_1_ = bf16[256,256]{1,0:T(8,128)(2,1)S(1)} collective-permute-done((bf16[256,256]{1,0:T(8,128)(2,1)S(1)}, bf16[256,256]{1,0:T(8,128)(2,1)S(1)}, u32[]{:S(2)}, u32[]{:S(2)}) %collective-permute-start.3) | collective-permute-done | bytes 131104 | tf_op jit(solution)/shard_map/ppermute | solution.py:195
  29.6 0.1 collective-permute-done.8.refs_2_
  29.8 0.1 collective-permute-start.9
  29.8 0.9 %collective-permute-start.6 = (bf16[1024,128]{1,0:T(8,128)(2,1)S(1)}, bf16[1024,128]{1,0:T(8,128)(2,1)S(1)}, u32[]{:S(2)}, u32[]{:S(2)}) collective-permute-start(bf16[1024,128]{1,0:T(8,128)(2,1)S(1)} %fusion), channel_id=1, source_target_pairs={{0,2},{1,3},{2,0},{3,1},{4,6},{5,7},{6,4},{7,5},{8,10},{9,11},{10,... | collective-permute-start | bytes 786440 | tf_op jit(solution)/shard_map/ppermute | solution.py:331
  30.8 0.9 %collective-permute-start.4 = (bf16[256,256]{1,0:T(8,128)(2,1)S(1)}, bf16[256,256]{1,0:T(8,128)(2,1)S(1)}, u32[]{:S(2)}, u32[]{:S(2)}) collective-permute-start(bf16[256,256]{1,0:T(8,128)(2,1)S(1)} %collective-permute-done.3.refs_1_), channel_id=1, source_target_pairs={{0,4},{1,5},{2,6},{3,7},{4,0},{5,1},{6,2},{7,3},{8,12},{9,13},{10,... | collective-permute-start | bytes 393224 | tf_op jit(solution)/shard_map/ppermute | solution.py:195
  31.7 2.3 %shard_map.88 = bf16[128,2048]{1,0:T(8,128)(2,1)} custom-call(bf16[128,2048]{1,0:T(8,128)(2,1)} %get-tuple-element.28.ds_hbm, bf16[128,256]{1,0:T(8,128)(2,1)} %k_hbm.3), custom_call_target="tpu_custom_call" | custom-call | flops 67108864 | bytes 1048576 | tf_op jit(solution)/shard_map/pallas_call | solution.py:342
  34.0 4.6 %collective-permute-done.6.refs_0_ = bf16[1024,128]{1,0:T(8,128)(2,1)S(1)} collective-permute-done((bf16[1024,128]{1,0:T(8,128)(2,1)S(1)}, bf16[1024,128]{1,0:T(8,128)(2,1)S(1)}, u32[]{:S(2)}, u32[]{:S(2)}) %collective-permute-start.6) | collective-permute-done | bytes 262176 | tf_op jit(solution)/shard_map/ppermute | solution.py:331
  38.6 1.0 %copy-done = bf16[2,1024,128]{2,1,0:T(8,128)(2,1)S(1)} copy-done((bf16[2,1024,128]{2,1,0:T(8,128)(2,1)S(1)}, bf16[2,1024,128]{2,1,0:T(8,128)(2,1)}, u32[]{:S(2)}) %copy-start) | copy-done | bytes 524312
  39.6 0.9 %shard_map.87 = bf16[128,1024]{1,0:T(8,128)(2,1)} custom-call(bf16[2,1024,128]{2,1,0:T(8,128)(2,1)S(1)} %copy-done, bf16[2,1024,128]{2,1,0:T(8,128)(2,1)S(1)} %collective-permute-done.5.came_ref, bf16[1024,128]{1,0:T(8,128)(2,1)S(1)} %collective-permute-done.6.refs_0_), custom_call_target="tpu_custom_call" | custom-call | flops 131072 | bytes 1048576 | tf_op jit(solution)/shard_map/pallas_call | solution.py:334
  40.5 0.4 shard_map.89.x_ref
  40.8 1.2 %shard_map.90 = f32[512,256]{1,0:T(8,128)} custom-call(bf16[512,1024]{1,0:T(8,128)(2,1)S(1)} %shard_map.89.x_ref, bf16[256,256]{1,0:T(8,128)(2,1)S(1)} %constant_dynamic-update-slice_fusion.refs_0_, bf16[256,256]{1,0:T(8,128)(2,1)S(1)} %collective-permute-done.3.refs_1_, bf16[256,256]{1,0:T(8,128)(2,1)S(1)} %collective-permute-done.8.refs_2_, ...), custom_call_target="tpu_custom_call" | custom-call | flops 268435456 | bytes 1572864 | tf_op jit(solution)/shard_map/pallas_call | solution.py:246
  (11 shorter events, 0.1 us)
Async XLA Ops:
  1.6 9.8 %collective-permute-start = (bf16[128,512]{1,0:T(8,128)(2,1)S(1)}, bf16[128,512]{1,0:T(8,128)(2,1)S(1)}, u32[]{:S(2)}, u32[]{:S(2)}) collective-permute-start(bf16[128,512]{1,0:T(8,128)(2,1)S(1)} %get-tuple-element.35), channel_id=1, source_target_pairs={{0,0},{1,5},{2,10},{3,15},{4,4},{5,1},{6,14},{7,11},{8,8},{9,13},{... | collective-permute-start | bytes 393224 | tf_op jit(solution)/shard_map/ppermute | solution.py:195
  2.3 9.1 %collective-permute-start.1 = (bf16[128,512]{1,0:T(8,128)(2,1)S(1)}, bf16[128,512]{1,0:T(8,128)(2,1)S(1)}, u32[]{:S(2)}, u32[]{:S(2)}) collective-permute-start(bf16[128,512]{1,0:T(8,128)(2,1)S(1)} %get-tuple-element.36), channel_id=1, source_target_pairs={{0,16},{1,21},{2,26},{3,31},{4,20},{5,17},{6,30},{7,27},{8,24},{9,... | collective-permute-start | bytes 393224 | tf_op jit(solution)/shard_map/ppermute | solution.py:195
  11.5 14.5 %collective-permute-start.5 = (bf16[2,1024,128]{2,1,0:T(8,128)(2,1)}, bf16[2,1024,128]{2,1,0:T(8,128)(2,1)S(1)}, u32[]{:S(2)}, u32[]{:S(2)}) collective-permute-start(bf16[2,1024,128]{2,1,0:T(8,128)(2,1)} %get-tuple-element.27), channel_id=1, source_target_pairs={{0,1},{1,0},{2,3},{3,2},{4,5},{5,4},{6,7},{7,6},{8,9},{9,8},{10,11... | collective-permute-start | bytes 1572872 | tf_op jit(solution)/shard_map/ppermute | solution.py:199
  14.7 9.7 %collective-permute-start.2 = (bf16[128,256]{1,0:T(8,128)(2,1)}, bf16[128,256]{1,0:T(8,128)(2,1)S(1)}, u32[]{:S(2)}, u32[]{:S(2)}) collective-permute-start(bf16[128,256]{1,0:T(8,128)(2,1)} %get-tuple-element.24.gk_ref), channel_id=1, source_target_pairs={{0,16},{1,17},{2,18},{3,19},{4,20},{5,21},{6,22},{7,23},{8,24},{9,... | collective-permute-start | bytes 196616 | tf_op jit(solution)/shard_map/ppermute | solution.py:195
  15.6 14.1 %collective-permute-start.7 = (bf16[256,512]{1,0:T(8,128)(2,1)S(1)}, bf16[256,512]{1,0:T(8,128)(2,1)S(1)}, u32[]{:S(2)}, u32[]{:S(2)}) collective-permute-start(bf16[256,512]{1,0:T(8,128)(2,1)S(1)} %pad_maximum_fusion), channel_id=1, source_target_pairs={{0,2},{1,3},{2,0},{3,1},{4,6},{5,7},{6,4},{7,5},{8,10},{9,11},{10,... | collective-permute-start | bytes 786440 | tf_op jit(solution)/shard_map/ppermute | solution.py:199
  24.5 5.1 %collective-permute-start.3 = (bf16[256,256]{1,0:T(8,128)(2,1)S(1)}, bf16[256,256]{1,0:T(8,128)(2,1)S(1)}, u32[]{:S(2)}, u32[]{:S(2)}) collective-permute-start(bf16[256,256]{1,0:T(8,128)(2,1)S(1)} %constant_dynamic-update-slice_fusion.refs_0_), channel_id=1, source_target_pairs={{0,8},{1,9},{2,10},{3,11},{4,12},{5,13},{6,14},{7,15},{8,0},{9,1},... | collective-permute-start | bytes 393224 | tf_op jit(solution)/shard_map/ppermute | solution.py:195
  24.6 5.1 %collective-permute-start.8 = (bf16[256,256]{1,0:T(8,128)(2,1)S(1)}, bf16[256,256]{1,0:T(8,128)(2,1)S(1)}, u32[]{:S(2)}, u32[]{:S(2)}) collective-permute-start(bf16[256,256]{1,0:T(8,128)(2,1)S(1)} %constant_dynamic-update-slice_fusion.refs_0_), channel_id=1, source_target_pairs={{0,4},{1,5},{2,6},{3,7},{4,0},{5,1},{6,2},{7,3},{8,12},{9,13},{10,... | collective-permute-start | bytes 393224 | tf_op jit(solution)/shard_map/ppermute | solution.py:195
  29.8 10.7 %collective-permute-start.9 = (bf16[512,512]{1,0:T(8,128)(2,1)S(1)}, bf16[512,512]{1,0:T(8,128)(2,1)S(1)}, u32[]{:S(2)}, u32[]{:S(2)}) collective-permute-start(bf16[512,512]{1,0:T(8,128)(2,1)S(1)} %constant_dynamic-update-slice_fusion.2.mine_ref), channel_id=1, source_target_pairs={{0,1},{1,0},{2,3},{3,2},{4,5},{5,4},{6,7},{7,6},{8,9},{9,8},{10,11... | collective-permute-start | bytes 1572872 | tf_op jit(solution)/shard_map/ppermute | solution.py:199
  29.8 8.7 %collective-permute-start.6 = (bf16[1024,128]{1,0:T(8,128)(2,1)S(1)}, bf16[1024,128]{1,0:T(8,128)(2,1)S(1)}, u32[]{:S(2)}, u32[]{:S(2)}) collective-permute-start(bf16[1024,128]{1,0:T(8,128)(2,1)S(1)} %fusion), channel_id=1, source_target_pairs={{0,2},{1,3},{2,0},{3,1},{4,6},{5,7},{6,4},{7,5},{8,10},{9,11},{10,... | collective-permute-start | bytes 786440 | tf_op jit(solution)/shard_map/ppermute | solution.py:331
  30.8 9.7 %collective-permute-start.4 = (bf16[256,256]{1,0:T(8,128)(2,1)S(1)}, bf16[256,256]{1,0:T(8,128)(2,1)S(1)}, u32[]{:S(2)}, u32[]{:S(2)}) collective-permute-start(bf16[256,256]{1,0:T(8,128)(2,1)S(1)} %collective-permute-done.3.refs_1_), channel_id=1, source_target_pairs={{0,4},{1,5},{2,6},{3,7},{4,0},{5,1},{6,2},{7,3},{8,12},{9,13},{10,... | collective-permute-start | bytes 393224 | tf_op jit(solution)/shard_map/ppermute | solution.py:195
  38.6 1.0 %copy-start = (bf16[2,1024,128]{2,1,0:T(8,128)(2,1)S(1)}, bf16[2,1024,128]{2,1,0:T(8,128)(2,1)}, u32[]{:S(2)}) copy-start(bf16[2,1024,128]{2,1,0:T(8,128)(2,1)} %shard_map.86.kept_ref) | copy-start | bytes 1572868

commit v5 on v3

v5 whole, which is shorter than its diff:
```python
import math

import jax
import jax.numpy as jnp
from jax import lax
from jax.experimental import pallas as pl
from jax.experimental.pallas import tpu as pltpu
from jax.sharding import PartitionSpec as P

HEAD_SIZE = 128
F32 = jnp.float32
BF16 = jnp.bfloat16
NN = (((1,), (0,)), ((), ()))
NT = (((1,), (1,)), ((), ()))
TN = (((0,), (0,)), ((), ()))
IN_HBM = pl.BlockSpec(memory_space=pltpu.HBM)
ANYWHERE = pl.BlockSpec(memory_space=pl.ANY)
IN_VMEM = pl.BlockSpec(memory_space=pltpu.VMEM)
CHUNK = 512
PARAMS = pltpu.CompilerParams(vmem_limit_bytes=24 * 1024 * 1024)
WHOLE = pltpu.CompilerParams(vmem_limit_bytes=60 * 1024 * 1024)


def dot(a, b, dims=NN):
    return lax.dot_general(a, b, dims, preferred_element_type=F32)


def cost(flops, moved, transcendentals=0):
    return pl.CostEstimate(flops=flops, bytes_accessed=moved, transcendentals=transcendentals)


def attention_scores(g, q, k, v, do, scores, grad_probs):
    per_group = q.shape[1] // k.shape[1]
    cols = slice(g * HEAD_SIZE, (g + 1) * HEAD_SIZE)
    scores[g] = dot(k[:, cols], stacked(q, g, per_group), NT)
    grad_probs[g] = dot(v[:, cols], stacked(do, g, per_group), NT)


def stacked(array, g, per_group):
    first = g * per_group * HEAD_SIZE
    heads = [array[:, first + h * HEAD_SIZE : first + (h + 1) * HEAD_SIZE] for h in range(per_group)]
    return jnp.concatenate(heads, axis=0)


def attention_softmax(g, scores, grad_probs, probs_b, ds):
    length = scores.shape[1]
    group = scores.shape[2]
    scale = 1.0 / math.sqrt(HEAD_SIZE)
    targets = lax.broadcasted_iota(jnp.int32, (length, length), 0)
    positions = lax.broadcasted_iota(jnp.int32, (length, length), 1)
    allowed = targets <= positions
    for at in range(0, group, length):
        cols = slice(at, at + length)
        masked = jnp.where(allowed, scores[g, :, cols], -1e30)
        raw = jnp.exp((masked - jnp.max(masked, axis=0, keepdims=True)) * scale)
        probs = raw * (1.0 / jnp.sum(raw, axis=0, keepdims=True))
        slopes = grad_probs[g, :, cols]
        delta = jnp.sum(probs * slopes, axis=0, keepdims=True)
        probs_b[:, g * group + at : g * group + at + length] = probs.astype(BF16)
        ds[:, g * group + at : g * group + at + length] = (probs * (slopes - delta)).astype(BF16)


def attention_kernel(
    q_hbm, k_hbm, v_hbm, do_hbm, p_hbm,
    gk_ref, ds_hbm, sent_hbm, kept_hbm,
    q, k, v, do, p, probs_b, ds, scores, grad_probs, partial, sems, p_sems, out_sems,
):
    kv_heads = k.shape[1] // HEAD_SIZE
    group = q.shape[1] // kv_heads
    per_group = group // HEAD_SIZE
    groups, features = p.shape[0], p.shape[2]
    chips = groups // 2
    member = lax.axis_index("mp")
    chip, core = lax.div(member, 2), lax.rem(member, 2)
    small = [
        pltpu.make_async_copy(k_hbm, k, sems.at[0]),
        pltpu.make_async_copy(v_hbm, v, sems.at[1]),
    ]
    large, stored = [], []
    for g in range(kv_heads):
        cols = pl.ds(g * group, group)
        large.append((
            pltpu.make_async_copy(q_hbm.at[:, cols], q.at[:, cols], sems.at[2 + 2 * g]),
            pltpu.make_async_copy(do_hbm.at[:, cols], do.at[:, cols], sems.at[3 + 2 * g]),
        ))
        stored.append(pltpu.make_async_copy(ds.at[:, cols], ds_hbm.at[:, cols], out_sems.at[g]))
    blocks = []
    for b in range(groups):
        column = core if b >= chips else 1 - core
        start = (2 * lax.rem(chip + b + 1, chips) + column) * features
        rows = pl.ds(pl.multiple_of(start, features), features)
        blocks.append(pltpu.make_async_copy(p_hbm.at[:, rows, :], p.at[b], p_sems.at[b]))
    for copy in small:
        copy.start()
    for pair in large:
        for copy in pair:
            copy.start()
    for copy in blocks:
        copy.start()
    for copy in small:
        copy.wait()
    for g in range(kv_heads):
        for copy in large[g]:
            copy.wait()
        attention_scores(g, q, k, v, do, scores, grad_probs)
    scale = 1.0 / math.sqrt(HEAD_SIZE)
    values, keys = [], []
    for g in range(kv_heads):
        attention_softmax(g, scores, grad_probs, probs_b, ds)
        stored[g].start()
        cols = slice(g * group, (g + 1) * group)
        values.append(dot(probs_b[:, cols], stacked(do, g, per_group)).astype(BF16))
        keys.append((dot(ds[:, cols], stacked(q, g, per_group)) * scale).astype(BF16))
    gk = jnp.concatenate(keys, axis=1)
    gk_ref[...] = gk
    grads = jnp.concatenate([gk] + values, axis=1)
    step = min(CHUNK, features)
    for b in range(groups):
        blocks[b].wait()
        for at in range(0, features, step):
            rows = slice(at, at + step)
            both = jnp.concatenate([p[b, 0, rows, :], p[b, 1, rows, :]], axis=1)
            partial[b, rows, :] = dot(both, grads, NT).astype(BF16)
        target = sent_hbm.at[b] if b < chips else kept_hbm.at[b - chips]
        stored.append(pltpu.make_async_copy(partial.at[b], target, out_sems.at[kv_heads + b]))
        stored[-1].start()
    for copy in stored:
        copy.wait()


def query_kernel(ds_hbm, k_hbm, gq_hbm, ds, k, gq, sems, out_sems):
    kv_heads = k.shape[1] // HEAD_SIZE
    group = gq.shape[1] // kv_heads
    scale = 1.0 / math.sqrt(HEAD_SIZE)
    key_copy = pltpu.make_async_copy(k_hbm, k, sems.at[kv_heads])
    key_copy.start()
    loads, stores = [], []
    for g in range(kv_heads):
        cols = pl.ds(g * group, group)
        loads.append(pltpu.make_async_copy(ds_hbm.at[:, cols], ds.at[:, cols], sems.at[g]))
        stores.append(pltpu.make_async_copy(gq.at[:, cols], gq_hbm.at[:, cols], out_sems.at[g]))
        loads[-1].start()
    key_copy.wait()
    for g in range(kv_heads):
        loads[g].wait()
        key = k[:, g * HEAD_SIZE : (g + 1) * HEAD_SIZE]
        for at in range(g * group, (g + 1) * group, HEAD_SIZE):
            grad = dot(ds[:, at : at + HEAD_SIZE], key, TN) * scale
            gq[:, at : at + HEAD_SIZE] = grad.astype(BF16)
        stores[g].start()
    for copy in stores:
        copy.wait()


def input_kernel(kept_ref, came_ref, *refs):
    out_ref = refs[-1]
    total = kept_ref[len(refs) - 1].astype(F32) + came_ref[len(refs) - 1].astype(F32)
    for ref in refs[:-1]:
        total += ref[...].astype(F32)
    out_ref[...] = total.T.astype(BF16)


def turned_kernel(mine_ref, theirs_ref, next_ref, x_hbm, out_ref, own, sem):
    rows, width = next_ref.shape
    parts = out_ref.shape[1] // rows
    far = groups = parts // 2
    part, member = lax.axis_index("dp"), lax.axis_index("mp")
    cols = pl.ds(pl.multiple_of(part * width, width), width)
    copy = pltpu.make_async_copy(x_hbm.at[:, cols], own, sem)
    copy.start()

    def put(k, piece):
        place = far * lax.rem(k, 2) + 2 * lax.div(lax.rem(k, far), 2) + lax.div(k, far)
        out_ref[:, pl.ds(pl.multiple_of(place * rows, rows), rows)] = piece.T

    partners = [far + (member ^ j) for j in range(0, groups, 2)]
    partners += [k + lax.rem(member, 2) for k in range(2, far, 2)]
    for at, k in enumerate(partners):
        put(k, mine_ref[at * rows : (at + 1) * rows, :])
        put(k ^ 1, theirs_ref[at * rows : (at + 1) * rows, :])
    put(jnp.int32(1), next_ref[...])
    copy.wait()
    put(jnp.int32(0), own[...])


def weights_kernel(x_ref, *refs):
    keys, out_ref = refs[:-1], refs[-1]
    rows = keys[0].shape[0]
    total = dot(x_ref[:, :rows], keys[0][...])
    for j in range(1, len(keys)):
        total += dot(x_ref[:, j * rows : (j + 1) * rows], keys[j][...])
    out_ref[...] = total * (1.0 / (2 * len(keys)))


def along_dp(array, partner, parts, groups):
    pairs = [
        (i * groups + m, (i ^ partner(m)) * groups + m)
        for i in range(parts)
        for m in range(groups)
    ]
    return lax.ppermute(array, ("dp", "mp"), pairs)


def along_mp(array, bit, groups):
    return lax.ppermute(array, "mp", [(m, m ^ bit) for m in range(groups)])


def sent_inputs(inputs, parts, groups):
    far = parts // 2
    part, member = lax.axis_index("dp"), lax.axis_index("mp")
    rows, width = inputs.shape[0], inputs.shape[1] // parts

    def block(k):
        return lax.dynamic_slice(inputs, (0, (part ^ k) * width), (rows, width))

    distant = along_dp(block(far + member), lambda m: far + m, parts, groups)
    near = []
    for k in range(2, far, 2):
        sent = block(k + lax.rem(member, 2))
        near.append(along_dp(sent, lambda m, k=k: k + m % 2, parts, groups))
    return distant, near, along_dp(block(1), lambda m: 1, parts, groups)


def shared_inputs(piece, groups):
    pieces = [piece]
    bit = 2
    while bit < groups:
        pieces += [along_mp(piece, bit, groups) for piece in pieces]
        bit *= 2
    return pieces


def turned_inputs(mine, theirs, next_inputs, inputs):
    rows, width = next_inputs.shape
    return pl.pallas_call(
        turned_kernel,
        in_specs=[IN_VMEM, IN_VMEM, IN_VMEM, IN_HBM],
        out_specs=IN_VMEM,
        out_shape=jax.ShapeDtypeStruct((width, inputs.shape[1] // width * rows), inputs.dtype),
        scratch_shapes=[pltpu.VMEM((rows, width), inputs.dtype), pltpu.SemaphoreType.DMA],
        compiler_params=PARAMS,
        cost_estimate=cost(0, 4 * inputs.size),
    )(mine, theirs, next_inputs, inputs)


def summed_weights(turned, keys):
    width, columns = turned.shape[0], keys[0].shape[1]
    return pl.pallas_call(
        weights_kernel,
        out_specs=IN_VMEM,
        out_shape=jax.ShapeDtypeStruct((width, columns), F32),
        compiler_params=PARAMS,
        cost_estimate=cost(
            2 * turned.size * columns, 2 * turned.size + 4 * width * columns
        ),
    )(turned, *keys)


def gathered_weights(inputs, grad_key, parts):
    rows = inputs.shape[0]
    width = inputs.shape[1] // parts
    blocks = inputs.reshape(rows, parts, width).transpose(1, 0, 2)
    mine = lax.all_to_all(blocks, "dp", split_axis=0, concat_axis=0, tiled=True)
    keys = lax.all_gather(grad_key, "dp", axis=0)
    return jnp.einsum("psd,psc->dc", mine, keys, preferred_element_type=F32) / parts


def body(query_states, key_states, value_states, grad_context, inputs_normed, projections):
    parts = lax.axis_size("dp")
    groups = lax.axis_size("mp")
    chips = groups // 2
    rows, width = key_states.shape
    query_width = query_states.shape[1]
    features = projections.shape[1] // groups
    kv_heads = width // HEAD_SIZE
    partial = jax.ShapeDtypeStruct((chips, features, rows), BF16)
    exchange = parts == 2 * groups and inputs_normed.shape[1] % (parts * 128) == 0
    if exchange:
        distant, near, next_inputs = sent_inputs(inputs_normed, parts, groups)

    whole = pltpu.VMEM((rows, query_width), BF16)
    narrow = pltpu.VMEM((rows, width), BF16)
    wide = pltpu.VMEM((kv_heads, rows, query_width // kv_heads), F32)
    grad_key, grad_scores, sent, kept = pl.pallas_call(
        attention_kernel,
        in_specs=[IN_HBM] * 5,
        out_specs=[IN_VMEM, ANYWHERE, ANYWHERE, ANYWHERE],
        out_shape=(
            jax.ShapeDtypeStruct((rows, width), BF16),
            jax.ShapeDtypeStruct((rows, query_width), BF16),
            partial,
            partial,
        ),
        scratch_shapes=[whole, narrow, narrow, whole]
        + [pltpu.VMEM((groups, 2, features, width), BF16), whole, whole, wide, wide]
        + [pltpu.VMEM((groups, features, rows), BF16)]
        + [pltpu.SemaphoreType.DMA((2 + 2 * kv_heads,)), pltpu.SemaphoreType.DMA((groups,))]
        + [pltpu.SemaphoreType.DMA((kv_heads + groups,))],
        compiler_params=WHOLE,
        cost_estimate=cost(
            8 * rows * rows * query_width + 4 * rows * width * features * groups,
            6 * rows * query_width + 4 * width * features * groups,
            rows * query_width,
        ),
    )(query_states, key_states, value_states, grad_context, projections)

    grad_query = pl.pallas_call(
        query_kernel,
        in_specs=[IN_HBM, IN_HBM],
        out_specs=ANYWHERE,
        out_shape=jax.ShapeDtypeStruct((rows, query_width), BF16),
        scratch_shapes=[whole, narrow, whole]
        + [pltpu.SemaphoreType.DMA((1 + kv_heads,)), pltpu.SemaphoreType.DMA((kv_heads,))],
        compiler_params=WHOLE,
        cost_estimate=cost(2 * rows * rows * query_width, 4 * rows * query_width),
    )(grad_scores, key_states)

    if exchange:
        ready, near, next_inputs = lax.optimization_barrier((grad_key, near, next_inputs))
        sent, distant, near = lax.optimization_barrier((sent, distant, near))
        first = along_dp(ready, lambda m: parts // 2, parts, groups)
        pieces = shared_inputs(distant, groups)
    came = along_mp(sent, 1, groups)
    pairs = [(kept[b].astype(F32) + came[b].astype(F32)).astype(BF16) for b in range(chips - 1)]
    if exchange:
        first, pieces, pairs = lax.optimization_barrier((first, pieces, pairs))
        keys = {0: jnp.concatenate([grad_key, first])}
        mine = jnp.concatenate(pieces + near)
        theirs = along_mp(mine, 1, groups)
        bit = parts // 4
        while bit > 1:
            for k in list(keys):
                keys[k ^ bit] = along_dp(keys[k], lambda m, bit=bit: bit, parts, groups)
            bit //= 2
    last = []
    for b in range(chips - 1):
        shift = [(m, (m + 2 * (b + 1)) % groups) for m in range(groups)]
        last.append(lax.ppermute(pairs[b], "mp", shift))
    grad_input = pl.pallas_call(
        input_kernel,
        out_specs=IN_VMEM,
        out_shape=jax.ShapeDtypeStruct((rows, features), BF16),
        compiler_params=PARAMS,
        cost_estimate=cost(rows * features, 8 * rows * features),
    )(kept, came, *last)

    if exchange:
        beside = []
        for k in range(0, parts // 2, 2):
            pair, beside = lax.optimization_barrier((keys[k], beside))
            beside.append(along_dp(pair, lambda m: 1, parts, groups))
        turned = turned_inputs(mine, theirs, next_inputs, inputs_normed)
        beside[-1], grad_input = lax.optimization_barrier((beside[-1], grad_input))
        keys = [keys[k] for k in range(0, parts // 2, 2)] + beside
        grad_weights = summed_weights(turned, keys)
    else:
        grad_weights = gathered_weights(inputs_normed, grad_key, parts)
    return (grad_query, grad_input, grad_weights)


def solution(mesh):
    placed = (
        P("dp", "mp"),
        P("dp", "mp"),
        P("dp", "mp"),
        P("dp", "mp"),
        P("dp", None),
        P(None, None, "mp"),
    )
    return jax.shard_map(
        body,
        mesh=mesh,
        in_specs=placed,
        out_specs=(P("dp", "mp"), P("dp", "mp"), P("dp", "mp")),
        check_vma=False,
    )
```

time: 38.1 us -> 38 us (level)
  waiting for transfers between devices: 10.4 us -> 7.03 us
  starting transfers between devices: 12.4 us -> 14.6 us
  Pallas kernels: 10.2 us -> 11.3 us
    ppermute x7, waiting for transfers between devices: 10.4 us -> 6.44 us  [along_dp(): return lax.ppermute(array, ('dp', 'mp'), pairs)]
    ppermute x7, starting transfers between devices: 8.78 us -> 11.2 us  [along_dp(): return lax.ppermute(array, ('dp', 'mp'), pairs)]
    ppermute x1, starting transfers between devices: 1.62 us -> 0.44 us  [body(): last.append(lax.ppermute(pairs[b], 'mp', shift))]
    pallas_call x3, Pallas kernels: 2.83 us -> 3.97 us  [the longest x1 2.26 us: body(): pl.pallas_call(query_kernel, in_specs=[IN_HBM, IN_HBM], out_specs=ANYWHER...]
    ppermute x3, starting transfers between devices: 1.99 us -> 2.97 us  [along_mp(): return lax.ppermute(array, 'mp', [(m, m ^ bit) for m in range(groups)])]
    ppermute x1, waiting for transfers between devices: 0.01 us -> 0.38 us  [body(): last.append(lax.ppermute(pairs[b], 'mp', shift))]
    unnamed x11 -> x7, local copies, waits for them, and re-layouts: 1.96 us -> 1.91 us
  transfers between devices with their start and end apart: 11 -> 11, of which waited for: 5 -> 6; matrix products, arithmetic and copies ran while one was open for 5% -> 5% of each run, Pallas kernels for 25% -> 25%
where the time goes in v5:
time: 38 us; the launch traced here: 37.7 us
  starting transfers between devices  14.6 us (38%)
  Pallas kernels  11.3 us (30%)
  waiting for transfers between devices  7.03 us (18%)
  local copies, waits for them, and re-layouts  3 us (8%)
  other arithmetic  1.02 us (3%)
  between operations  0.74 us (2%)
    ppermute x7, starting transfers between devices, along_dp(): return lax.ppermute(array, ('dp', 'mp'), pairs)  11.2 us
    pallas_call x1, Pallas kernels, body(): pl.pallas_call(attention_kernel, in_specs=[IN_HBM] * 5, out_specs=[IN_VME...  6.45 us
    ppermute x7, waiting for transfers between devices, along_dp(): return lax.ppermute(array, ('dp', 'mp'), pairs)  6.44 us
    ppermute x3, starting transfers between devices, along_mp(): return lax.ppermute(array, 'mp', [(m, m ^ bit) for m in range(groups)])  2.97 us
    pallas_call x1, Pallas kernels, body(): pl.pallas_call(query_kernel, in_specs=[IN_HBM, IN_HBM], out_specs=ANYWHER...  2.26 us
    unnamed x7, local copies, waits for them, and re-layouts  1.91 us
    pallas_call x1, Pallas kernels, summed_weights(): pl.pallas_call(weights_kernel, out_specs=IN_VMEM, out_shape=jax.ShapeDtyp...  1.24 us
    dynamic_slice x1, local copies, waits for them, and re-layouts, block(): return lax.dynamic_slice(inputs, (0, (part ^ k) * width), (rows, width))  1.07 us
  transfers between devices with their start and end apart: 11, of which 6 were waited for; matrix products, arithmetic and copies ran while one was open for 5% of the time, Pallas kernels for 25%

profile of v5, /device:TPU:0, one launch (start us, length us, event | category | flops | bytes accessed | tf_op | source)
XLA Modules:
  0.0 37.7 jit_solution(2096317094610474177)
XLA Ops:
  0.7 1.1 %constant_dynamic-slice_fusion = (bf16[128,512]{1,0:T(8,128)(2,1)S(1)}, bf16[128,512]{1,0:T(8,128)(2,1)S(1)}, bf16[128,512]{1,0:T(8,128)(2,1)S(1)}) fusion(bf16[128,4096]{1,0:T(8,128)(2,1)} %x_hbm.1, s32[]{:T(128)S(6)} %select_n.11, s32[]{:T(128)S(6)} %select_n.10, s32[]{:T(128)S(6)} %select_n.9), kind=kLoop, calls=%fused_computation.7 | loop fusion | bytes 786444 | tf_op jit(solution)/shard_map/dynamic_slice | solution.py:214
  1.7 3.0 %collective-permute-start.1 = (bf16[128,512]{1,0:T(8,128)(2,1)S(1)}, bf16[128,512]{1,0:T(8,128)(2,1)S(1)}, u32[]{:S(2)}, u32[]{:S(2)}) collective-permute-start(bf16[128,512]{1,0:T(8,128)(2,1)S(1)} %get-tuple-element.40), channel_id=1, source_target_pairs={{0,4},{1,5},{2,6},{3,7},{4,0},{5,1},{6,2},{7,3},{8,12},{9,13},{10,... | collective-permute-start | bytes 393224 | tf_op jit(solution)/shard_map/ppermute | solution.py:201
  4.7 1.6 %collective-permute-start = (bf16[128,512]{1,0:T(8,128)(2,1)S(1)}, bf16[128,512]{1,0:T(8,128)(2,1)S(1)}, u32[]{:S(2)}, u32[]{:S(2)}) collective-permute-start(bf16[128,512]{1,0:T(8,128)(2,1)S(1)} %get-tuple-element.41), channel_id=1, source_target_pairs={{0,8},{1,13},{2,10},{3,15},{4,12},{5,9},{6,14},{7,11},{8,0},{9,5},... | collective-permute-start | bytes 393224 | tf_op jit(solution)/shard_map/ppermute | solution.py:201
  6.3 2.6 %collective-permute-start.3 = (bf16[128,512]{1,0:T(8,128)(2,1)S(1)}, bf16[128,512]{1,0:T(8,128)(2,1)S(1)}, u32[]{:S(2)}, u32[]{:S(2)}) collective-permute-start(bf16[128,512]{1,0:T(8,128)(2,1)S(1)} %get-tuple-element.39), channel_id=1, source_target_pairs={{0,16},{1,21},{2,26},{3,31},{4,20},{5,17},{6,30},{7,27},{8,24},{9,... | collective-permute-start | bytes 393224 | tf_op jit(solution)/shard_map/ppermute | solution.py:201
  8.9 6.5 %shard_map.85 = (bf16[128,256]{1,0:T(8,128)(2,1)}, bf16[128,2048]{1,0:T(8,128)(2,1)}, bf16[2,1024,128]{2,1,0:T(8,128)(2,1)}, bf16[2,1024,128]{2,1,0:T(8,128)(2,1)}) custom-call(bf16[128,2048]{1,0:T(8,128)(2,1)} %q_hbm.1, bf16[128,256]{1,0:T(8,128)(2,1)} %k_hbm.3, bf16[128,256]{1,0:T(8,128)(2,1)} %v_hbm.1, bf16[128,2048]{1,0:T(8,128)(2,1)} %do_hbm.1, ...), custom_call_target="tpu_custom_call" | custom-call | flops 805306368 | bytes 5767168 | tf_op jit(solution)/shard_map/pallas_call | solution.py:284
  15.4 0.2 collective-permute-done.3
  15.6 0.3 collective-permute-start.2
  15.9 2.9 %collective-permute-start.4 = (bf16[128,512]{1,0:T(8,128)(2,1)S(1)}, bf16[128,512]{1,0:T(8,128)(2,1)S(1)}, u32[]{:S(2)}, u32[]{:S(2)}) collective-permute-start(bf16[128,512]{1,0:T(8,128)(2,1)S(1)} %collective-permute-done.3), channel_id=1, source_target_pairs={{0,2},{1,3},{2,0},{3,1},{4,6},{5,7},{6,4},{7,5},{8,10},{9,11},{10,... | collective-permute-start | bytes 393224 | tf_op jit(solution)/shard_map/ppermute | solution.py:205
  18.8 1.0 %fusion = bf16[1024,128]{1,0:T(8,128)(2,1)S(1)} fusion(bf16[2,1024,128]{2,1,0:T(8,128)(2,1)S(1)} %collective-permute-done.5.came_ref, bf16[2,1024,128]{2,1,0:T(8,128)(2,1)} %get-tuple-element.27.kept_ref), kind=kLoop, calls=%fused_computation.1 | loop fusion | flops 524288 | bytes 786432 | tf_op jit(solution)/shard_map/convert_element_type | solution.py:324
  19.8 2.7 %collective-permute-done.2 = bf16[128,256]{1,0:T(8,128)(2,1)S(1)} collective-permute-done((bf16[128,256]{1,0:T(8,128)(2,1)}, bf16[128,256]{1,0:T(8,128)(2,1)S(1)}, u32[]{:S(2)}, u32[]{:S(2)}) %collective-permute-start.2) | collective-permute-done | bytes 65568 | tf_op jit(solution)/shard_map/ppermute | solution.py:201
  22.5 0.2 collective-permute-done.4
  22.8 0.8 %constant_dynamic-update-slice_fusion.1 = bf16[256,256]{1,0:T(8,128)(2,1)S(1)} fusion(bf16[128,256]{1,0:T(8,128)(2,1)} %get-tuple-element.23), kind=kLoop, calls=%fused_computation.3 | loop fusion | bytes 131072
  23.7 0.6 %collective-permute-start.7 = (bf16[256,256]{1,0:T(8,128)(2,1)S(1)}, bf16[256,256]{1,0:T(8,128)(2,1)S(1)}, u32[]{:S(2)}, u32[]{:S(2)}) collective-permute-start(bf16[256,256]{1,0:T(8,128)(2,1)S(1)} %constant_dynamic-update-slice_fusion.refs_0_), channel_id=1, source_target_pairs={{0,4},{1,5},{2,6},{3,7},{4,0},{5,1},{6,2},{7,3},{8,12},{9,13},{10,... | collective-permute-start | bytes 393224 | tf_op jit(solution)/shard_map/ppermute | solution.py:201
  24.3 1.6 %collective-permute-start.6 = (bf16[256,256]{1,0:T(8,128)(2,1)S(1)}, bf16[256,256]{1,0:T(8,128)(2,1)S(1)}, u32[]{:S(2)}, u32[]{:S(2)}) collective-permute-start(bf16[256,256]{1,0:T(8,128)(2,1)S(1)} %constant_dynamic-update-slice_fusion.refs_0_), channel_id=1, source_target_pairs={{0,8},{1,9},{2,10},{3,11},{4,12},{5,13},{6,14},{7,15},{8,0},{9,1},... | collective-permute-start | bytes 393224 | tf_op jit(solution)/shard_map/ppermute | solution.py:201
  25.9 0.4 %collective-permute-start.9 = (bf16[1024,128]{1,0:T(8,128)(2,1)S(1)}, bf16[1024,128]{1,0:T(8,128)(2,1)S(1)}, u32[]{:S(2)}, u32[]{:S(2)}) collective-permute-start(bf16[1024,128]{1,0:T(8,128)(2,1)S(1)} %fusion), channel_id=1, source_target_pairs={{0,2},{1,3},{2,0},{3,1},{4,6},{5,7},{6,4},{7,5},{8,10},{9,11},{10,... | collective-permute-start | bytes 786440 | tf_op jit(solution)/shard_map/ppermute | solution.py:338
  26.3 3.3 %collective-permute-done.7.refs_2_ = bf16[256,256]{1,0:T(8,128)(2,1)S(1)} collective-permute-done((bf16[256,256]{1,0:T(8,128)(2,1)S(1)}, bf16[256,256]{1,0:T(8,128)(2,1)S(1)}, u32[]{:S(2)}, u32[]{:S(2)}) %collective-permute-start.7) | collective-permute-done | bytes 131104 | tf_op jit(solution)/shard_map/ppermute | solution.py:201
  29.6 0.3 collective-permute-done.6.refs_1_
  29.9 1.5 %collective-permute-start.8 = (bf16[256,256]{1,0:T(8,128)(2,1)S(1)}, bf16[256,256]{1,0:T(8,128)(2,1)S(1)}, u32[]{:S(2)}, u32[]{:S(2)}) collective-permute-start(bf16[256,256]{1,0:T(8,128)(2,1)S(1)} %collective-permute-done.6.refs_1_), channel_id=1, source_target_pairs={{0,4},{1,5},{2,6},{3,7},{4,0},{5,1},{6,2},{7,3},{8,12},{9,13},{10,... | collective-permute-start | bytes 393224 | tf_op jit(solution)/shard_map/ppermute | solution.py:201
  31.4 2.3 %shard_map.86 = bf16[128,2048]{1,0:T(8,128)(2,1)} custom-call(bf16[128,2048]{1,0:T(8,128)(2,1)} %get-tuple-element.21.ds_hbm, bf16[128,256]{1,0:T(8,128)(2,1)} %k_hbm.3), custom_call_target="tpu_custom_call" | custom-call | flops 67108864 | bytes 1048576 | tf_op jit(solution)/shard_map/pallas_call | solution.py:307
  33.7 0.4 %collective-permute-done.9.refs_0_ = bf16[1024,128]{1,0:T(8,128)(2,1)S(1)} collective-permute-done((bf16[1024,128]{1,0:T(8,128)(2,1)S(1)}, bf16[1024,128]{1,0:T(8,128)(2,1)S(1)}, u32[]{:S(2)}, u32[]{:S(2)}) %collective-permute-start.9) | collective-permute-done | bytes 262176 | tf_op jit(solution)/shard_map/ppermute | solution.py:338
  34.0 1.0 %copy-done.1 = bf16[2,1024,128]{2,1,0:T(8,128)(2,1)S(1)} copy-done((bf16[2,1024,128]{2,1,0:T(8,128)(2,1)S(1)}, bf16[2,1024,128]{2,1,0:T(8,128)(2,1)}, u32[]{:S(2)}) %copy-start.1) | copy-done | bytes 524312
  35.1 0.9 %shard_map.87 = bf16[128,1024]{1,0:T(8,128)(2,1)} custom-call(bf16[2,1024,128]{2,1,0:T(8,128)(2,1)S(1)} %copy-done.1, bf16[2,1024,128]{2,1,0:T(8,128)(2,1)S(1)} %collective-permute-done.5.came_ref, bf16[1024,128]{1,0:T(8,128)(2,1)S(1)} %collective-permute-done.9.refs_0_), custom_call_target="tpu_custom_call" | custom-call | flops 131072 | bytes 1048576 | tf_op jit(solution)/shard_map/pallas_call | solution.py:339
  36.0 0.5 %shard_map.88.x_ref = bf16[512,1024]{1,0:T(8,128)(2,1)S(1)} custom-call(bf16[384,512]{1,0:T(8,128)(2,1)S(1)} %constant_dynamic-update-slice_fusion.2.mine_ref, bf16[384,512]{1,0:T(8,128)(2,1)S(1)} %collective-permute-done.10.theirs_ref, bf16[128,512]{1,0:T(8,128)(2,1)S(1)} %collective-permute-done.1.next_ref, bf16[128,4096]{1,0:T(8,128)(2,1)S(1)} %copy-done), custom_call_target="tpu_custom_call" | custom-call | bytes 2097152 | tf_op jit(solution)/shard_map/pallas_call | solution.py:235
  36.4 1.2 %shard_map.89 = f32[512,256]{1,0:T(8,128)} custom-call(bf16[512,1024]{1,0:T(8,128)(2,1)S(1)} %shard_map.88.x_ref, bf16[256,256]{1,0:T(8,128)(2,1)S(1)} %constant_dynamic-update-slice_fusion.refs_0_, bf16[256,256]{1,0:T(8,128)(2,1)S(1)} %collective-permute-done.6.refs_1_, bf16[256,256]{1,0:T(8,128)(2,1)S(1)} %collective-permute-done.7.refs_2_, ...), custom_call_target="tpu_custom_call" | custom-call | flops 268435456 | bytes 1572864 | tf_op jit(solution)/shard_map/pallas_call | solution.py:248
  (14 shorter events, 0.1 us)
Async XLA Ops:
  1.7 13.6 %collective-permute-start.1 = (bf16[128,512]{1,0:T(8,128)(2,1)S(1)}, bf16[128,512]{1,0:T(8,128)(2,1)S(1)}, u32[]{:S(2)}, u32[]{:S(2)}) collective-permute-start(bf16[128,512]{1,0:T(8,128)(2,1)S(1)} %get-tuple-element.40), channel_id=1, source_target_pairs={{0,4},{1,5},{2,6},{3,7},{4,0},{5,1},{6,2},{7,3},{8,12},{9,13},{10,... | collective-permute-start | bytes 393224 | tf_op jit(solution)/shard_map/ppermute | solution.py:201
  4.7 10.6 %collective-permute-start = (bf16[128,512]{1,0:T(8,128)(2,1)S(1)}, bf16[128,512]{1,0:T(8,128)(2,1)S(1)}, u32[]{:S(2)}, u32[]{:S(2)}) collective-permute-start(bf16[128,512]{1,0:T(8,128)(2,1)S(1)} %get-tuple-element.41), channel_id=1, source_target_pairs={{0,8},{1,13},{2,10},{3,15},{4,12},{5,9},{6,14},{7,11},{8,0},{9,5},... | collective-permute-start | bytes 393224 | tf_op jit(solution)/shard_map/ppermute | solution.py:201
  6.3 29.7 %copy-start = (bf16[128,4096]{1,0:T(8,128)(2,1)S(1)}, bf16[128,4096]{1,0:T(8,128)(2,1)}, u32[]{:S(2)}) copy-start(bf16[128,4096]{1,0:T(8,128)(2,1)} %x_hbm.1) | copy-start | bytes 3145732
  6.3 9.3 %collective-permute-start.3 = (bf16[128,512]{1,0:T(8,128)(2,1)S(1)}, bf16[128,512]{1,0:T(8,128)(2,1)S(1)}, u32[]{:S(2)}, u32[]{:S(2)}) collective-permute-start(bf16[128,512]{1,0:T(8,128)(2,1)S(1)} %get-tuple-element.39), channel_id=1, source_target_pairs={{0,16},{1,21},{2,26},{3,31},{4,20},{5,17},{6,30},{7,27},{8,24},{9,... | collective-permute-start | bytes 393224 | tf_op jit(solution)/shard_map/ppermute | solution.py:201
  15.6 3.2 %collective-permute-start.5 = (bf16[2,1024,128]{2,1,0:T(8,128)(2,1)}, bf16[2,1024,128]{2,1,0:T(8,128)(2,1)S(1)}, u32[]{:S(2)}, u32[]{:S(2)}) collective-permute-start(bf16[2,1024,128]{2,1,0:T(8,128)(2,1)} %get-tuple-element.28), channel_id=1, source_target_pairs={{0,1},{1,0},{2,3},{3,2},{4,5},{5,4},{6,7},{7,6},{8,9},{9,8},{10,11... | collective-permute-start | bytes 1572872 | tf_op jit(solution)/shard_map/ppermute | solution.py:205
  15.6 6.9 %collective-permute-start.2 = (bf16[128,256]{1,0:T(8,128)(2,1)}, bf16[128,256]{1,0:T(8,128)(2,1)S(1)}, u32[]{:S(2)}, u32[]{:S(2)}) collective-permute-start(bf16[128,256]{1,0:T(8,128)(2,1)} %get-tuple-element.23), channel_id=1, source_target_pairs={{0,16},{1,17},{2,18},{3,19},{4,20},{5,21},{6,22},{7,23},{8,24},{9,... | collective-permute-start | bytes 196616 | tf_op jit(solution)/shard_map/ppermute | solution.py:201
  15.9 6.8 %collective-permute-start.4 = (bf16[128,512]{1,0:T(8,128)(2,1)S(1)}, bf16[128,512]{1,0:T(8,128)(2,1)S(1)}, u32[]{:S(2)}, u32[]{:S(2)}) collective-permute-start(bf16[128,512]{1,0:T(8,128)(2,1)S(1)} %collective-permute-done.3), channel_id=1, source_target_pairs={{0,2},{1,3},{2,0},{3,1},{4,6},{5,7},{6,4},{7,5},{8,10},{9,11},{10,... | collective-permute-start | bytes 393224 | tf_op jit(solution)/shard_map/ppermute | solution.py:205
  22.7 13.2 %collective-permute-start.10 = (bf16[384,512]{1,0:T(8,128)(2,1)S(1)}, bf16[384,512]{1,0:T(8,128)(2,1)S(1)}, u32[]{:S(2)}, u32[]{:S(2)}) collective-permute-start(bf16[384,512]{1,0:T(8,128)(2,1)S(1)} %constant_dynamic-update-slice_fusion.2.mine_ref), channel_id=1, source_target_pairs={{0,1},{1,0},{2,3},{3,2},{4,5},{5,4},{6,7},{7,6},{8,9},{9,8},{10,11... | collective-permute-start | bytes 1179656 | tf_op jit(solution)/shard_map/ppermute | solution.py:205
  23.7 6.0 %collective-permute-start.7 = (bf16[256,256]{1,0:T(8,128)(2,1)S(1)}, bf16[256,256]{1,0:T(8,128)(2,1)S(1)}, u32[]{:S(2)}, u32[]{:S(2)}) collective-permute-start(bf16[256,256]{1,0:T(8,128)(2,1)S(1)} %constant_dynamic-update-slice_fusion.refs_0_), channel_id=1, source_target_pairs={{0,4},{1,5},{2,6},{3,7},{4,0},{5,1},{6,2},{7,3},{8,12},{9,13},{10,... | collective-permute-start | bytes 393224 | tf_op jit(solution)/shard_map/ppermute | solution.py:201
  24.3 5.6 %collective-permute-start.6 = (bf16[256,256]{1,0:T(8,128)(2,1)S(1)}, bf16[256,256]{1,0:T(8,128)(2,1)S(1)}, u32[]{:S(2)}, u32[]{:S(2)}) collective-permute-start(bf16[256,256]{1,0:T(8,128)(2,1)S(1)} %constant_dynamic-update-slice_fusion.refs_0_), channel_id=1, source_target_pairs={{0,8},{1,9},{2,10},{3,11},{4,12},{5,13},{6,14},{7,15},{8,0},{9,1},... | collective-permute-start | bytes 393224 | tf_op jit(solution)/shard_map/ppermute | solution.py:201
  25.9 8.1 %collective-permute-start.9 = (bf16[1024,128]{1,0:T(8,128)(2,1)S(1)}, bf16[1024,128]{1,0:T(8,128)(2,1)S(1)}, u32[]{:S(2)}, u32[]{:S(2)}) collective-permute-start(bf16[1024,128]{1,0:T(8,128)(2,1)S(1)} %fusion), channel_id=1, source_target_pairs={{0,2},{1,3},{2,0},{3,1},{4,6},{5,7},{6,4},{7,5},{8,10},{9,11},{10,... | collective-permute-start | bytes 786440 | tf_op jit(solution)/shard_map/ppermute | solution.py:338
  29.9 6.1 %collective-permute-start.8 = (bf16[256,256]{1,0:T(8,128)(2,1)S(1)}, bf16[256,256]{1,0:T(8,128)(2,1)S(1)}, u32[]{:S(2)}, u32[]{:S(2)}) collective-permute-start(bf16[256,256]{1,0:T(8,128)(2,1)S(1)} %collective-permute-done.6.refs_1_), channel_id=1, source_target_pairs={{0,4},{1,5},{2,6},{3,7},{4,0},{5,1},{6,2},{7,3},{8,12},{9,13},{10,... | collective-permute-start | bytes 393224 | tf_op jit(solution)/shard_map/ppermute | solution.py:201
  34.0 1.0 %copy-start.1 = (bf16[2,1024,128]{2,1,0:T(8,128)(2,1)S(1)}, bf16[2,1024,128]{2,1,0:T(8,128)(2,1)}, u32[]{:S(2)}) copy-start(bf16[2,1024,128]{2,1,0:T(8,128)(2,1)} %get-tuple-element.27.kept_ref) | copy-start | bytes 1572868

commit v6 on v5

--- a/solution.py
+++ b/solution.py
@@ -120,7 +120,7 @@
         for at in range(0, features, step):
             rows = slice(at, at + step)
             both = jnp.concatenate([p[b, 0, rows, :], p[b, 1, rows, :]], axis=1)
-            partial[b, rows, :] = dot(both, grads, NT).astype(BF16)
+            partial[b, :, rows] = dot(grads, both, NT).astype(BF16)
         target = sent_hbm.at[b] if b < chips else kept_hbm.at[b - chips]
         stored.append(pltpu.make_async_copy(partial.at[b], target, out_sems.at[kv_heads + b]))
         stored[-1].start()
@@ -152,14 +152,6 @@
         copy.wait()
 
 
-def input_kernel(kept_ref, came_ref, *refs):
-    out_ref = refs[-1]
-    total = kept_ref[len(refs) - 1].astype(F32) + came_ref[len(refs) - 1].astype(F32)
-    for ref in refs[:-1]:
-        total += ref[...].astype(F32)
-    out_ref[...] = total.T.astype(BF16)
-
-
 def turned_kernel(mine_ref, theirs_ref, next_ref, x_hbm, out_ref, own, sem):
     rows, width = next_ref.shape
     parts = out_ref.shape[1] // rows
@@ -218,7 +210,7 @@
     for k in range(2, far, 2):
         sent = block(k + lax.rem(member, 2))
         near.append(along_dp(sent, lambda m, k=k: k + m % 2, parts, groups))
-    return distant, near, along_dp(block(1), lambda m: 1, parts, groups)
+    return distant, near, block(1)
 
 
 def shared_inputs(piece, groups):
@@ -273,10 +265,10 @@
     query_width = query_states.shape[1]
     features = projections.shape[1] // groups
     kv_heads = width // HEAD_SIZE
-    partial = jax.ShapeDtypeStruct((chips, features, rows), BF16)
+    partial = jax.ShapeDtypeStruct((chips, rows, features), BF16)
     exchange = parts == 2 * groups and inputs_normed.shape[1] % (parts * 128) == 0
     if exchange:
-        distant, near, next_inputs = sent_inputs(inputs_normed, parts, groups)
+        distant, near, next_block = sent_inputs(inputs_normed, parts, groups)
 
     whole = pltpu.VMEM((rows, query_width), BF16)
     narrow = pltpu.VMEM((rows, width), BF16)
@@ -293,7 +285,7 @@
         ),
         scratch_shapes=[whole, narrow, narrow, whole]
         + [pltpu.VMEM((groups, 2, features, width), BF16), whole, whole, wide, wide]
-        + [pltpu.VMEM((groups, features, rows), BF16)]
+        + [pltpu.VMEM((groups, rows, features), BF16)]
         + [pltpu.SemaphoreType.DMA((2 + 2 * kv_heads,)), pltpu.SemaphoreType.DMA((groups,))]
         + [pltpu.SemaphoreType.DMA((kv_heads + groups,))],
         compiler_params=WHOLE,
@@ -316,15 +308,24 @@
     )(grad_scores, key_states)
 
     if exchange:
-        ready, near, next_inputs = lax.optimization_barrier((grad_key, near, next_inputs))
-        sent, distant, near = lax.optimization_barrier((sent, distant, near))
+        distant, near = lax.optimization_barrier((distant, near))
+        ready, sent, distant, near = lax.optimization_barrier(
+            (grad_key, sent, distant, near)
+        )
         first = along_dp(ready, lambda m: parts // 2, parts, groups)
         pieces = shared_inputs(distant, groups)
+        next_inputs = along_dp(next_block, lambda m: 1, parts, groups)
     came = along_mp(sent, 1, groups)
-    pairs = [(kept[b].astype(F32) + came[b].astype(F32)).astype(BF16) for b in range(chips - 1)]
-    if exchange:
-        first, pieces, pairs = lax.optimization_barrier((first, pieces, pairs))
-        keys = {0: jnp.concatenate([grad_key, first])}
+    if exchange:
+        came, ready = lax.optimization_barrier((came, grad_key))
+        twice = jnp.concatenate([ready, ready])
+    total = kept.astype(F32) + came.astype(F32)
+    pairs = [total[b].astype(BF16) for b in range(chips - 1)]
+    if exchange:
+        first, twice, pieces, pairs, next_inputs = lax.optimization_barrier(
+            (first, twice, pieces, pairs, next_inputs)
+        )
+        keys = {0: lax.dynamic_update_slice(twice, first, (rows, 0))}
         mine = jnp.concatenate(pieces + near)
         theirs = along_mp(mine, 1, groups)
         bit = parts // 4
@@ -332,23 +333,20 @@
             for k in list(keys):
                 keys[k ^ bit] = along_dp(keys[k], lambda m, bit=bit: bit, parts, groups)
             bit //= 2
-    last = []
+    grad_input = total[chips - 1]
     for b in range(chips - 1):
         shift = [(m, (m + 2 * (b + 1)) % groups) for m in range(groups)]
-        last.append(lax.ppermute(pairs[b], "mp", shift))
-    grad_input = pl.pallas_call(
-        input_kernel,
-        out_specs=IN_VMEM,
-        out_shape=jax.ShapeDtypeStruct((rows, features), BF16),
-        compiler_params=PARAMS,
-        cost_estimate=cost(rows * features, 8 * rows * features),
-    )(kept, came, *last)
+        grad_input += lax.ppermute(pairs[b], "mp", shift).astype(F32)
+    grad_input = grad_input.astype(BF16)
 
     if exchange:
         beside = []
         for k in range(0, parts // 2, 2):
-            pair, beside = lax.optimization_barrier((keys[k], beside))
-            beside.append(along_dp(pair, lambda m: 1, parts, groups))
+            if k:
+                keys[k], beside, grad_query = lax.optimization_barrier(
+                    (keys[k], beside, grad_query)
+                )
+            beside.append(along_dp(keys[k], lambda m: 1, parts, groups))
         turned = turned_inputs(mine, theirs, next_inputs, inputs_normed)
         beside[-1], grad_input = lax.optimization_barrier((beside[-1], grad_input))
         keys = [keys[k] for k in range(0, parts // 2, 2)] + beside

time: 38 us -> 37.7 us (level)
  other arithmetic: 1.02 us -> 2.9 us
  local copies, waits for them, and re-layouts: 3 us -> 1.15 us
  Pallas kernels: 11.3 us -> 10.6 us
  waiting for transfers between devices: 7.03 us -> 7.46 us
    unnamed x7 -> x4, local copies, waits for them, and re-layouts: 1.91 us -> 0.03 us
    ppermute x7, starting transfers between devices: 11.2 us -> 9.55 us  [along_dp(): return lax.ppermute(array, ('dp', 'mp'), pairs)]
    ppermute x1, starting transfers between devices: 0.44 us -> 1.74 us  [body(): grad_input += lax.ppermute(pairs[b], 'mp', shift).astype(F32)]
    add x0 -> x1, other arithmetic: none -> 1.21 us  [body(): total = kept.astype(F32) + came.astype(F32)]
    concatenate x0 -> x1, other arithmetic: none -> 0.93 us  [body(): twice = jnp.concatenate([ready, ready])]
    pallas_call x1 -> x0, Pallas kernels: 0.87 us -> none  [body(): pl.pallas_call(input_kernel, out_specs=IN_VMEM, out_shape=jax.ShapeDtypeS...]
    ppermute x7, waiting for transfers between devices: 6.44 us -> 7.25 us  [along_dp(): return lax.ppermute(array, ('dp', 'mp'), pairs)]
    ppermute x1, waiting for transfers between devices: 0.38 us -> 0.01 us  [body(): grad_input += lax.ppermute(pairs[b], 'mp', shift).astype(F32)]
  transfers between devices with their start and end apart: 11 -> 11, of which waited for: 6 -> 6; matrix products, arithmetic and copies ran while one was open for 5% -> 8% of each run, Pallas kernels for 25% -> 24%
where the time goes in v6:
time: 37.7 us; the launch traced here: 37.4 us
  starting transfers between devices  14.5 us (38%)
  Pallas kernels  10.6 us (28%)
  waiting for transfers between devices  7.46 us (20%)
  other arithmetic  2.9 us (8%)
  local copies, waits for them, and re-layouts  1.15 us (3%)
  between operations  0.77 us (2%)
    ppermute x7, starting transfers between devices, along_dp(): return lax.ppermute(array, ('dp', 'mp'), pairs)  9.55 us
    ppermute x7, waiting for transfers between devices, along_dp(): return lax.ppermute(array, ('dp', 'mp'), pairs)  7.25 us
    pallas_call x1, Pallas kernels, body(): pl.pallas_call(attention_kernel, in_specs=[IN_HBM] * 5, out_specs=[IN_VME...  6.64 us
    ppermute x3, starting transfers between devices, along_mp(): return lax.ppermute(array, 'mp', [(m, m ^ bit) for m in range(groups)])  3.26 us
    pallas_call x1, Pallas kernels, body(): pl.pallas_call(query_kernel, in_specs=[IN_HBM, IN_HBM], out_specs=ANYWHER...  2.26 us
    ppermute x1, starting transfers between devices, body(): grad_input += lax.ppermute(pairs[b], 'mp', shift).astype(F32)  1.74 us
    pallas_call x1, Pallas kernels, summed_weights(): pl.pallas_call(weights_kernel, out_specs=IN_VMEM, out_shape=jax.ShapeDtyp...  1.24 us
    add x1, other arithmetic, body(): total = kept.astype(F32) + came.astype(F32)  1.21 us
  transfers between devices with their start and end apart: 11, of which 6 were waited for; matrix products, arithmetic and copies ran while one was open for 8% of the time, Pallas kernels for 24%

profile of v6, /device:TPU:0, one launch (start us, length us, event | category | flops | bytes accessed | tf_op | source)
XLA Modules:
  0.0 37.4 jit_solution(10702332076259369482)
XLA Ops:
  0.7 1.1 %constant_dynamic-slice_fusion = (bf16[128,512]{1,0:T(8,128)(2,1)S(1)}, bf16[128,512]{1,0:T(8,128)(2,1)S(1)}, bf16[128,512]{1,0:T(8,128)(2,1)S(1)}) fusion(bf16[128,4096]{1,0:T(8,128)(2,1)} %x_hbm.1, s32[]{:T(128)S(6)} %select_n.11, s32[]{:T(128)S(6)} %select_n.10, s32[]{:T(128)S(6)} %select_n.9), kind=kLoop, calls=%fused_computation.11 | loop fusion | bytes 786444 | tf_op jit(solution)/shard_map/dynamic_slice | solution.py:206
  1.7 3.1 %collective-permute-start.1 = (bf16[128,512]{1,0:T(8,128)(2,1)S(1)}, bf16[128,512]{1,0:T(8,128)(2,1)S(1)}, u32[]{:S(2)}, u32[]{:S(2)}) collective-permute-start(bf16[128,512]{1,0:T(8,128)(2,1)S(1)} %get-tuple-element.50), channel_id=1, source_target_pairs={{0,8},{1,13},{2,10},{3,15},{4,12},{5,9},{6,14},{7,11},{8,0},{9,5},... | collective-permute-start | bytes 393224 | tf_op jit(solution)/shard_map/ppermute | solution.py:193
  4.8 2.6 %collective-permute-start = (bf16[128,512]{1,0:T(8,128)(2,1)S(1)}, bf16[128,512]{1,0:T(8,128)(2,1)S(1)}, u32[]{:S(2)}, u32[]{:S(2)}) collective-permute-start(bf16[128,512]{1,0:T(8,128)(2,1)S(1)} %get-tuple-element.51), channel_id=1, source_target_pairs={{0,16},{1,21},{2,26},{3,31},{4,20},{5,17},{6,30},{7,27},{8,24},{9,... | collective-permute-start | bytes 393224 | tf_op jit(solution)/shard_map/ppermute | solution.py:193
  7.4 6.6 %shard_map.85 = (bf16[128,256]{1,0:T(8,128)(2,1)}, bf16[128,2048]{1,0:T(8,128)(2,1)}, bf16[2,128,1024]{2,1,0:T(8,128)(2,1)}, bf16[2,128,1024]{2,1,0:T(8,128)(2,1)}) custom-call(bf16[128,2048]{1,0:T(8,128)(2,1)} %q_hbm.1, bf16[128,256]{1,0:T(8,128)(2,1)} %k_hbm.3, bf16[128,256]{1,0:T(8,128)(2,1)} %v_hbm.1, bf16[128,2048]{1,0:T(8,128)(2,1)} %do_hbm.1, ...), custom_call_target="tpu_custom_call" | custom-call | flops 805306368 | bytes 5767168 | tf_op jit(solution)/shard_map/pallas_call | solution.py:276
  14.1 0.4 collective-permute-done
  14.4 0.2 collective-permute-start.3
  14.7 1.2 %collective-permute-start.5 = (bf16[128,512]{1,0:T(8,128)(2,1)S(1)}, bf16[128,512]{1,0:T(8,128)(2,1)S(1)}, u32[]{:S(2)}, u32[]{:S(2)}) collective-permute-start(bf16[128,512]{1,0:T(8,128)(2,1)S(1)} %get-tuple-element.49), channel_id=1, source_target_pairs={{0,4},{1,5},{2,6},{3,7},{4,0},{5,1},{6,2},{7,3},{8,12},{9,13},{10,... | collective-permute-start | bytes 393224 | tf_op jit(solution)/shard_map/ppermute | solution.py:193
  15.9 0.3 collective-permute-start.2
  16.1 2.9 %collective-permute-start.4 = (bf16[128,512]{1,0:T(8,128)(2,1)S(1)}, bf16[128,512]{1,0:T(8,128)(2,1)S(1)}, u32[]{:S(2)}, u32[]{:S(2)}) collective-permute-start(bf16[128,512]{1,0:T(8,128)(2,1)S(1)} %collective-permute-done), channel_id=1, source_target_pairs={{0,2},{1,3},{2,0},{3,1},{4,6},{5,7},{6,4},{7,5},{8,10},{9,11},{10,... | collective-permute-start | bytes 393224 | tf_op jit(solution)/shard_map/ppermute | solution.py:197
  19.1 1.2 %convert_add_fusion = f32[2,128,1024]{2,1,0:T(8,128)S(1)} fusion(bf16[2,128,1024]{2,1,0:T(8,128)(2,1)S(1)} %collective-permute-done.3, bf16[2,128,1024]{2,1,0:T(8,128)(2,1)} %get-tuple-element.34), kind=kLoop, calls=%fused_computation | loop fusion | flops 786432 | bytes 2097152 | tf_op jit(solution)/shard_map/add | solution.py:322
  20.3 0.9 %pad_maximum_fusion = bf16[256,256]{1,0:T(8,128)(2,1)S(1)} fusion(bf16[128,256]{1,0:T(8,128)(2,1)} %get-tuple-element.32), kind=kLoop, calls=%fused_computation.6 | loop fusion | flops 262144 | bytes 196608 | tf_op jit(solution)/shard_map/concatenate | solution.py:321
  21.3 1.2 %collective-permute-done.2 = bf16[128,256]{1,0:T(8,128)(2,1)S(1)} collective-permute-done((bf16[128,256]{1,0:T(8,128)(2,1)}, bf16[128,256]{1,0:T(8,128)(2,1)S(1)}, u32[]{:S(2)}, u32[]{:S(2)}) %collective-permute-start.2) | collective-permute-done | bytes 65568 | tf_op jit(solution)/shard_map/ppermute | solution.py:193
  22.5 0.2 collective-permute-done.4
  22.7 1.7 %collective-permute-start.9 = (bf16[128,1024]{1,0:T(8,128)(2,1)S(1)}, bf16[128,1024]{1,0:T(8,128)(2,1)S(1)}, u32[]{:S(2)}, u32[]{:S(2)}) collective-permute-start(bf16[128,1024]{1,0:T(8,128)(2,1)S(1)} %fusion.2), channel_id=1, source_target_pairs={{0,2},{1,3},{2,0},{3,1},{4,6},{5,7},{6,4},{7,5},{8,10},{9,11},{10,... | collective-permute-start | bytes 786440 | tf_op jit(solution)/shard_map/ppermute | solution.py:339
  24.6 0.6 %collective-permute-start.7 = (bf16[256,256]{1,0:T(8,128)(2,1)S(1)}, bf16[256,256]{1,0:T(8,128)(2,1)S(1)}, u32[]{:S(2)}, u32[]{:S(2)}) collective-permute-start(bf16[256,256]{1,0:T(8,128)(2,1)S(1)} %constant_dynamic-update-slice_fusion.3.refs_0_), channel_id=1, source_target_pairs={{0,4},{1,5},{2,6},{3,7},{4,0},{5,1},{6,2},{7,3},{8,12},{9,13},{10,... | collective-permute-start | bytes 393224 | tf_op jit(solution)/shard_map/ppermute | solution.py:193
  25.2 0.3 collective-permute-start.6
  25.5 2.3 %shard_map.86 = bf16[128,2048]{1,0:T(8,128)(2,1)} custom-call(bf16[128,2048]{1,0:T(8,128)(2,1)} %get-tuple-element.38.ds_hbm, bf16[128,256]{1,0:T(8,128)(2,1)} %k_hbm.3), custom_call_target="tpu_custom_call" | custom-call | flops 67108864 | bytes 1048576 | tf_op jit(solution)/shard_map/pallas_call | solution.py:299
  27.8 2.7 %collective-permute-done.7.refs_2_ = bf16[256,256]{1,0:T(8,128)(2,1)S(1)} collective-permute-done((bf16[256,256]{1,0:T(8,128)(2,1)S(1)}, bf16[256,256]{1,0:T(8,128)(2,1)S(1)}, u32[]{:S(2)}, u32[]{:S(2)}) %collective-permute-start.7) | collective-permute-done | bytes 131104 | tf_op jit(solution)/shard_map/ppermute | solution.py:193
  30.5 0.3 collective-permute-done.6.refs_1_
  30.7 1.5 %collective-permute-start.8 = (bf16[256,256]{1,0:T(8,128)(2,1)S(1)}, bf16[256,256]{1,0:T(8,128)(2,1)S(1)}, u32[]{:S(2)}, u32[]{:S(2)}) collective-permute-start(bf16[256,256]{1,0:T(8,128)(2,1)S(1)} %collective-permute-done.6.refs_1_), channel_id=1, source_target_pairs={{0,4},{1,5},{2,6},{3,7},{4,0},{5,1},{6,2},{7,3},{8,12},{9,13},{10,... | collective-permute-start | bytes 393224 | tf_op jit(solution)/shard_map/ppermute | solution.py:193
  32.2 0.8 %fusion.1 = bf16[128,1024]{1,0:T(8,128)(2,1)} fusion(f32[2,128,1024]{2,1,0:T(8,128)S(1)} %convert_add_fusion, bf16[128,1024]{1,0:T(8,128)(2,1)S(1)} %collective-permute-done.9), kind=kLoop, calls=%fused_computation.3 | loop fusion | flops 393216 | bytes 1048576 | tf_op jit(solution)/shard_map/convert_element_type | solution.py:340
  33.0 2.7 %collective-permute-done.8.refs_3_ = bf16[256,256]{1,0:T(8,128)(2,1)S(1)} collective-permute-done((bf16[256,256]{1,0:T(8,128)(2,1)S(1)}, bf16[256,256]{1,0:T(8,128)(2,1)S(1)}, u32[]{:S(2)}, u32[]{:S(2)}) %collective-permute-start.8) | collective-permute-done | bytes 131104 | tf_op jit(solution)/shard_map/ppermute | solution.py:193
  35.7 0.5 %shard_map.87.x_ref = bf16[512,1024]{1,0:T(8,128)(2,1)S(1)} custom-call(bf16[384,512]{1,0:T(8,128)(2,1)S(1)} %constant_dynamic-update-slice_fusion.mine_ref, bf16[384,512]{1,0:T(8,128)(2,1)S(1)} %collective-permute-done.10.theirs_ref, bf16[128,512]{1,0:T(8,128)(2,1)S(1)} %collective-permute-done.5.next_ref, bf16[128,4096]{1,0:T(8,128)(2,1)S(1)} %copy-done), custom_call_target="tpu_custom_call" | custom-call | bytes 2097152 | tf_op jit(solution)/shard_map/pallas_call | solution.py:227
  36.2 1.2 %shard_map.88 = f32[512,256]{1,0:T(8,128)} custom-call(bf16[512,1024]{1,0:T(8,128)(2,1)S(1)} %shard_map.87.x_ref, bf16[256,256]{1,0:T(8,128)(2,1)S(1)} %constant_dynamic-update-slice_fusion.3.refs_0_, bf16[256,256]{1,0:T(8,128)(2,1)S(1)} %collective-permute-done.6.refs_1_, bf16[256,256]{1,0:T(8,128)(2,1)S(1)} %collective-permute-done.7.refs_2_, ...), custom_call_target="tpu_custom_call" | custom-call | flops 268435456 | bytes 1572864 | tf_op jit(solution)/shard_map/pallas_call | solution.py:240
  (13 shorter events, 0.2 us)
Async XLA Ops:
  1.7 12.3 %collective-permute-start.1 = (bf16[128,512]{1,0:T(8,128)(2,1)S(1)}, bf16[128,512]{1,0:T(8,128)(2,1)S(1)}, u32[]{:S(2)}, u32[]{:S(2)}) collective-permute-start(bf16[128,512]{1,0:T(8,128)(2,1)S(1)} %get-tuple-element.50), channel_id=1, source_target_pairs={{0,8},{1,13},{2,10},{3,15},{4,12},{5,9},{6,14},{7,11},{8,0},{9,5},... | collective-permute-start | bytes 393224 | tf_op jit(solution)/shard_map/ppermute | solution.py:193
  4.8 9.6 %collective-permute-start = (bf16[128,512]{1,0:T(8,128)(2,1)S(1)}, bf16[128,512]{1,0:T(8,128)(2,1)S(1)}, u32[]{:S(2)}, u32[]{:S(2)}) collective-permute-start(bf16[128,512]{1,0:T(8,128)(2,1)S(1)} %get-tuple-element.51), channel_id=1, source_target_pairs={{0,16},{1,21},{2,26},{3,31},{4,20},{5,17},{6,30},{7,27},{8,24},{9,... | collective-permute-start | bytes 393224 | tf_op jit(solution)/shard_map/ppermute | solution.py:193
  14.0 21.7 %copy-start = (bf16[128,4096]{1,0:T(8,128)(2,1)S(1)}, bf16[128,4096]{1,0:T(8,128)(2,1)}, u32[]{:S(2)}) copy-start(bf16[128,4096]{1,0:T(8,128)(2,1)} %x_hbm.1) | copy-start | bytes 3145732
  14.4 4.7 %collective-permute-start.3 = (bf16[2,128,1024]{2,1,0:T(8,128)(2,1)}, bf16[2,128,1024]{2,1,0:T(8,128)(2,1)S(1)}, u32[]{:S(2)}, u32[]{:S(2)}) collective-permute-start(bf16[2,128,1024]{2,1,0:T(8,128)(2,1)} %get-tuple-element.31), channel_id=1, source_target_pairs={{0,1},{1,0},{2,3},{3,2},{4,5},{5,4},{6,7},{7,6},{8,9},{9,8},{10,11... | collective-permute-start | bytes 1572872 | tf_op jit(solution)/shard_map/ppermute | solution.py:197
  14.7 6.6 %collective-permute-start.5 = (bf16[128,512]{1,0:T(8,128)(2,1)S(1)}, bf16[128,512]{1,0:T(8,128)(2,1)S(1)}, u32[]{:S(2)}, u32[]{:S(2)}) collective-permute-start(bf16[128,512]{1,0:T(8,128)(2,1)S(1)} %get-tuple-element.49), channel_id=1, source_target_pairs={{0,4},{1,5},{2,6},{3,7},{4,0},{5,1},{6,2},{7,3},{8,12},{9,13},{10,... | collective-permute-start | bytes 393224 | tf_op jit(solution)/shard_map/ppermute | solution.py:193
  15.9 6.6 %collective-permute-start.2 = (bf16[128,256]{1,0:T(8,128)(2,1)}, bf16[128,256]{1,0:T(8,128)(2,1)S(1)}, u32[]{:S(2)}, u32[]{:S(2)}) collective-permute-start(bf16[128,256]{1,0:T(8,128)(2,1)} %get-tuple-element.32), channel_id=1, source_target_pairs={{0,16},{1,17},{2,18},{3,19},{4,20},{5,21},{6,22},{7,23},{8,24},{9,... | collective-permute-start | bytes 196616 | tf_op jit(solution)/shard_map/ppermute | solution.py:193
  16.1 6.5 %collective-permute-start.4 = (bf16[128,512]{1,0:T(8,128)(2,1)S(1)}, bf16[128,512]{1,0:T(8,128)(2,1)S(1)}, u32[]{:S(2)}, u32[]{:S(2)}) collective-permute-start(bf16[128,512]{1,0:T(8,128)(2,1)S(1)} %collective-permute-done), channel_id=1, source_target_pairs={{0,2},{1,3},{2,0},{3,1},{4,6},{5,7},{6,4},{7,5},{8,10},{9,11},{10,... | collective-permute-start | bytes 393224 | tf_op jit(solution)/shard_map/ppermute | solution.py:197
  22.7 9.5 %collective-permute-start.9 = (bf16[128,1024]{1,0:T(8,128)(2,1)S(1)}, bf16[128,1024]{1,0:T(8,128)(2,1)S(1)}, u32[]{:S(2)}, u32[]{:S(2)}) collective-permute-start(bf16[128,1024]{1,0:T(8,128)(2,1)S(1)} %fusion.2), channel_id=1, source_target_pairs={{0,2},{1,3},{2,0},{3,1},{4,6},{5,7},{6,4},{7,5},{8,10},{9,11},{10,... | collective-permute-start | bytes 786440 | tf_op jit(solution)/shard_map/ppermute | solution.py:339
  24.5 11.2 %collective-permute-start.10 = (bf16[384,512]{1,0:T(8,128)(2,1)S(1)}, bf16[384,512]{1,0:T(8,128)(2,1)S(1)}, u32[]{:S(2)}, u32[]{:S(2)}) collective-permute-start(bf16[384,512]{1,0:T(8,128)(2,1)S(1)} %constant_dynamic-update-slice_fusion.mine_ref), channel_id=1, source_target_pairs={{0,1},{1,0},{2,3},{3,2},{4,5},{5,4},{6,7},{7,6},{8,9},{9,8},{10,11... | collective-permute-start | bytes 1179656 | tf_op jit(solution)/shard_map/ppermute | solution.py:197
  24.6 5.9 %collective-permute-start.7 = (bf16[256,256]{1,0:T(8,128)(2,1)S(1)}, bf16[256,256]{1,0:T(8,128)(2,1)S(1)}, u32[]{:S(2)}, u32[]{:S(2)}) collective-permute-start(bf16[256,256]{1,0:T(8,128)(2,1)S(1)} %constant_dynamic-update-slice_fusion.3.refs_0_), channel_id=1, source_target_pairs={{0,4},{1,5},{2,6},{3,7},{4,0},{5,1},{6,2},{7,3},{8,12},{9,13},{10,... | collective-permute-start | bytes 393224 | tf_op jit(solution)/shard_map/ppermute | solution.py:193
  25.2 5.6 %collective-permute-start.6 = (bf16[256,256]{1,0:T(8,128)(2,1)S(1)}, bf16[256,256]{1,0:T(8,128)(2,1)S(1)}, u32[]{:S(2)}, u32[]{:S(2)}) collective-permute-start(bf16[256,256]{1,0:T(8,128)(2,1)S(1)} %constant_dynamic-update-slice_fusion.3.refs_0_), channel_id=1, source_target_pairs={{0,8},{1,9},{2,10},{3,11},{4,12},{5,13},{6,14},{7,15},{8,0},{9,1},... | collective-permute-start | bytes 393224 | tf_op jit(solution)/shard_map/ppermute | solution.py:193
  30.7 5.0 %collective-permute-start.8 = (bf16[256,256]{1,0:T(8,128)(2,1)S(1)}, bf16[256,256]{1,0:T(8,128)(2,1)S(1)}, u32[]{:S(2)}, u32[]{:S(2)}) collective-permute-start(bf16[256,256]{1,0:T(8,128)(2,1)S(1)} %collective-permute-done.6.refs_1_), channel_id=1, source_target_pairs={{0,4},{1,5},{2,6},{3,7},{4,0},{5,1},{6,2},{7,3},{8,12},{9,13},{10,... | collective-permute-start | bytes 393224 | tf_op jit(solution)/shard_map/ppermute | solution.py:193

commit v7 on v6

--- a/solution.py
+++ b/solution.py
@@ -248,6 +248,24 @@
     )(turned, *keys)
 
 
+def query_gradient(grad_scores, key_states):
+    rows, query_width = grad_scores.shape
+    width = key_states.shape[1]
+    kv_heads = width // HEAD_SIZE
+    whole = pltpu.VMEM((rows, query_width), BF16)
+    narrow = pltpu.VMEM((rows, width), BF16)
+    return pl.pallas_call(
+        query_kernel,
+        in_specs=[IN_HBM, IN_HBM],
+        out_specs=ANYWHERE,
+        out_shape=jax.ShapeDtypeStruct((rows, query_width), BF16),
+        scratch_shapes=[whole, narrow, whole]
+        + [pltpu.SemaphoreType.DMA((1 + kv_heads,)), pltpu.SemaphoreType.DMA((kv_heads,))],
+        compiler_params=WHOLE,
+        cost_estimate=cost(2 * rows * rows * query_width, 4 * rows * query_width),
+    )(grad_scores, key_states)
+
+
 def gathered_weights(inputs, grad_key, parts):
     rows = inputs.shape[0]
     width = inputs.shape[1] // parts
@@ -266,7 +284,7 @@
     features = projections.shape[1] // groups
     kv_heads = width // HEAD_SIZE
     partial = jax.ShapeDtypeStruct((chips, rows, features), BF16)
-    exchange = parts == 2 * groups and inputs_normed.shape[1] % (parts * 128) == 0
+    exchange = parts == 2 * groups and inputs_normed.shape[1] % (parts * width) == 0
     if exchange:
         distant, near, next_block = sent_inputs(inputs_normed, parts, groups)
 
@@ -296,59 +314,43 @@
         ),
     )(query_states, key_states, value_states, grad_context, projections)
 
-    grad_query = pl.pallas_call(
-        query_kernel,
-        in_specs=[IN_HBM, IN_HBM],
-        out_specs=ANYWHERE,
-        out_shape=jax.ShapeDtypeStruct((rows, query_width), BF16),
-        scratch_shapes=[whole, narrow, whole]
-        + [pltpu.SemaphoreType.DMA((1 + kv_heads,)), pltpu.SemaphoreType.DMA((kv_heads,))],
-        compiler_params=WHOLE,
-        cost_estimate=cost(2 * rows * rows * query_width, 4 * rows * query_width),
-    )(grad_scores, key_states)
-
-    if exchange:
-        distant, near = lax.optimization_barrier((distant, near))
-        ready, sent, distant, near = lax.optimization_barrier(
-            (grad_key, sent, distant, near)
+    if exchange:
+        ready, next_block = lax.optimization_barrier((grad_key, next_block))
+        first = along_dp(ready, lambda m: parts // 2, parts, groups)
+        next_inputs = along_dp(next_block, lambda m: 1, parts, groups)
+    grad_query = query_gradient(grad_scores, key_states)
+    if exchange:
+        twice = jnp.concatenate([grad_key, grad_key])
+        first, twice, grad_query, sent, kept, distant, near, next_inputs = (
+            lax.optimization_barrier(
+                (first, twice, grad_query, sent, kept, distant, near, next_inputs)
+            )
         )
-        first = along_dp(ready, lambda m: parts // 2, parts, groups)
         pieces = shared_inputs(distant, groups)
-        next_inputs = along_dp(next_block, lambda m: 1, parts, groups)
-    came = along_mp(sent, 1, groups)
-    if exchange:
-        came, ready = lax.optimization_barrier((came, grad_key))
-        twice = jnp.concatenate([ready, ready])
-    total = kept.astype(F32) + came.astype(F32)
-    pairs = [total[b].astype(BF16) for b in range(chips - 1)]
-    if exchange:
-        first, twice, pieces, pairs, next_inputs = lax.optimization_barrier(
-            (first, twice, pieces, pairs, next_inputs)
-        )
         keys = {0: lax.dynamic_update_slice(twice, first, (rows, 0))}
-        mine = jnp.concatenate(pieces + near)
-        theirs = along_mp(mine, 1, groups)
         bit = parts // 4
         while bit > 1:
             for k in list(keys):
                 keys[k ^ bit] = along_dp(keys[k], lambda m, bit=bit: bit, parts, groups)
             bit //= 2
+        beside = [along_dp(keys[0], lambda m: 1, parts, groups)]
+    came = along_mp(sent, 1, groups)
+    total = kept.astype(F32) + came.astype(F32)
+    if exchange:
+        keys, pieces, total, beside = lax.optimization_barrier((keys, pieces, total, beside))
+        beside += [
+            along_dp(keys[k], lambda m: 1, parts, groups) for k in range(2, parts // 2, 2)
+        ]
+        mine = jnp.concatenate(pieces + near)
+        theirs = along_mp(mine, 1, groups)
     grad_input = total[chips - 1]
     for b in range(chips - 1):
         shift = [(m, (m + 2 * (b + 1)) % groups) for m in range(groups)]
-        grad_input += lax.ppermute(pairs[b], "mp", shift).astype(F32)
+        grad_input += lax.ppermute(total[b].astype(BF16), "mp", shift).astype(F32)
     grad_input = grad_input.astype(BF16)
 
     if exchange:
-        beside = []
-        for k in range(0, parts // 2, 2):
-            if k:
-                keys[k], beside, grad_query = lax.optimization_barrier(
-                    (keys[k], beside, grad_query)
-                )
-            beside.append(along_dp(keys[k], lambda m: 1, parts, groups))
         turned = turned_inputs(mine, theirs, next_inputs, inputs_normed)
-        beside[-1], grad_input = lax.optimization_barrier((beside[-1], grad_input))
         keys = [keys[k] for k in range(0, parts // 2, 2)] + beside
         grad_weights = summed_weights(turned, keys)
     else:

time: 37.7 us -> 38.7 us (1.027)
  waiting for transfers between devices: 7.46 us -> 9.29 us
  starting transfers between devices: 14.5 us -> 13.7 us
    ppermute x1, waiting for transfers between devices: 0.01 us -> 4.19 us  [body(): grad_input += lax.ppermute(total[b].astype(BF16), 'mp', shift).astype(F32)]
    ppermute x7, waiting for transfers between devices: 7.25 us -> 4.76 us  [along_dp(): return lax.ppermute(array, ('dp', 'mp'), pairs)]
    ppermute x3, starting transfers between devices: 3.26 us -> 2.13 us  [along_mp(): return lax.ppermute(array, 'mp', [(m, m ^ bit) for m in range(groups)])]
  transfers between devices with their start and end apart: 11 -> 11, of which waited for: 6 -> 4; matrix products, arithmetic and copies ran while one was open for 8% -> 8% of each run, Pallas kernels for 24% -> 24%
where the time goes in v7:
time: 38.7 us; the launch traced here: 38.4 us
  starting transfers between devices  13.7 us (35%)
  Pallas kernels  10.6 us (27%)
  waiting for transfers between devices  9.29 us (24%)
  other arithmetic  2.9 us (7%)
  local copies, waits for them, and re-layouts  1.14 us (3%)
  between operations  0.78 us (2%)
    ppermute x7, starting transfers between devices, along_dp(): return lax.ppermute(array, ('dp', 'mp'), pairs)  9.79 us
    pallas_call x1, Pallas kernels, body(): pl.pallas_call(attention_kernel, in_specs=[IN_HBM] * 5, out_specs=[IN_VME...  6.65 us
    ppermute x7, waiting for transfers between devices, along_dp(): return lax.ppermute(array, ('dp', 'mp'), pairs)  4.76 us
    ppermute x1, waiting for transfers between devices, body(): grad_input += lax.ppermute(total[b].astype(BF16), 'mp', shift).astype(F32)  4.19 us
    pallas_call x1, Pallas kernels, query_gradient(): pl.pallas_call(query_kernel, in_specs=[IN_HBM, IN_HBM], out_specs=ANYWHER...  2.26 us
    ppermute x3, starting transfers between devices, along_mp(): return lax.ppermute(array, 'mp', [(m, m ^ bit) for m in range(groups)])  2.13 us
    ppermute x1, starting transfers between devices, body(): grad_input += lax.ppermute(total[b].astype(BF16), 'mp', shift).astype(F32)  1.79 us
    pallas_call x1, Pallas kernels, summed_weights(): pl.pallas_call(weights_kernel, out_specs=IN_VMEM, out_shape=jax.ShapeDtyp...  1.24 us
  transfers between devices with their start and end apart: 11, of which 4 were waited for; matrix products, arithmetic and copies ran while one was open for 8% of the time, Pallas kernels for 24%

profile of v7, /device:TPU:0, one launch (start us, length us, event | category | flops | bytes accessed | tf_op | source)
XLA Modules:
  0.0 38.4 jit_solution(9422277814208957012)
XLA Ops:
  0.7 1.1 %constant_dynamic-slice_fusion = (bf16[128,512]{1,0:T(8,128)(2,1)S(1)}, bf16[128,512]{1,0:T(8,128)(2,1)S(1)}, bf16[128,512]{1,0:T(8,128)(2,1)S(1)}) fusion(bf16[128,4096]{1,0:T(8,128)(2,1)} %x_hbm.1, s32[]{:T(128)S(6)} %select_n.11, s32[]{:T(128)S(6)} %select_n.10, s32[]{:T(128)S(6)} %select_n.9), kind=kLoop, calls=%fused_computation.10 | loop fusion | bytes 786444 | tf_op jit(solution)/shard_map/dynamic_slice | solution.py:206
  1.7 4.1 %collective-permute-start.1 = (bf16[128,512]{1,0:T(8,128)(2,1)S(1)}, bf16[128,512]{1,0:T(8,128)(2,1)S(1)}, u32[]{:S(2)}, u32[]{:S(2)}) collective-permute-start(bf16[128,512]{1,0:T(8,128)(2,1)S(1)} %get-tuple-element.44), channel_id=1, source_target_pairs={{0,16},{1,21},{2,26},{3,31},{4,20},{5,17},{6,30},{7,27},{8,24},{9,... | collective-permute-start | bytes 393224 | tf_op jit(solution)/shard_map/ppermute | solution.py:193
  5.8 1.6 %collective-permute-start.2 = (bf16[128,512]{1,0:T(8,128)(2,1)S(1)}, bf16[128,512]{1,0:T(8,128)(2,1)S(1)}, u32[]{:S(2)}, u32[]{:S(2)}) collective-permute-start(bf16[128,512]{1,0:T(8,128)(2,1)S(1)} %get-tuple-element.43), channel_id=1, source_target_pairs={{0,8},{1,13},{2,10},{3,15},{4,12},{5,9},{6,14},{7,11},{8,0},{9,5},... | collective-permute-start | bytes 393224 | tf_op jit(solution)/shard_map/ppermute | solution.py:193
  7.4 6.6 %shard_map.85 = (bf16[128,256]{1,0:T(8,128)(2,1)}, bf16[128,2048]{1,0:T(8,128)(2,1)}, bf16[2,128,1024]{2,1,0:T(8,128)(2,1)}, bf16[2,128,1024]{2,1,0:T(8,128)(2,1)}) custom-call(bf16[128,2048]{1,0:T(8,128)(2,1)} %q_hbm.1, bf16[128,256]{1,0:T(8,128)(2,1)} %k_hbm.3, bf16[128,256]{1,0:T(8,128)(2,1)} %v_hbm.1, bf16[128,2048]{1,0:T(8,128)(2,1)} %do_hbm.1, ...), custom_call_target="tpu_custom_call" | custom-call | flops 805306368 | bytes 5767168 | tf_op jit(solution)/shard_map/pallas_call | solution.py:294
  14.1 0.0 copy-start
  14.1 1.6 %collective-permute-start.3 = (bf16[128,512]{1,0:T(8,128)(2,1)S(1)}, bf16[128,512]{1,0:T(8,128)(2,1)S(1)}, u32[]{:S(2)}, u32[]{:S(2)}) collective-permute-start(bf16[128,512]{1,0:T(8,128)(2,1)S(1)} %get-tuple-element.28), channel_id=1, source_target_pairs={{0,4},{1,5},{2,6},{3,7},{4,0},{5,1},{6,2},{7,3},{8,12},{9,13},{10,... | collective-permute-start | bytes 393224 | tf_op jit(solution)/shard_map/ppermute | solution.py:193
  15.6 0.3 collective-permute-start
  16.0 2.3 %shard_map.86 = bf16[128,2048]{1,0:T(8,128)(2,1)} custom-call(bf16[128,2048]{1,0:T(8,128)(2,1)} %get-tuple-element.25.ds_hbm, bf16[128,256]{1,0:T(8,128)(2,1)} %k_hbm.3), custom_call_target="tpu_custom_call" | custom-call | flops 67108864 | bytes 1048576 | tf_op jit(solution)/shard_map/pallas_call | solution.py:257
  18.2 0.9 %pad_maximum_fusion = bf16[256,256]{1,0:T(8,128)(2,1)S(1)} fusion(bf16[128,256]{1,0:T(8,128)(2,1)} %get-tuple-element.24), kind=kLoop, calls=%fused_computation.5 | loop fusion | flops 262144 | bytes 196608 | tf_op jit(solution)/shard_map/concatenate | solution.py:323
  19.2 2.7 %collective-permute-done = bf16[128,256]{1,0:T(8,128)(2,1)S(1)} collective-permute-done((bf16[128,256]{1,0:T(8,128)(2,1)}, bf16[128,256]{1,0:T(8,128)(2,1)S(1)}, u32[]{:S(2)}, u32[]{:S(2)}) %collective-permute-start) | collective-permute-done | bytes 65568 | tf_op jit(solution)/shard_map/ppermute | solution.py:193
  21.9 0.1 collective-permute-start.6
  22.0 0.1 collective-permute-start.4
  22.1 0.6 %collective-permute-start.7 = (bf16[256,256]{1,0:T(8,128)(2,1)S(1)}, bf16[256,256]{1,0:T(8,128)(2,1)S(1)}, u32[]{:S(2)}, u32[]{:S(2)}) collective-permute-start(bf16[256,256]{1,0:T(8,128)(2,1)S(1)} %constant_dynamic-update-slice_fusion.3.refs_0_), channel_id=1, source_target_pairs={{0,4},{1,5},{2,6},{3,7},{4,0},{5,1},{6,2},{7,3},{8,12},{9,13},{10,... | collective-permute-start | bytes 393224 | tf_op jit(solution)/shard_map/ppermute | solution.py:193
  22.7 2.0 %collective-permute-start.5 = (bf16[128,512]{1,0:T(8,128)(2,1)S(1)}, bf16[128,512]{1,0:T(8,128)(2,1)S(1)}, u32[]{:S(2)}, u32[]{:S(2)}) collective-permute-start(bf16[128,512]{1,0:T(8,128)(2,1)S(1)} %collective-permute-done.1), channel_id=1, source_target_pairs={{0,2},{1,3},{2,0},{3,1},{4,6},{5,7},{6,4},{7,5},{8,10},{9,11},{10,... | collective-permute-start | bytes 393224 | tf_op jit(solution)/shard_map/ppermute | solution.py:197
  24.7 1.2 %convert_add_fusion = f32[2,128,1024]{2,1,0:T(8,128)S(1)} fusion(bf16[2,128,1024]{2,1,0:T(8,128)(2,1)S(1)} %collective-permute-done.6, bf16[2,128,1024]{2,1,0:T(8,128)(2,1)} %get-tuple-element.33), kind=kLoop, calls=%fused_computation | loop fusion | flops 786432 | bytes 2097152 | tf_op jit(solution)/shard_map/add | solution.py:338
  25.9 2.0 %collective-permute-done.4.refs_1_ = bf16[256,256]{1,0:T(8,128)(2,1)S(1)} collective-permute-done((bf16[256,256]{1,0:T(8,128)(2,1)S(1)}, bf16[256,256]{1,0:T(8,128)(2,1)S(1)}, u32[]{:S(2)}, u32[]{:S(2)}) %collective-permute-start.4) | collective-permute-done | bytes 131104 | tf_op jit(solution)/shard_map/ppermute | solution.py:193
  27.9 0.3 collective-permute-done.5
  28.3 1.8 %collective-permute-start.8 = (bf16[128,1024]{1,0:T(8,128)(2,1)S(1)}, bf16[128,1024]{1,0:T(8,128)(2,1)S(1)}, u32[]{:S(2)}, u32[]{:S(2)}) collective-permute-start(bf16[128,1024]{1,0:T(8,128)(2,1)S(1)} %fusion.1), channel_id=1, source_target_pairs={{0,2},{1,3},{2,0},{3,1},{4,6},{5,7},{6,4},{7,5},{8,10},{9,11},{10,... | collective-permute-start | bytes 786440 | tf_op jit(solution)/shard_map/ppermute | solution.py:349
  30.1 0.1 collective-permute-start.9
  30.2 1.5 %collective-permute-start.10 = (bf16[256,256]{1,0:T(8,128)(2,1)S(1)}, bf16[256,256]{1,0:T(8,128)(2,1)S(1)}, u32[]{:S(2)}, u32[]{:S(2)}) collective-permute-start(bf16[256,256]{1,0:T(8,128)(2,1)S(1)} %collective-permute-done.4.refs_1_), channel_id=1, source_target_pairs={{0,4},{1,5},{2,6},{3,7},{4,0},{5,1},{6,2},{7,3},{8,12},{9,13},{10,... | collective-permute-start | bytes 393224 | tf_op jit(solution)/shard_map/ppermute | solution.py:193
  31.8 4.2 %collective-permute-done.8 = bf16[128,1024]{1,0:T(8,128)(2,1)S(1)} collective-permute-done((bf16[128,1024]{1,0:T(8,128)(2,1)S(1)}, bf16[128,1024]{1,0:T(8,128)(2,1)S(1)}, u32[]{:S(2)}, u32[]{:S(2)}) %collective-permute-start.8) | collective-permute-done | bytes 262176 | tf_op jit(solution)/shard_map/ppermute | solution.py:349
  35.9 0.8 %fusion = bf16[128,1024]{1,0:T(8,128)(2,1)} fusion(bf16[128,1024]{1,0:T(8,128)(2,1)S(1)} %collective-permute-done.8, f32[2,128,1024]{2,1,0:T(8,128)S(1)} %convert_add_fusion), kind=kLoop, calls=%fused_computation.3 | loop fusion | flops 393216 | bytes 1048576 | tf_op jit(solution)/shard_map/convert_element_type | solution.py:350
  36.7 0.5 %shard_map.87.x_ref = bf16[512,1024]{1,0:T(8,128)(2,1)S(1)} custom-call(bf16[384,512]{1,0:T(8,128)(2,1)S(1)} %constant_dynamic-update-slice_fusion.mine_ref, bf16[384,512]{1,0:T(8,128)(2,1)S(1)} %collective-permute-done.9.theirs_ref, bf16[128,512]{1,0:T(8,128)(2,1)S(1)} %collective-permute-done.3.next_ref, bf16[128,4096]{1,0:T(8,128)(2,1)S(1)} %copy-done), custom_call_target="tpu_custom_call" | custom-call | bytes 2097152 | tf_op jit(solution)/shard_map/pallas_call | solution.py:227
  37.2 1.2 %shard_map.88 = f32[512,256]{1,0:T(8,128)} custom-call(bf16[512,1024]{1,0:T(8,128)(2,1)S(1)} %shard_map.87.x_ref, bf16[256,256]{1,0:T(8,128)(2,1)S(1)} %constant_dynamic-update-slice_fusion.3.refs_0_, bf16[256,256]{1,0:T(8,128)(2,1)S(1)} %collective-permute-done.4.refs_1_, bf16[256,256]{1,0:T(8,128)(2,1)S(1)} %collective-permute-done.7.refs_2_, ...), custom_call_target="tpu_custom_call" | custom-call | flops 268435456 | bytes 1572864 | tf_op jit(solution)/shard_map/pallas_call | solution.py:240
  (13 shorter events, 0.1 us)
Async XLA Ops:
  1.7 20.2 %collective-permute-start.1 = (bf16[128,512]{1,0:T(8,128)(2,1)S(1)}, bf16[128,512]{1,0:T(8,128)(2,1)S(1)}, u32[]{:S(2)}, u32[]{:S(2)}) collective-permute-start(bf16[128,512]{1,0:T(8,128)(2,1)S(1)} %get-tuple-element.44), channel_id=1, source_target_pairs={{0,16},{1,21},{2,26},{3,31},{4,20},{5,17},{6,30},{7,27},{8,24},{9,... | collective-permute-start | bytes 393224 | tf_op jit(solution)/shard_map/ppermute | solution.py:193
  5.8 16.1 %collective-permute-start.2 = (bf16[128,512]{1,0:T(8,128)(2,1)S(1)}, bf16[128,512]{1,0:T(8,128)(2,1)S(1)}, u32[]{:S(2)}, u32[]{:S(2)}) collective-permute-start(bf16[128,512]{1,0:T(8,128)(2,1)S(1)} %get-tuple-element.43), channel_id=1, source_target_pairs={{0,8},{1,13},{2,10},{3,15},{4,12},{5,9},{6,14},{7,11},{8,0},{9,5},... | collective-permute-start | bytes 393224 | tf_op jit(solution)/shard_map/ppermute | solution.py:193
  14.1 22.7 %copy-start = (bf16[128,4096]{1,0:T(8,128)(2,1)S(1)}, bf16[128,4096]{1,0:T(8,128)(2,1)}, u32[]{:S(2)}) copy-start(bf16[128,4096]{1,0:T(8,128)(2,1)} %x_hbm.1) | copy-start | bytes 3145732
  14.1 7.8 %collective-permute-start.3 = (bf16[128,512]{1,0:T(8,128)(2,1)S(1)}, bf16[128,512]{1,0:T(8,128)(2,1)S(1)}, u32[]{:S(2)}, u32[]{:S(2)}) collective-permute-start(bf16[128,512]{1,0:T(8,128)(2,1)S(1)} %get-tuple-element.28), channel_id=1, source_target_pairs={{0,4},{1,5},{2,6},{3,7},{4,0},{5,1},{6,2},{7,3},{8,12},{9,13},{10,... | collective-permute-start | bytes 393224 | tf_op jit(solution)/shard_map/ppermute | solution.py:193
  15.6 6.3 %collective-permute-start = (bf16[128,256]{1,0:T(8,128)(2,1)}, bf16[128,256]{1,0:T(8,128)(2,1)S(1)}, u32[]{:S(2)}, u32[]{:S(2)}) collective-permute-start(bf16[128,256]{1,0:T(8,128)(2,1)} %get-tuple-element.24), channel_id=1, source_target_pairs={{0,16},{1,17},{2,18},{3,19},{4,20},{5,21},{6,22},{7,23},{8,24},{9,... | collective-permute-start | bytes 196616 | tf_op jit(solution)/shard_map/ppermute | solution.py:193
  21.9 2.8 %collective-permute-start.6 = (bf16[2,128,1024]{2,1,0:T(8,128)(2,1)}, bf16[2,128,1024]{2,1,0:T(8,128)(2,1)S(1)}, u32[]{:S(2)}, u32[]{:S(2)}) collective-permute-start(bf16[2,128,1024]{2,1,0:T(8,128)(2,1)} %get-tuple-element.34), channel_id=1, source_target_pairs={{0,1},{1,0},{2,3},{3,2},{4,5},{5,4},{6,7},{7,6},{8,9},{9,8},{10,11... | collective-permute-start | bytes 1572872 | tf_op jit(solution)/shard_map/ppermute | solution.py:197
  22.0 5.9 %collective-permute-start.4 = (bf16[256,256]{1,0:T(8,128)(2,1)S(1)}, bf16[256,256]{1,0:T(8,128)(2,1)S(1)}, u32[]{:S(2)}, u32[]{:S(2)}) collective-permute-start(bf16[256,256]{1,0:T(8,128)(2,1)S(1)} %constant_dynamic-update-slice_fusion.3.refs_0_), channel_id=1, source_target_pairs={{0,8},{1,9},{2,10},{3,11},{4,12},{5,13},{6,14},{7,15},{8,0},{9,1},... | collective-permute-start | bytes 393224 | tf_op jit(solution)/shard_map/ppermute | solution.py:193
  22.1 6.2 %collective-permute-start.7 = (bf16[256,256]{1,0:T(8,128)(2,1)S(1)}, bf16[256,256]{1,0:T(8,128)(2,1)S(1)}, u32[]{:S(2)}, u32[]{:S(2)}) collective-permute-start(bf16[256,256]{1,0:T(8,128)(2,1)S(1)} %constant_dynamic-update-slice_fusion.3.refs_0_), channel_id=1, source_target_pairs={{0,4},{1,5},{2,6},{3,7},{4,0},{5,1},{6,2},{7,3},{8,12},{9,13},{10,... | collective-permute-start | bytes 393224 | tf_op jit(solution)/shard_map/ppermute | solution.py:193
  22.7 5.6 %collective-permute-start.5 = (bf16[128,512]{1,0:T(8,128)(2,1)S(1)}, bf16[128,512]{1,0:T(8,128)(2,1)S(1)}, u32[]{:S(2)}, u32[]{:S(2)}) collective-permute-start(bf16[128,512]{1,0:T(8,128)(2,1)S(1)} %collective-permute-done.1), channel_id=1, source_target_pairs={{0,2},{1,3},{2,0},{3,1},{4,6},{5,7},{6,4},{7,5},{8,10},{9,11},{10,... | collective-permute-start | bytes 393224 | tf_op jit(solution)/shard_map/ppermute | solution.py:197
  28.3 7.6 %collective-permute-start.8 = (bf16[128,1024]{1,0:T(8,128)(2,1)S(1)}, bf16[128,1024]{1,0:T(8,128)(2,1)S(1)}, u32[]{:S(2)}, u32[]{:S(2)}) collective-permute-start(bf16[128,1024]{1,0:T(8,128)(2,1)S(1)} %fusion.1), channel_id=1, source_target_pairs={{0,2},{1,3},{2,0},{3,1},{4,6},{5,7},{6,4},{7,5},{8,10},{9,11},{10,... | collective-permute-start | bytes 786440 | tf_op jit(solution)/shard_map/ppermute | solution.py:349
  30.1 6.6 %collective-permute-start.9 = (bf16[384,512]{1,0:T(8,128)(2,1)S(1)}, bf16[384,512]{1,0:T(8,128)(2,1)S(1)}, u32[]{:S(2)}, u32[]{:S(2)}) collective-permute-start(bf16[384,512]{1,0:T(8,128)(2,1)S(1)} %constant_dynamic-update-slice_fusion.mine_ref), channel_id=1, source_target_pairs={{0,1},{1,0},{2,3},{3,2},{4,5},{5,4},{6,7},{7,6},{8,9},{9,8},{10,11... | collective-permute-start | bytes 1179656 | tf_op jit(solution)/shard_map/ppermute | solution.py:197
  30.2 7.0 %collective-permute-start.10 = (bf16[256,256]{1,0:T(8,128)(2,1)S(1)}, bf16[256,256]{1,0:T(8,128)(2,1)S(1)}, u32[]{:S(2)}, u32[]{:S(2)}) collective-permute-start(bf16[256,256]{1,0:T(8,128)(2,1)S(1)} %collective-permute-done.4.refs_1_), channel_id=1, source_target_pairs={{0,4},{1,5},{2,6},{3,7},{4,0},{5,1},{6,2},{7,3},{8,12},{9,13},{10,... | collective-permute-start | bytes 393224 | tf_op jit(solution)/shard_map/ppermute | solution.py:193

commit v8 on v6

--- a/solution.py
+++ b/solution.py
@@ -62,8 +62,8 @@
 
 def attention_kernel(
     q_hbm, k_hbm, v_hbm, do_hbm, p_hbm,
-    gk_ref, ds_hbm, sent_hbm, kept_hbm,
-    q, k, v, do, p, probs_b, ds, scores, grad_probs, partial, sems, p_sems, out_sems,
+    gk_ref, gq_hbm, sent_hbm, kept_hbm,
+    q, k, v, do, p, probs_b, ds, gq, scores, grad_probs, partial, sems, p_sems, out_sems,
 ):
     kv_heads = k.shape[1] // HEAD_SIZE
     group = q.shape[1] // kv_heads
@@ -83,7 +83,7 @@
             pltpu.make_async_copy(q_hbm.at[:, cols], q.at[:, cols], sems.at[2 + 2 * g]),
             pltpu.make_async_copy(do_hbm.at[:, cols], do.at[:, cols], sems.at[3 + 2 * g]),
         ))
-        stored.append(pltpu.make_async_copy(ds.at[:, cols], ds_hbm.at[:, cols], out_sems.at[g]))
+        stored.append(pltpu.make_async_copy(gq.at[:, cols], gq_hbm.at[:, cols], out_sems.at[g]))
     blocks = []
     for b in range(groups):
         column = core if b >= chips else 1 - core
@@ -107,10 +107,15 @@
     values, keys = [], []
     for g in range(kv_heads):
         attention_softmax(g, scores, grad_probs, probs_b, ds)
-        stored[g].start()
         cols = slice(g * group, (g + 1) * group)
         values.append(dot(probs_b[:, cols], stacked(do, g, per_group)).astype(BF16))
         keys.append((dot(ds[:, cols], stacked(q, g, per_group)) * scale).astype(BF16))
+        grad_query = dot(ds[:, cols], k[:, g * HEAD_SIZE : (g + 1) * HEAD_SIZE], TN) * scale
+        length = q.shape[0]
+        for h in range(per_group):
+            at = g * group + h * HEAD_SIZE
+            gq[:, at : at + HEAD_SIZE] = grad_query[h * length : (h + 1) * length].astype(BF16)
+        stored[g].start()
     gk = jnp.concatenate(keys, axis=1)
     gk_ref[...] = gk
     grads = jnp.concatenate([gk] + values, axis=1)
@@ -128,32 +133,9 @@
         copy.wait()
 
 
-def query_kernel(ds_hbm, k_hbm, gq_hbm, ds, k, gq, sems, out_sems):
-    kv_heads = k.shape[1] // HEAD_SIZE
-    group = gq.shape[1] // kv_heads
-    scale = 1.0 / math.sqrt(HEAD_SIZE)
-    key_copy = pltpu.make_async_copy(k_hbm, k, sems.at[kv_heads])
-    key_copy.start()
-    loads, stores = [], []
-    for g in range(kv_heads):
-        cols = pl.ds(g * group, group)
-        loads.append(pltpu.make_async_copy(ds_hbm.at[:, cols], ds.at[:, cols], sems.at[g]))
-        stores.append(pltpu.make_async_copy(gq.at[:, cols], gq_hbm.at[:, cols], out_sems.at[g]))
-        loads[-1].start()
-    key_copy.wait()
-    for g in range(kv_heads):
-        loads[g].wait()
-        key = k[:, g * HEAD_SIZE : (g + 1) * HEAD_SIZE]
-        for at in range(g * group, (g + 1) * group, HEAD_SIZE):
-            grad = dot(ds[:, at : at + HEAD_SIZE], key, TN) * scale
-            gq[:, at : at + HEAD_SIZE] = grad.astype(BF16)
-        stores[g].start()
-    for copy in stores:
-        copy.wait()
-
-
-def turned_kernel(mine_ref, theirs_ref, next_ref, x_hbm, out_ref, own, sem):
-    rows, width = next_ref.shape
+def turned_kernel(*refs):
+    *blocks, next_ref, x_hbm, out_ref, own, sem = refs
+    rows, width = own.shape
     parts = out_ref.shape[1] // rows
     far = groups = parts // 2
     part, member = lax.axis_index("dp"), lax.axis_index("mp")
@@ -167,9 +149,9 @@
 
     partners = [far + (member ^ j) for j in range(0, groups, 2)]
     partners += [k + lax.rem(member, 2) for k in range(2, far, 2)]
-    for at, k in enumerate(partners):
-        put(k, mine_ref[at * rows : (at + 1) * rows, :])
-        put(k ^ 1, theirs_ref[at * rows : (at + 1) * rows, :])
+    for k, mine, theirs in zip(partners, blocks[: len(partners)], blocks[len(partners) :]):
+        put(k, mine[...])
+        put(k ^ 1, theirs[...])
     put(jnp.int32(1), next_ref[...])
     copy.wait()
     put(jnp.int32(0), own[...])
@@ -210,7 +192,7 @@
     for k in range(2, far, 2):
         sent = block(k + lax.rem(member, 2))
         near.append(along_dp(sent, lambda m, k=k: k + m % 2, parts, groups))
-    return distant, near, block(1)
+    return distant, near, along_dp(block(1), lambda m: 1, parts, groups)
 
 
 def shared_inputs(piece, groups):
@@ -224,15 +206,16 @@
 
 def turned_inputs(mine, theirs, next_inputs, inputs):
     rows, width = next_inputs.shape
+    blocks = [*mine, *theirs, next_inputs]
     return pl.pallas_call(
         turned_kernel,
-        in_specs=[IN_VMEM, IN_VMEM, IN_VMEM, IN_HBM],
+        in_specs=[IN_VMEM] * len(blocks) + [IN_HBM],
         out_specs=IN_VMEM,
         out_shape=jax.ShapeDtypeStruct((width, inputs.shape[1] // width * rows), inputs.dtype),
         scratch_shapes=[pltpu.VMEM((rows, width), inputs.dtype), pltpu.SemaphoreType.DMA],
         compiler_params=PARAMS,
         cost_estimate=cost(0, 4 * inputs.size),
-    )(mine, theirs, next_inputs, inputs)
+    )(*blocks, inputs)
 
 
 def summed_weights(turned, keys):
@@ -268,12 +251,12 @@
     partial = jax.ShapeDtypeStruct((chips, rows, features), BF16)
     exchange = parts == 2 * groups and inputs_normed.shape[1] % (parts * 128) == 0
     if exchange:
-        distant, near, next_block = sent_inputs(inputs_normed, parts, groups)
+        distant, near, next_inputs = sent_inputs(inputs_normed, parts, groups)
 
     whole = pltpu.VMEM((rows, query_width), BF16)
     narrow = pltpu.VMEM((rows, width), BF16)
     wide = pltpu.VMEM((kv_heads, rows, query_width // kv_heads), F32)
-    grad_key, grad_scores, sent, kept = pl.pallas_call(
+    grad_key, grad_query, sent, kept = pl.pallas_call(
         attention_kernel,
         in_specs=[IN_HBM] * 5,
         out_specs=[IN_VMEM, ANYWHERE, ANYWHERE, ANYWHERE],
@@ -284,7 +267,7 @@
             partial,
         ),
         scratch_shapes=[whole, narrow, narrow, whole]
-        + [pltpu.VMEM((groups, 2, features, width), BF16), whole, whole, wide, wide]
+        + [pltpu.VMEM((groups, 2, features, width), BF16), whole, whole, whole, wide, wide]
         + [pltpu.VMEM((groups, rows, features), BF16)]
         + [pltpu.SemaphoreType.DMA((2 + 2 * kv_heads,)), pltpu.SemaphoreType.DMA((groups,))]
         + [pltpu.SemaphoreType.DMA((kv_heads + groups,))],
@@ -296,25 +279,13 @@
         ),
     )(query_states, key_states, value_states, grad_context, projections)
 
-    grad_query = pl.pallas_call(
-        query_kernel,
-        in_specs=[IN_HBM, IN_HBM],
-        out_specs=ANYWHERE,
-        out_shape=jax.ShapeDtypeStruct((rows, query_width), BF16),
-        scratch_shapes=[whole, narrow, whole]
-        + [pltpu.SemaphoreType.DMA((1 + kv_heads,)), pltpu.SemaphoreType.DMA((kv_heads,))],
-        compiler_params=WHOLE,
-        cost_estimate=cost(2 * rows * rows * query_width, 4 * rows * query_width),
-    )(grad_scores, key_states)
-
-    if exchange:
-        distant, near = lax.optimization_barrier((distant, near))
-        ready, sent, distant, near = lax.optimization_barrier(
-            (grad_key, sent, distant, near)
+    if exchange:
+        ready, distant = lax.optimization_barrier((grad_key, distant))
+        sent, distant, near, next_inputs = lax.optimization_barrier(
+            (sent, distant, near, next_inputs)
         )
         first = along_dp(ready, lambda m: parts // 2, parts, groups)
         pieces = shared_inputs(distant, groups)
-        next_inputs = along_dp(next_block, lambda m: 1, parts, groups)
     came = along_mp(sent, 1, groups)
     if exchange:
         came, ready = lax.optimization_barrier((came, grad_key))
@@ -322,12 +293,10 @@
     total = kept.astype(F32) + came.astype(F32)
     pairs = [total[b].astype(BF16) for b in range(chips - 1)]
     if exchange:
-        first, twice, pieces, pairs, next_inputs = lax.optimization_barrier(
-            (first, twice, pieces, pairs, next_inputs)
-        )
+        first, twice, pieces, pairs = lax.optimization_barrier((first, twice, pieces, pairs))
         keys = {0: lax.dynamic_update_slice(twice, first, (rows, 0))}
-        mine = jnp.concatenate(pieces + near)
-        theirs = along_mp(mine, 1, groups)
+        mine = pieces + near
+        theirs = [along_mp(piece, 1, groups) for piece in mine]
         bit = parts // 4
         while bit > 1:
             for k in list(keys):
@@ -343,9 +312,7 @@
         beside = []
         for k in range(0, parts // 2, 2):
             if k:
-                keys[k], beside, grad_query = lax.optimization_barrier(
-                    (keys[k], beside, grad_query)
-                )
+                keys[k], beside = lax.optimization_barrier((keys[k], beside))
             beside.append(along_dp(keys[k], lambda m: 1, parts, groups))
         turned = turned_inputs(mine, theirs, next_inputs, inputs_normed)
         beside[-1], grad_input = lax.optimization_barrier((beside[-1], grad_input))

time: 37.7 us -> 36.2 us (0.960)
  Pallas kernels: 10.6 us -> 8.54 us
  waiting for transfers between devices: 7.46 us -> 9.3 us
  starting transfers between devices: 14.5 us -> 13.3 us
    pallas_call x2 -> x1, Pallas kernels: 2.72 us -> 0.47 us  [turned_inputs(): pl.pallas_call(turned_kernel, in_specs=[IN_VMEM] * len(blocks) + [IN_HBM]...]
    ppermute x7, waiting for transfers between devices: 7.25 us -> 8.9 us  [along_dp(): return lax.ppermute(array, ('dp', 'mp'), pairs)]
    ppermute x3 -> x5, starting transfers between devices: 3.26 us -> 2 us  [along_mp(): return lax.ppermute(array, 'mp', [(m, m ^ bit) for m in range(groups)])]
  transfers between devices with their start and end apart: 11 -> 13, of which waited for: 6 -> 6; matrix products, arithmetic and copies ran while one was open for 8% -> 8% of each run, Pallas kernels for 24% -> 20%
where the time goes in v8:
time: 36.2 us; the launch traced here: 35.9 us
  starting transfers between devices  13.3 us (37%)
  waiting for transfers between devices  9.3 us (26%)
  Pallas kernels  8.54 us (24%)
  other arithmetic  2.9 us (8%)
  local copies, waits for them, and re-layouts  1.11 us (3%)
  between operations  0.76 us (2%)
    ppermute x7, starting transfers between devices, along_dp(): return lax.ppermute(array, ('dp', 'mp'), pairs)  9.57 us
    ppermute x7, waiting for transfers between devices, along_dp(): return lax.ppermute(array, ('dp', 'mp'), pairs)  8.9 us
    pallas_call x1, Pallas kernels, body(): pl.pallas_call(attention_kernel, in_specs=[IN_HBM] * 5, out_specs=[IN_VME...  6.84 us
    ppermute x5, starting transfers between devices, along_mp(): return lax.ppermute(array, 'mp', [(m, m ^ bit) for m in range(groups)])  2 us
    ppermute x1, starting transfers between devices, body(): grad_input += lax.ppermute(pairs[b], 'mp', shift).astype(F32)  1.74 us
    pallas_call x1, Pallas kernels, summed_weights(): pl.pallas_call(weights_kernel, out_specs=IN_VMEM, out_shape=jax.ShapeDtyp...  1.24 us
    add x1, other arithmetic, body(): total = kept.astype(F32) + came.astype(F32)  1.21 us
    dynamic_slice x1, local copies, waits for them, and re-layouts, block(): return lax.dynamic_slice(inputs, (0, (part ^ k) * width), (rows, width))  1.07 us
  transfers between devices with their start and end apart: 13, of which 6 were waited for; matrix products, arithmetic and copies ran while one was open for 8% of the time, Pallas kernels for 20%

profile of v8, /device:TPU:0, one launch (start us, length us, event | category | flops | bytes accessed | tf_op | source)
XLA Modules:
  0.0 35.9 jit_solution(8074603008547329266)
XLA Ops:
  0.7 1.1 %constant_dynamic-slice_fusion = (bf16[128,512]{1,0:T(8,128)(2,1)S(1)}, bf16[128,512]{1,0:T(8,128)(2,1)S(1)}, bf16[128,512]{1,0:T(8,128)(2,1)S(1)}) fusion(bf16[128,4096]{1,0:T(8,128)(2,1)} %refs_7_.1, s32[]{:T(128)S(6)} %select_n.11, s32[]{:T(128)S(6)} %select_n.10, s32[]{:T(128)S(6)} %select_n.9), kind=kLoop, calls=%fused_computation.8 | loop fusion | bytes 786444 | tf_op jit(solution)/shard_map/dynamic_slice | solution.py:188
  1.7 4.1 %collective-permute-start = (bf16[128,512]{1,0:T(8,128)(2,1)S(1)}, bf16[128,512]{1,0:T(8,128)(2,1)S(1)}, u32[]{:S(2)}, u32[]{:S(2)}) collective-permute-start(bf16[128,512]{1,0:T(8,128)(2,1)S(1)} %get-tuple-element.47), channel_id=1, source_target_pairs={{0,16},{1,21},{2,26},{3,31},{4,20},{5,17},{6,30},{7,27},{8,24},{9,... | collective-permute-start | bytes 393224 | tf_op jit(solution)/shard_map/ppermute | solution.py:175
  5.8 1.6 %collective-permute-start.2 = (bf16[128,512]{1,0:T(8,128)(2,1)S(1)}, bf16[128,512]{1,0:T(8,128)(2,1)S(1)}, u32[]{:S(2)}, u32[]{:S(2)}) collective-permute-start(bf16[128,512]{1,0:T(8,128)(2,1)S(1)} %get-tuple-element.46), channel_id=1, source_target_pairs={{0,8},{1,13},{2,10},{3,15},{4,12},{5,9},{6,14},{7,11},{8,0},{9,5},... | collective-permute-start | bytes 393224 | tf_op jit(solution)/shard_map/ppermute | solution.py:175
  7.4 1.5 %collective-permute-start.3 = (bf16[128,512]{1,0:T(8,128)(2,1)S(1)}, bf16[128,512]{1,0:T(8,128)(2,1)S(1)}, u32[]{:S(2)}, u32[]{:S(2)}) collective-permute-start(bf16[128,512]{1,0:T(8,128)(2,1)S(1)} %get-tuple-element.45), channel_id=1, source_target_pairs={{0,4},{1,5},{2,6},{3,7},{4,0},{5,1},{6,2},{7,3},{8,12},{9,13},{10,... | collective-permute-start | bytes 393224 | tf_op jit(solution)/shard_map/ppermute | solution.py:175
  8.9 6.8 %shard_map.85 = (bf16[128,256]{1,0:T(8,128)(2,1)}, bf16[128,2048]{1,0:T(8,128)(2,1)}, bf16[2,128,1024]{2,1,0:T(8,128)(2,1)}, bf16[2,128,1024]{2,1,0:T(8,128)(2,1)}) custom-call(bf16[128,2048]{1,0:T(8,128)(2,1)} %q_hbm.1, bf16[128,256]{1,0:T(8,128)(2,1)} %k_hbm.1, bf16[128,256]{1,0:T(8,128)(2,1)} %v_hbm.1, bf16[128,2048]{1,0:T(8,128)(2,1)} %do_hbm.1, ...), custom_call_target="tpu_custom_call" | custom-call | flops 805306368 | bytes 5767168 | tf_op jit(solution)/shard_map/pallas_call | solution.py:259
  15.8 0.1 collective-permute-start.4
  15.9 0.4 %collective-permute-start.1 = (bf16[128,256]{1,0:T(8,128)(2,1)}, bf16[128,256]{1,0:T(8,128)(2,1)S(1)}, u32[]{:S(2)}, u32[]{:S(2)}) collective-permute-start(bf16[128,256]{1,0:T(8,128)(2,1)} %get-tuple-element.30), channel_id=1, source_target_pairs={{0,16},{1,17},{2,18},{3,19},{4,20},{5,21},{6,22},{7,23},{8,24},{9,... | collective-permute-start | bytes 196616 | tf_op jit(solution)/shard_map/ppermute | solution.py:175
  16.2 1.4 %collective-permute-start.5 = (bf16[128,512]{1,0:T(8,128)(2,1)S(1)}, bf16[128,512]{1,0:T(8,128)(2,1)S(1)}, u32[]{:S(2)}, u32[]{:S(2)}) collective-permute-start(bf16[128,512]{1,0:T(8,128)(2,1)S(1)} %collective-permute-done.refs_0_), channel_id=1, source_target_pairs={{0,2},{1,3},{2,0},{3,1},{4,6},{5,7},{6,4},{7,5},{8,10},{9,11},{10,... | collective-permute-start | bytes 393224 | tf_op jit(solution)/shard_map/ppermute | solution.py:179
  17.7 0.3 collective-permute-done.4
  18.0 1.2 %convert_add_fusion = f32[2,128,1024]{2,1,0:T(8,128)S(1)} fusion(bf16[2,128,1024]{2,1,0:T(8,128)(2,1)S(1)} %collective-permute-done.4, bf16[2,128,1024]{2,1,0:T(8,128)(2,1)} %get-tuple-element.32), kind=kLoop, calls=%fused_computation | loop fusion | flops 786432 | bytes 2097152 | tf_op jit(solution)/shard_map/add | solution.py:293
  19.2 0.9 %pad_maximum_fusion = bf16[256,256]{1,0:T(8,128)(2,1)S(1)} fusion(bf16[128,256]{1,0:T(8,128)(2,1)} %get-tuple-element.30), kind=kLoop, calls=%fused_computation.6 | loop fusion | flops 262144 | bytes 196608 | tf_op jit(solution)/shard_map/concatenate | solution.py:292
  20.2 2.6 %collective-permute-done.1 = bf16[128,256]{1,0:T(8,128)(2,1)S(1)} collective-permute-done((bf16[128,256]{1,0:T(8,128)(2,1)}, bf16[128,256]{1,0:T(8,128)(2,1)S(1)}, u32[]{:S(2)}, u32[]{:S(2)}) %collective-permute-start.1) | collective-permute-done | bytes 65568 | tf_op jit(solution)/shard_map/ppermute | solution.py:175
  22.8 0.2 collective-permute-start.6
  23.0 1.7 %collective-permute-start.9 = (bf16[128,1024]{1,0:T(8,128)(2,1)S(1)}, bf16[128,1024]{1,0:T(8,128)(2,1)S(1)}, u32[]{:S(2)}, u32[]{:S(2)}) collective-permute-start(bf16[128,1024]{1,0:T(8,128)(2,1)S(1)} %fusion.2), channel_id=1, source_target_pairs={{0,2},{1,3},{2,0},{3,1},{4,6},{5,7},{6,4},{7,5},{8,10},{9,11},{10,... | collective-permute-start | bytes 786440 | tf_op jit(solution)/shard_map/ppermute | solution.py:308
  24.8 0.9 %collective-permute-start.7 = (bf16[256,256]{1,0:T(8,128)(2,1)S(1)}, bf16[256,256]{1,0:T(8,128)(2,1)S(1)}, u32[]{:S(2)}, u32[]{:S(2)}) collective-permute-start(bf16[256,256]{1,0:T(8,128)(2,1)S(1)} %constant_dynamic-update-slice_fusion.refs_0_), channel_id=1, source_target_pairs={{0,4},{1,5},{2,6},{3,7},{4,0},{5,1},{6,2},{7,3},{8,12},{9,13},{10,... | collective-permute-start | bytes 393224 | tf_op jit(solution)/shard_map/ppermute | solution.py:175
  25.6 0.5 %collective-permute-start.10 = (bf16[128,512]{1,0:T(8,128)(2,1)S(1)}, bf16[128,512]{1,0:T(8,128)(2,1)S(1)}, u32[]{:S(2)}, u32[]{:S(2)}) collective-permute-start(bf16[128,512]{1,0:T(8,128)(2,1)S(1)} %collective-permute-done.refs_0_), channel_id=1, source_target_pairs={{0,1},{1,0},{2,3},{3,2},{4,5},{5,4},{6,7},{7,6},{8,9},{9,8},{10,11... | collective-permute-start | bytes 393224 | tf_op jit(solution)/shard_map/ppermute | solution.py:179
  26.2 2.2 %collective-permute-done.6.refs_1_ = bf16[256,256]{1,0:T(8,128)(2,1)S(1)} collective-permute-done((bf16[256,256]{1,0:T(8,128)(2,1)S(1)}, bf16[256,256]{1,0:T(8,128)(2,1)S(1)}, u32[]{:S(2)}, u32[]{:S(2)}) %collective-permute-start.6) | collective-permute-done | bytes 131104 | tf_op jit(solution)/shard_map/ppermute | solution.py:175
  28.3 1.4 %collective-permute-done.7.refs_2_ = bf16[256,256]{1,0:T(8,128)(2,1)S(1)} collective-permute-done((bf16[256,256]{1,0:T(8,128)(2,1)S(1)}, bf16[256,256]{1,0:T(8,128)(2,1)S(1)}, u32[]{:S(2)}, u32[]{:S(2)}) %collective-permute-start.7) | collective-permute-done | bytes 131104 | tf_op jit(solution)/shard_map/ppermute | solution.py:175
  29.7 0.9 %collective-permute-start.8 = (bf16[256,256]{1,0:T(8,128)(2,1)S(1)}, bf16[256,256]{1,0:T(8,128)(2,1)S(1)}, u32[]{:S(2)}, u32[]{:S(2)}) collective-permute-start(bf16[256,256]{1,0:T(8,128)(2,1)S(1)} %collective-permute-done.6.refs_1_), channel_id=1, source_target_pairs={{0,4},{1,5},{2,6},{3,7},{4,0},{5,1},{6,2},{7,3},{8,12},{9,13},{10,... | collective-permute-start | bytes 393224 | tf_op jit(solution)/shard_map/ppermute | solution.py:175
  30.6 0.5 %shard_map.86.x_ref = bf16[512,1024]{1,0:T(8,128)(2,1)S(1)} custom-call(bf16[128,512]{1,0:T(8,128)(2,1)S(1)} %collective-permute-done.refs_0_, bf16[128,512]{1,0:T(8,128)(2,1)S(1)} %collective-permute-done.5.refs_1_, bf16[128,512]{1,0:T(8,128)(2,1)S(1)} %collective-permute-done.2.refs_2_, bf16[128,512]{1,0:T(8,128)(2,1)S(1)} %collective-permute-done.10.refs_3_, ...), custom_call_target="tpu_custom_call" | custom-call | bytes 2097152 | tf_op jit(solution)/shard_map/pallas_call | solution.py:210
  31.1 0.1 collective-permute-done.9
  31.2 0.8 %fusion.1 = bf16[128,1024]{1,0:T(8,128)(2,1)} fusion(f32[2,128,1024]{2,1,0:T(8,128)S(1)} %convert_add_fusion, bf16[128,1024]{1,0:T(8,128)(2,1)S(1)} %collective-permute-done.9), kind=kLoop, calls=%fused_computation.3 | loop fusion | flops 393216 | bytes 1048576 | tf_op jit(solution)/shard_map/convert_element_type | solution.py:309
  32.0 2.7 %collective-permute-done.8.refs_3_ = bf16[256,256]{1,0:T(8,128)(2,1)S(1)} collective-permute-done((bf16[256,256]{1,0:T(8,128)(2,1)S(1)}, bf16[256,256]{1,0:T(8,128)(2,1)S(1)}, u32[]{:S(2)}, u32[]{:S(2)}) %collective-permute-start.8) | collective-permute-done | bytes 131104 | tf_op jit(solution)/shard_map/ppermute | solution.py:175
  34.7 1.2 %shard_map.87 = f32[512,256]{1,0:T(8,128)} custom-call(bf16[512,1024]{1,0:T(8,128)(2,1)S(1)} %shard_map.86.x_ref, bf16[256,256]{1,0:T(8,128)(2,1)S(1)} %constant_dynamic-update-slice_fusion.refs_0_, bf16[256,256]{1,0:T(8,128)(2,1)S(1)} %collective-permute-done.6.refs_1_, bf16[256,256]{1,0:T(8,128)(2,1)S(1)} %collective-permute-done.7.refs_2_, ...), custom_call_target="tpu_custom_call" | custom-call | flops 268435456 | bytes 1572864 | tf_op jit(solution)/shard_map/pallas_call | solution.py:223
  (13 shorter events, 0.1 us)
Async XLA Ops:
  1.7 28.9 %copy-start = (bf16[128,4096]{1,0:T(8,128)(2,1)S(1)}, bf16[128,4096]{1,0:T(8,128)(2,1)}, u32[]{:S(2)}) copy-start(bf16[128,4096]{1,0:T(8,128)(2,1)} %refs_7_.1) | copy-start | bytes 3145732
  1.7 14.0 %collective-permute-start = (bf16[128,512]{1,0:T(8,128)(2,1)S(1)}, bf16[128,512]{1,0:T(8,128)(2,1)S(1)}, u32[]{:S(2)}, u32[]{:S(2)}) collective-permute-start(bf16[128,512]{1,0:T(8,128)(2,1)S(1)} %get-tuple-element.47), channel_id=1, source_target_pairs={{0,16},{1,21},{2,26},{3,31},{4,20},{5,17},{6,30},{7,27},{8,24},{9,... | collective-permute-start | bytes 393224 | tf_op jit(solution)/shard_map/ppermute | solution.py:175
  5.8 9.9 %collective-permute-start.2 = (bf16[128,512]{1,0:T(8,128)(2,1)S(1)}, bf16[128,512]{1,0:T(8,128)(2,1)S(1)}, u32[]{:S(2)}, u32[]{:S(2)}) collective-permute-start(bf16[128,512]{1,0:T(8,128)(2,1)S(1)} %get-tuple-element.46), channel_id=1, source_target_pairs={{0,8},{1,13},{2,10},{3,15},{4,12},{5,9},{6,14},{7,11},{8,0},{9,5},... | collective-permute-start | bytes 393224 | tf_op jit(solution)/shard_map/ppermute | solution.py:175
  7.4 8.4 %collective-permute-start.3 = (bf16[128,512]{1,0:T(8,128)(2,1)S(1)}, bf16[128,512]{1,0:T(8,128)(2,1)S(1)}, u32[]{:S(2)}, u32[]{:S(2)}) collective-permute-start(bf16[128,512]{1,0:T(8,128)(2,1)S(1)} %get-tuple-element.45), channel_id=1, source_target_pairs={{0,4},{1,5},{2,6},{3,7},{4,0},{5,1},{6,2},{7,3},{8,12},{9,13},{10,... | collective-permute-start | bytes 393224 | tf_op jit(solution)/shard_map/ppermute | solution.py:175
  15.8 2.2 %collective-permute-start.4 = (bf16[2,128,1024]{2,1,0:T(8,128)(2,1)}, bf16[2,128,1024]{2,1,0:T(8,128)(2,1)S(1)}, u32[]{:S(2)}, u32[]{:S(2)}) collective-permute-start(bf16[2,128,1024]{2,1,0:T(8,128)(2,1)} %get-tuple-element.29), channel_id=1, source_target_pairs={{0,1},{1,0},{2,3},{3,2},{4,5},{5,4},{6,7},{7,6},{8,9},{9,8},{10,11... | collective-permute-start | bytes 1572872 | tf_op jit(solution)/shard_map/ppermute | solution.py:179
  15.9 6.9 %collective-permute-start.1 = (bf16[128,256]{1,0:T(8,128)(2,1)}, bf16[128,256]{1,0:T(8,128)(2,1)S(1)}, u32[]{:S(2)}, u32[]{:S(2)}) collective-permute-start(bf16[128,256]{1,0:T(8,128)(2,1)} %get-tuple-element.30), channel_id=1, source_target_pairs={{0,16},{1,17},{2,18},{3,19},{4,20},{5,21},{6,22},{7,23},{8,24},{9,... | collective-permute-start | bytes 196616 | tf_op jit(solution)/shard_map/ppermute | solution.py:175
  16.2 6.5 %collective-permute-start.5 = (bf16[128,512]{1,0:T(8,128)(2,1)S(1)}, bf16[128,512]{1,0:T(8,128)(2,1)S(1)}, u32[]{:S(2)}, u32[]{:S(2)}) collective-permute-start(bf16[128,512]{1,0:T(8,128)(2,1)S(1)} %collective-permute-done.refs_0_), channel_id=1, source_target_pairs={{0,2},{1,3},{2,0},{3,1},{4,6},{5,7},{6,4},{7,5},{8,10},{9,11},{10,... | collective-permute-start | bytes 393224 | tf_op jit(solution)/shard_map/ppermute | solution.py:179
  22.8 5.5 %collective-permute-start.6 = (bf16[256,256]{1,0:T(8,128)(2,1)S(1)}, bf16[256,256]{1,0:T(8,128)(2,1)S(1)}, u32[]{:S(2)}, u32[]{:S(2)}) collective-permute-start(bf16[256,256]{1,0:T(8,128)(2,1)S(1)} %constant_dynamic-update-slice_fusion.refs_0_), channel_id=1, source_target_pairs={{0,8},{1,9},{2,10},{3,11},{4,12},{5,13},{6,14},{7,15},{8,0},{9,1},... | collective-permute-start | bytes 393224 | tf_op jit(solution)/shard_map/ppermute | solution.py:175
  23.0 8.2 %collective-permute-start.9 = (bf16[128,1024]{1,0:T(8,128)(2,1)S(1)}, bf16[128,1024]{1,0:T(8,128)(2,1)S(1)}, u32[]{:S(2)}, u32[]{:S(2)}) collective-permute-start(bf16[128,1024]{1,0:T(8,128)(2,1)S(1)} %fusion.2), channel_id=1, source_target_pairs={{0,2},{1,3},{2,0},{3,1},{4,6},{5,7},{6,4},{7,5},{8,10},{9,11},{10,... | collective-permute-start | bytes 786440 | tf_op jit(solution)/shard_map/ppermute | solution.py:308
  24.8 5.0 %collective-permute-start.7 = (bf16[256,256]{1,0:T(8,128)(2,1)S(1)}, bf16[256,256]{1,0:T(8,128)(2,1)S(1)}, u32[]{:S(2)}, u32[]{:S(2)}) collective-permute-start(bf16[256,256]{1,0:T(8,128)(2,1)S(1)} %constant_dynamic-update-slice_fusion.refs_0_), channel_id=1, source_target_pairs={{0,4},{1,5},{2,6},{3,7},{4,0},{5,1},{6,2},{7,3},{8,12},{9,13},{10,... | collective-permute-start | bytes 393224 | tf_op jit(solution)/shard_map/ppermute | solution.py:175
  25.6 5.0 %collective-permute-start.12 = (bf16[128,512]{1,0:T(8,128)(2,1)S(1)}, bf16[128,512]{1,0:T(8,128)(2,1)S(1)}, u32[]{:S(2)}, u32[]{:S(2)}) collective-permute-start(bf16[128,512]{1,0:T(8,128)(2,1)S(1)} %collective-permute-done.2.refs_2_), channel_id=1, source_target_pairs={{0,1},{1,0},{2,3},{3,2},{4,5},{5,4},{6,7},{7,6},{8,9},{9,8},{10,11... | collective-permute-start | bytes 393224 | tf_op jit(solution)/shard_map/ppermute | solution.py:179
  25.6 5.0 %collective-permute-start.10 = (bf16[128,512]{1,0:T(8,128)(2,1)S(1)}, bf16[128,512]{1,0:T(8,128)(2,1)S(1)}, u32[]{:S(2)}, u32[]{:S(2)}) collective-permute-start(bf16[128,512]{1,0:T(8,128)(2,1)S(1)} %collective-permute-done.refs_0_), channel_id=1, source_target_pairs={{0,1},{1,0},{2,3},{3,2},{4,5},{5,4},{6,7},{7,6},{8,9},{9,8},{10,11... | collective-permute-start | bytes 393224 | tf_op jit(solution)/shard_map/ppermute | solution.py:179
  28.3 2.3 %collective-permute-start.11 = (bf16[128,512]{1,0:T(8,128)(2,1)S(1)}, bf16[128,512]{1,0:T(8,128)(2,1)S(1)}, u32[]{:S(2)}, u32[]{:S(2)}) collective-permute-start(bf16[128,512]{1,0:T(8,128)(2,1)S(1)} %collective-permute-done.5.refs_1_), channel_id=1, source_target_pairs={{0,1},{1,0},{2,3},{3,2},{4,5},{5,4},{6,7},{7,6},{8,9},{9,8},{10,11... | collective-permute-start | bytes 393224 | tf_op jit(solution)/shard_map/ppermute | solution.py:179
  29.7 5.0 %collective-permute-start.8 = (bf16[256,256]{1,0:T(8,128)(2,1)S(1)}, bf16[256,256]{1,0:T(8,128)(2,1)S(1)}, u32[]{:S(2)}, u32[]{:S(2)}) collective-permute-start(bf16[256,256]{1,0:T(8,128)(2,1)S(1)} %collective-permute-done.6.refs_1_), channel_id=1, source_target_pairs={{0,4},{1,5},{2,6},{3,7},{4,0},{5,1},{6,2},{7,3},{8,12},{9,13},{10,... | collective-permute-start | bytes 393224 | tf_op jit(solution)/shard_map/ppermute | solution.py:175

commit v9 on v8

--- a/solution.py
+++ b/solution.py
@@ -61,17 +61,13 @@
 
 
 def attention_kernel(
-    q_hbm, k_hbm, v_hbm, do_hbm, p_hbm,
-    gk_ref, gq_hbm, sent_hbm, kept_hbm,
-    q, k, v, do, p, probs_b, ds, gq, scores, grad_probs, partial, sems, p_sems, out_sems,
+    q_hbm, k_hbm, v_hbm, do_hbm, gk_ref, gv_ref, gq_hbm,
+    q, k, v, do, probs_b, ds, gq, scores, grad_probs, sems, out_sems,
 ):
+    length = q.shape[0]
     kv_heads = k.shape[1] // HEAD_SIZE
     group = q.shape[1] // kv_heads
     per_group = group // HEAD_SIZE
-    groups, features = p.shape[0], p.shape[2]
-    chips = groups // 2
-    member = lax.axis_index("mp")
-    chip, core = lax.div(member, 2), lax.rem(member, 2)
     small = [
         pltpu.make_async_copy(k_hbm, k, sems.at[0]),
         pltpu.make_async_copy(v_hbm, v, sems.at[1]),
@@ -84,19 +80,11 @@
             pltpu.make_async_copy(do_hbm.at[:, cols], do.at[:, cols], sems.at[3 + 2 * g]),
         ))
         stored.append(pltpu.make_async_copy(gq.at[:, cols], gq_hbm.at[:, cols], out_sems.at[g]))
-    blocks = []
-    for b in range(groups):
-        column = core if b >= chips else 1 - core
-        start = (2 * lax.rem(chip + b + 1, chips) + column) * features
-        rows = pl.ds(pl.multiple_of(start, features), features)
-        blocks.append(pltpu.make_async_copy(p_hbm.at[:, rows, :], p.at[b], p_sems.at[b]))
     for copy in small:
         copy.start()
     for pair in large:
         for copy in pair:
             copy.start()
-    for copy in blocks:
-        copy.start()
     for copy in small:
         copy.wait()
     for g in range(kv_heads):
@@ -104,21 +92,36 @@
             copy.wait()
         attention_scores(g, q, k, v, do, scores, grad_probs)
     scale = 1.0 / math.sqrt(HEAD_SIZE)
-    values, keys = [], []
     for g in range(kv_heads):
         attention_softmax(g, scores, grad_probs, probs_b, ds)
         cols = slice(g * group, (g + 1) * group)
-        values.append(dot(probs_b[:, cols], stacked(do, g, per_group)).astype(BF16))
-        keys.append((dot(ds[:, cols], stacked(q, g, per_group)) * scale).astype(BF16))
-        grad_query = dot(ds[:, cols], k[:, g * HEAD_SIZE : (g + 1) * HEAD_SIZE], TN) * scale
-        length = q.shape[0]
+        head = slice(g * HEAD_SIZE, (g + 1) * HEAD_SIZE)
+        grad_query = dot(ds[:, cols], k[:, head], TN) * scale
         for h in range(per_group):
             at = g * group + h * HEAD_SIZE
             gq[:, at : at + HEAD_SIZE] = grad_query[h * length : (h + 1) * length].astype(BF16)
         stored[g].start()
-    gk = jnp.concatenate(keys, axis=1)
-    gk_ref[...] = gk
-    grads = jnp.concatenate([gk] + values, axis=1)
+        grad_key = dot(ds[:, cols], stacked(q, g, per_group)) * scale
+        gk_ref[:, head] = grad_key.astype(BF16)
+        gv_ref[:, head] = dot(probs_b[:, cols], stacked(do, g, per_group)).astype(BF16)
+    for copy in stored:
+        copy.wait()
+
+
+def partials_kernel(gk_ref, gv_ref, p_hbm, sent_hbm, kept_hbm, p, partial, p_sems, out_sems):
+    groups, features = p.shape[0], p.shape[2]
+    chips = groups // 2
+    member = lax.axis_index("mp")
+    chip, core = lax.div(member, 2), lax.rem(member, 2)
+    blocks, stored = [], []
+    for b in range(groups):
+        column = core if b >= chips else 1 - core
+        start = (2 * lax.rem(chip + b + 1, chips) + column) * features
+        rows = pl.ds(pl.multiple_of(start, features), features)
+        blocks.append(pltpu.make_async_copy(p_hbm.at[:, rows, :], p.at[b], p_sems.at[b]))
+    for copy in blocks:
+        copy.start()
+    grads = jnp.concatenate([gk_ref[...], gv_ref[...]], axis=1)
     step = min(CHUNK, features)
     for b in range(groups):
         blocks[b].wait()
@@ -127,7 +130,7 @@
             both = jnp.concatenate([p[b, 0, rows, :], p[b, 1, rows, :]], axis=1)
             partial[b, :, rows] = dot(grads, both, NT).astype(BF16)
         target = sent_hbm.at[b] if b < chips else kept_hbm.at[b - chips]
-        stored.append(pltpu.make_async_copy(partial.at[b], target, out_sems.at[kv_heads + b]))
+        stored.append(pltpu.make_async_copy(partial.at[b], target, out_sems.at[b]))
         stored[-1].start()
     for copy in stored:
         copy.wait()
@@ -256,44 +259,48 @@
     whole = pltpu.VMEM((rows, query_width), BF16)
     narrow = pltpu.VMEM((rows, width), BF16)
     wide = pltpu.VMEM((kv_heads, rows, query_width // kv_heads), F32)
-    grad_key, grad_query, sent, kept = pl.pallas_call(
+    grad_key, grad_value, grad_query = pl.pallas_call(
         attention_kernel,
-        in_specs=[IN_HBM] * 5,
-        out_specs=[IN_VMEM, ANYWHERE, ANYWHERE, ANYWHERE],
+        in_specs=[IN_HBM] * 4,
+        out_specs=[IN_VMEM, IN_VMEM, ANYWHERE],
         out_shape=(
             jax.ShapeDtypeStruct((rows, width), BF16),
+            jax.ShapeDtypeStruct((rows, width), BF16),
             jax.ShapeDtypeStruct((rows, query_width), BF16),
-            partial,
-            partial,
         ),
-        scratch_shapes=[whole, narrow, narrow, whole]
-        + [pltpu.VMEM((groups, 2, features, width), BF16), whole, whole, whole, wide, wide]
-        + [pltpu.VMEM((groups, rows, features), BF16)]
-        + [pltpu.SemaphoreType.DMA((2 + 2 * kv_heads,)), pltpu.SemaphoreType.DMA((groups,))]
-        + [pltpu.SemaphoreType.DMA((kv_heads + groups,))],
+        scratch_shapes=[whole, narrow, narrow, whole, whole, whole, whole, wide, wide]
+        + [pltpu.SemaphoreType.DMA((2 + 2 * kv_heads,)), pltpu.SemaphoreType.DMA((kv_heads,))],
         compiler_params=WHOLE,
         cost_estimate=cost(
-            8 * rows * rows * query_width + 4 * rows * width * features * groups,
-            6 * rows * query_width + 4 * width * features * groups,
-            rows * query_width,
+            10 * rows * rows * query_width, 6 * rows * query_width, rows * query_width
         ),
-    )(query_states, key_states, value_states, grad_context, projections)
+    )(query_states, key_states, value_states, grad_context)
+
+    sent, kept = pl.pallas_call(
+        partials_kernel,
+        in_specs=[IN_VMEM, IN_VMEM, IN_HBM],
+        out_specs=[ANYWHERE, ANYWHERE],
+        out_shape=(partial, partial),
+        scratch_shapes=[
+            pltpu.VMEM((groups, 2, features, width), BF16),
+            pltpu.VMEM((groups, rows, features), BF16),
+            pltpu.SemaphoreType.DMA((groups,)),
+            pltpu.SemaphoreType.DMA((groups,)),
+        ],
+        compiler_params=WHOLE,
+        cost_estimate=cost(
+            4 * rows * width * features * groups, 4 * width * features * groups
+        ),
+    )(grad_key, grad_value, projections)
 
     if exchange:
-        ready, distant = lax.optimization_barrier((grad_key, distant))
-        sent, distant, near, next_inputs = lax.optimization_barrier(
-            (sent, distant, near, next_inputs)
+        ready, near = lax.optimization_barrier((grad_key, near))
+        first = along_dp(ready, lambda m: parts // 2, parts, groups)
+        twice = jnp.concatenate([grad_key, grad_key])
+        first, twice, sent, kept, distant, near, next_inputs = lax.optimization_barrier(
+            (first, twice, sent, kept, distant, near, next_inputs)
         )
-        first = along_dp(ready, lambda m: parts // 2, parts, groups)
         pieces = shared_inputs(distant, groups)
-    came = along_mp(sent, 1, groups)
-    if exchange:
-        came, ready = lax.optimization_barrier((came, grad_key))
-        twice = jnp.concatenate([ready, ready])
-    total = kept.astype(F32) + came.astype(F32)
-    pairs = [total[b].astype(BF16) for b in range(chips - 1)]
-    if exchange:
-        first, twice, pieces, pairs = lax.optimization_barrier((first, twice, pieces, pairs))
         keys = {0: lax.dynamic_update_slice(twice, first, (rows, 0))}
         mine = pieces + near
         theirs = [along_mp(piece, 1, groups) for piece in mine]
@@ -302,10 +309,12 @@
             for k in list(keys):
                 keys[k ^ bit] = along_dp(keys[k], lambda m, bit=bit: bit, parts, groups)
             bit //= 2
+    came = along_mp(sent, 1, groups)
+    total = kept.astype(F32) + came.astype(F32)
     grad_input = total[chips - 1]
     for b in range(chips - 1):
         shift = [(m, (m + 2 * (b + 1)) % groups) for m in range(groups)]
-        grad_input += lax.ppermute(pairs[b], "mp", shift).astype(F32)
+        grad_input += lax.ppermute(total[b].astype(BF16), "mp", shift).astype(F32)
     grad_input = grad_input.astype(BF16)
 
     if exchange:

time: 36.2 us -> 37 us (1.022)
  Pallas kernels: 8.54 us -> 10.5 us
  waiting for transfers between devices: 9.3 us -> 8.2 us
    ppermute x7, waiting for transfers between devices: 8.9 us -> 4.52 us  [along_dp(): return lax.ppermute(array, ('dp', 'mp'), pairs)]
    pallas_call x1 -> x2, Pallas kernels: 6.84 us -> 8.81 us  [the longest x1 4.77 us: body(): pl.pallas_call(partials_kernel, in_specs=[IN_VMEM, IN_VMEM, IN_HBM], out_...]
    ppermute x1, waiting for transfers between devices: 0.09 us -> 1.96 us  [body(): grad_input += lax.ppermute(total[b].astype(BF16), 'mp', shift).astype(F32)]
    ppermute x1, starting transfers between devices: 1.74 us -> 0.07 us  [body(): grad_input += lax.ppermute(total[b].astype(BF16), 'mp', shift).astype(F32)]
    ppermute x5, waiting for transfers between devices: 0.32 us -> 1.73 us  [along_mp(): return lax.ppermute(array, 'mp', [(m, m ^ bit) for m in range(groups)])]
    ppermute x5, starting transfers between devices: 2 us -> 3.24 us  [along_mp(): return lax.ppermute(array, 'mp', [(m, m ^ bit) for m in range(groups)])]
  transfers between devices with their start and end apart: 13 -> 13, of which waited for: 6 -> 5; matrix products, arithmetic and copies ran while one was open for 8% -> 8% of each run, Pallas kernels for 20% -> 25%
where the time goes in v9:
time: 37 us; the launch traced here: 36.7 us
  starting transfers between devices  13.2 us (36%)
  Pallas kernels  10.5 us (28%)
  waiting for transfers between devices  8.2 us (22%)
  other arithmetic  2.89 us (8%)
  local copies, waits for them, and re-layouts  1.11 us (3%)
  between operations  0.76 us (2%)
    ppermute x7, starting transfers between devices, along_dp(): return lax.ppermute(array, ('dp', 'mp'), pairs)  9.88 us
    pallas_call x1, Pallas kernels, body(): pl.pallas_call(partials_kernel, in_specs=[IN_VMEM, IN_VMEM, IN_HBM], out_...  4.77 us
    ppermute x7, waiting for transfers between devices, along_dp(): return lax.ppermute(array, ('dp', 'mp'), pairs)  4.52 us
    pallas_call x1, Pallas kernels, body(): pl.pallas_call(attention_kernel, in_specs=[IN_HBM] * 4, out_specs=[IN_VME...  4.04 us
    ppermute x5, starting transfers between devices, along_mp(): return lax.ppermute(array, 'mp', [(m, m ^ bit) for m in range(groups)])  3.24 us
    ppermute x1, waiting for transfers between devices, body(): grad_input += lax.ppermute(total[b].astype(BF16), 'mp', shift).astype(F32)  1.96 us
    ppermute x5, waiting for transfers between devices, along_mp(): return lax.ppermute(array, 'mp', [(m, m ^ bit) for m in range(groups)])  1.73 us
    pallas_call x1, Pallas kernels, summed_weights(): pl.pallas_call(weights_kernel, out_specs=IN_VMEM, out_shape=jax.ShapeDtyp...  1.24 us
  transfers between devices with their start and end apart: 13, of which 5 were waited for; matrix products, arithmetic and copies ran while one was open for 8% of the time, Pallas kernels for 25%

profile of v9, /device:TPU:0, one launch (start us, length us, event | category | flops | bytes accessed | tf_op | source)
XLA Modules:
  0.0 36.7 jit_solution(8401053814287445208)
XLA Ops:
  0.7 1.1 %constant_dynamic-slice_fusion = (bf16[128,512]{1,0:T(8,128)(2,1)S(1)}, bf16[128,512]{1,0:T(8,128)(2,1)S(1)}, bf16[128,512]{1,0:T(8,128)(2,1)S(1)}) fusion(bf16[128,4096]{1,0:T(8,128)(2,1)} %refs_7_.1, s32[]{:T(128)S(6)} %select_n.11, s32[]{:T(128)S(6)} %select_n.10, s32[]{:T(128)S(6)} %select_n.9), kind=kLoop, calls=%fused_computation.8 | loop fusion | bytes 786444 | tf_op jit(solution)/shard_map/dynamic_slice | solution.py:191
  1.7 3.1 %collective-permute-start = (bf16[128,512]{1,0:T(8,128)(2,1)S(1)}, bf16[128,512]{1,0:T(8,128)(2,1)S(1)}, u32[]{:S(2)}, u32[]{:S(2)}) collective-permute-start(bf16[128,512]{1,0:T(8,128)(2,1)S(1)} %get-tuple-element.41), channel_id=1, source_target_pairs={{0,8},{1,13},{2,10},{3,15},{4,12},{5,9},{6,14},{7,11},{8,0},{9,5},... | collective-permute-start | bytes 393224 | tf_op jit(solution)/shard_map/ppermute | solution.py:178
  4.8 2.6 %collective-permute-start.2 = (bf16[128,512]{1,0:T(8,128)(2,1)S(1)}, bf16[128,512]{1,0:T(8,128)(2,1)S(1)}, u32[]{:S(2)}, u32[]{:S(2)}) collective-permute-start(bf16[128,512]{1,0:T(8,128)(2,1)S(1)} %get-tuple-element.40), channel_id=1, source_target_pairs={{0,16},{1,21},{2,26},{3,31},{4,20},{5,17},{6,30},{7,27},{8,24},{9,... | collective-permute-start | bytes 393224 | tf_op jit(solution)/shard_map/ppermute | solution.py:178
  7.4 1.5 %collective-permute-start.3 = (bf16[128,512]{1,0:T(8,128)(2,1)S(1)}, bf16[128,512]{1,0:T(8,128)(2,1)S(1)}, u32[]{:S(2)}, u32[]{:S(2)}) collective-permute-start(bf16[128,512]{1,0:T(8,128)(2,1)S(1)} %get-tuple-element.39), channel_id=1, source_target_pairs={{0,4},{1,5},{2,6},{3,7},{4,0},{5,1},{6,2},{7,3},{8,12},{9,13},{10,... | collective-permute-start | bytes 393224 | tf_op jit(solution)/shard_map/ppermute | solution.py:178
  8.9 4.0 %shard_map.85 = (bf16[128,256]{1,0:T(8,128)(2,1)}, bf16[128,256]{1,0:T(8,128)(2,1)}, bf16[128,2048]{1,0:T(8,128)(2,1)}) custom-call(bf16[128,2048]{1,0:T(8,128)(2,1)} %q_hbm.1, bf16[128,256]{1,0:T(8,128)(2,1)} %k_hbm.1, bf16[128,256]{1,0:T(8,128)(2,1)} %v_hbm.1, bf16[128,2048]{1,0:T(8,128)(2,1)} %do_hbm.1), custom_call_target="tpu_custom_call" | custom-call | flops 335544320 | bytes 1572864 | tf_op jit(solution)/shard_map/pallas_call | solution.py:262
  13.0 0.4 %collective-permute-start.1 = (bf16[128,256]{1,0:T(8,128)(2,1)}, bf16[128,256]{1,0:T(8,128)(2,1)S(1)}, u32[]{:S(2)}, u32[]{:S(2)}) collective-permute-start(bf16[128,256]{1,0:T(8,128)(2,1)} %get-tuple-element.23.gk_ref), channel_id=1, source_target_pairs={{0,16},{1,17},{2,18},{3,19},{4,20},{5,21},{6,22},{7,23},{8,24},{9,... | collective-permute-start | bytes 196616 | tf_op jit(solution)/shard_map/ppermute | solution.py:178
  13.4 0.9 %pad_maximum_fusion = bf16[256,256]{1,0:T(8,128)(2,1)S(1)} fusion(bf16[128,256]{1,0:T(8,128)(2,1)} %get-tuple-element.23.gk_ref), kind=kLoop, calls=%fused_computation.6 | loop fusion | flops 262144 | bytes 196608 | tf_op jit(solution)/shard_map/concatenate | solution.py:299
  14.3 4.8 %shard_map.86 = (bf16[2,128,1024]{2,1,0:T(8,128)(2,1)}, bf16[2,128,1024]{2,1,0:T(8,128)(2,1)}) custom-call(bf16[128,256]{1,0:T(8,128)(2,1)} %get-tuple-element.23.gk_ref, bf16[128,256]{1,0:T(8,128)(2,1)} %get-tuple-element.24.gv_ref, bf16[2,4096,256]{2,1,0:T(8,128)(2,1)} %p_hbm.1), custom_call_target="tpu_custom_call" | custom-call | flops 536870912 | bytes 4194304 | tf_op jit(solution)/shard_map/pallas_call | solution.py:279
  19.1 0.2 collective-permute-done.1
  19.3 1.7 %collective-permute-start.4 = (bf16[256,256]{1,0:T(8,128)(2,1)S(1)}, bf16[256,256]{1,0:T(8,128)(2,1)S(1)}, u32[]{:S(2)}, u32[]{:S(2)}) collective-permute-start(bf16[256,256]{1,0:T(8,128)(2,1)S(1)} %constant_dynamic-update-slice_fusion.refs_0_), channel_id=1, source_target_pairs={{0,8},{1,9},{2,10},{3,11},{4,12},{5,13},{6,14},{7,15},{8,0},{9,1},... | collective-permute-start | bytes 393224 | tf_op jit(solution)/shard_map/ppermute | solution.py:178
  21.1 2.7 %collective-permute-start.9 = (bf16[128,512]{1,0:T(8,128)(2,1)S(1)}, bf16[128,512]{1,0:T(8,128)(2,1)S(1)}, u32[]{:S(2)}, u32[]{:S(2)}) collective-permute-start(bf16[128,512]{1,0:T(8,128)(2,1)S(1)} %collective-permute-done.2.refs_0_), channel_id=1, source_target_pairs={{0,2},{1,3},{2,0},{3,1},{4,6},{5,7},{6,4},{7,5},{8,10},{9,11},{10,... | collective-permute-start | bytes 393224 | tf_op jit(solution)/shard_map/ppermute | solution.py:182
  23.8 1.2 %convert_add_fusion = f32[2,128,1024]{2,1,0:T(8,128)S(1)} fusion(bf16[2,128,1024]{2,1,0:T(8,128)(2,1)S(1)} %collective-permute-done.7, bf16[2,128,1024]{2,1,0:T(8,128)(2,1)} %get-tuple-element.31), kind=kLoop, calls=%fused_computation | loop fusion | flops 786432 | bytes 2097152 | tf_op jit(solution)/shard_map/add | solution.py:313
  25.0 0.1 collective-permute-start.8
  25.1 0.3 collective-permute-start.5
  25.4 0.0 collective-permute-start.10
  25.4 0.5 %collective-permute-start.12 = (bf16[128,512]{1,0:T(8,128)(2,1)S(1)}, bf16[128,512]{1,0:T(8,128)(2,1)S(1)}, u32[]{:S(2)}, u32[]{:S(2)}) collective-permute-start(bf16[128,512]{1,0:T(8,128)(2,1)S(1)} %collective-permute-done.refs_2_), channel_id=1, source_target_pairs={{0,1},{1,0},{2,3},{3,2},{4,5},{5,4},{6,7},{7,6},{8,9},{9,8},{10,11... | collective-permute-start | bytes 393224 | tf_op jit(solution)/shard_map/ppermute | solution.py:182
  25.9 1.7 %collective-permute-done.9.refs_1_ = bf16[128,512]{1,0:T(8,128)(2,1)S(1)} collective-permute-done((bf16[128,512]{1,0:T(8,128)(2,1)S(1)}, bf16[128,512]{1,0:T(8,128)(2,1)S(1)}, u32[]{:S(2)}, u32[]{:S(2)}) %collective-permute-start.9) | collective-permute-done | bytes 131104 | tf_op jit(solution)/shard_map/ppermute | solution.py:182
  27.6 2.8 %collective-permute-done.5.refs_2_ = bf16[256,256]{1,0:T(8,128)(2,1)S(1)} collective-permute-done((bf16[256,256]{1,0:T(8,128)(2,1)S(1)}, bf16[256,256]{1,0:T(8,128)(2,1)S(1)}, u32[]{:S(2)}, u32[]{:S(2)}) %collective-permute-start.5) | collective-permute-done | bytes 131104 | tf_op jit(solution)/shard_map/ppermute | solution.py:178
  30.5 0.3 collective-permute-start.6
  30.8 0.5 %shard_map.87.x_ref = bf16[512,1024]{1,0:T(8,128)(2,1)S(1)} custom-call(bf16[128,512]{1,0:T(8,128)(2,1)S(1)} %collective-permute-done.2.refs_0_, bf16[128,512]{1,0:T(8,128)(2,1)S(1)} %collective-permute-done.9.refs_1_, bf16[128,512]{1,0:T(8,128)(2,1)S(1)} %collective-permute-done.refs_2_, bf16[128,512]{1,0:T(8,128)(2,1)S(1)} %collective-permute-done.10.refs_3_, ...), custom_call_target="tpu_custom_call" | custom-call | bytes 2097152 | tf_op jit(solution)/shard_map/pallas_call | solution.py:213
  31.3 2.0 %collective-permute-done.8 = bf16[128,1024]{1,0:T(8,128)(2,1)S(1)} collective-permute-done((bf16[128,1024]{1,0:T(8,128)(2,1)S(1)}, bf16[128,1024]{1,0:T(8,128)(2,1)S(1)}, u32[]{:S(2)}, u32[]{:S(2)}) %collective-permute-start.8) | collective-permute-done | bytes 262176 | tf_op jit(solution)/shard_map/ppermute | solution.py:317
  33.2 0.8 %fusion.1 = bf16[128,1024]{1,0:T(8,128)(2,1)} fusion(f32[2,128,1024]{2,1,0:T(8,128)S(1)} %convert_add_fusion, bf16[128,1024]{1,0:T(8,128)(2,1)S(1)} %collective-permute-done.8), kind=kLoop, calls=%fused_computation.4 | loop fusion | flops 393216 | bytes 1048576 | tf_op jit(solution)/shard_map/convert_element_type | solution.py:318
  34.0 1.5 %collective-permute-done.6.refs_3_ = bf16[256,256]{1,0:T(8,128)(2,1)S(1)} collective-permute-done((bf16[256,256]{1,0:T(8,128)(2,1)S(1)}, bf16[256,256]{1,0:T(8,128)(2,1)S(1)}, u32[]{:S(2)}, u32[]{:S(2)}) %collective-permute-start.6) | collective-permute-done | bytes 131104 | tf_op jit(solution)/shard_map/ppermute | solution.py:178
  35.4 1.2 %shard_map.88 = f32[512,256]{1,0:T(8,128)} custom-call(bf16[512,1024]{1,0:T(8,128)(2,1)S(1)} %shard_map.87.x_ref, bf16[256,256]{1,0:T(8,128)(2,1)S(1)} %constant_dynamic-update-slice_fusion.refs_0_, bf16[256,256]{1,0:T(8,128)(2,1)S(1)} %collective-permute-done.4.refs_1_, bf16[256,256]{1,0:T(8,128)(2,1)S(1)} %collective-permute-done.5.refs_2_, ...), custom_call_target="tpu_custom_call" | custom-call | flops 268435456 | bytes 1572864 | tf_op jit(solution)/shard_map/pallas_call | solution.py:226
  (14 shorter events, 0.1 us)
Async XLA Ops:
  1.7 11.2 %collective-permute-start = (bf16[128,512]{1,0:T(8,128)(2,1)S(1)}, bf16[128,512]{1,0:T(8,128)(2,1)S(1)}, u32[]{:S(2)}, u32[]{:S(2)}) collective-permute-start(bf16[128,512]{1,0:T(8,128)(2,1)S(1)} %get-tuple-element.41), channel_id=1, source_target_pairs={{0,8},{1,13},{2,10},{3,15},{4,12},{5,9},{6,14},{7,11},{8,0},{9,5},... | collective-permute-start | bytes 393224 | tf_op jit(solution)/shard_map/ppermute | solution.py:178
  4.8 14.3 %collective-permute-start.2 = (bf16[128,512]{1,0:T(8,128)(2,1)S(1)}, bf16[128,512]{1,0:T(8,128)(2,1)S(1)}, u32[]{:S(2)}, u32[]{:S(2)}) collective-permute-start(bf16[128,512]{1,0:T(8,128)(2,1)S(1)} %get-tuple-element.40), channel_id=1, source_target_pairs={{0,16},{1,21},{2,26},{3,31},{4,20},{5,17},{6,30},{7,27},{8,24},{9,... | collective-permute-start | bytes 393224 | tf_op jit(solution)/shard_map/ppermute | solution.py:178
  7.4 23.4 %copy-start = (bf16[128,4096]{1,0:T(8,128)(2,1)S(1)}, bf16[128,4096]{1,0:T(8,128)(2,1)}, u32[]{:S(2)}) copy-start(bf16[128,4096]{1,0:T(8,128)(2,1)} %refs_7_.1) | copy-start | bytes 3145732
  7.4 11.7 %collective-permute-start.3 = (bf16[128,512]{1,0:T(8,128)(2,1)S(1)}, bf16[128,512]{1,0:T(8,128)(2,1)S(1)}, u32[]{:S(2)}, u32[]{:S(2)}) collective-permute-start(bf16[128,512]{1,0:T(8,128)(2,1)S(1)} %get-tuple-element.39), channel_id=1, source_target_pairs={{0,4},{1,5},{2,6},{3,7},{4,0},{5,1},{6,2},{7,3},{8,12},{9,13},{10,... | collective-permute-start | bytes 393224 | tf_op jit(solution)/shard_map/ppermute | solution.py:178
  13.0 6.4 %collective-permute-start.1 = (bf16[128,256]{1,0:T(8,128)(2,1)}, bf16[128,256]{1,0:T(8,128)(2,1)S(1)}, u32[]{:S(2)}, u32[]{:S(2)}) collective-permute-start(bf16[128,256]{1,0:T(8,128)(2,1)} %get-tuple-element.23.gk_ref), channel_id=1, source_target_pairs={{0,16},{1,17},{2,18},{3,19},{4,20},{5,21},{6,22},{7,23},{8,24},{9,... | collective-permute-start | bytes 196616 | tf_op jit(solution)/shard_map/ppermute | solution.py:178
  19.3 4.5 %collective-permute-start.7 = (bf16[2,128,1024]{2,1,0:T(8,128)(2,1)}, bf16[2,128,1024]{2,1,0:T(8,128)(2,1)S(1)}, u32[]{:S(2)}, u32[]{:S(2)}) collective-permute-start(bf16[2,128,1024]{2,1,0:T(8,128)(2,1)} %get-tuple-element.32), channel_id=1, source_target_pairs={{0,1},{1,0},{2,3},{3,2},{4,5},{5,4},{6,7},{7,6},{8,9},{9,8},{10,11... | collective-permute-start | bytes 1572872 | tf_op jit(solution)/shard_map/ppermute | solution.py:182
  19.3 6.1 %collective-permute-start.4 = (bf16[256,256]{1,0:T(8,128)(2,1)S(1)}, bf16[256,256]{1,0:T(8,128)(2,1)S(1)}, u32[]{:S(2)}, u32[]{:S(2)}) collective-permute-start(bf16[256,256]{1,0:T(8,128)(2,1)S(1)} %constant_dynamic-update-slice_fusion.refs_0_), channel_id=1, source_target_pairs={{0,8},{1,9},{2,10},{3,11},{4,12},{5,13},{6,14},{7,15},{8,0},{9,1},... | collective-permute-start | bytes 393224 | tf_op jit(solution)/shard_map/ppermute | solution.py:178
  21.1 6.6 %collective-permute-start.9 = (bf16[128,512]{1,0:T(8,128)(2,1)S(1)}, bf16[128,512]{1,0:T(8,128)(2,1)S(1)}, u32[]{:S(2)}, u32[]{:S(2)}) collective-permute-start(bf16[128,512]{1,0:T(8,128)(2,1)S(1)} %collective-permute-done.2.refs_0_), channel_id=1, source_target_pairs={{0,2},{1,3},{2,0},{3,1},{4,6},{5,7},{6,4},{7,5},{8,10},{9,11},{10,... | collective-permute-start | bytes 393224 | tf_op jit(solution)/shard_map/ppermute | solution.py:182
  25.0 8.2 %collective-permute-start.8 = (bf16[128,1024]{1,0:T(8,128)(2,1)S(1)}, bf16[128,1024]{1,0:T(8,128)(2,1)S(1)}, u32[]{:S(2)}, u32[]{:S(2)}) collective-permute-start(bf16[128,1024]{1,0:T(8,128)(2,1)S(1)} %fusion.2), channel_id=1, source_target_pairs={{0,2},{1,3},{2,0},{3,1},{4,6},{5,7},{6,4},{7,5},{8,10},{9,11},{10,... | collective-permute-start | bytes 786440 | tf_op jit(solution)/shard_map/ppermute | solution.py:317
  25.1 5.3 %collective-permute-start.5 = (bf16[256,256]{1,0:T(8,128)(2,1)S(1)}, bf16[256,256]{1,0:T(8,128)(2,1)S(1)}, u32[]{:S(2)}, u32[]{:S(2)}) collective-permute-start(bf16[256,256]{1,0:T(8,128)(2,1)S(1)} %constant_dynamic-update-slice_fusion.refs_0_), channel_id=1, source_target_pairs={{0,4},{1,5},{2,6},{3,7},{4,0},{5,1},{6,2},{7,3},{8,12},{9,13},{10,... | collective-permute-start | bytes 393224 | tf_op jit(solution)/shard_map/ppermute | solution.py:178
  25.4 5.3 %collective-permute-start.10 = (bf16[128,512]{1,0:T(8,128)(2,1)S(1)}, bf16[128,512]{1,0:T(8,128)(2,1)S(1)}, u32[]{:S(2)}, u32[]{:S(2)}) collective-permute-start(bf16[128,512]{1,0:T(8,128)(2,1)S(1)} %collective-permute-done.2.refs_0_), channel_id=1, source_target_pairs={{0,1},{1,0},{2,3},{3,2},{4,5},{5,4},{6,7},{7,6},{8,9},{9,8},{10,11... | collective-permute-start | bytes 393224 | tf_op jit(solution)/shard_map/ppermute | solution.py:182
  25.4 5.3 %collective-permute-start.12 = (bf16[128,512]{1,0:T(8,128)(2,1)S(1)}, bf16[128,512]{1,0:T(8,128)(2,1)S(1)}, u32[]{:S(2)}, u32[]{:S(2)}) collective-permute-start(bf16[128,512]{1,0:T(8,128)(2,1)S(1)} %collective-permute-done.refs_2_), channel_id=1, source_target_pairs={{0,1},{1,0},{2,3},{3,2},{4,5},{5,4},{6,7},{7,6},{8,9},{9,8},{10,11... | collective-permute-start | bytes 393224 | tf_op jit(solution)/shard_map/ppermute | solution.py:182
  27.6 3.1 %collective-permute-start.11 = (bf16[128,512]{1,0:T(8,128)(2,1)S(1)}, bf16[128,512]{1,0:T(8,128)(2,1)S(1)}, u32[]{:S(2)}, u32[]{:S(2)}) collective-permute-start(bf16[128,512]{1,0:T(8,128)(2,1)S(1)} %collective-permute-done.9.refs_1_), channel_id=1, source_target_pairs={{0,1},{1,0},{2,3},{3,2},{4,5},{5,4},{6,7},{7,6},{8,9},{9,8},{10,11... | collective-permute-start | bytes 393224 | tf_op jit(solution)/shard_map/ppermute | solution.py:182
  30.5 5.0 %collective-permute-start.6 = (bf16[256,256]{1,0:T(8,128)(2,1)S(1)}, bf16[256,256]{1,0:T(8,128)(2,1)S(1)}, u32[]{:S(2)}, u32[]{:S(2)}) collective-permute-start(bf16[256,256]{1,0:T(8,128)(2,1)S(1)} %collective-permute-done.4.refs_1_), channel_id=1, source_target_pairs={{0,4},{1,5},{2,6},{3,7},{4,0},{5,1},{6,2},{7,3},{8,12},{9,13},{10,... | collective-permute-start | bytes 393224 | tf_op jit(solution)/shard_map/ppermute | solution.py:178

commit v10 on v9

--- a/solution.py
+++ b/solution.py
@@ -61,7 +61,7 @@
 
 
 def attention_kernel(
-    q_hbm, k_hbm, v_hbm, do_hbm, gk_ref, gv_ref, gq_hbm,
+    q_hbm, k_hbm, v_hbm, do_hbm, gk_ref, gv_ref, twice_ref, gq_hbm,
     q, k, v, do, probs_b, ds, gq, scores, grad_probs, sems, out_sems,
 ):
     length = q.shape[0]
@@ -103,6 +103,8 @@
         stored[g].start()
         grad_key = dot(ds[:, cols], stacked(q, g, per_group)) * scale
         gk_ref[:, head] = grad_key.astype(BF16)
+        twice_ref[:length, head] = grad_key.astype(BF16)
+        twice_ref[length:, head] = grad_key.astype(BF16)
         gv_ref[:, head] = dot(probs_b[:, cols], stacked(do, g, per_group)).astype(BF16)
     for copy in stored:
         copy.wait()
@@ -113,25 +115,28 @@
     chips = groups // 2
     member = lax.axis_index("mp")
     chip, core = lax.div(member, 2), lax.rem(member, 2)
-    blocks, stored = [], []
-    for b in range(groups):
+    step = min(CHUNK, features)
+    pieces = [(b, at) for b in range(groups) for at in range(0, features, step)]
+    loads, stored = [], []
+    for j, (b, at) in enumerate(pieces):
         column = core if b >= chips else 1 - core
-        start = (2 * lax.rem(chip + b + 1, chips) + column) * features
-        rows = pl.ds(pl.multiple_of(start, features), features)
-        blocks.append(pltpu.make_async_copy(p_hbm.at[:, rows, :], p.at[b], p_sems.at[b]))
-    for copy in blocks:
+        start = (2 * lax.rem(chip + b + 1, chips) + column) * features + at
+        rows = pl.ds(pl.multiple_of(start, step), step)
+        target = p.at[b, :, pl.ds(at, step), :]
+        loads.append(pltpu.make_async_copy(p_hbm.at[:, rows, :], target, p_sems.at[j]))
+    for copy in loads:
         copy.start()
     grads = jnp.concatenate([gk_ref[...], gv_ref[...]], axis=1)
-    step = min(CHUNK, features)
-    for b in range(groups):
-        blocks[b].wait()
-        for at in range(0, features, step):
-            rows = slice(at, at + step)
-            both = jnp.concatenate([p[b, 0, rows, :], p[b, 1, rows, :]], axis=1)
-            partial[b, :, rows] = dot(grads, both, NT).astype(BF16)
+    for j, (b, at) in enumerate(pieces):
+        loads[j].wait()
+        rows = slice(at, at + step)
+        both = jnp.concatenate([p[b, 0, rows, :], p[b, 1, rows, :]], axis=1)
+        partial[b, :, rows] = dot(grads, both, NT).astype(BF16)
         target = sent_hbm.at[b] if b < chips else kept_hbm.at[b - chips]
-        stored.append(pltpu.make_async_copy(partial.at[b], target, out_sems.at[b]))
-        stored[-1].start()
+        cols = pl.ds(at, step)
+        copy = pltpu.make_async_copy(partial.at[b, :, cols], target.at[:, cols], out_sems.at[j])
+        copy.start()
+        stored.append(copy)
     for copy in stored:
         copy.wait()
 
@@ -161,12 +166,20 @@
 
 
 def weights_kernel(x_ref, *refs):
-    keys, out_ref = refs[:-1], refs[-1]
+    *keys, out_hbm, out, sems = refs
     rows = keys[0].shape[0]
-    total = dot(x_ref[:, :rows], keys[0][...])
-    for j in range(1, len(keys)):
-        total += dot(x_ref[:, j * rows : (j + 1) * rows], keys[j][...])
-    out_ref[...] = total * (1.0 / (2 * len(keys)))
+    half = x_ref.shape[0] // 2
+    copies = []
+    for h in range(2):
+        part = slice(h * half, (h + 1) * half)
+        total = dot(x_ref[part, :rows], keys[0][...])
+        for j in range(1, len(keys)):
+            total += dot(x_ref[part, j * rows : (j + 1) * rows], keys[j][...])
+        out[part, :] = total * (1.0 / (2 * len(keys)))
+        copies.append(pltpu.make_async_copy(out.at[part, :], out_hbm.at[part, :], sems.at[h]))
+        copies[h].start()
+    for copy in copies:
+        copy.wait()
 
 
 def along_dp(array, partner, parts, groups):
@@ -225,8 +238,9 @@
     width, columns = turned.shape[0], keys[0].shape[1]
     return pl.pallas_call(
         weights_kernel,
-        out_specs=IN_VMEM,
+        out_specs=ANYWHERE,
         out_shape=jax.ShapeDtypeStruct((width, columns), F32),
+        scratch_shapes=[pltpu.VMEM((width, columns), F32), pltpu.SemaphoreType.DMA((2,))],
         compiler_params=PARAMS,
         cost_estimate=cost(
             2 * turned.size * columns, 2 * turned.size + 4 * width * columns
@@ -259,13 +273,14 @@
     whole = pltpu.VMEM((rows, query_width), BF16)
     narrow = pltpu.VMEM((rows, width), BF16)
     wide = pltpu.VMEM((kv_heads, rows, query_width // kv_heads), F32)
-    grad_key, grad_value, grad_query = pl.pallas_call(
+    grad_key, grad_value, twice, grad_query = pl.pallas_call(
         attention_kernel,
         in_specs=[IN_HBM] * 4,
-        out_specs=[IN_VMEM, IN_VMEM, ANYWHERE],
+        out_specs=[IN_VMEM, IN_VMEM, IN_VMEM, ANYWHERE],
         out_shape=(
             jax.ShapeDtypeStruct((rows, width), BF16),
             jax.ShapeDtypeStruct((rows, width), BF16),
+            jax.ShapeDtypeStruct((2 * rows, width), BF16),
             jax.ShapeDtypeStruct((rows, query_width), BF16),
         ),
         scratch_shapes=[whole, narrow, narrow, whole, whole, whole, whole, wide, wide]
@@ -276,6 +291,7 @@
         ),
     )(query_states, key_states, value_states, grad_context)
 
+    copies = groups * (features // min(CHUNK, features))
     sent, kept = pl.pallas_call(
         partials_kernel,
         in_specs=[IN_VMEM, IN_VMEM, IN_HBM],
@@ -284,8 +300,8 @@
         scratch_shapes=[
             pltpu.VMEM((groups, 2, features, width), BF16),
             pltpu.VMEM((groups, rows, features), BF16),
-            pltpu.SemaphoreType.DMA((groups,)),
-            pltpu.SemaphoreType.DMA((groups,)),
+            pltpu.SemaphoreType.DMA((copies,)),
+            pltpu.SemaphoreType.DMA((copies,)),
         ],
         compiler_params=WHOLE,
         cost_estimate=cost(
@@ -296,19 +312,20 @@
     if exchange:
         ready, near = lax.optimization_barrier((grad_key, near))
         first = along_dp(ready, lambda m: parts // 2, parts, groups)
-        twice = jnp.concatenate([grad_key, grad_key])
         first, twice, sent, kept, distant, near, next_inputs = lax.optimization_barrier(
             (first, twice, sent, kept, distant, near, next_inputs)
         )
         pieces = shared_inputs(distant, groups)
         keys = {0: lax.dynamic_update_slice(twice, first, (rows, 0))}
-        mine = pieces + near
-        theirs = [along_mp(piece, 1, groups) for piece in mine]
         bit = parts // 4
         while bit > 1:
             for k in list(keys):
                 keys[k ^ bit] = along_dp(keys[k], lambda m, bit=bit: bit, parts, groups)
             bit //= 2
+        beside = [along_dp(keys[0], lambda m: 1, parts, groups)]
+        pieces[1:], _ = lax.optimization_barrier((pieces[1:], (beside, keys)))
+        mine = pieces + near
+        theirs = [along_mp(piece, 1, groups) for piece in mine]
     came = along_mp(sent, 1, groups)
     total = kept.astype(F32) + came.astype(F32)
     grad_input = total[chips - 1]
@@ -318,10 +335,7 @@
     grad_input = grad_input.astype(BF16)
 
     if exchange:
-        beside = []
-        for k in range(0, parts // 2, 2):
-            if k:
-                keys[k], beside = lax.optimization_barrier((keys[k], beside))
+        for k in range(2, parts // 2, 2):
             beside.append(along_dp(keys[k], lambda m: 1, parts, groups))
         turned = turned_inputs(mine, theirs, next_inputs, inputs_normed)
         beside[-1], grad_input = lax.optimization_barrier((beside[-1], grad_input))

time: 37 us -> 35.1 us (0.949)
  waiting for transfers between devices: 8.2 us -> 5.78 us
  starting transfers between devices: 13.2 us -> 14.2 us
  other arithmetic: 2.89 us -> 1.97 us
  Pallas kernels: 10.5 us -> 11 us
    ppermute x7, waiting for transfers between devices: 4.52 us -> 1.05 us  [along_dp(): return lax.ppermute(array, ('dp', 'mp'), pairs)]
    ppermute x7, starting transfers between devices: 9.88 us -> 11.9 us  [along_dp(): return lax.ppermute(array, ('dp', 'mp'), pairs)]
    ppermute x5, starting transfers between devices: 3.24 us -> 1.85 us  [along_mp(): return lax.ppermute(array, 'mp', [(m, m ^ bit) for m in range(groups)])]
    ppermute x1, waiting for transfers between devices: 1.96 us -> 3.06 us  [body(): grad_input += lax.ppermute(total[b].astype(BF16), 'mp', shift).astype(F32)]
    concatenate x1 -> x0, other arithmetic: 0.92 us -> none  [body(): twice = jnp.concatenate([grad_key, grad_key])]
    pallas_call x1, Pallas kernels: 4.77 us -> 5.23 us  [body(): pl.pallas_call(partials_kernel, in_specs=[IN_VMEM, IN_VMEM, IN_HBM], out_...]
  transfers between devices with their start and end apart: 13 -> 13, of which waited for: 5 -> 4; matrix products, arithmetic and copies ran while one was open for 8% -> 6% of each run, Pallas kernels for 25% -> 28%
where the time goes in v10:
time: 35.1 us; the launch traced here: 34.8 us
  starting transfers between devices  14.2 us (40%)
  Pallas kernels  11 us (31%)
  waiting for transfers between devices  5.78 us (16%)
  other arithmetic  1.97 us (6%)
  local copies, waits for them, and re-layouts  1.12 us (3%)
  between operations  0.76 us (2%)
    ppermute x7, starting transfers between devices, along_dp(): return lax.ppermute(array, ('dp', 'mp'), pairs)  11.9 us
    pallas_call x1, Pallas kernels, body(): pl.pallas_call(partials_kernel, in_specs=[IN_VMEM, IN_VMEM, IN_HBM], out_...  5.23 us
    pallas_call x1, Pallas kernels, body(): pl.pallas_call(attention_kernel, in_specs=[IN_HBM] * 4, out_specs=[IN_VME...  4.1 us
    ppermute x1, waiting for transfers between devices, body(): grad_input += lax.ppermute(total[b].astype(BF16), 'mp', shift).astype(F32)  3.06 us
    ppermute x5, starting transfers between devices, along_mp(): return lax.ppermute(array, 'mp', [(m, m ^ bit) for m in range(groups)])  1.85 us
    ppermute x5, waiting for transfers between devices, along_mp(): return lax.ppermute(array, 'mp', [(m, m ^ bit) for m in range(groups)])  1.67 us
    pallas_call x1, Pallas kernels, summed_weights(): pl.pallas_call(weights_kernel, out_specs=ANYWHERE, out_shape=jax.ShapeDty...  1.24 us
    add x1, other arithmetic, body(): total = kept.astype(F32) + came.astype(F32)  1.21 us
  transfers between devices with their start and end apart: 13, of which 4 were waited for; matrix products, arithmetic and copies ran while one was open for 6% of the time, Pallas kernels for 28%

profile of v10, /device:TPU:0, one launch (start us, length us, event | category | flops | bytes accessed | tf_op | source)
XLA Modules:
  0.0 34.8 jit_solution(6251069910743038154)
XLA Ops:
  0.7 1.1 %constant_dynamic-slice_fusion = (bf16[128,512]{1,0:T(8,128)(2,1)S(1)}, bf16[128,512]{1,0:T(8,128)(2,1)S(1)}, bf16[128,512]{1,0:T(8,128)(2,1)S(1)}) fusion(bf16[128,4096]{1,0:T(8,128)(2,1)} %refs_7_.1, s32[]{:T(128)S(6)} %select_n.11, s32[]{:T(128)S(6)} %select_n.10, s32[]{:T(128)S(6)} %select_n.9), kind=kLoop, calls=%fused_computation.7 | loop fusion | bytes 786444 | tf_op jit(solution)/shard_map/dynamic_slice | solution.py:204
  1.7 0.0 copy-start
  1.7 3.1 %collective-permute-start = (bf16[128,512]{1,0:T(8,128)(2,1)S(1)}, bf16[128,512]{1,0:T(8,128)(2,1)S(1)}, u32[]{:S(2)}, u32[]{:S(2)}) collective-permute-start(bf16[128,512]{1,0:T(8,128)(2,1)S(1)} %get-tuple-element.41), channel_id=1, source_target_pairs={{0,8},{1,13},{2,10},{3,15},{4,12},{5,9},{6,14},{7,11},{8,0},{9,5},... | collective-permute-start | bytes 393224 | tf_op jit(solution)/shard_map/ppermute | solution.py:191
  4.8 2.6 %collective-permute-start.2 = (bf16[128,512]{1,0:T(8,128)(2,1)S(1)}, bf16[128,512]{1,0:T(8,128)(2,1)S(1)}, u32[]{:S(2)}, u32[]{:S(2)}) collective-permute-start(bf16[128,512]{1,0:T(8,128)(2,1)S(1)} %get-tuple-element.40), channel_id=1, source_target_pairs={{0,16},{1,21},{2,26},{3,31},{4,20},{5,17},{6,30},{7,27},{8,24},{9,... | collective-permute-start | bytes 393224 | tf_op jit(solution)/shard_map/ppermute | solution.py:191
  7.4 1.5 %collective-permute-start.3 = (bf16[128,512]{1,0:T(8,128)(2,1)S(1)}, bf16[128,512]{1,0:T(8,128)(2,1)S(1)}, u32[]{:S(2)}, u32[]{:S(2)}) collective-permute-start(bf16[128,512]{1,0:T(8,128)(2,1)S(1)} %get-tuple-element.39), channel_id=1, source_target_pairs={{0,4},{1,5},{2,6},{3,7},{4,0},{5,1},{6,2},{7,3},{8,12},{9,13},{10,... | collective-permute-start | bytes 393224 | tf_op jit(solution)/shard_map/ppermute | solution.py:191
  8.9 4.1 %shard_map.85 = (bf16[128,256]{1,0:T(8,128)(2,1)}, bf16[128,256]{1,0:T(8,128)(2,1)}, bf16[256,256]{1,0:T(8,128)(2,1)}, bf16[128,2048]{1,0:T(8,128)(2,1)}) custom-call(bf16[128,2048]{1,0:T(8,128)(2,1)} %q_hbm.1, bf16[128,256]{1,0:T(8,128)(2,1)} %k_hbm.1, bf16[128,256]{1,0:T(8,128)(2,1)} %v_hbm.1, bf16[128,2048]{1,0:T(8,128)(2,1)} %do_hbm.1), custom_call_target="tpu_custom_call" | custom-call | flops 335544320 | bytes 1572864 | tf_op jit(solution)/shard_map/pallas_call | solution.py:276
  13.0 0.0 copy-start.1
  13.0 0.4 %collective-permute-start.1 = (bf16[128,256]{1,0:T(8,128)(2,1)}, bf16[128,256]{1,0:T(8,128)(2,1)S(1)}, u32[]{:S(2)}, u32[]{:S(2)}) collective-permute-start(bf16[128,256]{1,0:T(8,128)(2,1)} %get-tuple-element.23.gk_ref), channel_id=1, source_target_pairs={{0,16},{1,17},{2,18},{3,19},{4,20},{5,21},{6,22},{7,23},{8,24},{9,... | collective-permute-start | bytes 196616 | tf_op jit(solution)/shard_map/ppermute | solution.py:191
  13.4 5.2 %shard_map.86 = (bf16[2,128,1024]{2,1,0:T(8,128)(2,1)}, bf16[2,128,1024]{2,1,0:T(8,128)(2,1)}) custom-call(bf16[128,256]{1,0:T(8,128)(2,1)} %get-tuple-element.23.gk_ref, bf16[128,256]{1,0:T(8,128)(2,1)} %get-tuple-element.25.gv_ref, bf16[2,4096,256]{2,1,0:T(8,128)(2,1)} %p_hbm.1), custom_call_target="tpu_custom_call" | custom-call | flops 536870912 | bytes 4194304 | tf_op jit(solution)/shard_map/pallas_call | solution.py:295
  18.7 0.0 collective-permute-done.3.refs_6_
  18.7 0.7 %collective-permute-done.1 = bf16[128,256]{1,0:T(8,128)(2,1)S(1)} collective-permute-done((bf16[128,256]{1,0:T(8,128)(2,1)}, bf16[128,256]{1,0:T(8,128)(2,1)S(1)}, u32[]{:S(2)}, u32[]{:S(2)}) %collective-permute-start.1) | collective-permute-done | bytes 65568 | tf_op jit(solution)/shard_map/ppermute | solution.py:191
  19.4 1.2 %collective-permute-start.4 = (bf16[256,256]{1,0:T(8,128)(2,1)S(1)}, bf16[256,256]{1,0:T(8,128)(2,1)S(1)}, u32[]{:S(2)}, u32[]{:S(2)}) collective-permute-start(bf16[256,256]{1,0:T(8,128)(2,1)S(1)} %constant_dynamic-update-slice_fusion.refs_0_), channel_id=1, source_target_pairs={{0,8},{1,9},{2,10},{3,11},{4,12},{5,13},{6,14},{7,15},{8,0},{9,1},... | collective-permute-start | bytes 393224 | tf_op jit(solution)/shard_map/ppermute | solution.py:191
  20.6 1.1 %collective-permute-start.9 = (bf16[256,256]{1,0:T(8,128)(2,1)S(1)}, bf16[256,256]{1,0:T(8,128)(2,1)S(1)}, u32[]{:S(2)}, u32[]{:S(2)}) collective-permute-start(bf16[256,256]{1,0:T(8,128)(2,1)S(1)} %constant_dynamic-update-slice_fusion.refs_0_), channel_id=1, source_target_pairs={{0,4},{1,5},{2,6},{3,7},{4,0},{5,1},{6,2},{7,3},{8,12},{9,13},{10,... | collective-permute-start | bytes 393224 | tf_op jit(solution)/shard_map/ppermute | solution.py:191
  21.7 1.7 %collective-permute-start.8 = (bf16[128,512]{1,0:T(8,128)(2,1)S(1)}, bf16[128,512]{1,0:T(8,128)(2,1)S(1)}, u32[]{:S(2)}, u32[]{:S(2)}) collective-permute-start(bf16[128,512]{1,0:T(8,128)(2,1)S(1)} %collective-permute-done.2.refs_0_), channel_id=1, source_target_pairs={{0,2},{1,3},{2,0},{3,1},{4,6},{5,7},{6,4},{7,5},{8,10},{9,11},{10,... | collective-permute-start | bytes 393224 | tf_op jit(solution)/shard_map/ppermute | solution.py:195
  23.3 1.2 %convert_add_fusion = f32[2,128,1024]{2,1,0:T(8,128)S(1)} fusion(bf16[2,128,1024]{2,1,0:T(8,128)(2,1)S(1)} %collective-permute-done.6, bf16[2,128,1024]{2,1,0:T(8,128)(2,1)} %get-tuple-element.31), kind=kLoop, calls=%fused_computation | loop fusion | flops 786432 | bytes 2097152 | tf_op jit(solution)/shard_map/add | solution.py:330
  24.6 0.4 %collective-permute-start.7 = (bf16[128,1024]{1,0:T(8,128)(2,1)S(1)}, bf16[128,1024]{1,0:T(8,128)(2,1)S(1)}, u32[]{:S(2)}, u32[]{:S(2)}) collective-permute-start(bf16[128,1024]{1,0:T(8,128)(2,1)S(1)} %fusion.2), channel_id=1, source_target_pairs={{0,2},{1,3},{2,0},{3,1},{4,6},{5,7},{6,4},{7,5},{8,10},{9,11},{10,... | collective-permute-start | bytes 786440 | tf_op jit(solution)/shard_map/ppermute | solution.py:334
  25.0 0.3 collective-permute-done.4.refs_1_
  25.4 0.2 collective-permute-start.12
  25.5 1.7 %collective-permute-done.8.refs_1_ = bf16[128,512]{1,0:T(8,128)(2,1)S(1)} collective-permute-done((bf16[128,512]{1,0:T(8,128)(2,1)S(1)}, bf16[128,512]{1,0:T(8,128)(2,1)S(1)}, u32[]{:S(2)}, u32[]{:S(2)}) %collective-permute-start.8) | collective-permute-done | bytes 131104 | tf_op jit(solution)/shard_map/ppermute | solution.py:195
  27.2 2.1 %collective-permute-start.5 = (bf16[256,256]{1,0:T(8,128)(2,1)S(1)}, bf16[256,256]{1,0:T(8,128)(2,1)S(1)}, u32[]{:S(2)}, u32[]{:S(2)}) collective-permute-start(bf16[256,256]{1,0:T(8,128)(2,1)S(1)} %collective-permute-done.4.refs_1_), channel_id=1, source_target_pairs={{0,4},{1,5},{2,6},{3,7},{4,0},{5,1},{6,2},{7,3},{8,12},{9,13},{10,... | collective-permute-start | bytes 393224 | tf_op jit(solution)/shard_map/ppermute | solution.py:191
  29.3 0.5 %shard_map.87.x_ref = bf16[512,1024]{1,0:T(8,128)(2,1)S(1)} custom-call(bf16[128,512]{1,0:T(8,128)(2,1)S(1)} %collective-permute-done.2.refs_0_, bf16[128,512]{1,0:T(8,128)(2,1)S(1)} %collective-permute-done.8.refs_1_, bf16[128,512]{1,0:T(8,128)(2,1)S(1)} %collective-permute-done.refs_2_, bf16[128,512]{1,0:T(8,128)(2,1)S(1)} %collective-permute-done.10.refs_3_, ...), custom_call_target="tpu_custom_call" | custom-call | bytes 2097152 | tf_op jit(solution)/shard_map/pallas_call | solution.py:226
  29.8 3.1 %collective-permute-done.7 = bf16[128,1024]{1,0:T(8,128)(2,1)S(1)} collective-permute-done((bf16[128,1024]{1,0:T(8,128)(2,1)S(1)}, bf16[128,1024]{1,0:T(8,128)(2,1)S(1)}, u32[]{:S(2)}, u32[]{:S(2)}) %collective-permute-start.7) | collective-permute-done | bytes 262176 | tf_op jit(solution)/shard_map/ppermute | solution.py:334
  32.8 0.8 %fusion.1 = bf16[128,1024]{1,0:T(8,128)(2,1)} fusion(f32[2,128,1024]{2,1,0:T(8,128)S(1)} %convert_add_fusion, bf16[128,1024]{1,0:T(8,128)(2,1)S(1)} %collective-permute-done.7), kind=kLoop, calls=%fused_computation.4 | loop fusion | flops 393216 | bytes 1048576 | tf_op jit(solution)/shard_map/convert_element_type | solution.py:335
  33.6 1.2 %shard_map.88 = f32[512,256]{1,0:T(8,128)} custom-call(bf16[512,1024]{1,0:T(8,128)(2,1)S(1)} %shard_map.87.x_ref, bf16[256,256]{1,0:T(8,128)(2,1)S(1)} %constant_dynamic-update-slice_fusion.refs_0_, bf16[256,256]{1,0:T(8,128)(2,1)S(1)} %collective-permute-done.4.refs_1_, bf16[256,256]{1,0:T(8,128)(2,1)S(1)} %collective-permute-done.9.refs_2_, ...), custom_call_target="tpu_custom_call" | custom-call | flops 268435456 | bytes 1572864 | tf_op jit(solution)/shard_map/pallas_call | solution.py:239
  (15 shorter events, 0.1 us)
Async XLA Ops:
  1.7 27.6 %copy-start = (bf16[128,4096]{1,0:T(8,128)(2,1)S(1)}, bf16[128,4096]{1,0:T(8,128)(2,1)}, u32[]{:S(2)}) copy-start(bf16[128,4096]{1,0:T(8,128)(2,1)} %refs_7_.1) | copy-start | bytes 3145732
  1.7 11.3 %collective-permute-start = (bf16[128,512]{1,0:T(8,128)(2,1)S(1)}, bf16[128,512]{1,0:T(8,128)(2,1)S(1)}, u32[]{:S(2)}, u32[]{:S(2)}) collective-permute-start(bf16[128,512]{1,0:T(8,128)(2,1)S(1)} %get-tuple-element.41), channel_id=1, source_target_pairs={{0,8},{1,13},{2,10},{3,15},{4,12},{5,9},{6,14},{7,11},{8,0},{9,5},... | collective-permute-start | bytes 393224 | tf_op jit(solution)/shard_map/ppermute | solution.py:191
  4.8 13.8 %collective-permute-start.2 = (bf16[128,512]{1,0:T(8,128)(2,1)S(1)}, bf16[128,512]{1,0:T(8,128)(2,1)S(1)}, u32[]{:S(2)}, u32[]{:S(2)}) collective-permute-start(bf16[128,512]{1,0:T(8,128)(2,1)S(1)} %get-tuple-element.40), channel_id=1, source_target_pairs={{0,16},{1,21},{2,26},{3,31},{4,20},{5,17},{6,30},{7,27},{8,24},{9,... | collective-permute-start | bytes 393224 | tf_op jit(solution)/shard_map/ppermute | solution.py:191
  7.4 11.3 %collective-permute-start.3 = (bf16[128,512]{1,0:T(8,128)(2,1)S(1)}, bf16[128,512]{1,0:T(8,128)(2,1)S(1)}, u32[]{:S(2)}, u32[]{:S(2)}) collective-permute-start(bf16[128,512]{1,0:T(8,128)(2,1)S(1)} %get-tuple-element.39), channel_id=1, source_target_pairs={{0,4},{1,5},{2,6},{3,7},{4,0},{5,1},{6,2},{7,3},{8,12},{9,13},{10,... | collective-permute-start | bytes 393224 | tf_op jit(solution)/shard_map/ppermute | solution.py:191
  13.0 6.4 %copy-start.1 = (bf16[256,256]{1,0:T(8,128)(2,1)S(1)}, bf16[256,256]{1,0:T(8,128)(2,1)}, u32[]{:S(2)}) copy-start(bf16[256,256]{1,0:T(8,128)(2,1)} %get-tuple-element.29) | copy-start | bytes 393220
  13.0 6.4 %collective-permute-start.1 = (bf16[128,256]{1,0:T(8,128)(2,1)}, bf16[128,256]{1,0:T(8,128)(2,1)S(1)}, u32[]{:S(2)}, u32[]{:S(2)}) collective-permute-start(bf16[128,256]{1,0:T(8,128)(2,1)} %get-tuple-element.23.gk_ref), channel_id=1, source_target_pairs={{0,16},{1,17},{2,18},{3,19},{4,20},{5,21},{6,22},{7,23},{8,24},{9,... | collective-permute-start | bytes 196616 | tf_op jit(solution)/shard_map/ppermute | solution.py:191
  19.4 4.0 %collective-permute-start.6 = (bf16[2,128,1024]{2,1,0:T(8,128)(2,1)}, bf16[2,128,1024]{2,1,0:T(8,128)(2,1)S(1)}, u32[]{:S(2)}, u32[]{:S(2)}) collective-permute-start(bf16[2,128,1024]{2,1,0:T(8,128)(2,1)} %get-tuple-element.32), channel_id=1, source_target_pairs={{0,1},{1,0},{2,3},{3,2},{4,5},{5,4},{6,7},{7,6},{8,9},{9,8},{10,11... | collective-permute-start | bytes 1572872 | tf_op jit(solution)/shard_map/ppermute | solution.py:195
  19.4 6.0 %collective-permute-start.4 = (bf16[256,256]{1,0:T(8,128)(2,1)S(1)}, bf16[256,256]{1,0:T(8,128)(2,1)S(1)}, u32[]{:S(2)}, u32[]{:S(2)}) collective-permute-start(bf16[256,256]{1,0:T(8,128)(2,1)S(1)} %constant_dynamic-update-slice_fusion.refs_0_), channel_id=1, source_target_pairs={{0,8},{1,9},{2,10},{3,11},{4,12},{5,13},{6,14},{7,15},{8,0},{9,1},... | collective-permute-start | bytes 393224 | tf_op jit(solution)/shard_map/ppermute | solution.py:191
  20.6 6.6 %collective-permute-start.9 = (bf16[256,256]{1,0:T(8,128)(2,1)S(1)}, bf16[256,256]{1,0:T(8,128)(2,1)S(1)}, u32[]{:S(2)}, u32[]{:S(2)}) collective-permute-start(bf16[256,256]{1,0:T(8,128)(2,1)S(1)} %constant_dynamic-update-slice_fusion.refs_0_), channel_id=1, source_target_pairs={{0,4},{1,5},{2,6},{3,7},{4,0},{5,1},{6,2},{7,3},{8,12},{9,13},{10,... | collective-permute-start | bytes 393224 | tf_op jit(solution)/shard_map/ppermute | solution.py:191
  21.7 5.5 %collective-permute-start.8 = (bf16[128,512]{1,0:T(8,128)(2,1)S(1)}, bf16[128,512]{1,0:T(8,128)(2,1)S(1)}, u32[]{:S(2)}, u32[]{:S(2)}) collective-permute-start(bf16[128,512]{1,0:T(8,128)(2,1)S(1)} %collective-permute-done.2.refs_0_), channel_id=1, source_target_pairs={{0,2},{1,3},{2,0},{3,1},{4,6},{5,7},{6,4},{7,5},{8,10},{9,11},{10,... | collective-permute-start | bytes 393224 | tf_op jit(solution)/shard_map/ppermute | solution.py:195
  24.6 8.2 %collective-permute-start.7 = (bf16[128,1024]{1,0:T(8,128)(2,1)S(1)}, bf16[128,1024]{1,0:T(8,128)(2,1)S(1)}, u32[]{:S(2)}, u32[]{:S(2)}) collective-permute-start(bf16[128,1024]{1,0:T(8,128)(2,1)S(1)} %fusion.2), channel_id=1, source_target_pairs={{0,2},{1,3},{2,0},{3,1},{4,6},{5,7},{6,4},{7,5},{8,10},{9,11},{10,... | collective-permute-start | bytes 786440 | tf_op jit(solution)/shard_map/ppermute | solution.py:334
  25.0 4.2 %collective-permute-start.10 = (bf16[128,512]{1,0:T(8,128)(2,1)S(1)}, bf16[128,512]{1,0:T(8,128)(2,1)S(1)}, u32[]{:S(2)}, u32[]{:S(2)}) collective-permute-start(bf16[128,512]{1,0:T(8,128)(2,1)S(1)} %collective-permute-done.2.refs_0_), channel_id=1, source_target_pairs={{0,1},{1,0},{2,3},{3,2},{4,5},{5,4},{6,7},{7,6},{8,9},{9,8},{10,11... | collective-permute-start | bytes 393224 | tf_op jit(solution)/shard_map/ppermute | solution.py:195
  25.4 3.9 %collective-permute-start.12 = (bf16[128,512]{1,0:T(8,128)(2,1)S(1)}, bf16[128,512]{1,0:T(8,128)(2,1)S(1)}, u32[]{:S(2)}, u32[]{:S(2)}) collective-permute-start(bf16[128,512]{1,0:T(8,128)(2,1)S(1)} %collective-permute-done.refs_2_), channel_id=1, source_target_pairs={{0,1},{1,0},{2,3},{3,2},{4,5},{5,4},{6,7},{7,6},{8,9},{9,8},{10,11... | collective-permute-start | bytes 393224 | tf_op jit(solution)/shard_map/ppermute | solution.py:195
  27.2 2.1 %collective-permute-start.11 = (bf16[128,512]{1,0:T(8,128)(2,1)S(1)}, bf16[128,512]{1,0:T(8,128)(2,1)S(1)}, u32[]{:S(2)}, u32[]{:S(2)}) collective-permute-start(bf16[128,512]{1,0:T(8,128)(2,1)S(1)} %collective-permute-done.8.refs_1_), channel_id=1, source_target_pairs={{0,1},{1,0},{2,3},{3,2},{4,5},{5,4},{6,7},{7,6},{8,9},{9,8},{10,11... | collective-permute-start | bytes 393224 | tf_op jit(solution)/shard_map/ppermute | solution.py:195
  27.2 6.4 %collective-permute-start.5 = (bf16[256,256]{1,0:T(8,128)(2,1)S(1)}, bf16[256,256]{1,0:T(8,128)(2,1)S(1)}, u32[]{:S(2)}, u32[]{:S(2)}) collective-permute-start(bf16[256,256]{1,0:T(8,128)(2,1)S(1)} %collective-permute-done.4.refs_1_), channel_id=1, source_target_pairs={{0,4},{1,5},{2,6},{3,7},{4,0},{5,1},{6,2},{7,3},{8,12},{9,13},{10,... | collective-permute-start | bytes 393224 | tf_op jit(solution)/shard_map/ppermute | solution.py:191

commit v11 on v10

--- a/solution.py
+++ b/solution.py
@@ -110,7 +110,9 @@
         copy.wait()
 
 
-def partials_kernel(gk_ref, gv_ref, p_hbm, sent_hbm, kept_hbm, p, partial, p_sems, out_sems):
+def partials_kernel(
+    gk_hbm, gv_hbm, p_hbm, sent_hbm, kept_hbm, grads, p, partial, sems, p_sems, out_sems,
+):
     groups, features = p.shape[0], p.shape[2]
     chips = groups // 2
     member = lax.axis_index("mp")
@@ -124,14 +126,21 @@
         rows = pl.ds(pl.multiple_of(start, step), step)
         target = p.at[b, :, pl.ds(at, step), :]
         loads.append(pltpu.make_async_copy(p_hbm.at[:, rows, :], target, p_sems.at[j]))
-    for copy in loads:
+    width = p.shape[3]
+    small = [
+        pltpu.make_async_copy(gk_hbm, grads.at[:, pl.ds(0, width)], sems.at[0]),
+        pltpu.make_async_copy(gv_hbm, grads.at[:, pl.ds(width, width)], sems.at[1]),
+    ]
+    for copy in small + loads:
         copy.start()
-    grads = jnp.concatenate([gk_ref[...], gv_ref[...]], axis=1)
+    for copy in small:
+        copy.wait()
+    both_grads = grads[...]
     for j, (b, at) in enumerate(pieces):
         loads[j].wait()
         rows = slice(at, at + step)
         both = jnp.concatenate([p[b, 0, rows, :], p[b, 1, rows, :]], axis=1)
-        partial[b, :, rows] = dot(grads, both, NT).astype(BF16)
+        partial[b, :, rows] = dot(both_grads, both, NT).astype(BF16)
         target = sent_hbm.at[b] if b < chips else kept_hbm.at[b - chips]
         cols = pl.ds(at, step)
         copy = pltpu.make_async_copy(partial.at[b, :, cols], target.at[:, cols], out_sems.at[j])
@@ -294,12 +303,14 @@
     copies = groups * (features // min(CHUNK, features))
     sent, kept = pl.pallas_call(
         partials_kernel,
-        in_specs=[IN_VMEM, IN_VMEM, IN_HBM],
+        in_specs=[IN_HBM] * 3,
         out_specs=[ANYWHERE, ANYWHERE],
         out_shape=(partial, partial),
         scratch_shapes=[
+            pltpu.VMEM((rows, 2 * width), BF16),
             pltpu.VMEM((groups, 2, features, width), BF16),
             pltpu.VMEM((groups, rows, features), BF16),
+            pltpu.SemaphoreType.DMA((2,)),
             pltpu.SemaphoreType.DMA((copies,)),
             pltpu.SemaphoreType.DMA((copies,)),
         ],
@@ -327,11 +338,11 @@
         mine = pieces + near
         theirs = [along_mp(piece, 1, groups) for piece in mine]
     came = along_mp(sent, 1, groups)
-    total = kept.astype(F32) + came.astype(F32)
-    grad_input = total[chips - 1]
+    pairs = (kept[: chips - 1].astype(F32) + came[: chips - 1].astype(F32)).astype(BF16)
+    grad_input = kept[chips - 1].astype(F32) + came[chips - 1].astype(F32)
     for b in range(chips - 1):
         shift = [(m, (m + 2 * (b + 1)) % groups) for m in range(groups)]
-        grad_input += lax.ppermute(total[b].astype(BF16), "mp", shift).astype(F32)
+        grad_input += lax.ppermute(pairs[b], "mp", shift).astype(F32)
     grad_input = grad_input.astype(BF16)
 
     if exchange:

time: 35.1 us -> 36.2 us (1.031)
  other arithmetic: 1.97 us -> 2.8 us
  waiting for transfers between devices: 5.78 us -> 6.32 us
    add x1 -> x0, other arithmetic: 1.21 us -> none  [body(): total = kept.astype(F32) + came.astype(F32)]
    convert_element_type x1, other arithmetic: 0.76 us -> 1.78 us  [body(): grad_input = grad_input.astype(BF16)]
    squeeze x0 -> x1, other arithmetic: none -> 1.02 us  [body(): grad_input += lax.ppermute(pairs[b], 'mp', shift).astype(F32)]
    ppermute x5, waiting for transfers between devices: 1.67 us -> 2.09 us  [along_mp(): return lax.ppermute(array, 'mp', [(m, m ^ bit) for m in range(groups)])]
  transfers between devices with their start and end apart: 13 -> 13, of which waited for: 4 -> 4; matrix products, arithmetic and copies ran while one was open for 6% -> 8% of each run, Pallas kernels for 28% -> 27%
where the time goes in v11:
time: 36.2 us; the launch traced here: 36 us
  starting transfers between devices  13.9 us (38%)
  Pallas kernels  11.1 us (31%)
  waiting for transfers between devices  6.32 us (17%)
  other arithmetic  2.8 us (8%)
  local copies, waits for them, and re-layouts  1.16 us (3%)
  between operations  0.75 us (2%)
    ppermute x7, starting transfers between devices, along_dp(): return lax.ppermute(array, ('dp', 'mp'), pairs)  11.8 us
    pallas_call x1, Pallas kernels, body(): pl.pallas_call(partials_kernel, in_specs=[IN_HBM] * 3, out_specs=[ANYWHER...  5.29 us
    pallas_call x1, Pallas kernels, body(): pl.pallas_call(attention_kernel, in_specs=[IN_HBM] * 4, out_specs=[IN_VME...  4.09 us
    ppermute x1, waiting for transfers between devices, body(): grad_input += lax.ppermute(pairs[b], 'mp', shift).astype(F32)  3.06 us
    ppermute x5, waiting for transfers between devices, along_mp(): return lax.ppermute(array, 'mp', [(m, m ^ bit) for m in range(groups)])  2.09 us
    convert_element_type x1, other arithmetic, body(): grad_input = grad_input.astype(BF16)  1.78 us
    ppermute x5, starting transfers between devices, along_mp(): return lax.ppermute(array, 'mp', [(m, m ^ bit) for m in range(groups)])  1.68 us
    pallas_call x1, Pallas kernels, summed_weights(): pl.pallas_call(weights_kernel, out_specs=ANYWHERE, out_shape=jax.ShapeDty...  1.24 us
  transfers between devices with their start and end apart: 13, of which 4 were waited for; matrix products, arithmetic and copies ran while one was open for 8% of the time, Pallas kernels for 27%

profile of v11, /device:TPU:0, one launch (start us, length us, event | category | flops | bytes accessed | tf_op | source)
XLA Modules:
  0.0 36.0 jit_solution(9141260287975829246)
XLA Ops:
  0.7 1.1 %constant_dynamic-slice_fusion = (bf16[128,512]{1,0:T(8,128)(2,1)S(1)}, bf16[128,512]{1,0:T(8,128)(2,1)S(1)}, bf16[128,512]{1,0:T(8,128)(2,1)S(1)}) fusion(bf16[128,4096]{1,0:T(8,128)(2,1)} %refs_7_.1, s32[]{:T(128)S(6)} %select_n.11, s32[]{:T(128)S(6)} %select_n.10, s32[]{:T(128)S(6)} %select_n.9), kind=kLoop, calls=%fused_computation.5 | loop fusion | bytes 786444 | tf_op jit(solution)/shard_map/dynamic_slice | solution.py:213
  1.8 3.1 %collective-permute-start = (bf16[128,512]{1,0:T(8,128)(2,1)S(1)}, bf16[128,512]{1,0:T(8,128)(2,1)S(1)}, u32[]{:S(2)}, u32[]{:S(2)}) collective-permute-start(bf16[128,512]{1,0:T(8,128)(2,1)S(1)} %get-tuple-element.41), channel_id=1, source_target_pairs={{0,8},{1,13},{2,10},{3,15},{4,12},{5,9},{6,14},{7,11},{8,0},{9,5},... | collective-permute-start | bytes 393224 | tf_op jit(solution)/shard_map/ppermute | solution.py:200
  4.9 2.6 %collective-permute-start.2 = (bf16[128,512]{1,0:T(8,128)(2,1)S(1)}, bf16[128,512]{1,0:T(8,128)(2,1)S(1)}, u32[]{:S(2)}, u32[]{:S(2)}) collective-permute-start(bf16[128,512]{1,0:T(8,128)(2,1)S(1)} %get-tuple-element.40), channel_id=1, source_target_pairs={{0,16},{1,21},{2,26},{3,31},{4,20},{5,17},{6,30},{7,27},{8,24},{9,... | collective-permute-start | bytes 393224 | tf_op jit(solution)/shard_map/ppermute | solution.py:200
  7.5 1.5 %collective-permute-start.3 = (bf16[128,512]{1,0:T(8,128)(2,1)S(1)}, bf16[128,512]{1,0:T(8,128)(2,1)S(1)}, u32[]{:S(2)}, u32[]{:S(2)}) collective-permute-start(bf16[128,512]{1,0:T(8,128)(2,1)S(1)} %get-tuple-element.39), channel_id=1, source_target_pairs={{0,4},{1,5},{2,6},{3,7},{4,0},{5,1},{6,2},{7,3},{8,12},{9,13},{10,... | collective-permute-start | bytes 393224 | tf_op jit(solution)/shard_map/ppermute | solution.py:200
  9.0 4.1 %shard_map.85 = (bf16[128,256]{1,0:T(8,128)(2,1)}, bf16[128,256]{1,0:T(8,128)(2,1)}, bf16[256,256]{1,0:T(8,128)(2,1)}, bf16[128,2048]{1,0:T(8,128)(2,1)}) custom-call(bf16[128,2048]{1,0:T(8,128)(2,1)} %q_hbm.1, bf16[128,256]{1,0:T(8,128)(2,1)} %k_hbm.1, bf16[128,256]{1,0:T(8,128)(2,1)} %v_hbm.1, bf16[128,2048]{1,0:T(8,128)(2,1)} %do_hbm.1), custom_call_target="tpu_custom_call" | custom-call | flops 335544320 | bytes 1572864 | tf_op jit(solution)/shard_map/pallas_call | solution.py:285
  13.1 0.0 copy-start.1
  13.1 0.0 collective-permute-done.refs_2_
  13.1 0.4 %collective-permute-start.1 = (bf16[128,256]{1,0:T(8,128)(2,1)}, bf16[128,256]{1,0:T(8,128)(2,1)S(1)}, u32[]{:S(2)}, u32[]{:S(2)}) collective-permute-start(bf16[128,256]{1,0:T(8,128)(2,1)} %get-tuple-element.23.gk_hbm), channel_id=1, source_target_pairs={{0,16},{1,17},{2,18},{3,19},{4,20},{5,21},{6,22},{7,23},{8,24},{9,... | collective-permute-start | bytes 196616 | tf_op jit(solution)/shard_map/ppermute | solution.py:200
  13.5 5.3 %shard_map.86 = (bf16[2,128,1024]{2,1,0:T(8,128)(2,1)}, bf16[2,128,1024]{2,1,0:T(8,128)(2,1)}) custom-call(bf16[128,256]{1,0:T(8,128)(2,1)} %get-tuple-element.23.gk_hbm, bf16[128,256]{1,0:T(8,128)(2,1)} %get-tuple-element.25.gv_hbm, bf16[2,4096,256]{2,1,0:T(8,128)(2,1)} %p_hbm.1), custom_call_target="tpu_custom_call" | custom-call | flops 536870912 | bytes 4194304 | tf_op jit(solution)/shard_map/pallas_call | solution.py:304
  18.8 0.0 collective-permute-done.2.refs_0_
  18.8 0.6 %collective-permute-done.1 = bf16[128,256]{1,0:T(8,128)(2,1)S(1)} collective-permute-done((bf16[128,256]{1,0:T(8,128)(2,1)}, bf16[128,256]{1,0:T(8,128)(2,1)S(1)}, u32[]{:S(2)}, u32[]{:S(2)}) %collective-permute-start.1) | collective-permute-done | bytes 65568 | tf_op jit(solution)/shard_map/ppermute | solution.py:200
  19.5 0.0 collective-permute-start.6
  19.5 1.3 %collective-permute-start.4 = (bf16[256,256]{1,0:T(8,128)(2,1)S(1)}, bf16[256,256]{1,0:T(8,128)(2,1)S(1)}, u32[]{:S(2)}, u32[]{:S(2)}) collective-permute-start(bf16[256,256]{1,0:T(8,128)(2,1)S(1)} %constant_dynamic-update-slice_fusion.refs_0_), channel_id=1, source_target_pairs={{0,8},{1,9},{2,10},{3,11},{4,12},{5,13},{6,14},{7,15},{8,0},{9,1},... | collective-permute-start | bytes 393224 | tf_op jit(solution)/shard_map/ppermute | solution.py:200
  20.7 1.1 %collective-permute-start.9 = (bf16[256,256]{1,0:T(8,128)(2,1)S(1)}, bf16[256,256]{1,0:T(8,128)(2,1)S(1)}, u32[]{:S(2)}, u32[]{:S(2)}) collective-permute-start(bf16[256,256]{1,0:T(8,128)(2,1)S(1)} %constant_dynamic-update-slice_fusion.refs_0_), channel_id=1, source_target_pairs={{0,4},{1,5},{2,6},{3,7},{4,0},{5,1},{6,2},{7,3},{8,12},{9,13},{10,... | collective-permute-start | bytes 393224 | tf_op jit(solution)/shard_map/ppermute | solution.py:200
  21.8 1.7 %collective-permute-start.8 = (bf16[128,512]{1,0:T(8,128)(2,1)S(1)}, bf16[128,512]{1,0:T(8,128)(2,1)S(1)}, u32[]{:S(2)}, u32[]{:S(2)}) collective-permute-start(bf16[128,512]{1,0:T(8,128)(2,1)S(1)} %collective-permute-done.2.refs_0_), channel_id=1, source_target_pairs={{0,2},{1,3},{2,0},{3,1},{4,6},{5,7},{6,4},{7,5},{8,10},{9,11},{10,... | collective-permute-start | bytes 393224 | tf_op jit(solution)/shard_map/ppermute | solution.py:204
  23.5 1.0 %fusion.1 = bf16[128,1024]{1,0:T(8,128)(2,1)S(1)} fusion(bf16[2,128,1024]{2,1,0:T(8,128)(2,1)S(1)} %collective-permute-done.6, bf16[2,128,1024]{2,1,0:T(8,128)(2,1)} %get-tuple-element.31), kind=kLoop, calls=%fused_computation.3 | loop fusion | flops 524288 | bytes 786432 | tf_op jit(solution)/shard_map/squeeze | solution.py:345
  24.5 0.4 %collective-permute-start.7 = (bf16[128,1024]{1,0:T(8,128)(2,1)S(1)}, bf16[128,1024]{1,0:T(8,128)(2,1)S(1)}, u32[]{:S(2)}, u32[]{:S(2)}) collective-permute-start(bf16[128,1024]{1,0:T(8,128)(2,1)S(1)} %fusion.1), channel_id=1, source_target_pairs={{0,2},{1,3},{2,0},{3,1},{4,6},{5,7},{6,4},{7,5},{8,10},{9,11},{10,... | collective-permute-start | bytes 786440 | tf_op jit(solution)/shard_map/ppermute | solution.py:345
  24.9 0.5 %collective-permute-done.4.refs_1_ = bf16[256,256]{1,0:T(8,128)(2,1)S(1)} collective-permute-done((bf16[256,256]{1,0:T(8,128)(2,1)S(1)}, bf16[256,256]{1,0:T(8,128)(2,1)S(1)}, u32[]{:S(2)}, u32[]{:S(2)}) %collective-permute-start.4) | collective-permute-done | bytes 131104 | tf_op jit(solution)/shard_map/ppermute | solution.py:200
  25.5 2.1 %collective-permute-done.8.refs_1_ = bf16[128,512]{1,0:T(8,128)(2,1)S(1)} collective-permute-done((bf16[128,512]{1,0:T(8,128)(2,1)S(1)}, bf16[128,512]{1,0:T(8,128)(2,1)S(1)}, u32[]{:S(2)}, u32[]{:S(2)}) %collective-permute-start.8) | collective-permute-done | bytes 131104 | tf_op jit(solution)/shard_map/ppermute | solution.py:204
  27.5 1.9 %collective-permute-start.5 = (bf16[256,256]{1,0:T(8,128)(2,1)S(1)}, bf16[256,256]{1,0:T(8,128)(2,1)S(1)}, u32[]{:S(2)}, u32[]{:S(2)}) collective-permute-start(bf16[256,256]{1,0:T(8,128)(2,1)S(1)} %collective-permute-done.4.refs_1_), channel_id=1, source_target_pairs={{0,4},{1,5},{2,6},{3,7},{4,0},{5,1},{6,2},{7,3},{8,12},{9,13},{10,... | collective-permute-start | bytes 393224 | tf_op jit(solution)/shard_map/ppermute | solution.py:200
  29.4 0.5 %shard_map.87.x_ref = bf16[512,1024]{1,0:T(8,128)(2,1)S(1)} custom-call(bf16[128,512]{1,0:T(8,128)(2,1)S(1)} %collective-permute-done.2.refs_0_, bf16[128,512]{1,0:T(8,128)(2,1)S(1)} %collective-permute-done.8.refs_1_, bf16[128,512]{1,0:T(8,128)(2,1)S(1)} %collective-permute-done.refs_2_, bf16[128,512]{1,0:T(8,128)(2,1)S(1)} %collective-permute-done.10.refs_3_, ...), custom_call_target="tpu_custom_call" | custom-call | bytes 2097152 | tf_op jit(solution)/shard_map/pallas_call | solution.py:235
  29.9 3.1 %collective-permute-done.7 = bf16[128,1024]{1,0:T(8,128)(2,1)S(1)} collective-permute-done((bf16[128,1024]{1,0:T(8,128)(2,1)S(1)}, bf16[128,1024]{1,0:T(8,128)(2,1)S(1)}, u32[]{:S(2)}, u32[]{:S(2)}) %collective-permute-start.7) | collective-permute-done | bytes 262176 | tf_op jit(solution)/shard_map/ppermute | solution.py:345
  33.0 1.8 %fusion = bf16[128,1024]{1,0:T(8,128)(2,1)} fusion(bf16[128,1024]{1,0:T(8,128)(2,1)S(1)} %collective-permute-done.7, bf16[2,128,1024]{2,1,0:T(8,128)(2,1)S(1)} %collective-permute-done.6, bf16[2,128,1024]{2,1,0:T(8,128)(2,1)} %get-tuple-element.31), kind=kLoop, calls=%fused_computation.1 | loop fusion | flops 786432 | bytes 1048576 | tf_op jit(solution)/shard_map/convert_element_type | solution.py:346
  34.7 1.2 %shard_map.88 = f32[512,256]{1,0:T(8,128)} custom-call(bf16[512,1024]{1,0:T(8,128)(2,1)S(1)} %shard_map.87.x_ref, bf16[256,256]{1,0:T(8,128)(2,1)S(1)} %constant_dynamic-update-slice_fusion.refs_0_, bf16[256,256]{1,0:T(8,128)(2,1)S(1)} %collective-permute-done.4.refs_1_, bf16[256,256]{1,0:T(8,128)(2,1)S(1)} %collective-permute-done.9.refs_2_, ...), custom_call_target="tpu_custom_call" | custom-call | flops 268435456 | bytes 1572864 | tf_op jit(solution)/shard_map/pallas_call | solution.py:248
  (14 shorter events, 0.0 us)
Async XLA Ops:
  0.6 28.8 %copy-start = (bf16[128,4096]{1,0:T(8,128)(2,1)S(1)}, bf16[128,4096]{1,0:T(8,128)(2,1)}, u32[]{:S(2)}) copy-start(bf16[128,4096]{1,0:T(8,128)(2,1)} %refs_7_.1) | copy-start | bytes 3145732
  1.8 11.3 %collective-permute-start = (bf16[128,512]{1,0:T(8,128)(2,1)S(1)}, bf16[128,512]{1,0:T(8,128)(2,1)S(1)}, u32[]{:S(2)}, u32[]{:S(2)}) collective-permute-start(bf16[128,512]{1,0:T(8,128)(2,1)S(1)} %get-tuple-element.41), channel_id=1, source_target_pairs={{0,8},{1,13},{2,10},{3,15},{4,12},{5,9},{6,14},{7,11},{8,0},{9,5},... | collective-permute-start | bytes 393224 | tf_op jit(solution)/shard_map/ppermute | solution.py:200
  4.9 13.9 %collective-permute-start.2 = (bf16[128,512]{1,0:T(8,128)(2,1)S(1)}, bf16[128,512]{1,0:T(8,128)(2,1)S(1)}, u32[]{:S(2)}, u32[]{:S(2)}) collective-permute-start(bf16[128,512]{1,0:T(8,128)(2,1)S(1)} %get-tuple-element.40), channel_id=1, source_target_pairs={{0,16},{1,21},{2,26},{3,31},{4,20},{5,17},{6,30},{7,27},{8,24},{9,... | collective-permute-start | bytes 393224 | tf_op jit(solution)/shard_map/ppermute | solution.py:200
  7.5 11.3 %collective-permute-start.3 = (bf16[128,512]{1,0:T(8,128)(2,1)S(1)}, bf16[128,512]{1,0:T(8,128)(2,1)S(1)}, u32[]{:S(2)}, u32[]{:S(2)}) collective-permute-start(bf16[128,512]{1,0:T(8,128)(2,1)S(1)} %get-tuple-element.39), channel_id=1, source_target_pairs={{0,4},{1,5},{2,6},{3,7},{4,0},{5,1},{6,2},{7,3},{8,12},{9,13},{10,... | collective-permute-start | bytes 393224 | tf_op jit(solution)/shard_map/ppermute | solution.py:200
  13.1 6.4 %copy-start.1 = (bf16[256,256]{1,0:T(8,128)(2,1)S(1)}, bf16[256,256]{1,0:T(8,128)(2,1)}, u32[]{:S(2)}) copy-start(bf16[256,256]{1,0:T(8,128)(2,1)} %get-tuple-element.29) | copy-start | bytes 393220
  13.1 6.4 %collective-permute-start.1 = (bf16[128,256]{1,0:T(8,128)(2,1)}, bf16[128,256]{1,0:T(8,128)(2,1)S(1)}, u32[]{:S(2)}, u32[]{:S(2)}) collective-permute-start(bf16[128,256]{1,0:T(8,128)(2,1)} %get-tuple-element.23.gk_hbm), channel_id=1, source_target_pairs={{0,16},{1,17},{2,18},{3,19},{4,20},{5,21},{6,22},{7,23},{8,24},{9,... | collective-permute-start | bytes 196616 | tf_op jit(solution)/shard_map/ppermute | solution.py:200
  19.5 4.0 %collective-permute-start.6 = (bf16[2,128,1024]{2,1,0:T(8,128)(2,1)}, bf16[2,128,1024]{2,1,0:T(8,128)(2,1)S(1)}, u32[]{:S(2)}, u32[]{:S(2)}) collective-permute-start(bf16[2,128,1024]{2,1,0:T(8,128)(2,1)} %get-tuple-element.32), channel_id=1, source_target_pairs={{0,1},{1,0},{2,3},{3,2},{4,5},{5,4},{6,7},{7,6},{8,9},{9,8},{10,11... | collective-permute-start | bytes 1572872 | tf_op jit(solution)/shard_map/ppermute | solution.py:204
  19.5 6.0 %collective-permute-start.4 = (bf16[256,256]{1,0:T(8,128)(2,1)S(1)}, bf16[256,256]{1,0:T(8,128)(2,1)S(1)}, u32[]{:S(2)}, u32[]{:S(2)}) collective-permute-start(bf16[256,256]{1,0:T(8,128)(2,1)S(1)} %constant_dynamic-update-slice_fusion.refs_0_), channel_id=1, source_target_pairs={{0,8},{1,9},{2,10},{3,11},{4,12},{5,13},{6,14},{7,15},{8,0},{9,1},... | collective-permute-start | bytes 393224 | tf_op jit(solution)/shard_map/ppermute | solution.py:200
  20.7 6.8 %collective-permute-start.9 = (bf16[256,256]{1,0:T(8,128)(2,1)S(1)}, bf16[256,256]{1,0:T(8,128)(2,1)S(1)}, u32[]{:S(2)}, u32[]{:S(2)}) collective-permute-start(bf16[256,256]{1,0:T(8,128)(2,1)S(1)} %constant_dynamic-update-slice_fusion.refs_0_), channel_id=1, source_target_pairs={{0,4},{1,5},{2,6},{3,7},{4,0},{5,1},{6,2},{7,3},{8,12},{9,13},{10,... | collective-permute-start | bytes 393224 | tf_op jit(solution)/shard_map/ppermute | solution.py:200
  21.8 5.7 %collective-permute-start.8 = (bf16[128,512]{1,0:T(8,128)(2,1)S(1)}, bf16[128,512]{1,0:T(8,128)(2,1)S(1)}, u32[]{:S(2)}, u32[]{:S(2)}) collective-permute-start(bf16[128,512]{1,0:T(8,128)(2,1)S(1)} %collective-permute-done.2.refs_0_), channel_id=1, source_target_pairs={{0,2},{1,3},{2,0},{3,1},{4,6},{5,7},{6,4},{7,5},{8,10},{9,11},{10,... | collective-permute-start | bytes 393224 | tf_op jit(solution)/shard_map/ppermute | solution.py:204
  24.5 8.5 %collective-permute-start.7 = (bf16[128,1024]{1,0:T(8,128)(2,1)S(1)}, bf16[128,1024]{1,0:T(8,128)(2,1)S(1)}, u32[]{:S(2)}, u32[]{:S(2)}) collective-permute-start(bf16[128,1024]{1,0:T(8,128)(2,1)S(1)} %fusion.1), channel_id=1, source_target_pairs={{0,2},{1,3},{2,0},{3,1},{4,6},{5,7},{6,4},{7,5},{8,10},{9,11},{10,... | collective-permute-start | bytes 786440 | tf_op jit(solution)/shard_map/ppermute | solution.py:345
  24.9 4.5 %collective-permute-start.10 = (bf16[128,512]{1,0:T(8,128)(2,1)S(1)}, bf16[128,512]{1,0:T(8,128)(2,1)S(1)}, u32[]{:S(2)}, u32[]{:S(2)}) collective-permute-start(bf16[128,512]{1,0:T(8,128)(2,1)S(1)} %collective-permute-done.2.refs_0_), channel_id=1, source_target_pairs={{0,1},{1,0},{2,3},{3,2},{4,5},{5,4},{6,7},{7,6},{8,9},{9,8},{10,11... | collective-permute-start | bytes 393224 | tf_op jit(solution)/shard_map/ppermute | solution.py:204
  25.5 4.0 %collective-permute-start.12 = (bf16[128,512]{1,0:T(8,128)(2,1)S(1)}, bf16[128,512]{1,0:T(8,128)(2,1)S(1)}, u32[]{:S(2)}, u32[]{:S(2)}) collective-permute-start(bf16[128,512]{1,0:T(8,128)(2,1)S(1)} %collective-permute-done.refs_2_), channel_id=1, source_target_pairs={{0,1},{1,0},{2,3},{3,2},{4,5},{5,4},{6,7},{7,6},{8,9},{9,8},{10,11... | collective-permute-start | bytes 393224 | tf_op jit(solution)/shard_map/ppermute | solution.py:204
  27.5 1.9 %collective-permute-start.11 = (bf16[128,512]{1,0:T(8,128)(2,1)S(1)}, bf16[128,512]{1,0:T(8,128)(2,1)S(1)}, u32[]{:S(2)}, u32[]{:S(2)}) collective-permute-start(bf16[128,512]{1,0:T(8,128)(2,1)S(1)} %collective-permute-done.8.refs_1_), channel_id=1, source_target_pairs={{0,1},{1,0},{2,3},{3,2},{4,5},{5,4},{6,7},{7,6},{8,9},{9,8},{10,11... | collective-permute-start | bytes 393224 | tf_op jit(solution)/shard_map/ppermute | solution.py:204
  27.5 7.2 %collective-permute-start.5 = (bf16[256,256]{1,0:T(8,128)(2,1)S(1)}, bf16[256,256]{1,0:T(8,128)(2,1)S(1)}, u32[]{:S(2)}, u32[]{:S(2)}) collective-permute-start(bf16[256,256]{1,0:T(8,128)(2,1)S(1)} %collective-permute-done.4.refs_1_), channel_id=1, source_target_pairs={{0,4},{1,5},{2,6},{3,7},{4,0},{5,1},{6,2},{7,3},{8,12},{9,13},{10,... | collective-permute-start | bytes 393224 | tf_op jit(solution)/shard_map/ppermute | solution.py:200

commit v12 on v10

--- a/solution.py
+++ b/solution.py
@@ -115,28 +115,25 @@
     chips = groups // 2
     member = lax.axis_index("mp")
     chip, core = lax.div(member, 2), lax.rem(member, 2)
-    step = min(CHUNK, features)
-    pieces = [(b, at) for b in range(groups) for at in range(0, features, step)]
-    loads, stored = [], []
-    for j, (b, at) in enumerate(pieces):
+    blocks, stored = [], []
+    for b in range(groups):
         column = core if b >= chips else 1 - core
-        start = (2 * lax.rem(chip + b + 1, chips) + column) * features + at
-        rows = pl.ds(pl.multiple_of(start, step), step)
-        target = p.at[b, :, pl.ds(at, step), :]
-        loads.append(pltpu.make_async_copy(p_hbm.at[:, rows, :], target, p_sems.at[j]))
-    for copy in loads:
+        start = (2 * lax.rem(chip + b + 1, chips) + column) * features
+        rows = pl.ds(pl.multiple_of(start, features), features)
+        blocks.append(pltpu.make_async_copy(p_hbm.at[:, rows, :], p.at[b], p_sems.at[b]))
+    for copy in blocks:
         copy.start()
     grads = jnp.concatenate([gk_ref[...], gv_ref[...]], axis=1)
-    for j, (b, at) in enumerate(pieces):
-        loads[j].wait()
-        rows = slice(at, at + step)
-        both = jnp.concatenate([p[b, 0, rows, :], p[b, 1, rows, :]], axis=1)
-        partial[b, :, rows] = dot(grads, both, NT).astype(BF16)
+    step = min(CHUNK, features)
+    for b in range(groups):
+        blocks[b].wait()
+        for at in range(0, features, step):
+            rows = slice(at, at + step)
+            both = jnp.concatenate([p[b, 0, rows, :], p[b, 1, rows, :]], axis=1)
+            partial[b, :, rows] = dot(grads, both, NT).astype(BF16)
         target = sent_hbm.at[b] if b < chips else kept_hbm.at[b - chips]
-        cols = pl.ds(at, step)
-        copy = pltpu.make_async_copy(partial.at[b, :, cols], target.at[:, cols], out_sems.at[j])
-        copy.start()
-        stored.append(copy)
+        stored.append(pltpu.make_async_copy(partial.at[b], target, out_sems.at[b]))
+        stored[-1].start()
     for copy in stored:
         copy.wait()
 
@@ -291,7 +288,6 @@
         ),
     )(query_states, key_states, value_states, grad_context)
 
-    copies = groups * (features // min(CHUNK, features))
     sent, kept = pl.pallas_call(
         partials_kernel,
         in_specs=[IN_VMEM, IN_VMEM, IN_HBM],
@@ -300,8 +296,8 @@
         scratch_shapes=[
             pltpu.VMEM((groups, 2, features, width), BF16),
             pltpu.VMEM((groups, rows, features), BF16),
-            pltpu.SemaphoreType.DMA((copies,)),
-            pltpu.SemaphoreType.DMA((copies,)),
+            pltpu.SemaphoreType.DMA((groups,)),
+            pltpu.SemaphoreType.DMA((groups,)),
         ],
         compiler_params=WHOLE,
         cost_estimate=cost(
@@ -310,12 +306,12 @@
     )(grad_key, grad_value, projections)
 
     if exchange:
-        ready, near = lax.optimization_barrier((grad_key, near))
-        first = along_dp(ready, lambda m: parts // 2, parts, groups)
-        first, twice, sent, kept, distant, near, next_inputs = lax.optimization_barrier(
-            (first, twice, sent, kept, distant, near, next_inputs)
+        first = along_dp(grad_key, lambda m: parts // 2, parts, groups)
+        _, distant = lax.optimization_barrier((grad_key, distant))
+        pieces = shared_inputs(distant, groups)
+        first, twice, sent, kept, pieces, near, next_inputs = lax.optimization_barrier(
+            (first, twice, sent, kept, pieces, near, next_inputs)
         )
-        pieces = shared_inputs(distant, groups)
         keys = {0: lax.dynamic_update_slice(twice, first, (rows, 0))}
         bit = parts // 4
         while bit > 1:

time: 35.1 us -> 35.3 us (level)
  starting transfers between devices: 14.2 us -> 16.2 us
  waiting for transfers between devices: 5.78 us -> 4.46 us
  Pallas kernels: 11 us -> 10.6 us
    ppermute x5, waiting for transfers between devices: 1.67 us -> 0.01 us  [along_mp(): return lax.ppermute(array, 'mp', [(m, m ^ bit) for m in range(groups)])]
    ppermute x7, starting transfers between devices: 11.9 us -> 13.2 us  [along_dp(): return lax.ppermute(array, ('dp', 'mp'), pairs)]
    ppermute x1, starting transfers between devices: 0.42 us -> 1.32 us  [body(): grad_input += lax.ppermute(total[b].astype(BF16), 'mp', shift).astype(F32)]
    pallas_call x1, Pallas kernels: 5.23 us -> 4.76 us  [body(): pl.pallas_call(partials_kernel, in_specs=[IN_VMEM, IN_VMEM, IN_HBM], out_...]
  transfers between devices with their start and end apart: 13 -> 13, of which waited for: 4 -> 3; matrix products, arithmetic and copies ran while one was open for 6% -> 6% of each run, Pallas kernels for 28% -> 27%
where the time goes in v12:
time: 35.3 us; the launch traced here: 35.1 us
  starting transfers between devices  16.2 us (46%)
  Pallas kernels  10.6 us (30%)
  waiting for transfers between devices  4.46 us (13%)
  other arithmetic  1.97 us (6%)
  local copies, waits for them, and re-layouts  1.12 us (3%)
  between operations  0.79 us (2%)
    ppermute x7, starting transfers between devices, along_dp(): return lax.ppermute(array, ('dp', 'mp'), pairs)  13.2 us
    pallas_call x1, Pallas kernels, body(): pl.pallas_call(partials_kernel, in_specs=[IN_VMEM, IN_VMEM, IN_HBM], out_...  4.76 us
    pallas_call x1, Pallas kernels, body(): pl.pallas_call(attention_kernel, in_specs=[IN_HBM] * 4, out_specs=[IN_VME...  4.09 us
    ppermute x1, waiting for transfers between devices, body(): grad_input += lax.ppermute(total[b].astype(BF16), 'mp', shift).astype(F32)  3.35 us
    ppermute x5, starting transfers between devices, along_mp(): return lax.ppermute(array, 'mp', [(m, m ^ bit) for m in range(groups)])  1.61 us
    ppermute x1, starting transfers between devices, body(): grad_input += lax.ppermute(total[b].astype(BF16), 'mp', shift).astype(F32)  1.32 us
    pallas_call x1, Pallas kernels, summed_weights(): pl.pallas_call(weights_kernel, out_specs=ANYWHERE, out_shape=jax.ShapeDty...  1.24 us
    add x1, other arithmetic, body(): total = kept.astype(F32) + came.astype(F32)  1.21 us
  transfers between devices with their start and end apart: 13, of which 3 were waited for; matrix products, arithmetic and copies ran while one was open for 6% of the time, Pallas kernels for 27%

profile of v12, /device:TPU:0, one launch (start us, length us, event | category | flops | bytes accessed | tf_op | source)
XLA Modules:
  0.0 35.1 jit_solution(15437136412465487758)
XLA Ops:
  0.7 1.1 %constant_dynamic-slice_fusion = (bf16[128,512]{1,0:T(8,128)(2,1)S(1)}, bf16[128,512]{1,0:T(8,128)(2,1)S(1)}, bf16[128,512]{1,0:T(8,128)(2,1)S(1)}) fusion(bf16[128,4096]{1,0:T(8,128)(2,1)} %refs_7_.1, s32[]{:T(128)S(6)} %select_n.11, s32[]{:T(128)S(6)} %select_n.10, s32[]{:T(128)S(6)} %select_n.9), kind=kLoop, calls=%fused_computation.7 | loop fusion | bytes 786444 | tf_op jit(solution)/shard_map/dynamic_slice | solution.py:201
  1.7 0.0 copy-start
  1.7 4.1 %collective-permute-start.1 = (bf16[128,512]{1,0:T(8,128)(2,1)S(1)}, bf16[128,512]{1,0:T(8,128)(2,1)S(1)}, u32[]{:S(2)}, u32[]{:S(2)}) collective-permute-start(bf16[128,512]{1,0:T(8,128)(2,1)S(1)} %get-tuple-element.41), channel_id=1, source_target_pairs={{0,16},{1,21},{2,26},{3,31},{4,20},{5,17},{6,30},{7,27},{8,24},{9,... | collective-permute-start | bytes 393224 | tf_op jit(solution)/shard_map/ppermute | solution.py:188
  5.8 1.6 %collective-permute-start.3 = (bf16[128,512]{1,0:T(8,128)(2,1)S(1)}, bf16[128,512]{1,0:T(8,128)(2,1)S(1)}, u32[]{:S(2)}, u32[]{:S(2)}) collective-permute-start(bf16[128,512]{1,0:T(8,128)(2,1)S(1)} %get-tuple-element.40), channel_id=1, source_target_pairs={{0,8},{1,13},{2,10},{3,15},{4,12},{5,9},{6,14},{7,11},{8,0},{9,5},... | collective-permute-start | bytes 393224 | tf_op jit(solution)/shard_map/ppermute | solution.py:188
  7.4 1.5 %collective-permute-start.4 = (bf16[128,512]{1,0:T(8,128)(2,1)S(1)}, bf16[128,512]{1,0:T(8,128)(2,1)S(1)}, u32[]{:S(2)}, u32[]{:S(2)}) collective-permute-start(bf16[128,512]{1,0:T(8,128)(2,1)S(1)} %get-tuple-element.39), channel_id=1, source_target_pairs={{0,4},{1,5},{2,6},{3,7},{4,0},{5,1},{6,2},{7,3},{8,12},{9,13},{10,... | collective-permute-start | bytes 393224 | tf_op jit(solution)/shard_map/ppermute | solution.py:188
  8.9 4.1 %shard_map.85 = (bf16[128,256]{1,0:T(8,128)(2,1)}, bf16[128,256]{1,0:T(8,128)(2,1)}, bf16[256,256]{1,0:T(8,128)(2,1)}, bf16[128,2048]{1,0:T(8,128)(2,1)}) custom-call(bf16[128,2048]{1,0:T(8,128)(2,1)} %q_hbm.1, bf16[128,256]{1,0:T(8,128)(2,1)} %k_hbm.1, bf16[128,256]{1,0:T(8,128)(2,1)} %v_hbm.1, bf16[128,2048]{1,0:T(8,128)(2,1)} %do_hbm.1), custom_call_target="tpu_custom_call" | custom-call | flops 335544320 | bytes 1572864 | tf_op jit(solution)/shard_map/pallas_call | solution.py:273
  13.0 0.0 copy-start.1
  13.0 0.0 collective-permute-done.1.refs_0_
  13.0 1.0 %collective-permute-start.2 = (bf16[128,512]{1,0:T(8,128)(2,1)S(1)}, bf16[128,512]{1,0:T(8,128)(2,1)S(1)}, u32[]{:S(2)}, u32[]{:S(2)}) collective-permute-start(bf16[128,512]{1,0:T(8,128)(2,1)S(1)} %collective-permute-done.1.refs_0_), channel_id=1, source_target_pairs={{0,2},{1,3},{2,0},{3,1},{4,6},{5,7},{6,4},{7,5},{8,10},{9,11},{10,... | collective-permute-start | bytes 393224 | tf_op jit(solution)/shard_map/ppermute | solution.py:192
  14.1 2.3 %collective-permute-start = (bf16[128,256]{1,0:T(8,128)(2,1)}, bf16[128,256]{1,0:T(8,128)(2,1)S(1)}, u32[]{:S(2)}, u32[]{:S(2)}) collective-permute-start(bf16[128,256]{1,0:T(8,128)(2,1)} %get-tuple-element.22.gk_ref), channel_id=1, source_target_pairs={{0,16},{1,17},{2,18},{3,19},{4,20},{5,21},{6,22},{7,23},{8,24},{9,... | collective-permute-start | bytes 196616 | tf_op jit(solution)/shard_map/ppermute | solution.py:188
  16.3 4.8 %shard_map.86 = (bf16[2,128,1024]{2,1,0:T(8,128)(2,1)}, bf16[2,128,1024]{2,1,0:T(8,128)(2,1)}) custom-call(bf16[128,256]{1,0:T(8,128)(2,1)} %get-tuple-element.22.gk_ref, bf16[128,256]{1,0:T(8,128)(2,1)} %get-tuple-element.24.gv_ref, bf16[2,4096,256]{2,1,0:T(8,128)(2,1)} %p_hbm.1), custom_call_target="tpu_custom_call" | custom-call | flops 536870912 | bytes 4194304 | tf_op jit(solution)/shard_map/pallas_call | solution.py:291
  21.1 0.1 collective-permute-start.7
  21.2 0.9 %collective-permute-start.5 = (bf16[256,256]{1,0:T(8,128)(2,1)S(1)}, bf16[256,256]{1,0:T(8,128)(2,1)S(1)}, u32[]{:S(2)}, u32[]{:S(2)}) collective-permute-start(bf16[256,256]{1,0:T(8,128)(2,1)S(1)} %constant_dynamic-update-slice_fusion.refs_0_), channel_id=1, source_target_pairs={{0,8},{1,9},{2,10},{3,11},{4,12},{5,13},{6,14},{7,15},{8,0},{9,1},... | collective-permute-start | bytes 393224 | tf_op jit(solution)/shard_map/ppermute | solution.py:188
  22.2 1.4 %collective-permute-start.9 = (bf16[256,256]{1,0:T(8,128)(2,1)S(1)}, bf16[256,256]{1,0:T(8,128)(2,1)S(1)}, u32[]{:S(2)}, u32[]{:S(2)}) collective-permute-start(bf16[256,256]{1,0:T(8,128)(2,1)S(1)} %constant_dynamic-update-slice_fusion.refs_0_), channel_id=1, source_target_pairs={{0,4},{1,5},{2,6},{3,7},{4,0},{5,1},{6,2},{7,3},{8,12},{9,13},{10,... | collective-permute-start | bytes 393224 | tf_op jit(solution)/shard_map/ppermute | solution.py:188
  23.6 1.2 %convert_add_fusion = f32[2,128,1024]{2,1,0:T(8,128)S(1)} fusion(bf16[2,128,1024]{2,1,0:T(8,128)(2,1)S(1)} %collective-permute-done.7, bf16[2,128,1024]{2,1,0:T(8,128)(2,1)} %get-tuple-element.30), kind=kLoop, calls=%fused_computation | loop fusion | flops 786432 | bytes 2097152 | tf_op jit(solution)/shard_map/add | solution.py:326
  24.9 1.3 %collective-permute-start.8 = (bf16[128,1024]{1,0:T(8,128)(2,1)S(1)}, bf16[128,1024]{1,0:T(8,128)(2,1)S(1)}, u32[]{:S(2)}, u32[]{:S(2)}) collective-permute-start(bf16[128,1024]{1,0:T(8,128)(2,1)S(1)} %fusion.2), channel_id=1, source_target_pairs={{0,2},{1,3},{2,0},{3,1},{4,6},{5,7},{6,4},{7,5},{8,10},{9,11},{10,... | collective-permute-start | bytes 786440 | tf_op jit(solution)/shard_map/ppermute | solution.py:330
  26.2 0.5 %collective-permute-start.12 = (bf16[128,512]{1,0:T(8,128)(2,1)S(1)}, bf16[128,512]{1,0:T(8,128)(2,1)S(1)}, u32[]{:S(2)}, u32[]{:S(2)}) collective-permute-start(bf16[128,512]{1,0:T(8,128)(2,1)S(1)} %collective-permute-done.3.refs_2_), channel_id=1, source_target_pairs={{0,1},{1,0},{2,3},{3,2},{4,5},{5,4},{6,7},{7,6},{8,9},{9,8},{10,11... | collective-permute-start | bytes 393224 | tf_op jit(solution)/shard_map/ppermute | solution.py:192
  26.7 0.5 %collective-permute-done.5.refs_1_ = bf16[256,256]{1,0:T(8,128)(2,1)S(1)} collective-permute-done((bf16[256,256]{1,0:T(8,128)(2,1)S(1)}, bf16[256,256]{1,0:T(8,128)(2,1)S(1)}, u32[]{:S(2)}, u32[]{:S(2)}) %collective-permute-start.5) | collective-permute-done | bytes 131104 | tf_op jit(solution)/shard_map/ppermute | solution.py:188
  27.2 0.6 %collective-permute-done.9.refs_2_ = bf16[256,256]{1,0:T(8,128)(2,1)S(1)} collective-permute-done((bf16[256,256]{1,0:T(8,128)(2,1)S(1)}, bf16[256,256]{1,0:T(8,128)(2,1)S(1)}, u32[]{:S(2)}, u32[]{:S(2)}) %collective-permute-start.9) | collective-permute-done | bytes 131104 | tf_op jit(solution)/shard_map/ppermute | solution.py:188
  27.8 1.4 %collective-permute-start.6 = (bf16[256,256]{1,0:T(8,128)(2,1)S(1)}, bf16[256,256]{1,0:T(8,128)(2,1)S(1)}, u32[]{:S(2)}, u32[]{:S(2)}) collective-permute-start(bf16[256,256]{1,0:T(8,128)(2,1)S(1)} %collective-permute-done.5.refs_1_), channel_id=1, source_target_pairs={{0,4},{1,5},{2,6},{3,7},{4,0},{5,1},{6,2},{7,3},{8,12},{9,13},{10,... | collective-permute-start | bytes 393224 | tf_op jit(solution)/shard_map/ppermute | solution.py:188
  29.2 0.5 %shard_map.87.x_ref = bf16[512,1024]{1,0:T(8,128)(2,1)S(1)} custom-call(bf16[128,512]{1,0:T(8,128)(2,1)S(1)} %collective-permute-done.1.refs_0_, bf16[128,512]{1,0:T(8,128)(2,1)S(1)} %collective-permute-done.2.refs_1_, bf16[128,512]{1,0:T(8,128)(2,1)S(1)} %collective-permute-done.3.refs_2_, bf16[128,512]{1,0:T(8,128)(2,1)S(1)} %collective-permute-done.10.refs_3_, ...), custom_call_target="tpu_custom_call" | custom-call | bytes 2097152 | tf_op jit(solution)/shard_map/pallas_call | solution.py:223
  29.7 3.4 %collective-permute-done.8 = bf16[128,1024]{1,0:T(8,128)(2,1)S(1)} collective-permute-done((bf16[128,1024]{1,0:T(8,128)(2,1)S(1)}, bf16[128,1024]{1,0:T(8,128)(2,1)S(1)}, u32[]{:S(2)}, u32[]{:S(2)}) %collective-permute-start.8) | collective-permute-done | bytes 262176 | tf_op jit(solution)/shard_map/ppermute | solution.py:330
  33.1 0.8 %fusion.1 = bf16[128,1024]{1,0:T(8,128)(2,1)} fusion(f32[2,128,1024]{2,1,0:T(8,128)S(1)} %convert_add_fusion, bf16[128,1024]{1,0:T(8,128)(2,1)S(1)} %collective-permute-done.8), kind=kLoop, calls=%fused_computation.4 | loop fusion | flops 393216 | bytes 1048576 | tf_op jit(solution)/shard_map/convert_element_type | solution.py:331
  33.8 1.2 %shard_map.88 = f32[512,256]{1,0:T(8,128)} custom-call(bf16[512,1024]{1,0:T(8,128)(2,1)S(1)} %shard_map.87.x_ref, bf16[256,256]{1,0:T(8,128)(2,1)S(1)} %constant_dynamic-update-slice_fusion.refs_0_, bf16[256,256]{1,0:T(8,128)(2,1)S(1)} %collective-permute-done.5.refs_1_, bf16[256,256]{1,0:T(8,128)(2,1)S(1)} %collective-permute-done.9.refs_2_, ...), custom_call_target="tpu_custom_call" | custom-call | flops 268435456 | bytes 1572864 | tf_op jit(solution)/shard_map/pallas_call | solution.py:236
  (15 shorter events, 0.1 us)
Async XLA Ops:
  1.7 27.5 %copy-start = (bf16[128,4096]{1,0:T(8,128)(2,1)S(1)}, bf16[128,4096]{1,0:T(8,128)(2,1)}, u32[]{:S(2)}) copy-start(bf16[128,4096]{1,0:T(8,128)(2,1)} %refs_7_.1) | copy-start | bytes 3145732
  1.7 11.3 %collective-permute-start.1 = (bf16[128,512]{1,0:T(8,128)(2,1)S(1)}, bf16[128,512]{1,0:T(8,128)(2,1)S(1)}, u32[]{:S(2)}, u32[]{:S(2)}) collective-permute-start(bf16[128,512]{1,0:T(8,128)(2,1)S(1)} %get-tuple-element.41), channel_id=1, source_target_pairs={{0,16},{1,21},{2,26},{3,31},{4,20},{5,17},{6,30},{7,27},{8,24},{9,... | collective-permute-start | bytes 393224 | tf_op jit(solution)/shard_map/ppermute | solution.py:188
  5.8 15.3 %collective-permute-start.3 = (bf16[128,512]{1,0:T(8,128)(2,1)S(1)}, bf16[128,512]{1,0:T(8,128)(2,1)S(1)}, u32[]{:S(2)}, u32[]{:S(2)}) collective-permute-start(bf16[128,512]{1,0:T(8,128)(2,1)S(1)} %get-tuple-element.40), channel_id=1, source_target_pairs={{0,8},{1,13},{2,10},{3,15},{4,12},{5,9},{6,14},{7,11},{8,0},{9,5},... | collective-permute-start | bytes 393224 | tf_op jit(solution)/shard_map/ppermute | solution.py:188
  7.4 13.7 %collective-permute-start.4 = (bf16[128,512]{1,0:T(8,128)(2,1)S(1)}, bf16[128,512]{1,0:T(8,128)(2,1)S(1)}, u32[]{:S(2)}, u32[]{:S(2)}) collective-permute-start(bf16[128,512]{1,0:T(8,128)(2,1)S(1)} %get-tuple-element.39), channel_id=1, source_target_pairs={{0,4},{1,5},{2,6},{3,7},{4,0},{5,1},{6,2},{7,3},{8,12},{9,13},{10,... | collective-permute-start | bytes 393224 | tf_op jit(solution)/shard_map/ppermute | solution.py:188
  13.0 8.2 %copy-start.1 = (bf16[256,256]{1,0:T(8,128)(2,1)S(1)}, bf16[256,256]{1,0:T(8,128)(2,1)}, u32[]{:S(2)}) copy-start(bf16[256,256]{1,0:T(8,128)(2,1)} %get-tuple-element.28) | copy-start | bytes 393220
  13.0 8.1 %collective-permute-start.2 = (bf16[128,512]{1,0:T(8,128)(2,1)S(1)}, bf16[128,512]{1,0:T(8,128)(2,1)S(1)}, u32[]{:S(2)}, u32[]{:S(2)}) collective-permute-start(bf16[128,512]{1,0:T(8,128)(2,1)S(1)} %collective-permute-done.1.refs_0_), channel_id=1, source_target_pairs={{0,2},{1,3},{2,0},{3,1},{4,6},{5,7},{6,4},{7,5},{8,10},{9,11},{10,... | collective-permute-start | bytes 393224 | tf_op jit(solution)/shard_map/ppermute | solution.py:192
  14.1 7.0 %collective-permute-start = (bf16[128,256]{1,0:T(8,128)(2,1)}, bf16[128,256]{1,0:T(8,128)(2,1)S(1)}, u32[]{:S(2)}, u32[]{:S(2)}) collective-permute-start(bf16[128,256]{1,0:T(8,128)(2,1)} %get-tuple-element.22.gk_ref), channel_id=1, source_target_pairs={{0,16},{1,17},{2,18},{3,19},{4,20},{5,21},{6,22},{7,23},{8,24},{9,... | collective-permute-start | bytes 196616 | tf_op jit(solution)/shard_map/ppermute | solution.py:188
  21.1 2.5 %collective-permute-start.7 = (bf16[2,128,1024]{2,1,0:T(8,128)(2,1)}, bf16[2,128,1024]{2,1,0:T(8,128)(2,1)S(1)}, u32[]{:S(2)}, u32[]{:S(2)}) collective-permute-start(bf16[2,128,1024]{2,1,0:T(8,128)(2,1)} %get-tuple-element.31), channel_id=1, source_target_pairs={{0,1},{1,0},{2,3},{3,2},{4,5},{5,4},{6,7},{7,6},{8,9},{9,8},{10,11... | collective-permute-start | bytes 1572872 | tf_op jit(solution)/shard_map/ppermute | solution.py:192
  21.2 6.0 %collective-permute-start.5 = (bf16[256,256]{1,0:T(8,128)(2,1)S(1)}, bf16[256,256]{1,0:T(8,128)(2,1)S(1)}, u32[]{:S(2)}, u32[]{:S(2)}) collective-permute-start(bf16[256,256]{1,0:T(8,128)(2,1)S(1)} %constant_dynamic-update-slice_fusion.refs_0_), channel_id=1, source_target_pairs={{0,8},{1,9},{2,10},{3,11},{4,12},{5,13},{6,14},{7,15},{8,0},{9,1},... | collective-permute-start | bytes 393224 | tf_op jit(solution)/shard_map/ppermute | solution.py:188
  22.2 5.6 %collective-permute-start.9 = (bf16[256,256]{1,0:T(8,128)(2,1)S(1)}, bf16[256,256]{1,0:T(8,128)(2,1)S(1)}, u32[]{:S(2)}, u32[]{:S(2)}) collective-permute-start(bf16[256,256]{1,0:T(8,128)(2,1)S(1)} %constant_dynamic-update-slice_fusion.refs_0_), channel_id=1, source_target_pairs={{0,4},{1,5},{2,6},{3,7},{4,0},{5,1},{6,2},{7,3},{8,12},{9,13},{10,... | collective-permute-start | bytes 393224 | tf_op jit(solution)/shard_map/ppermute | solution.py:188
  24.9 8.2 %collective-permute-start.8 = (bf16[128,1024]{1,0:T(8,128)(2,1)S(1)}, bf16[128,1024]{1,0:T(8,128)(2,1)S(1)}, u32[]{:S(2)}, u32[]{:S(2)}) collective-permute-start(bf16[128,1024]{1,0:T(8,128)(2,1)S(1)} %fusion.2), channel_id=1, source_target_pairs={{0,2},{1,3},{2,0},{3,1},{4,6},{5,7},{6,4},{7,5},{8,10},{9,11},{10,... | collective-permute-start | bytes 786440 | tf_op jit(solution)/shard_map/ppermute | solution.py:330
  26.2 3.0 %collective-permute-start.10 = (bf16[128,512]{1,0:T(8,128)(2,1)S(1)}, bf16[128,512]{1,0:T(8,128)(2,1)S(1)}, u32[]{:S(2)}, u32[]{:S(2)}) collective-permute-start(bf16[128,512]{1,0:T(8,128)(2,1)S(1)} %collective-permute-done.1.refs_0_), channel_id=1, source_target_pairs={{0,1},{1,0},{2,3},{3,2},{4,5},{5,4},{6,7},{7,6},{8,9},{9,8},{10,11... | collective-permute-start | bytes 393224 | tf_op jit(solution)/shard_map/ppermute | solution.py:192
  26.2 3.0 %collective-permute-start.12 = (bf16[128,512]{1,0:T(8,128)(2,1)S(1)}, bf16[128,512]{1,0:T(8,128)(2,1)S(1)}, u32[]{:S(2)}, u32[]{:S(2)}) collective-permute-start(bf16[128,512]{1,0:T(8,128)(2,1)S(1)} %collective-permute-done.3.refs_2_), channel_id=1, source_target_pairs={{0,1},{1,0},{2,3},{3,2},{4,5},{5,4},{6,7},{7,6},{8,9},{9,8},{10,11... | collective-permute-start | bytes 393224 | tf_op jit(solution)/shard_map/ppermute | solution.py:192
  27.8 1.4 %collective-permute-start.11 = (bf16[128,512]{1,0:T(8,128)(2,1)S(1)}, bf16[128,512]{1,0:T(8,128)(2,1)S(1)}, u32[]{:S(2)}, u32[]{:S(2)}) collective-permute-start(bf16[128,512]{1,0:T(8,128)(2,1)S(1)} %collective-permute-done.2.refs_1_), channel_id=1, source_target_pairs={{0,1},{1,0},{2,3},{3,2},{4,5},{5,4},{6,7},{7,6},{8,9},{9,8},{10,11... | collective-permute-start | bytes 393224 | tf_op jit(solution)/shard_map/ppermute | solution.py:192
  27.8 6.1 %collective-permute-start.6 = (bf16[256,256]{1,0:T(8,128)(2,1)S(1)}, bf16[256,256]{1,0:T(8,128)(2,1)S(1)}, u32[]{:S(2)}, u32[]{:S(2)}) collective-permute-start(bf16[256,256]{1,0:T(8,128)(2,1)S(1)} %collective-permute-done.5.refs_1_), channel_id=1, source_target_pairs={{0,4},{1,5},{2,6},{3,7},{4,0},{5,1},{6,2},{7,3},{8,12},{9,13},{10,... | collective-permute-start | bytes 393224 | tf_op jit(solution)/shard_map/ppermute | solution.py:188

commit v13 on v12

--- a/solution.py
+++ b/solution.py
@@ -307,11 +307,10 @@
 
     if exchange:
         first = along_dp(grad_key, lambda m: parts // 2, parts, groups)
-        _, distant = lax.optimization_barrier((grad_key, distant))
+        first, twice, sent, kept, distant, near, next_inputs = lax.optimization_barrier(
+            (first, twice, sent, kept, distant, near, next_inputs)
+        )
         pieces = shared_inputs(distant, groups)
-        first, twice, sent, kept, pieces, near, next_inputs = lax.optimization_barrier(
-            (first, twice, sent, kept, pieces, near, next_inputs)
-        )
         keys = {0: lax.dynamic_update_slice(twice, first, (rows, 0))}
         bit = parts // 4
         while bit > 1:

time: 35.3 us -> 33.6 us (0.952)
  starting transfers between devices: 16.2 us -> 12 us
  waiting for transfers between devices: 4.46 us -> 6.96 us
    ppermute x7, starting transfers between devices: 13.2 us -> 9.73 us  [along_dp(): return lax.ppermute(array, ('dp', 'mp'), pairs)]
    ppermute x7, waiting for transfers between devices: 1.09 us -> 2.99 us  [along_dp(): return lax.ppermute(array, ('dp', 'mp'), pairs)]
    ppermute x1, starting transfers between devices: 1.32 us -> 0.22 us  [body(): grad_input += lax.ppermute(total[b].astype(BF16), 'mp', shift).astype(F32)]
    ppermute x5, waiting for transfers between devices: 0.01 us -> 0.62 us  [along_mp(): return lax.ppermute(array, 'mp', [(m, m ^ bit) for m in range(groups)])]
    ppermute x5, starting transfers between devices: 1.61 us -> 2.07 us  [along_mp(): return lax.ppermute(array, 'mp', [(m, m ^ bit) for m in range(groups)])]
  transfers between devices with their start and end apart: 13 -> 13, of which waited for: 3 -> 4; matrix products, arithmetic and copies ran while one was open for 6% -> 6% of each run, Pallas kernels for 27% -> 28%
where the time goes in v13:
time: 33.6 us; the launch traced here: 33.4 us
  starting transfers between devices  12 us (36%)
  Pallas kernels  10.6 us (32%)
  waiting for transfers between devices  6.96 us (21%)
  other arithmetic  1.97 us (6%)
  local copies, waits for them, and re-layouts  1.12 us (3%)
  between operations  0.77 us (2%)
    ppermute x7, starting transfers between devices, along_dp(): return lax.ppermute(array, ('dp', 'mp'), pairs)  9.73 us
    pallas_call x1, Pallas kernels, body(): pl.pallas_call(partials_kernel, in_specs=[IN_VMEM, IN_VMEM, IN_HBM], out_...  4.75 us
    pallas_call x1, Pallas kernels, body(): pl.pallas_call(attention_kernel, in_specs=[IN_HBM] * 4, out_specs=[IN_VME...  4.09 us
    ppermute x1, waiting for transfers between devices, body(): grad_input += lax.ppermute(total[b].astype(BF16), 'mp', shift).astype(F32)  3.34 us
    ppermute x7, waiting for transfers between devices, along_dp(): return lax.ppermute(array, ('dp', 'mp'), pairs)  2.99 us
    ppermute x5, starting transfers between devices, along_mp(): return lax.ppermute(array, 'mp', [(m, m ^ bit) for m in range(groups)])  2.07 us
    pallas_call x1, Pallas kernels, summed_weights(): pl.pallas_call(weights_kernel, out_specs=ANYWHERE, out_shape=jax.ShapeDty...  1.24 us
    add x1, other arithmetic, body(): total = kept.astype(F32) + came.astype(F32)  1.21 us
  transfers between devices with their start and end apart: 13, of which 4 were waited for; matrix products, arithmetic and copies ran while one was open for 6% of the time, Pallas kernels for 28%

profile of v13, /device:TPU:0, one launch (start us, length us, event | category | flops | bytes accessed | tf_op | source)
XLA Modules:
  0.0 33.4 jit_solution(14473880437831519829)
XLA Ops:
  0.7 1.1 %constant_dynamic-slice_fusion = (bf16[128,512]{1,0:T(8,128)(2,1)S(1)}, bf16[128,512]{1,0:T(8,128)(2,1)S(1)}, bf16[128,512]{1,0:T(8,128)(2,1)S(1)}) fusion(bf16[128,4096]{1,0:T(8,128)(2,1)} %refs_7_.1, s32[]{:T(128)S(6)} %select_n.11, s32[]{:T(128)S(6)} %select_n.10, s32[]{:T(128)S(6)} %select_n.9), kind=kLoop, calls=%fused_computation.7 | loop fusion | bytes 786444 | tf_op jit(solution)/shard_map/dynamic_slice | solution.py:201
  1.7 0.0 copy-start
  1.7 4.1 %collective-permute-start.1 = (bf16[128,512]{1,0:T(8,128)(2,1)S(1)}, bf16[128,512]{1,0:T(8,128)(2,1)S(1)}, u32[]{:S(2)}, u32[]{:S(2)}) collective-permute-start(bf16[128,512]{1,0:T(8,128)(2,1)S(1)} %get-tuple-element.37), channel_id=1, source_target_pairs={{0,16},{1,21},{2,26},{3,31},{4,20},{5,17},{6,30},{7,27},{8,24},{9,... | collective-permute-start | bytes 393224 | tf_op jit(solution)/shard_map/ppermute | solution.py:188
  5.8 1.6 %collective-permute-start.2 = (bf16[128,512]{1,0:T(8,128)(2,1)S(1)}, bf16[128,512]{1,0:T(8,128)(2,1)S(1)}, u32[]{:S(2)}, u32[]{:S(2)}) collective-permute-start(bf16[128,512]{1,0:T(8,128)(2,1)S(1)} %get-tuple-element.36), channel_id=1, source_target_pairs={{0,8},{1,13},{2,10},{3,15},{4,12},{5,9},{6,14},{7,11},{8,0},{9,5},... | collective-permute-start | bytes 393224 | tf_op jit(solution)/shard_map/ppermute | solution.py:188
  7.4 1.5 %collective-permute-start.3 = (bf16[128,512]{1,0:T(8,128)(2,1)S(1)}, bf16[128,512]{1,0:T(8,128)(2,1)S(1)}, u32[]{:S(2)}, u32[]{:S(2)}) collective-permute-start(bf16[128,512]{1,0:T(8,128)(2,1)S(1)} %get-tuple-element.35), channel_id=1, source_target_pairs={{0,4},{1,5},{2,6},{3,7},{4,0},{5,1},{6,2},{7,3},{8,12},{9,13},{10,... | collective-permute-start | bytes 393224 | tf_op jit(solution)/shard_map/ppermute | solution.py:188
  8.9 4.1 %shard_map.85 = (bf16[128,256]{1,0:T(8,128)(2,1)}, bf16[128,256]{1,0:T(8,128)(2,1)}, bf16[256,256]{1,0:T(8,128)(2,1)}, bf16[128,2048]{1,0:T(8,128)(2,1)}) custom-call(bf16[128,2048]{1,0:T(8,128)(2,1)} %q_hbm.1, bf16[128,256]{1,0:T(8,128)(2,1)} %k_hbm.1, bf16[128,256]{1,0:T(8,128)(2,1)} %v_hbm.1, bf16[128,2048]{1,0:T(8,128)(2,1)} %do_hbm.1), custom_call_target="tpu_custom_call" | custom-call | flops 335544320 | bytes 1572864 | tf_op jit(solution)/shard_map/pallas_call | solution.py:273
  13.0 0.0 copy-start.1
  13.0 0.4 %collective-permute-start = (bf16[128,256]{1,0:T(8,128)(2,1)}, bf16[128,256]{1,0:T(8,128)(2,1)S(1)}, u32[]{:S(2)}, u32[]{:S(2)}) collective-permute-start(bf16[128,256]{1,0:T(8,128)(2,1)} %get-tuple-element.20.gk_ref), channel_id=1, source_target_pairs={{0,16},{1,17},{2,18},{3,19},{4,20},{5,21},{6,22},{7,23},{8,24},{9,... | collective-permute-start | bytes 196616 | tf_op jit(solution)/shard_map/ppermute | solution.py:188
  13.4 4.8 %shard_map.86 = (bf16[2,128,1024]{2,1,0:T(8,128)(2,1)}, bf16[2,128,1024]{2,1,0:T(8,128)(2,1)}) custom-call(bf16[128,256]{1,0:T(8,128)(2,1)} %get-tuple-element.20.gk_ref, bf16[128,256]{1,0:T(8,128)(2,1)} %get-tuple-element.22.gv_ref, bf16[2,4096,256]{2,1,0:T(8,128)(2,1)} %p_hbm.1), custom_call_target="tpu_custom_call" | custom-call | flops 536870912 | bytes 4194304 | tf_op jit(solution)/shard_map/pallas_call | solution.py:291
  18.2 1.2 %collective-permute-done = bf16[128,256]{1,0:T(8,128)(2,1)S(1)} collective-permute-done((bf16[128,256]{1,0:T(8,128)(2,1)}, bf16[128,256]{1,0:T(8,128)(2,1)S(1)}, u32[]{:S(2)}, u32[]{:S(2)}) %collective-permute-start) | collective-permute-done | bytes 65568 | tf_op jit(solution)/shard_map/ppermute | solution.py:188
  19.4 0.0 collective-permute-done.3.refs_6_
  19.4 0.1 collective-permute-start.6
  19.5 0.1 collective-permute-start.4
  19.6 0.6 %collective-permute-start.9 = (bf16[256,256]{1,0:T(8,128)(2,1)S(1)}, bf16[256,256]{1,0:T(8,128)(2,1)S(1)}, u32[]{:S(2)}, u32[]{:S(2)}) collective-permute-start(bf16[256,256]{1,0:T(8,128)(2,1)S(1)} %constant_dynamic-update-slice_fusion.refs_0_), channel_id=1, source_target_pairs={{0,4},{1,5},{2,6},{3,7},{4,0},{5,1},{6,2},{7,3},{8,12},{9,13},{10,... | collective-permute-start | bytes 393224 | tf_op jit(solution)/shard_map/ppermute | solution.py:188
  20.2 2.0 %collective-permute-start.8 = (bf16[128,512]{1,0:T(8,128)(2,1)S(1)}, bf16[128,512]{1,0:T(8,128)(2,1)S(1)}, u32[]{:S(2)}, u32[]{:S(2)}) collective-permute-start(bf16[128,512]{1,0:T(8,128)(2,1)S(1)} %collective-permute-done.1.refs_0_), channel_id=1, source_target_pairs={{0,2},{1,3},{2,0},{3,1},{4,6},{5,7},{6,4},{7,5},{8,10},{9,11},{10,... | collective-permute-start | bytes 393224 | tf_op jit(solution)/shard_map/ppermute | solution.py:192
  22.2 1.2 %convert_add_fusion = f32[2,128,1024]{2,1,0:T(8,128)S(1)} fusion(bf16[2,128,1024]{2,1,0:T(8,128)(2,1)S(1)} %collective-permute-done.6, bf16[2,128,1024]{2,1,0:T(8,128)(2,1)} %get-tuple-element.27), kind=kLoop, calls=%fused_computation | loop fusion | flops 786432 | bytes 2097152 | tf_op jit(solution)/shard_map/add | solution.py:325
  23.4 0.2 collective-permute-start.7
  23.6 1.8 %collective-permute-done.4.refs_1_ = bf16[256,256]{1,0:T(8,128)(2,1)S(1)} collective-permute-done((bf16[256,256]{1,0:T(8,128)(2,1)S(1)}, bf16[256,256]{1,0:T(8,128)(2,1)S(1)}, u32[]{:S(2)}, u32[]{:S(2)}) %collective-permute-start.4) | collective-permute-done | bytes 131104 | tf_op jit(solution)/shard_map/ppermute | solution.py:188
  25.4 0.6 %collective-permute-done.8.refs_1_ = bf16[128,512]{1,0:T(8,128)(2,1)S(1)} collective-permute-done((bf16[128,512]{1,0:T(8,128)(2,1)S(1)}, bf16[128,512]{1,0:T(8,128)(2,1)S(1)}, u32[]{:S(2)}, u32[]{:S(2)}) %collective-permute-start.8) | collective-permute-done | bytes 131104 | tf_op jit(solution)/shard_map/ppermute | solution.py:192
  26.1 1.5 %collective-permute-start.5 = (bf16[256,256]{1,0:T(8,128)(2,1)S(1)}, bf16[256,256]{1,0:T(8,128)(2,1)S(1)}, u32[]{:S(2)}, u32[]{:S(2)}) collective-permute-start(bf16[256,256]{1,0:T(8,128)(2,1)S(1)} %collective-permute-done.4.refs_1_), channel_id=1, source_target_pairs={{0,4},{1,5},{2,6},{3,7},{4,0},{5,1},{6,2},{7,3},{8,12},{9,13},{10,... | collective-permute-start | bytes 393224 | tf_op jit(solution)/shard_map/ppermute | solution.py:188
  27.6 0.5 %shard_map.87.x_ref = bf16[512,1024]{1,0:T(8,128)(2,1)S(1)} custom-call(bf16[128,512]{1,0:T(8,128)(2,1)S(1)} %collective-permute-done.1.refs_0_, bf16[128,512]{1,0:T(8,128)(2,1)S(1)} %collective-permute-done.8.refs_1_, bf16[128,512]{1,0:T(8,128)(2,1)S(1)} %collective-permute-done.2.refs_2_, bf16[128,512]{1,0:T(8,128)(2,1)S(1)} %collective-permute-done.10.refs_3_, ...), custom_call_target="tpu_custom_call" | custom-call | bytes 2097152 | tf_op jit(solution)/shard_map/pallas_call | solution.py:223
  28.0 3.3 %collective-permute-done.7 = bf16[128,1024]{1,0:T(8,128)(2,1)S(1)} collective-permute-done((bf16[128,1024]{1,0:T(8,128)(2,1)S(1)}, bf16[128,1024]{1,0:T(8,128)(2,1)S(1)}, u32[]{:S(2)}, u32[]{:S(2)}) %collective-permute-start.7) | collective-permute-done | bytes 262176 | tf_op jit(solution)/shard_map/ppermute | solution.py:329
  31.4 0.8 %fusion.1 = bf16[128,1024]{1,0:T(8,128)(2,1)} fusion(f32[2,128,1024]{2,1,0:T(8,128)S(1)} %convert_add_fusion, bf16[128,1024]{1,0:T(8,128)(2,1)S(1)} %collective-permute-done.7), kind=kLoop, calls=%fused_computation.4 | loop fusion | flops 393216 | bytes 1048576 | tf_op jit(solution)/shard_map/convert_element_type | solution.py:330
  32.2 1.2 %shard_map.88 = f32[512,256]{1,0:T(8,128)} custom-call(bf16[512,1024]{1,0:T(8,128)(2,1)S(1)} %shard_map.87.x_ref, bf16[256,256]{1,0:T(8,128)(2,1)S(1)} %constant_dynamic-update-slice_fusion.refs_0_, bf16[256,256]{1,0:T(8,128)(2,1)S(1)} %collective-permute-done.4.refs_1_, bf16[256,256]{1,0:T(8,128)(2,1)S(1)} %collective-permute-done.9.refs_2_, ...), custom_call_target="tpu_custom_call" | custom-call | flops 268435456 | bytes 1572864 | tf_op jit(solution)/shard_map/pallas_call | solution.py:236
  (15 shorter events, 0.1 us)
Async XLA Ops:
  1.7 25.8 %copy-start = (bf16[128,4096]{1,0:T(8,128)(2,1)S(1)}, bf16[128,4096]{1,0:T(8,128)(2,1)}, u32[]{:S(2)}) copy-start(bf16[128,4096]{1,0:T(8,128)(2,1)} %refs_7_.1) | copy-start | bytes 3145732
  1.7 17.6 %collective-permute-start.1 = (bf16[128,512]{1,0:T(8,128)(2,1)S(1)}, bf16[128,512]{1,0:T(8,128)(2,1)S(1)}, u32[]{:S(2)}, u32[]{:S(2)}) collective-permute-start(bf16[128,512]{1,0:T(8,128)(2,1)S(1)} %get-tuple-element.37), channel_id=1, source_target_pairs={{0,16},{1,21},{2,26},{3,31},{4,20},{5,17},{6,30},{7,27},{8,24},{9,... | collective-permute-start | bytes 393224 | tf_op jit(solution)/shard_map/ppermute | solution.py:188
  5.8 13.5 %collective-permute-start.2 = (bf16[128,512]{1,0:T(8,128)(2,1)S(1)}, bf16[128,512]{1,0:T(8,128)(2,1)S(1)}, u32[]{:S(2)}, u32[]{:S(2)}) collective-permute-start(bf16[128,512]{1,0:T(8,128)(2,1)S(1)} %get-tuple-element.36), channel_id=1, source_target_pairs={{0,8},{1,13},{2,10},{3,15},{4,12},{5,9},{6,14},{7,11},{8,0},{9,5},... | collective-permute-start | bytes 393224 | tf_op jit(solution)/shard_map/ppermute | solution.py:188
  7.4 12.0 %collective-permute-start.3 = (bf16[128,512]{1,0:T(8,128)(2,1)S(1)}, bf16[128,512]{1,0:T(8,128)(2,1)S(1)}, u32[]{:S(2)}, u32[]{:S(2)}) collective-permute-start(bf16[128,512]{1,0:T(8,128)(2,1)S(1)} %get-tuple-element.35), channel_id=1, source_target_pairs={{0,4},{1,5},{2,6},{3,7},{4,0},{5,1},{6,2},{7,3},{8,12},{9,13},{10,... | collective-permute-start | bytes 393224 | tf_op jit(solution)/shard_map/ppermute | solution.py:188
  13.0 6.5 %copy-start.1 = (bf16[256,256]{1,0:T(8,128)(2,1)S(1)}, bf16[256,256]{1,0:T(8,128)(2,1)}, u32[]{:S(2)}) copy-start(bf16[256,256]{1,0:T(8,128)(2,1)} %get-tuple-element.25) | copy-start | bytes 393220
  13.0 6.4 %collective-permute-start = (bf16[128,256]{1,0:T(8,128)(2,1)}, bf16[128,256]{1,0:T(8,128)(2,1)S(1)}, u32[]{:S(2)}, u32[]{:S(2)}) collective-permute-start(bf16[128,256]{1,0:T(8,128)(2,1)} %get-tuple-element.20.gk_ref), channel_id=1, source_target_pairs={{0,16},{1,17},{2,18},{3,19},{4,20},{5,21},{6,22},{7,23},{8,24},{9,... | collective-permute-start | bytes 196616 | tf_op jit(solution)/shard_map/ppermute | solution.py:188
  19.4 2.8 %collective-permute-start.6 = (bf16[2,128,1024]{2,1,0:T(8,128)(2,1)}, bf16[2,128,1024]{2,1,0:T(8,128)(2,1)S(1)}, u32[]{:S(2)}, u32[]{:S(2)}) collective-permute-start(bf16[2,128,1024]{2,1,0:T(8,128)(2,1)} %get-tuple-element.28), channel_id=1, source_target_pairs={{0,1},{1,0},{2,3},{3,2},{4,5},{5,4},{6,7},{7,6},{8,9},{9,8},{10,11... | collective-permute-start | bytes 1572872 | tf_op jit(solution)/shard_map/ppermute | solution.py:192
  19.5 6.0 %collective-permute-start.4 = (bf16[256,256]{1,0:T(8,128)(2,1)S(1)}, bf16[256,256]{1,0:T(8,128)(2,1)S(1)}, u32[]{:S(2)}, u32[]{:S(2)}) collective-permute-start(bf16[256,256]{1,0:T(8,128)(2,1)S(1)} %constant_dynamic-update-slice_fusion.refs_0_), channel_id=1, source_target_pairs={{0,8},{1,9},{2,10},{3,11},{4,12},{5,13},{6,14},{7,15},{8,0},{9,1},... | collective-permute-start | bytes 393224 | tf_op jit(solution)/shard_map/ppermute | solution.py:188
  19.6 6.5 %collective-permute-start.9 = (bf16[256,256]{1,0:T(8,128)(2,1)S(1)}, bf16[256,256]{1,0:T(8,128)(2,1)S(1)}, u32[]{:S(2)}, u32[]{:S(2)}) collective-permute-start(bf16[256,256]{1,0:T(8,128)(2,1)S(1)} %constant_dynamic-update-slice_fusion.refs_0_), channel_id=1, source_target_pairs={{0,4},{1,5},{2,6},{3,7},{4,0},{5,1},{6,2},{7,3},{8,12},{9,13},{10,... | collective-permute-start | bytes 393224 | tf_op jit(solution)/shard_map/ppermute | solution.py:188
  20.2 5.9 %collective-permute-start.8 = (bf16[128,512]{1,0:T(8,128)(2,1)S(1)}, bf16[128,512]{1,0:T(8,128)(2,1)S(1)}, u32[]{:S(2)}, u32[]{:S(2)}) collective-permute-start(bf16[128,512]{1,0:T(8,128)(2,1)S(1)} %collective-permute-done.1.refs_0_), channel_id=1, source_target_pairs={{0,2},{1,3},{2,0},{3,1},{4,6},{5,7},{6,4},{7,5},{8,10},{9,11},{10,... | collective-permute-start | bytes 393224 | tf_op jit(solution)/shard_map/ppermute | solution.py:192
  23.4 8.0 %collective-permute-start.7 = (bf16[128,1024]{1,0:T(8,128)(2,1)S(1)}, bf16[128,1024]{1,0:T(8,128)(2,1)S(1)}, u32[]{:S(2)}, u32[]{:S(2)}) collective-permute-start(bf16[128,1024]{1,0:T(8,128)(2,1)S(1)} %fusion.2), channel_id=1, source_target_pairs={{0,2},{1,3},{2,0},{3,1},{4,6},{5,7},{6,4},{7,5},{8,10},{9,11},{10,... | collective-permute-start | bytes 786440 | tf_op jit(solution)/shard_map/ppermute | solution.py:329
  23.6 3.9 %collective-permute-start.10 = (bf16[128,512]{1,0:T(8,128)(2,1)S(1)}, bf16[128,512]{1,0:T(8,128)(2,1)S(1)}, u32[]{:S(2)}, u32[]{:S(2)}) collective-permute-start(bf16[128,512]{1,0:T(8,128)(2,1)S(1)} %collective-permute-done.1.refs_0_), channel_id=1, source_target_pairs={{0,1},{1,0},{2,3},{3,2},{4,5},{5,4},{6,7},{7,6},{8,9},{9,8},{10,11... | collective-permute-start | bytes 393224 | tf_op jit(solution)/shard_map/ppermute | solution.py:192
  25.4 2.1 %collective-permute-start.12 = (bf16[128,512]{1,0:T(8,128)(2,1)S(1)}, bf16[128,512]{1,0:T(8,128)(2,1)S(1)}, u32[]{:S(2)}, u32[]{:S(2)}) collective-permute-start(bf16[128,512]{1,0:T(8,128)(2,1)S(1)} %collective-permute-done.2.refs_2_), channel_id=1, source_target_pairs={{0,1},{1,0},{2,3},{3,2},{4,5},{5,4},{6,7},{7,6},{8,9},{9,8},{10,11... | collective-permute-start | bytes 393224 | tf_op jit(solution)/shard_map/ppermute | solution.py:192
  26.1 1.5 %collective-permute-start.11 = (bf16[128,512]{1,0:T(8,128)(2,1)S(1)}, bf16[128,512]{1,0:T(8,128)(2,1)S(1)}, u32[]{:S(2)}, u32[]{:S(2)}) collective-permute-start(bf16[128,512]{1,0:T(8,128)(2,1)S(1)} %collective-permute-done.8.refs_1_), channel_id=1, source_target_pairs={{0,1},{1,0},{2,3},{3,2},{4,5},{5,4},{6,7},{7,6},{8,9},{9,8},{10,11... | collective-permute-start | bytes 393224 | tf_op jit(solution)/shard_map/ppermute | solution.py:192
  26.1 6.1 %collective-permute-start.5 = (bf16[256,256]{1,0:T(8,128)(2,1)S(1)}, bf16[256,256]{1,0:T(8,128)(2,1)S(1)}, u32[]{:S(2)}, u32[]{:S(2)}) collective-permute-start(bf16[256,256]{1,0:T(8,128)(2,1)S(1)} %collective-permute-done.4.refs_1_), channel_id=1, source_target_pairs={{0,4},{1,5},{2,6},{3,7},{4,0},{5,1},{6,2},{7,3},{8,12},{9,13},{10,... | collective-permute-start | bytes 393224 | tf_op jit(solution)/shard_map/ppermute | solution.py:188

commit v14 on v13

--- a/solution.py
+++ b/solution.py
@@ -139,7 +139,7 @@
 
 
 def turned_kernel(*refs):
-    *blocks, next_ref, x_hbm, out_ref, own, sem = refs
+    *blocks, beside_ref, x_hbm, out_ref, own, sem = refs
     rows, width = own.shape
     parts = out_ref.shape[1] // rows
     far = groups = parts // 2
@@ -148,30 +148,33 @@
     copy = pltpu.make_async_copy(x_hbm.at[:, cols], own, sem)
     copy.start()
 
-    def put(k, piece):
+    def put(k, piece, at=0):
         place = far * lax.rem(k, 2) + 2 * lax.div(lax.rem(k, far), 2) + lax.div(k, far)
-        out_ref[:, pl.ds(pl.multiple_of(place * rows, rows), rows)] = piece.T
+        tokens = pl.ds(pl.multiple_of(place * rows, rows), rows)
+        out_ref[at : at + piece.shape[1], tokens] = piece.T
 
     partners = [far + (member ^ j) for j in range(0, groups, 2)]
     partners += [k + lax.rem(member, 2) for k in range(2, far, 2)]
     for k, mine, theirs in zip(partners, blocks[: len(partners)], blocks[len(partners) :]):
         put(k, mine[...])
         put(k ^ 1, theirs[...])
-    put(jnp.int32(1), next_ref[...])
+    chunk = beside_ref.shape[1]
+    for e in range(width // chunk):
+        put(jnp.int32(1), beside_ref[(2 + e) * rows : (3 + e) * rows, :], e * chunk)
     copy.wait()
     put(jnp.int32(0), own[...])
 
 
 def weights_kernel(x_ref, *refs):
     *keys, out_hbm, out, sems = refs
-    rows = keys[0].shape[0]
+    rows = x_ref.shape[1] // len(keys)
     half = x_ref.shape[0] // 2
     copies = []
     for h in range(2):
         part = slice(h * half, (h + 1) * half)
-        total = dot(x_ref[part, :rows], keys[0][...])
+        total = dot(x_ref[part, :rows], keys[0][:rows, :])
         for j in range(1, len(keys)):
-            total += dot(x_ref[part, j * rows : (j + 1) * rows], keys[j][...])
+            total += dot(x_ref[part, j * rows : (j + 1) * rows], keys[j][:rows, :])
         out[part, :] = total * (1.0 / (2 * len(keys)))
         copies.append(pltpu.make_async_copy(out.at[part, :], out_hbm.at[part, :], sems.at[h]))
         copies[h].start()
@@ -205,7 +208,7 @@
     for k in range(2, far, 2):
         sent = block(k + lax.rem(member, 2))
         near.append(along_dp(sent, lambda m, k=k: k + m % 2, parts, groups))
-    return distant, near, along_dp(block(1), lambda m: 1, parts, groups)
+    return distant, near, block(1)
 
 
 def shared_inputs(piece, groups):
@@ -217,14 +220,14 @@
     return pieces
 
 
-def turned_inputs(mine, theirs, next_inputs, inputs):
-    rows, width = next_inputs.shape
-    blocks = [*mine, *theirs, next_inputs]
+def turned_inputs(mine, theirs, beside, inputs, parts):
+    rows, width = inputs.shape[0], inputs.shape[1] // parts
+    blocks = [*mine, *theirs, beside]
     return pl.pallas_call(
         turned_kernel,
         in_specs=[IN_VMEM] * len(blocks) + [IN_HBM],
         out_specs=IN_VMEM,
-        out_shape=jax.ShapeDtypeStruct((width, inputs.shape[1] // width * rows), inputs.dtype),
+        out_shape=jax.ShapeDtypeStruct((width, parts * rows), inputs.dtype),
         scratch_shapes=[pltpu.VMEM((rows, width), inputs.dtype), pltpu.SemaphoreType.DMA],
         compiler_params=PARAMS,
         cost_estimate=cost(0, 4 * inputs.size),
@@ -263,9 +266,9 @@
     features = projections.shape[1] // groups
     kv_heads = width // HEAD_SIZE
     partial = jax.ShapeDtypeStruct((chips, rows, features), BF16)
-    exchange = parts == 2 * groups and inputs_normed.shape[1] % (parts * 128) == 0
+    exchange = parts == 2 * groups and inputs_normed.shape[1] % (parts * width) == 0
     if exchange:
-        distant, near, next_inputs = sent_inputs(inputs_normed, parts, groups)
+        distant, near, next_block = sent_inputs(inputs_normed, parts, groups)
 
     whole = pltpu.VMEM((rows, query_width), BF16)
     narrow = pltpu.VMEM((rows, width), BF16)
@@ -307,8 +310,8 @@
 
     if exchange:
         first = along_dp(grad_key, lambda m: parts // 2, parts, groups)
-        first, twice, sent, kept, distant, near, next_inputs = lax.optimization_barrier(
-            (first, twice, sent, kept, distant, near, next_inputs)
+        first, twice, sent, kept, distant, near = lax.optimization_barrier(
+            (first, twice, sent, kept, distant, near)
         )
         pieces = shared_inputs(distant, groups)
         keys = {0: lax.dynamic_update_slice(twice, first, (rows, 0))}
@@ -317,8 +320,9 @@
             for k in list(keys):
                 keys[k ^ bit] = along_dp(keys[k], lambda m, bit=bit: bit, parts, groups)
             bit //= 2
-        beside = [along_dp(keys[0], lambda m: 1, parts, groups)]
-        pieces[1:], _ = lax.optimization_barrier((pieces[1:], (beside, keys)))
+        chunks = [next_block[:, at : at + width] for at in range(0, next_block.shape[1], width)]
+        beside = [along_dp(jnp.concatenate([keys[0], *chunks]), lambda m: 1, parts, groups)]
+        pieces[1:], _ = lax.optimization_barrier((pieces[1:], keys))
         mine = pieces + near
         theirs = [along_mp(piece, 1, groups) for piece in mine]
     came = along_mp(sent, 1, groups)
@@ -332,7 +336,7 @@
     if exchange:
         for k in range(2, parts // 2, 2):
             beside.append(along_dp(keys[k], lambda m: 1, parts, groups))
-        turned = turned_inputs(mine, theirs, next_inputs, inputs_normed)
+        turned = turned_inputs(mine, theirs, beside[0], inputs_normed, parts)
         beside[-1], grad_input = lax.optimization_barrier((beside[-1], grad_input))
         keys = [keys[k] for k in range(0, parts // 2, 2)] + beside
         grad_weights = summed_weights(turned, keys)

time: 33.6 us -> 33.1 us (0.985)
  waiting for transfers between devices: 6.96 us -> 6.6 us
    ppermute x7 -> x6, waiting for transfers between devices: 2.99 us -> 5.28 us  [along_dp(): return lax.ppermute(array, ('dp', 'mp'), pairs)]
    ppermute x1, waiting for transfers between devices: 3.34 us -> 1.23 us  [body(): grad_input += lax.ppermute(total[b].astype(BF16), 'mp', shift).astype(F32)]
    ppermute x7 -> x6, starting transfers between devices: 9.73 us -> 9.18 us  [along_dp(): return lax.ppermute(array, ('dp', 'mp'), pairs)]
    ppermute x5, waiting for transfers between devices: 0.62 us -> 0.09 us  [along_mp(): return lax.ppermute(array, 'mp', [(m, m ^ bit) for m in range(groups)])]
  transfers between devices with their start and end apart: 13 -> 12, of which waited for: 4 -> 5; matrix products, arithmetic and copies ran while one was open for 6% -> 6% of each run, Pallas kernels for 28% -> 28%
where the time goes in v14:
time: 33.1 us; the launch traced here: 32.9 us
  starting transfers between devices  11.8 us (36%)
  Pallas kernels  10.6 us (32%)
  waiting for transfers between devices  6.6 us (20%)
  other arithmetic  1.99 us (6%)
  local copies, waits for them, and re-layouts  1.15 us (3%)
  between operations  0.76 us (2%)
    ppermute x6, starting transfers between devices, along_dp(): return lax.ppermute(array, ('dp', 'mp'), pairs)  9.18 us
    ppermute x6, waiting for transfers between devices, along_dp(): return lax.ppermute(array, ('dp', 'mp'), pairs)  5.28 us
    pallas_call x1, Pallas kernels, body(): pl.pallas_call(partials_kernel, in_specs=[IN_VMEM, IN_VMEM, IN_HBM], out_...  4.77 us
    pallas_call x1, Pallas kernels, body(): pl.pallas_call(attention_kernel, in_specs=[IN_HBM] * 4, out_specs=[IN_VME...  4.1 us
    ppermute x5, starting transfers between devices, along_mp(): return lax.ppermute(array, 'mp', [(m, m ^ bit) for m in range(groups)])  2.24 us
    pallas_call x1, Pallas kernels, summed_weights(): pl.pallas_call(weights_kernel, out_specs=ANYWHERE, out_shape=jax.ShapeDty...  1.24 us
    ppermute x1, waiting for transfers between devices, body(): grad_input += lax.ppermute(total[b].astype(BF16), 'mp', shift).astype(F32)  1.23 us
    add x1, other arithmetic, body(): total = kept.astype(F32) + came.astype(F32)  1.21 us
  transfers between devices with their start and end apart: 12, of which 5 were waited for; matrix products, arithmetic and copies ran while one was open for 6% of the time, Pallas kernels for 28%

profile of v14, /device:TPU:0, one launch (start us, length us, event | category | flops | bytes accessed | tf_op | source)
XLA Modules:
  0.0 32.9 jit_solution(113748032826130989)
XLA Ops:
  0.7 1.1 %constant_dynamic-slice_fusion.2 = (bf16[128,512]{1,0:T(8,128)(2,1)S(1)}, bf16[128,512]{1,0:T(8,128)(2,1)S(1)}) fusion(bf16[128,4096]{1,0:T(8,128)(2,1)} %refs_7_.1, s32[]{:T(128)S(6)} %select_n.10, s32[]{:T(128)S(6)} %select_n.9), kind=kLoop, calls=%fused_computation.10 | loop fusion | bytes 524296 | tf_op jit(solution)/shard_map/dynamic_slice | solution.py:204
  1.7 4.1 %collective-permute-start.1 = (bf16[128,512]{1,0:T(8,128)(2,1)S(1)}, bf16[128,512]{1,0:T(8,128)(2,1)S(1)}, u32[]{:S(2)}, u32[]{:S(2)}) collective-permute-start(bf16[128,512]{1,0:T(8,128)(2,1)S(1)} %get-tuple-element.36), channel_id=1, source_target_pairs={{0,16},{1,21},{2,26},{3,31},{4,20},{5,17},{6,30},{7,27},{8,24},{9,... | collective-permute-start | bytes 393224 | tf_op jit(solution)/shard_map/ppermute | solution.py:191
  5.8 1.6 %collective-permute-start.2 = (bf16[128,512]{1,0:T(8,128)(2,1)S(1)}, bf16[128,512]{1,0:T(8,128)(2,1)S(1)}, u32[]{:S(2)}, u32[]{:S(2)}) collective-permute-start(bf16[128,512]{1,0:T(8,128)(2,1)S(1)} %get-tuple-element.35), channel_id=1, source_target_pairs={{0,8},{1,13},{2,10},{3,15},{4,12},{5,9},{6,14},{7,11},{8,0},{9,5},... | collective-permute-start | bytes 393224 | tf_op jit(solution)/shard_map/ppermute | solution.py:191
  7.4 4.1 %shard_map.85 = (bf16[128,256]{1,0:T(8,128)(2,1)}, bf16[128,256]{1,0:T(8,128)(2,1)}, bf16[256,256]{1,0:T(8,128)(2,1)}, bf16[128,2048]{1,0:T(8,128)(2,1)}) custom-call(bf16[128,2048]{1,0:T(8,128)(2,1)} %q_hbm.1, bf16[128,256]{1,0:T(8,128)(2,1)} %k_hbm.1, bf16[128,256]{1,0:T(8,128)(2,1)} %v_hbm.1, bf16[128,2048]{1,0:T(8,128)(2,1)} %do_hbm.1), custom_call_target="tpu_custom_call" | custom-call | flops 335544320 | bytes 1572864 | tf_op jit(solution)/shard_map/pallas_call | solution.py:276
  11.5 0.0 copy-start.1
  11.5 0.4 %collective-permute-start = (bf16[128,256]{1,0:T(8,128)(2,1)}, bf16[128,256]{1,0:T(8,128)(2,1)S(1)}, u32[]{:S(2)}, u32[]{:S(2)}) collective-permute-start(bf16[128,256]{1,0:T(8,128)(2,1)} %get-tuple-element.19.gk_ref), channel_id=1, source_target_pairs={{0,16},{1,17},{2,18},{3,19},{4,20},{5,21},{6,22},{7,23},{8,24},{9,... | collective-permute-start | bytes 196616 | tf_op jit(solution)/shard_map/ppermute | solution.py:191
  11.9 4.8 %shard_map.86 = (bf16[2,128,1024]{2,1,0:T(8,128)(2,1)}, bf16[2,128,1024]{2,1,0:T(8,128)(2,1)}) custom-call(bf16[128,256]{1,0:T(8,128)(2,1)} %get-tuple-element.19.gk_ref, bf16[128,256]{1,0:T(8,128)(2,1)} %get-tuple-element.21.gv_ref, bf16[2,4096,256]{2,1,0:T(8,128)(2,1)} %p_hbm.1), custom_call_target="tpu_custom_call" | custom-call | flops 536870912 | bytes 4194304 | tf_op jit(solution)/shard_map/pallas_call | solution.py:294
  16.7 1.5 %collective-permute-done = bf16[128,256]{1,0:T(8,128)(2,1)S(1)} collective-permute-done((bf16[128,256]{1,0:T(8,128)(2,1)}, bf16[128,256]{1,0:T(8,128)(2,1)S(1)}, u32[]{:S(2)}, u32[]{:S(2)}) %collective-permute-start) | collective-permute-done | bytes 65568 | tf_op jit(solution)/shard_map/ppermute | solution.py:191
  18.2 0.0 collective-permute-done.2.refs_2_
  18.2 0.0 collective-permute-start.5
  18.3 0.1 collective-permute-start.3
  18.3 1.8 %collective-permute-start.7 = (bf16[128,512]{1,0:T(8,128)(2,1)S(1)}, bf16[128,512]{1,0:T(8,128)(2,1)S(1)}, u32[]{:S(2)}, u32[]{:S(2)}) collective-permute-start(bf16[128,512]{1,0:T(8,128)(2,1)S(1)} %collective-permute-done.1.refs_0_), channel_id=1, source_target_pairs={{0,2},{1,3},{2,0},{3,1},{4,6},{5,7},{6,4},{7,5},{8,10},{9,11},{10,... | collective-permute-start | bytes 393224 | tf_op jit(solution)/shard_map/ppermute | solution.py:195
  20.1 1.5 %collective-permute-start.11 = (bf16[512,256]{1,0:T(8,128)(2,1)S(1)}, bf16[512,256]{1,0:T(8,128)(2,1)S(1)}, u32[]{:S(2)}, u32[]{:S(2)}) collective-permute-start(bf16[512,256]{1,0:T(8,128)(2,1)S(1)} %pad_maximum_fusion), channel_id=1, source_target_pairs={{0,4},{1,5},{2,6},{3,7},{4,0},{5,1},{6,2},{7,3},{8,12},{9,13},{10,... | collective-permute-start | bytes 786440 | tf_op jit(solution)/shard_map/ppermute | solution.py:191
  21.7 1.2 %convert_add_fusion = f32[2,128,1024]{2,1,0:T(8,128)S(1)} fusion(bf16[2,128,1024]{2,1,0:T(8,128)(2,1)S(1)} %collective-permute-done.5, bf16[2,128,1024]{2,1,0:T(8,128)(2,1)} %get-tuple-element.26), kind=kLoop, calls=%fused_computation | loop fusion | flops 786432 | bytes 2097152 | tf_op jit(solution)/shard_map/add | solution.py:329
  22.9 0.4 %collective-permute-start.6 = (bf16[128,1024]{1,0:T(8,128)(2,1)S(1)}, bf16[128,1024]{1,0:T(8,128)(2,1)S(1)}, u32[]{:S(2)}, u32[]{:S(2)}) collective-permute-start(bf16[128,1024]{1,0:T(8,128)(2,1)S(1)} %fusion.2), channel_id=1, source_target_pairs={{0,2},{1,3},{2,0},{3,1},{4,6},{5,7},{6,4},{7,5},{8,10},{9,11},{10,... | collective-permute-start | bytes 786440 | tf_op jit(solution)/shard_map/ppermute | solution.py:333
  23.3 0.9 %collective-permute-done.3.refs_1_ = bf16[256,256]{1,0:T(8,128)(2,1)S(1)} collective-permute-done((bf16[256,256]{1,0:T(8,128)(2,1)S(1)}, bf16[256,256]{1,0:T(8,128)(2,1)S(1)}, u32[]{:S(2)}, u32[]{:S(2)}) %collective-permute-start.3) | collective-permute-done | bytes 131104 | tf_op jit(solution)/shard_map/ppermute | solution.py:191
  24.2 0.1 collective-permute-done.7.refs_1_
  24.3 0.4 %collective-permute-start.9 = (bf16[128,512]{1,0:T(8,128)(2,1)S(1)}, bf16[128,512]{1,0:T(8,128)(2,1)S(1)}, u32[]{:S(2)}, u32[]{:S(2)}) collective-permute-start(bf16[128,512]{1,0:T(8,128)(2,1)S(1)} %collective-permute-done.7.refs_1_), channel_id=1, source_target_pairs={{0,1},{1,0},{2,3},{3,2},{4,5},{5,4},{6,7},{7,6},{8,9},{9,8},{10,11... | collective-permute-start | bytes 393224 | tf_op jit(solution)/shard_map/ppermute | solution.py:195
  24.7 1.5 %collective-permute-start.4 = (bf16[256,256]{1,0:T(8,128)(2,1)S(1)}, bf16[256,256]{1,0:T(8,128)(2,1)S(1)}, u32[]{:S(2)}, u32[]{:S(2)}) collective-permute-start(bf16[256,256]{1,0:T(8,128)(2,1)S(1)} %collective-permute-done.3.refs_1_), channel_id=1, source_target_pairs={{0,4},{1,5},{2,6},{3,7},{4,0},{5,1},{6,2},{7,3},{8,12},{9,13},{10,... | collective-permute-start | bytes 393224 | tf_op jit(solution)/shard_map/ppermute | solution.py:191
  26.2 2.9 %collective-permute-done.11.refs_6_.refs_2_ = bf16[512,256]{1,0:T(8,128)(2,1)S(1)} collective-permute-done((bf16[512,256]{1,0:T(8,128)(2,1)S(1)}, bf16[512,256]{1,0:T(8,128)(2,1)S(1)}, u32[]{:S(2)}, u32[]{:S(2)}) %collective-permute-start.11) | collective-permute-done | bytes 262176 | tf_op jit(solution)/shard_map/ppermute | solution.py:191
  29.2 0.5 %shard_map.87.x_ref = bf16[512,1024]{1,0:T(8,128)(2,1)S(1)} custom-call(bf16[128,512]{1,0:T(8,128)(2,1)S(1)} %collective-permute-done.1.refs_0_, bf16[128,512]{1,0:T(8,128)(2,1)S(1)} %collective-permute-done.7.refs_1_, bf16[128,512]{1,0:T(8,128)(2,1)S(1)} %collective-permute-done.2.refs_2_, bf16[128,512]{1,0:T(8,128)(2,1)S(1)} %collective-permute-done.8.refs_3_, ...), custom_call_target="tpu_custom_call" | custom-call | bytes 2097152 | tf_op jit(solution)/shard_map/pallas_call | solution.py:226
  29.6 1.2 %collective-permute-done.6 = bf16[128,1024]{1,0:T(8,128)(2,1)S(1)} collective-permute-done((bf16[128,1024]{1,0:T(8,128)(2,1)S(1)}, bf16[128,1024]{1,0:T(8,128)(2,1)S(1)}, u32[]{:S(2)}, u32[]{:S(2)}) %collective-permute-start.6) | collective-permute-done | bytes 262176 | tf_op jit(solution)/shard_map/ppermute | solution.py:333
  30.9 0.8 %fusion.1 = bf16[128,1024]{1,0:T(8,128)(2,1)} fusion(f32[2,128,1024]{2,1,0:T(8,128)S(1)} %convert_add_fusion, bf16[128,1024]{1,0:T(8,128)(2,1)S(1)} %collective-permute-done.6), kind=kLoop, calls=%fused_computation.4 | loop fusion | flops 393216 | bytes 1048576 | tf_op jit(solution)/shard_map/convert_element_type | solution.py:334
  31.6 1.2 %shard_map.88 = f32[512,256]{1,0:T(8,128)} custom-call(bf16[512,1024]{1,0:T(8,128)(2,1)S(1)} %shard_map.87.x_ref, bf16[256,256]{1,0:T(8,128)(2,1)S(1)} %constant_dynamic-update-slice_fusion.refs_0_, bf16[256,256]{1,0:T(8,128)(2,1)S(1)} %collective-permute-done.3.refs_1_, bf16[512,256]{1,0:T(8,128)(2,1)S(1)} %collective-permute-done.11.refs_6_.refs_2_, ...), custom_call_target="tpu_custom_call" | custom-call | flops 268435456 | bytes 1572864 | tf_op jit(solution)/shard_map/pallas_call | solution.py:239
  (15 shorter events, 0.1 us)
Async XLA Ops:
  0.6 17.6 %copy-start = (bf16[128,4096]{1,0:T(8,128)(2,1)S(1)}, bf16[128,4096]{1,0:T(8,128)(2,1)}, u32[]{:S(2)}) copy-start(bf16[128,4096]{1,0:T(8,128)(2,1)} %refs_7_.1) | copy-start | bytes 3145732
  1.7 16.4 %collective-permute-start.1 = (bf16[128,512]{1,0:T(8,128)(2,1)S(1)}, bf16[128,512]{1,0:T(8,128)(2,1)S(1)}, u32[]{:S(2)}, u32[]{:S(2)}) collective-permute-start(bf16[128,512]{1,0:T(8,128)(2,1)S(1)} %get-tuple-element.36), channel_id=1, source_target_pairs={{0,16},{1,21},{2,26},{3,31},{4,20},{5,17},{6,30},{7,27},{8,24},{9,... | collective-permute-start | bytes 393224 | tf_op jit(solution)/shard_map/ppermute | solution.py:191
  5.8 12.3 %collective-permute-start.2 = (bf16[128,512]{1,0:T(8,128)(2,1)S(1)}, bf16[128,512]{1,0:T(8,128)(2,1)S(1)}, u32[]{:S(2)}, u32[]{:S(2)}) collective-permute-start(bf16[128,512]{1,0:T(8,128)(2,1)S(1)} %get-tuple-element.35), channel_id=1, source_target_pairs={{0,8},{1,13},{2,10},{3,15},{4,12},{5,9},{6,14},{7,11},{8,0},{9,5},... | collective-permute-start | bytes 393224 | tf_op jit(solution)/shard_map/ppermute | solution.py:191
  11.5 6.7 %copy-start.1 = (bf16[256,256]{1,0:T(8,128)(2,1)S(1)}, bf16[256,256]{1,0:T(8,128)(2,1)}, u32[]{:S(2)}) copy-start(bf16[256,256]{1,0:T(8,128)(2,1)} %get-tuple-element.24) | copy-start | bytes 393220
  11.5 6.6 %collective-permute-start = (bf16[128,256]{1,0:T(8,128)(2,1)}, bf16[128,256]{1,0:T(8,128)(2,1)S(1)}, u32[]{:S(2)}, u32[]{:S(2)}) collective-permute-start(bf16[128,256]{1,0:T(8,128)(2,1)} %get-tuple-element.19.gk_ref), channel_id=1, source_target_pairs={{0,16},{1,17},{2,18},{3,19},{4,20},{5,21},{6,22},{7,23},{8,24},{9,... | collective-permute-start | bytes 196616 | tf_op jit(solution)/shard_map/ppermute | solution.py:191
  18.2 3.5 %collective-permute-start.5 = (bf16[2,128,1024]{2,1,0:T(8,128)(2,1)}, bf16[2,128,1024]{2,1,0:T(8,128)(2,1)S(1)}, u32[]{:S(2)}, u32[]{:S(2)}) collective-permute-start(bf16[2,128,1024]{2,1,0:T(8,128)(2,1)} %get-tuple-element.27), channel_id=1, source_target_pairs={{0,1},{1,0},{2,3},{3,2},{4,5},{5,4},{6,7},{7,6},{8,9},{9,8},{10,11... | collective-permute-start | bytes 1572872 | tf_op jit(solution)/shard_map/ppermute | solution.py:195
  18.3 5.9 %collective-permute-start.3 = (bf16[256,256]{1,0:T(8,128)(2,1)S(1)}, bf16[256,256]{1,0:T(8,128)(2,1)S(1)}, u32[]{:S(2)}, u32[]{:S(2)}) collective-permute-start(bf16[256,256]{1,0:T(8,128)(2,1)S(1)} %constant_dynamic-update-slice_fusion.refs_0_), channel_id=1, source_target_pairs={{0,8},{1,9},{2,10},{3,11},{4,12},{5,13},{6,14},{7,15},{8,0},{9,1},... | collective-permute-start | bytes 393224 | tf_op jit(solution)/shard_map/ppermute | solution.py:191
  18.3 5.9 %collective-permute-start.7 = (bf16[128,512]{1,0:T(8,128)(2,1)S(1)}, bf16[128,512]{1,0:T(8,128)(2,1)S(1)}, u32[]{:S(2)}, u32[]{:S(2)}) collective-permute-start(bf16[128,512]{1,0:T(8,128)(2,1)S(1)} %collective-permute-done.1.refs_0_), channel_id=1, source_target_pairs={{0,2},{1,3},{2,0},{3,1},{4,6},{5,7},{6,4},{7,5},{8,10},{9,11},{10,... | collective-permute-start | bytes 393224 | tf_op jit(solution)/shard_map/ppermute | solution.py:195
  20.1 9.0 %collective-permute-start.11 = (bf16[512,256]{1,0:T(8,128)(2,1)S(1)}, bf16[512,256]{1,0:T(8,128)(2,1)S(1)}, u32[]{:S(2)}, u32[]{:S(2)}) collective-permute-start(bf16[512,256]{1,0:T(8,128)(2,1)S(1)} %pad_maximum_fusion), channel_id=1, source_target_pairs={{0,4},{1,5},{2,6},{3,7},{4,0},{5,1},{6,2},{7,3},{8,12},{9,13},{10,... | collective-permute-start | bytes 786440 | tf_op jit(solution)/shard_map/ppermute | solution.py:191
  22.9 7.9 %collective-permute-start.6 = (bf16[128,1024]{1,0:T(8,128)(2,1)S(1)}, bf16[128,1024]{1,0:T(8,128)(2,1)S(1)}, u32[]{:S(2)}, u32[]{:S(2)}) collective-permute-start(bf16[128,1024]{1,0:T(8,128)(2,1)S(1)} %fusion.2), channel_id=1, source_target_pairs={{0,2},{1,3},{2,0},{3,1},{4,6},{5,7},{6,4},{7,5},{8,10},{9,11},{10,... | collective-permute-start | bytes 786440 | tf_op jit(solution)/shard_map/ppermute | solution.py:333
  23.3 1.4 %collective-permute-start.8 = (bf16[128,512]{1,0:T(8,128)(2,1)S(1)}, bf16[128,512]{1,0:T(8,128)(2,1)S(1)}, u32[]{:S(2)}, u32[]{:S(2)}) collective-permute-start(bf16[128,512]{1,0:T(8,128)(2,1)S(1)} %collective-permute-done.1.refs_0_), channel_id=1, source_target_pairs={{0,1},{1,0},{2,3},{3,2},{4,5},{5,4},{6,7},{7,6},{8,9},{9,8},{10,11... | collective-permute-start | bytes 393224 | tf_op jit(solution)/shard_map/ppermute | solution.py:195
  24.2 2.0 %collective-permute-start.10 = (bf16[128,512]{1,0:T(8,128)(2,1)S(1)}, bf16[128,512]{1,0:T(8,128)(2,1)S(1)}, u32[]{:S(2)}, u32[]{:S(2)}) collective-permute-start(bf16[128,512]{1,0:T(8,128)(2,1)S(1)} %collective-permute-done.2.refs_2_), channel_id=1, source_target_pairs={{0,1},{1,0},{2,3},{3,2},{4,5},{5,4},{6,7},{7,6},{8,9},{9,8},{10,11... | collective-permute-start | bytes 393224 | tf_op jit(solution)/shard_map/ppermute | solution.py:195
  24.3 1.9 %collective-permute-start.9 = (bf16[128,512]{1,0:T(8,128)(2,1)S(1)}, bf16[128,512]{1,0:T(8,128)(2,1)S(1)}, u32[]{:S(2)}, u32[]{:S(2)}) collective-permute-start(bf16[128,512]{1,0:T(8,128)(2,1)S(1)} %collective-permute-done.7.refs_1_), channel_id=1, source_target_pairs={{0,1},{1,0},{2,3},{3,2},{4,5},{5,4},{6,7},{7,6},{8,9},{9,8},{10,11... | collective-permute-start | bytes 393224 | tf_op jit(solution)/shard_map/ppermute | solution.py:195
  24.7 6.9 %collective-permute-start.4 = (bf16[256,256]{1,0:T(8,128)(2,1)S(1)}, bf16[256,256]{1,0:T(8,128)(2,1)S(1)}, u32[]{:S(2)}, u32[]{:S(2)}) collective-permute-start(bf16[256,256]{1,0:T(8,128)(2,1)S(1)} %collective-permute-done.3.refs_1_), channel_id=1, source_target_pairs={{0,4},{1,5},{2,6},{3,7},{4,0},{5,1},{6,2},{7,3},{8,12},{9,13},{10,... | collective-permute-start | bytes 393224 | tf_op jit(solution)/shard_map/ppermute | solution.py:191

commit v15 on v14

--- a/solution.py
+++ b/solution.py
@@ -1,3 +1,4 @@
+import functools
 import math
 
 import jax
@@ -166,16 +167,22 @@
 
 
 def weights_kernel(x_ref, *refs):
-    *keys, out_hbm, out, sems = refs
-    rows = x_ref.shape[1] // len(keys)
+    *keys, out_ref = refs
+    rows = x_ref.shape[1] // (len(keys) + 1)
+    total = dot(x_ref[:, :rows], keys[0][:rows, :])
+    for j in range(1, len(keys)):
+        total += dot(x_ref[:, j * rows : (j + 1) * rows], keys[j][:rows, :])
+    out_ref[...] = total
+
+
+def last_kernel(parts, x_ref, sum_ref, key_ref, out_hbm, out, sems):
+    rows = key_ref.shape[0]
     half = x_ref.shape[0] // 2
     copies = []
     for h in range(2):
         part = slice(h * half, (h + 1) * half)
-        total = dot(x_ref[part, :rows], keys[0][:rows, :])
-        for j in range(1, len(keys)):
-            total += dot(x_ref[part, j * rows : (j + 1) * rows], keys[j][:rows, :])
-        out[part, :] = total * (1.0 / (2 * len(keys)))
+        done = sum_ref[part, :] + dot(x_ref[part, x_ref.shape[1] - rows :], key_ref[...])
+        out[part, :] = done * (1.0 / parts)
         copies.append(pltpu.make_async_copy(out.at[part, :], out_hbm.at[part, :], sems.at[h]))
         copies[h].start()
     for copy in copies:
@@ -234,18 +241,26 @@
     )(*blocks, inputs)
 
 
-def summed_weights(turned, keys):
+def summed_weights(turned, keys, parts):
     width, columns = turned.shape[0], keys[0].shape[1]
-    return pl.pallas_call(
+    weights = jax.ShapeDtypeStruct((width, columns), F32)
+    most = pl.pallas_call(
         weights_kernel,
-        out_specs=ANYWHERE,
-        out_shape=jax.ShapeDtypeStruct((width, columns), F32),
-        scratch_shapes=[pltpu.VMEM((width, columns), F32), pltpu.SemaphoreType.DMA((2,))],
+        out_specs=IN_VMEM,
+        out_shape=weights,
         compiler_params=PARAMS,
         cost_estimate=cost(
             2 * turned.size * columns, 2 * turned.size + 4 * width * columns
         ),
-    )(turned, *keys)
+    )(turned, *keys[:-1])
+    return pl.pallas_call(
+        functools.partial(last_kernel, parts),
+        out_specs=ANYWHERE,
+        out_shape=weights,
+        scratch_shapes=[pltpu.VMEM(weights.shape, F32), pltpu.SemaphoreType.DMA((2,))],
+        compiler_params=PARAMS,
+        cost_estimate=cost(2 * width * columns * keys[-1].shape[0], 8 * width * columns),
+    )(turned, most, keys[-1])
 
 
 def gathered_weights(inputs, grad_key, parts):
@@ -339,7 +354,7 @@
         turned = turned_inputs(mine, theirs, beside[0], inputs_normed, parts)
         beside[-1], grad_input = lax.optimization_barrier((beside[-1], grad_input))
         keys = [keys[k] for k in range(0, parts // 2, 2)] + beside
-        grad_weights = summed_weights(turned, keys)
+        grad_weights = summed_weights(turned, keys, parts)
     else:
         grad_weights = gathered_weights(inputs_normed, grad_key, parts)
     return (grad_query, grad_input, grad_weights)

time: 33.1 us -> 32.9 us (level)
  waiting for transfers between devices: 6.6 us -> 6.22 us
    ppermute x1, waiting for transfers between devices: 1.23 us -> 0.85 us  [body(): grad_input += lax.ppermute(total[b].astype(BF16), 'mp', shift).astype(F32)]
    pallas_call x1 -> x2, Pallas kernels: 1.24 us -> 1.41 us  [the longest x1 1.04 us: summed_weights(): pl.pallas_call(functools.partial(last_kernel, parts), out_specs=ANYWHERE,...]
  transfers between devices with their start and end apart: 12 -> 12, of which waited for: 5 -> 5; matrix products, arithmetic and copies ran while one was open for 6% -> 6% of each run, Pallas kernels for 28% -> 30%
where the time goes in v15:
time: 32.9 us; the launch traced here: 32.7 us
  starting transfers between devices  11.8 us (36%)
  Pallas kernels  10.7 us (33%)
  waiting for transfers between devices  6.22 us (19%)
  other arithmetic  1.99 us (6%)
  local copies, waits for them, and re-layouts  1.15 us (3%)
  between operations  0.77 us (2%)
    ppermute x6, starting transfers between devices, along_dp(): return lax.ppermute(array, ('dp', 'mp'), pairs)  9.18 us
    ppermute x6, waiting for transfers between devices, along_dp(): return lax.ppermute(array, ('dp', 'mp'), pairs)  5.28 us
    pallas_call x1, Pallas kernels, body(): pl.pallas_call(partials_kernel, in_specs=[IN_VMEM, IN_VMEM, IN_HBM], out_...  4.77 us
    pallas_call x1, Pallas kernels, body(): pl.pallas_call(attention_kernel, in_specs=[IN_HBM] * 4, out_specs=[IN_VME...  4.1 us
    ppermute x5, starting transfers between devices, along_mp(): return lax.ppermute(array, 'mp', [(m, m ^ bit) for m in range(groups)])  2.24 us
    add x1, other arithmetic, body(): total = kept.astype(F32) + came.astype(F32)  1.21 us
    dynamic_slice x1, local copies, waits for them, and re-layouts, block(): return lax.dynamic_slice(inputs, (0, (part ^ k) * width), (rows, width))  1.07 us
    pallas_call x1, Pallas kernels, summed_weights(): pl.pallas_call(functools.partial(last_kernel, parts), out_specs=ANYWHERE,...  1.04 us
  transfers between devices with their start and end apart: 12, of which 5 were waited for; matrix products, arithmetic and copies ran while one was open for 6% of the time, Pallas kernels for 30%

profile of v15, /device:TPU:0, one launch (start us, length us, event | category | flops | bytes accessed | tf_op | source)
XLA Modules:
  0.0 32.7 jit_solution(9032182278290725608)
XLA Ops:
  0.7 1.1 %constant_dynamic-slice_fusion.2 = (bf16[128,512]{1,0:T(8,128)(2,1)S(1)}, bf16[128,512]{1,0:T(8,128)(2,1)S(1)}) fusion(bf16[128,4096]{1,0:T(8,128)(2,1)} %refs_7_.1, s32[]{:T(128)S(6)} %select_n.10, s32[]{:T(128)S(6)} %select_n.9), kind=kLoop, calls=%fused_computation.10 | loop fusion | bytes 524296 | tf_op jit(solution)/shard_map/dynamic_slice | solution.py:211
  1.7 4.1 %collective-permute-start.1 = (bf16[128,512]{1,0:T(8,128)(2,1)S(1)}, bf16[128,512]{1,0:T(8,128)(2,1)S(1)}, u32[]{:S(2)}, u32[]{:S(2)}) collective-permute-start(bf16[128,512]{1,0:T(8,128)(2,1)S(1)} %get-tuple-element.36), channel_id=1, source_target_pairs={{0,16},{1,21},{2,26},{3,31},{4,20},{5,17},{6,30},{7,27},{8,24},{9,... | collective-permute-start | bytes 393224 | tf_op jit(solution)/shard_map/ppermute | solution.py:198
  5.8 1.6 %collective-permute-start.2 = (bf16[128,512]{1,0:T(8,128)(2,1)S(1)}, bf16[128,512]{1,0:T(8,128)(2,1)S(1)}, u32[]{:S(2)}, u32[]{:S(2)}) collective-permute-start(bf16[128,512]{1,0:T(8,128)(2,1)S(1)} %get-tuple-element.35), channel_id=1, source_target_pairs={{0,8},{1,13},{2,10},{3,15},{4,12},{5,9},{6,14},{7,11},{8,0},{9,5},... | collective-permute-start | bytes 393224 | tf_op jit(solution)/shard_map/ppermute | solution.py:198
  7.4 4.1 %shard_map.85 = (bf16[128,256]{1,0:T(8,128)(2,1)}, bf16[128,256]{1,0:T(8,128)(2,1)}, bf16[256,256]{1,0:T(8,128)(2,1)}, bf16[128,2048]{1,0:T(8,128)(2,1)}) custom-call(bf16[128,2048]{1,0:T(8,128)(2,1)} %q_hbm.1, bf16[128,256]{1,0:T(8,128)(2,1)} %k_hbm.1, bf16[128,256]{1,0:T(8,128)(2,1)} %v_hbm.1, bf16[128,2048]{1,0:T(8,128)(2,1)} %do_hbm.1), custom_call_target="tpu_custom_call" | custom-call | flops 335544320 | bytes 1572864 | tf_op jit(solution)/shard_map/pallas_call | solution.py:291
  11.5 0.0 copy-start.1
  11.5 0.4 %collective-permute-start = (bf16[128,256]{1,0:T(8,128)(2,1)}, bf16[128,256]{1,0:T(8,128)(2,1)S(1)}, u32[]{:S(2)}, u32[]{:S(2)}) collective-permute-start(bf16[128,256]{1,0:T(8,128)(2,1)} %get-tuple-element.19.gk_ref), channel_id=1, source_target_pairs={{0,16},{1,17},{2,18},{3,19},{4,20},{5,21},{6,22},{7,23},{8,24},{9,... | collective-permute-start | bytes 196616 | tf_op jit(solution)/shard_map/ppermute | solution.py:198
  11.9 4.8 %shard_map.86 = (bf16[2,128,1024]{2,1,0:T(8,128)(2,1)}, bf16[2,128,1024]{2,1,0:T(8,128)(2,1)}) custom-call(bf16[128,256]{1,0:T(8,128)(2,1)} %get-tuple-element.19.gk_ref, bf16[128,256]{1,0:T(8,128)(2,1)} %get-tuple-element.21.gv_ref, bf16[2,4096,256]{2,1,0:T(8,128)(2,1)} %p_hbm.1), custom_call_target="tpu_custom_call" | custom-call | flops 536870912 | bytes 4194304 | tf_op jit(solution)/shard_map/pallas_call | solution.py:309
  16.7 1.5 %collective-permute-done = bf16[128,256]{1,0:T(8,128)(2,1)S(1)} collective-permute-done((bf16[128,256]{1,0:T(8,128)(2,1)}, bf16[128,256]{1,0:T(8,128)(2,1)S(1)}, u32[]{:S(2)}, u32[]{:S(2)}) %collective-permute-start) | collective-permute-done | bytes 65568 | tf_op jit(solution)/shard_map/ppermute | solution.py:198
  18.2 0.0 collective-permute-start.5
  18.3 0.1 collective-permute-start.3
  18.3 1.8 %collective-permute-start.7 = (bf16[128,512]{1,0:T(8,128)(2,1)S(1)}, bf16[128,512]{1,0:T(8,128)(2,1)S(1)}, u32[]{:S(2)}, u32[]{:S(2)}) collective-permute-start(bf16[128,512]{1,0:T(8,128)(2,1)S(1)} %collective-permute-done.1.refs_0_), channel_id=1, source_target_pairs={{0,2},{1,3},{2,0},{3,1},{4,6},{5,7},{6,4},{7,5},{8,10},{9,11},{10,... | collective-permute-start | bytes 393224 | tf_op jit(solution)/shard_map/ppermute | solution.py:202
  20.1 1.5 %collective-permute-start.11 = (bf16[512,256]{1,0:T(8,128)(2,1)S(1)}, bf16[512,256]{1,0:T(8,128)(2,1)S(1)}, u32[]{:S(2)}, u32[]{:S(2)}) collective-permute-start(bf16[512,256]{1,0:T(8,128)(2,1)S(1)} %pad_maximum_fusion), channel_id=1, source_target_pairs={{0,4},{1,5},{2,6},{3,7},{4,0},{5,1},{6,2},{7,3},{8,12},{9,13},{10,... | collective-permute-start | bytes 786440 | tf_op jit(solution)/shard_map/ppermute | solution.py:198
  21.7 1.2 %convert_add_fusion = f32[2,128,1024]{2,1,0:T(8,128)S(1)} fusion(bf16[2,128,1024]{2,1,0:T(8,128)(2,1)S(1)} %collective-permute-done.5, bf16[2,128,1024]{2,1,0:T(8,128)(2,1)} %get-tuple-element.26), kind=kLoop, calls=%fused_computation | loop fusion | flops 786432 | bytes 2097152 | tf_op jit(solution)/shard_map/add | solution.py:344
  22.9 0.4 %collective-permute-start.6 = (bf16[128,1024]{1,0:T(8,128)(2,1)S(1)}, bf16[128,1024]{1,0:T(8,128)(2,1)S(1)}, u32[]{:S(2)}, u32[]{:S(2)}) collective-permute-start(bf16[128,1024]{1,0:T(8,128)(2,1)S(1)} %fusion.2), channel_id=1, source_target_pairs={{0,2},{1,3},{2,0},{3,1},{4,6},{5,7},{6,4},{7,5},{8,10},{9,11},{10,... | collective-permute-start | bytes 786440 | tf_op jit(solution)/shard_map/ppermute | solution.py:348
  23.3 0.9 %collective-permute-done.3.refs_1_ = bf16[256,256]{1,0:T(8,128)(2,1)S(1)} collective-permute-done((bf16[256,256]{1,0:T(8,128)(2,1)S(1)}, bf16[256,256]{1,0:T(8,128)(2,1)S(1)}, u32[]{:S(2)}, u32[]{:S(2)}) %collective-permute-start.3) | collective-permute-done | bytes 131104 | tf_op jit(solution)/shard_map/ppermute | solution.py:198
  24.2 0.1 collective-permute-done.7.refs_1_
  24.3 0.4 %collective-permute-start.9 = (bf16[128,512]{1,0:T(8,128)(2,1)S(1)}, bf16[128,512]{1,0:T(8,128)(2,1)S(1)}, u32[]{:S(2)}, u32[]{:S(2)}) collective-permute-start(bf16[128,512]{1,0:T(8,128)(2,1)S(1)} %collective-permute-done.7.refs_1_), channel_id=1, source_target_pairs={{0,1},{1,0},{2,3},{3,2},{4,5},{5,4},{6,7},{7,6},{8,9},{9,8},{10,11... | collective-permute-start | bytes 393224 | tf_op jit(solution)/shard_map/ppermute | solution.py:202
  24.7 1.5 %collective-permute-start.4 = (bf16[256,256]{1,0:T(8,128)(2,1)S(1)}, bf16[256,256]{1,0:T(8,128)(2,1)S(1)}, u32[]{:S(2)}, u32[]{:S(2)}) collective-permute-start(bf16[256,256]{1,0:T(8,128)(2,1)S(1)} %collective-permute-done.3.refs_1_), channel_id=1, source_target_pairs={{0,4},{1,5},{2,6},{3,7},{4,0},{5,1},{6,2},{7,3},{8,12},{9,13},{10,... | collective-permute-start | bytes 393224 | tf_op jit(solution)/shard_map/ppermute | solution.py:198
  26.2 2.9 %collective-permute-done.11.refs_6_.refs_2_ = bf16[512,256]{1,0:T(8,128)(2,1)S(1)} collective-permute-done((bf16[512,256]{1,0:T(8,128)(2,1)S(1)}, bf16[512,256]{1,0:T(8,128)(2,1)S(1)}, u32[]{:S(2)}, u32[]{:S(2)}) %collective-permute-start.11) | collective-permute-done | bytes 262176 | tf_op jit(solution)/shard_map/ppermute | solution.py:198
  29.2 0.5 %shard_map.87.x_ref = bf16[512,1024]{1,0:T(8,128)(2,1)S(1)} custom-call(bf16[128,512]{1,0:T(8,128)(2,1)S(1)} %collective-permute-done.1.refs_0_, bf16[128,512]{1,0:T(8,128)(2,1)S(1)} %collective-permute-done.7.refs_1_, bf16[128,512]{1,0:T(8,128)(2,1)S(1)} %collective-permute-done.2.refs_2_, bf16[128,512]{1,0:T(8,128)(2,1)S(1)} %collective-permute-done.8.refs_3_, ...), custom_call_target="tpu_custom_call" | custom-call | bytes 2097152 | tf_op jit(solution)/shard_map/pallas_call | solution.py:233
  29.6 0.4 %shard_map.88.sum_ref = f32[512,256]{1,0:T(8,128)S(1)} custom-call(bf16[512,1024]{1,0:T(8,128)(2,1)S(1)} %shard_map.87.x_ref, bf16[256,256]{1,0:T(8,128)(2,1)S(1)} %constant_dynamic-update-slice_fusion.refs_0_, bf16[256,256]{1,0:T(8,128)(2,1)S(1)} %collective-permute-done.3.refs_1_, bf16[512,256]{1,0:T(8,128)(2,1)S(1)} %collective-permute-done.11.refs_6_.refs_2_), custom_call_target="tpu_custom_call" | custom-call | flops 268435456 | bytes 1572864 | tf_op jit(solution)/shard_map/pallas_call | solution.py:247
  30.0 0.9 %collective-permute-done.6 = bf16[128,1024]{1,0:T(8,128)(2,1)S(1)} collective-permute-done((bf16[128,1024]{1,0:T(8,128)(2,1)S(1)}, bf16[128,1024]{1,0:T(8,128)(2,1)S(1)}, u32[]{:S(2)}, u32[]{:S(2)}) %collective-permute-start.6) | collective-permute-done | bytes 262176 | tf_op jit(solution)/shard_map/ppermute | solution.py:348
  30.9 0.8 %fusion.1 = bf16[128,1024]{1,0:T(8,128)(2,1)} fusion(f32[2,128,1024]{2,1,0:T(8,128)S(1)} %convert_add_fusion, bf16[128,1024]{1,0:T(8,128)(2,1)S(1)} %collective-permute-done.6), kind=kLoop, calls=%fused_computation.4 | loop fusion | flops 393216 | bytes 1048576 | tf_op jit(solution)/shard_map/convert_element_type | solution.py:349
  31.6 1.0 %shard_map.89 = f32[512,256]{1,0:T(8,128)} custom-call(bf16[512,1024]{1,0:T(8,128)(2,1)S(1)} %shard_map.87.x_ref, f32[512,256]{1,0:T(8,128)S(1)} %shard_map.88.sum_ref, bf16[256,256]{1,0:T(8,128)(2,1)S(1)} %collective-permute-done.4.key_ref), custom_call_target="tpu_custom_call" | custom-call | flops 67108864 | bytes 1048576 | tf_op jit(solution)/shard_map/pallas_call | solution.py:256
  (16 shorter events, 0.1 us)
Async XLA Ops:
  0.6 17.6 %copy-start = (bf16[128,4096]{1,0:T(8,128)(2,1)S(1)}, bf16[128,4096]{1,0:T(8,128)(2,1)}, u32[]{:S(2)}) copy-start(bf16[128,4096]{1,0:T(8,128)(2,1)} %refs_7_.1) | copy-start | bytes 3145732
  1.7 16.4 %collective-permute-start.1 = (bf16[128,512]{1,0:T(8,128)(2,1)S(1)}, bf16[128,512]{1,0:T(8,128)(2,1)S(1)}, u32[]{:S(2)}, u32[]{:S(2)}) collective-permute-start(bf16[128,512]{1,0:T(8,128)(2,1)S(1)} %get-tuple-element.36), channel_id=1, source_target_pairs={{0,16},{1,21},{2,26},{3,31},{4,20},{5,17},{6,30},{7,27},{8,24},{9,... | collective-permute-start | bytes 393224 | tf_op jit(solution)/shard_map/ppermute | solution.py:198
  5.8 12.3 %collective-permute-start.2 = (bf16[128,512]{1,0:T(8,128)(2,1)S(1)}, bf16[128,512]{1,0:T(8,128)(2,1)S(1)}, u32[]{:S(2)}, u32[]{:S(2)}) collective-permute-start(bf16[128,512]{1,0:T(8,128)(2,1)S(1)} %get-tuple-element.35), channel_id=1, source_target_pairs={{0,8},{1,13},{2,10},{3,15},{4,12},{5,9},{6,14},{7,11},{8,0},{9,5},... | collective-permute-start | bytes 393224 | tf_op jit(solution)/shard_map/ppermute | solution.py:198
  11.5 6.7 %copy-start.1 = (bf16[256,256]{1,0:T(8,128)(2,1)S(1)}, bf16[256,256]{1,0:T(8,128)(2,1)}, u32[]{:S(2)}) copy-start(bf16[256,256]{1,0:T(8,128)(2,1)} %get-tuple-element.24) | copy-start | bytes 393220
  11.5 6.6 %collective-permute-start = (bf16[128,256]{1,0:T(8,128)(2,1)}, bf16[128,256]{1,0:T(8,128)(2,1)S(1)}, u32[]{:S(2)}, u32[]{:S(2)}) collective-permute-start(bf16[128,256]{1,0:T(8,128)(2,1)} %get-tuple-element.19.gk_ref), channel_id=1, source_target_pairs={{0,16},{1,17},{2,18},{3,19},{4,20},{5,21},{6,22},{7,23},{8,24},{9,... | collective-permute-start | bytes 196616 | tf_op jit(solution)/shard_map/ppermute | solution.py:198
  18.2 3.5 %collective-permute-start.5 = (bf16[2,128,1024]{2,1,0:T(8,128)(2,1)}, bf16[2,128,1024]{2,1,0:T(8,128)(2,1)S(1)}, u32[]{:S(2)}, u32[]{:S(2)}) collective-permute-start(bf16[2,128,1024]{2,1,0:T(8,128)(2,1)} %get-tuple-element.27), channel_id=1, source_target_pairs={{0,1},{1,0},{2,3},{3,2},{4,5},{5,4},{6,7},{7,6},{8,9},{9,8},{10,11... | collective-permute-start | bytes 1572872 | tf_op jit(solution)/shard_map/ppermute | solution.py:202
  18.3 5.9 %collective-permute-start.3 = (bf16[256,256]{1,0:T(8,128)(2,1)S(1)}, bf16[256,256]{1,0:T(8,128)(2,1)S(1)}, u32[]{:S(2)}, u32[]{:S(2)}) collective-permute-start(bf16[256,256]{1,0:T(8,128)(2,1)S(1)} %constant_dynamic-update-slice_fusion.refs_0_), channel_id=1, source_target_pairs={{0,8},{1,9},{2,10},{3,11},{4,12},{5,13},{6,14},{7,15},{8,0},{9,1},... | collective-permute-start | bytes 393224 | tf_op jit(solution)/shard_map/ppermute | solution.py:198
  18.3 5.9 %collective-permute-start.7 = (bf16[128,512]{1,0:T(8,128)(2,1)S(1)}, bf16[128,512]{1,0:T(8,128)(2,1)S(1)}, u32[]{:S(2)}, u32[]{:S(2)}) collective-permute-start(bf16[128,512]{1,0:T(8,128)(2,1)S(1)} %collective-permute-done.1.refs_0_), channel_id=1, source_target_pairs={{0,2},{1,3},{2,0},{3,1},{4,6},{5,7},{6,4},{7,5},{8,10},{9,11},{10,... | collective-permute-start | bytes 393224 | tf_op jit(solution)/shard_map/ppermute | solution.py:202
  20.1 9.0 %collective-permute-start.11 = (bf16[512,256]{1,0:T(8,128)(2,1)S(1)}, bf16[512,256]{1,0:T(8,128)(2,1)S(1)}, u32[]{:S(2)}, u32[]{:S(2)}) collective-permute-start(bf16[512,256]{1,0:T(8,128)(2,1)S(1)} %pad_maximum_fusion), channel_id=1, source_target_pairs={{0,4},{1,5},{2,6},{3,7},{4,0},{5,1},{6,2},{7,3},{8,12},{9,13},{10,... | collective-permute-start | bytes 786440 | tf_op jit(solution)/shard_map/ppermute | solution.py:198
  22.9 7.9 %collective-permute-start.6 = (bf16[128,1024]{1,0:T(8,128)(2,1)S(1)}, bf16[128,1024]{1,0:T(8,128)(2,1)S(1)}, u32[]{:S(2)}, u32[]{:S(2)}) collective-permute-start(bf16[128,1024]{1,0:T(8,128)(2,1)S(1)} %fusion.2), channel_id=1, source_target_pairs={{0,2},{1,3},{2,0},{3,1},{4,6},{5,7},{6,4},{7,5},{8,10},{9,11},{10,... | collective-permute-start | bytes 786440 | tf_op jit(solution)/shard_map/ppermute | solution.py:348
  23.3 1.4 %collective-permute-start.8 = (bf16[128,512]{1,0:T(8,128)(2,1)S(1)}, bf16[128,512]{1,0:T(8,128)(2,1)S(1)}, u32[]{:S(2)}, u32[]{:S(2)}) collective-permute-start(bf16[128,512]{1,0:T(8,128)(2,1)S(1)} %collective-permute-done.1.refs_0_), channel_id=1, source_target_pairs={{0,1},{1,0},{2,3},{3,2},{4,5},{5,4},{6,7},{7,6},{8,9},{9,8},{10,11... | collective-permute-start | bytes 393224 | tf_op jit(solution)/shard_map/ppermute | solution.py:202
  24.2 2.0 %collective-permute-start.10 = (bf16[128,512]{1,0:T(8,128)(2,1)S(1)}, bf16[128,512]{1,0:T(8,128)(2,1)S(1)}, u32[]{:S(2)}, u32[]{:S(2)}) collective-permute-start(bf16[128,512]{1,0:T(8,128)(2,1)S(1)} %collective-permute-done.2.refs_2_), channel_id=1, source_target_pairs={{0,1},{1,0},{2,3},{3,2},{4,5},{5,4},{6,7},{7,6},{8,9},{9,8},{10,11... | collective-permute-start | bytes 393224 | tf_op jit(solution)/shard_map/ppermute | solution.py:202
  24.3 1.9 %collective-permute-start.9 = (bf16[128,512]{1,0:T(8,128)(2,1)S(1)}, bf16[128,512]{1,0:T(8,128)(2,1)S(1)}, u32[]{:S(2)}, u32[]{:S(2)}) collective-permute-start(bf16[128,512]{1,0:T(8,128)(2,1)S(1)} %collective-permute-done.7.refs_1_), channel_id=1, source_target_pairs={{0,1},{1,0},{2,3},{3,2},{4,5},{5,4},{6,7},{7,6},{8,9},{9,8},{10,11... | collective-permute-start | bytes 393224 | tf_op jit(solution)/shard_map/ppermute | solution.py:202
  24.7 6.9 %collective-permute-start.4 = (bf16[256,256]{1,0:T(8,128)(2,1)S(1)}, bf16[256,256]{1,0:T(8,128)(2,1)S(1)}, u32[]{:S(2)}, u32[]{:S(2)}) collective-permute-start(bf16[256,256]{1,0:T(8,128)(2,1)S(1)} %collective-permute-done.3.refs_1_), channel_id=1, source_target_pairs={{0,4},{1,5},{2,6},{3,7},{4,0},{5,1},{6,2},{7,3},{8,12},{9,13},{10,... | collective-permute-start | bytes 393224 | tf_op jit(solution)/shard_map/ppermute | solution.py:198

commit v16 on v15

--- a/solution.py
+++ b/solution.py
@@ -102,6 +102,9 @@
             at = g * group + h * HEAD_SIZE
             gq[:, at : at + HEAD_SIZE] = grad_query[h * length : (h + 1) * length].astype(BF16)
         stored[g].start()
+    for g in range(kv_heads):
+        cols = slice(g * group, (g + 1) * group)
+        head = slice(g * HEAD_SIZE, (g + 1) * HEAD_SIZE)
         grad_key = dot(ds[:, cols], stacked(q, g, per_group)) * scale
         gk_ref[:, head] = grad_key.astype(BF16)
         twice_ref[:length, head] = grad_key.astype(BF16)

time: 32.9 us -> 32.7 us (level)
  transfers between devices with their start and end apart: 12 -> 12, of which waited for: 5 -> 5; matrix products, arithmetic and copies ran while one was open for 6% -> 6% of each run, Pallas kernels for 30% -> 29%
where the time goes in v16:
time: 32.7 us; the launch traced here: 32.5 us
  starting transfers between devices  11.8 us (36%)
  Pallas kernels  10.5 us (32%)
  waiting for transfers between devices  6.21 us (19%)
  other arithmetic  1.99 us (6%)
  local copies, waits for them, and re-layouts  1.15 us (4%)
  between operations  0.77 us (2%)
    ppermute x6, starting transfers between devices, along_dp(): return lax.ppermute(array, ('dp', 'mp'), pairs)  9.18 us
    ppermute x6, waiting for transfers between devices, along_dp(): return lax.ppermute(array, ('dp', 'mp'), pairs)  5.27 us
    pallas_call x1, Pallas kernels, body(): pl.pallas_call(partials_kernel, in_specs=[IN_VMEM, IN_VMEM, IN_HBM], out_...  4.77 us
    pallas_call x1, Pallas kernels, body(): pl.pallas_call(attention_kernel, in_specs=[IN_HBM] * 4, out_specs=[IN_VME...  3.91 us
    ppermute x5, starting transfers between devices, along_mp(): return lax.ppermute(array, 'mp', [(m, m ^ bit) for m in range(groups)])  2.23 us
    add x1, other arithmetic, body(): total = kept.astype(F32) + came.astype(F32)  1.21 us
    dynamic_slice x1, local copies, waits for them, and re-layouts, block(): return lax.dynamic_slice(inputs, (0, (part ^ k) * width), (rows, width))  1.07 us
    pallas_call x1, Pallas kernels, summed_weights(): pl.pallas_call(functools.partial(last_kernel, parts), out_specs=ANYWHERE,...  1.03 us
  transfers between devices with their start and end apart: 12, of which 5 were waited for; matrix products, arithmetic and copies ran while one was open for 6% of the time, Pallas kernels for 29%

profile of v16, /device:TPU:0, one launch (start us, length us, event | category | flops | bytes accessed | tf_op | source)
XLA Modules:
  0.0 32.5 jit_solution(8167978675720953807)
XLA Ops:
  0.7 1.1 %constant_dynamic-slice_fusion.2 = (bf16[128,512]{1,0:T(8,128)(2,1)S(1)}, bf16[128,512]{1,0:T(8,128)(2,1)S(1)}) fusion(bf16[128,4096]{1,0:T(8,128)(2,1)} %refs_7_.1, s32[]{:T(128)S(6)} %select_n.10, s32[]{:T(128)S(6)} %select_n.9), kind=kLoop, calls=%fused_computation.10 | loop fusion | bytes 524296 | tf_op jit(solution)/shard_map/dynamic_slice | solution.py:214
  1.7 4.1 %collective-permute-start.1 = (bf16[128,512]{1,0:T(8,128)(2,1)S(1)}, bf16[128,512]{1,0:T(8,128)(2,1)S(1)}, u32[]{:S(2)}, u32[]{:S(2)}) collective-permute-start(bf16[128,512]{1,0:T(8,128)(2,1)S(1)} %get-tuple-element.36), channel_id=1, source_target_pairs={{0,16},{1,21},{2,26},{3,31},{4,20},{5,17},{6,30},{7,27},{8,24},{9,... | collective-permute-start | bytes 393224 | tf_op jit(solution)/shard_map/ppermute | solution.py:201
  5.8 1.6 %collective-permute-start.2 = (bf16[128,512]{1,0:T(8,128)(2,1)S(1)}, bf16[128,512]{1,0:T(8,128)(2,1)S(1)}, u32[]{:S(2)}, u32[]{:S(2)}) collective-permute-start(bf16[128,512]{1,0:T(8,128)(2,1)S(1)} %get-tuple-element.35), channel_id=1, source_target_pairs={{0,8},{1,13},{2,10},{3,15},{4,12},{5,9},{6,14},{7,11},{8,0},{9,5},... | collective-permute-start | bytes 393224 | tf_op jit(solution)/shard_map/ppermute | solution.py:201
  7.4 3.9 %shard_map.85 = (bf16[128,256]{1,0:T(8,128)(2,1)}, bf16[128,256]{1,0:T(8,128)(2,1)}, bf16[256,256]{1,0:T(8,128)(2,1)}, bf16[128,2048]{1,0:T(8,128)(2,1)}) custom-call(bf16[128,2048]{1,0:T(8,128)(2,1)} %q_hbm.1, bf16[128,256]{1,0:T(8,128)(2,1)} %k_hbm.1, bf16[128,256]{1,0:T(8,128)(2,1)} %v_hbm.1, bf16[128,2048]{1,0:T(8,128)(2,1)} %do_hbm.1), custom_call_target="tpu_custom_call" | custom-call | flops 335544320 | bytes 1572864 | tf_op jit(solution)/shard_map/pallas_call | solution.py:294
  11.3 0.0 copy-start.1
  11.3 0.4 %collective-permute-start = (bf16[128,256]{1,0:T(8,128)(2,1)}, bf16[128,256]{1,0:T(8,128)(2,1)S(1)}, u32[]{:S(2)}, u32[]{:S(2)}) collective-permute-start(bf16[128,256]{1,0:T(8,128)(2,1)} %get-tuple-element.19.gk_ref), channel_id=1, source_target_pairs={{0,16},{1,17},{2,18},{3,19},{4,20},{5,21},{6,22},{7,23},{8,24},{9,... | collective-permute-start | bytes 196616 | tf_op jit(solution)/shard_map/ppermute | solution.py:201
  11.7 4.8 %shard_map.86 = (bf16[2,128,1024]{2,1,0:T(8,128)(2,1)}, bf16[2,128,1024]{2,1,0:T(8,128)(2,1)}) custom-call(bf16[128,256]{1,0:T(8,128)(2,1)} %get-tuple-element.19.gk_ref, bf16[128,256]{1,0:T(8,128)(2,1)} %get-tuple-element.21.gv_ref, bf16[2,4096,256]{2,1,0:T(8,128)(2,1)} %p_hbm.1), custom_call_target="tpu_custom_call" | custom-call | flops 536870912 | bytes 4194304 | tf_op jit(solution)/shard_map/pallas_call | solution.py:312
  16.5 1.5 %collective-permute-done = bf16[128,256]{1,0:T(8,128)(2,1)S(1)} collective-permute-done((bf16[128,256]{1,0:T(8,128)(2,1)}, bf16[128,256]{1,0:T(8,128)(2,1)S(1)}, u32[]{:S(2)}, u32[]{:S(2)}) %collective-permute-start) | collective-permute-done | bytes 65568 | tf_op jit(solution)/shard_map/ppermute | solution.py:201
  18.0 0.0 collective-permute-start.5
  18.1 0.1 collective-permute-start.3
  18.1 1.8 %collective-permute-start.7 = (bf16[128,512]{1,0:T(8,128)(2,1)S(1)}, bf16[128,512]{1,0:T(8,128)(2,1)S(1)}, u32[]{:S(2)}, u32[]{:S(2)}) collective-permute-start(bf16[128,512]{1,0:T(8,128)(2,1)S(1)} %collective-permute-done.1.refs_0_), channel_id=1, source_target_pairs={{0,2},{1,3},{2,0},{3,1},{4,6},{5,7},{6,4},{7,5},{8,10},{9,11},{10,... | collective-permute-start | bytes 393224 | tf_op jit(solution)/shard_map/ppermute | solution.py:205
  19.9 1.5 %collective-permute-start.11 = (bf16[512,256]{1,0:T(8,128)(2,1)S(1)}, bf16[512,256]{1,0:T(8,128)(2,1)S(1)}, u32[]{:S(2)}, u32[]{:S(2)}) collective-permute-start(bf16[512,256]{1,0:T(8,128)(2,1)S(1)} %pad_maximum_fusion), channel_id=1, source_target_pairs={{0,4},{1,5},{2,6},{3,7},{4,0},{5,1},{6,2},{7,3},{8,12},{9,13},{10,... | collective-permute-start | bytes 786440 | tf_op jit(solution)/shard_map/ppermute | solution.py:201
  21.5 1.2 %convert_add_fusion = f32[2,128,1024]{2,1,0:T(8,128)S(1)} fusion(bf16[2,128,1024]{2,1,0:T(8,128)(2,1)S(1)} %collective-permute-done.5, bf16[2,128,1024]{2,1,0:T(8,128)(2,1)} %get-tuple-element.26), kind=kLoop, calls=%fused_computation | loop fusion | flops 786432 | bytes 2097152 | tf_op jit(solution)/shard_map/add | solution.py:347
  22.8 0.4 %collective-permute-start.6 = (bf16[128,1024]{1,0:T(8,128)(2,1)S(1)}, bf16[128,1024]{1,0:T(8,128)(2,1)S(1)}, u32[]{:S(2)}, u32[]{:S(2)}) collective-permute-start(bf16[128,1024]{1,0:T(8,128)(2,1)S(1)} %fusion.2), channel_id=1, source_target_pairs={{0,2},{1,3},{2,0},{3,1},{4,6},{5,7},{6,4},{7,5},{8,10},{9,11},{10,... | collective-permute-start | bytes 786440 | tf_op jit(solution)/shard_map/ppermute | solution.py:351
  23.1 0.9 %collective-permute-done.3.refs_1_ = bf16[256,256]{1,0:T(8,128)(2,1)S(1)} collective-permute-done((bf16[256,256]{1,0:T(8,128)(2,1)S(1)}, bf16[256,256]{1,0:T(8,128)(2,1)S(1)}, u32[]{:S(2)}, u32[]{:S(2)}) %collective-permute-start.3) | collective-permute-done | bytes 131104 | tf_op jit(solution)/shard_map/ppermute | solution.py:201
  24.0 0.1 collective-permute-done.7.refs_1_
  24.1 0.4 %collective-permute-start.9 = (bf16[128,512]{1,0:T(8,128)(2,1)S(1)}, bf16[128,512]{1,0:T(8,128)(2,1)S(1)}, u32[]{:S(2)}, u32[]{:S(2)}) collective-permute-start(bf16[128,512]{1,0:T(8,128)(2,1)S(1)} %collective-permute-done.7.refs_1_), channel_id=1, source_target_pairs={{0,1},{1,0},{2,3},{3,2},{4,5},{5,4},{6,7},{7,6},{8,9},{9,8},{10,11... | collective-permute-start | bytes 393224 | tf_op jit(solution)/shard_map/ppermute | solution.py:205
  24.5 1.5 %collective-permute-start.4 = (bf16[256,256]{1,0:T(8,128)(2,1)S(1)}, bf16[256,256]{1,0:T(8,128)(2,1)S(1)}, u32[]{:S(2)}, u32[]{:S(2)}) collective-permute-start(bf16[256,256]{1,0:T(8,128)(2,1)S(1)} %collective-permute-done.3.refs_1_), channel_id=1, source_target_pairs={{0,4},{1,5},{2,6},{3,7},{4,0},{5,1},{6,2},{7,3},{8,12},{9,13},{10,... | collective-permute-start | bytes 393224 | tf_op jit(solution)/shard_map/ppermute | solution.py:201
  26.0 2.9 %collective-permute-done.11.refs_6_.refs_2_ = bf16[512,256]{1,0:T(8,128)(2,1)S(1)} collective-permute-done((bf16[512,256]{1,0:T(8,128)(2,1)S(1)}, bf16[512,256]{1,0:T(8,128)(2,1)S(1)}, u32[]{:S(2)}, u32[]{:S(2)}) %collective-permute-start.11) | collective-permute-done | bytes 262176 | tf_op jit(solution)/shard_map/ppermute | solution.py:201
  29.0 0.5 %shard_map.87.x_ref = bf16[512,1024]{1,0:T(8,128)(2,1)S(1)} custom-call(bf16[128,512]{1,0:T(8,128)(2,1)S(1)} %collective-permute-done.1.refs_0_, bf16[128,512]{1,0:T(8,128)(2,1)S(1)} %collective-permute-done.7.refs_1_, bf16[128,512]{1,0:T(8,128)(2,1)S(1)} %collective-permute-done.2.refs_2_, bf16[128,512]{1,0:T(8,128)(2,1)S(1)} %collective-permute-done.8.refs_3_, ...), custom_call_target="tpu_custom_call" | custom-call | bytes 2097152 | tf_op jit(solution)/shard_map/pallas_call | solution.py:236
  29.4 0.4 %shard_map.88.sum_ref = f32[512,256]{1,0:T(8,128)S(1)} custom-call(bf16[512,1024]{1,0:T(8,128)(2,1)S(1)} %shard_map.87.x_ref, bf16[256,256]{1,0:T(8,128)(2,1)S(1)} %constant_dynamic-update-slice_fusion.refs_0_, bf16[256,256]{1,0:T(8,128)(2,1)S(1)} %collective-permute-done.3.refs_1_, bf16[512,256]{1,0:T(8,128)(2,1)S(1)} %collective-permute-done.11.refs_6_.refs_2_), custom_call_target="tpu_custom_call" | custom-call | flops 268435456 | bytes 1572864 | tf_op jit(solution)/shard_map/pallas_call | solution.py:250
  29.8 0.9 %collective-permute-done.6 = bf16[128,1024]{1,0:T(8,128)(2,1)S(1)} collective-permute-done((bf16[128,1024]{1,0:T(8,128)(2,1)S(1)}, bf16[128,1024]{1,0:T(8,128)(2,1)S(1)}, u32[]{:S(2)}, u32[]{:S(2)}) %collective-permute-start.6) | collective-permute-done | bytes 262176 | tf_op jit(solution)/shard_map/ppermute | solution.py:351
  30.7 0.8 %fusion.1 = bf16[128,1024]{1,0:T(8,128)(2,1)} fusion(f32[2,128,1024]{2,1,0:T(8,128)S(1)} %convert_add_fusion, bf16[128,1024]{1,0:T(8,128)(2,1)S(1)} %collective-permute-done.6), kind=kLoop, calls=%fused_computation.4 | loop fusion | flops 393216 | bytes 1048576 | tf_op jit(solution)/shard_map/convert_element_type | solution.py:352
  31.4 1.0 %shard_map.89 = f32[512,256]{1,0:T(8,128)} custom-call(bf16[512,1024]{1,0:T(8,128)(2,1)S(1)} %shard_map.87.x_ref, f32[512,256]{1,0:T(8,128)S(1)} %shard_map.88.sum_ref, bf16[256,256]{1,0:T(8,128)(2,1)S(1)} %collective-permute-done.4.key_ref), custom_call_target="tpu_custom_call" | custom-call | flops 67108864 | bytes 1048576 | tf_op jit(solution)/shard_map/pallas_call | solution.py:259
  (16 shorter events, 0.1 us)
Async XLA Ops:
  0.6 17.4 %copy-start = (bf16[128,4096]{1,0:T(8,128)(2,1)S(1)}, bf16[128,4096]{1,0:T(8,128)(2,1)}, u32[]{:S(2)}) copy-start(bf16[128,4096]{1,0:T(8,128)(2,1)} %refs_7_.1) | copy-start | bytes 3145732
  1.7 16.2 %collective-permute-start.1 = (bf16[128,512]{1,0:T(8,128)(2,1)S(1)}, bf16[128,512]{1,0:T(8,128)(2,1)S(1)}, u32[]{:S(2)}, u32[]{:S(2)}) collective-permute-start(bf16[128,512]{1,0:T(8,128)(2,1)S(1)} %get-tuple-element.36), channel_id=1, source_target_pairs={{0,16},{1,21},{2,26},{3,31},{4,20},{5,17},{6,30},{7,27},{8,24},{9,... | collective-permute-start | bytes 393224 | tf_op jit(solution)/shard_map/ppermute | solution.py:201
  5.8 12.1 %collective-permute-start.2 = (bf16[128,512]{1,0:T(8,128)(2,1)S(1)}, bf16[128,512]{1,0:T(8,128)(2,1)S(1)}, u32[]{:S(2)}, u32[]{:S(2)}) collective-permute-start(bf16[128,512]{1,0:T(8,128)(2,1)S(1)} %get-tuple-element.35), channel_id=1, source_target_pairs={{0,8},{1,13},{2,10},{3,15},{4,12},{5,9},{6,14},{7,11},{8,0},{9,5},... | collective-permute-start | bytes 393224 | tf_op jit(solution)/shard_map/ppermute | solution.py:201
  11.3 6.7 %copy-start.1 = (bf16[256,256]{1,0:T(8,128)(2,1)S(1)}, bf16[256,256]{1,0:T(8,128)(2,1)}, u32[]{:S(2)}) copy-start(bf16[256,256]{1,0:T(8,128)(2,1)} %get-tuple-element.24) | copy-start | bytes 393220
  11.3 6.6 %collective-permute-start = (bf16[128,256]{1,0:T(8,128)(2,1)}, bf16[128,256]{1,0:T(8,128)(2,1)S(1)}, u32[]{:S(2)}, u32[]{:S(2)}) collective-permute-start(bf16[128,256]{1,0:T(8,128)(2,1)} %get-tuple-element.19.gk_ref), channel_id=1, source_target_pairs={{0,16},{1,17},{2,18},{3,19},{4,20},{5,21},{6,22},{7,23},{8,24},{9,... | collective-permute-start | bytes 196616 | tf_op jit(solution)/shard_map/ppermute | solution.py:201
  18.0 3.5 %collective-permute-start.5 = (bf16[2,128,1024]{2,1,0:T(8,128)(2,1)}, bf16[2,128,1024]{2,1,0:T(8,128)(2,1)S(1)}, u32[]{:S(2)}, u32[]{:S(2)}) collective-permute-start(bf16[2,128,1024]{2,1,0:T(8,128)(2,1)} %get-tuple-element.27), channel_id=1, source_target_pairs={{0,1},{1,0},{2,3},{3,2},{4,5},{5,4},{6,7},{7,6},{8,9},{9,8},{10,11... | collective-permute-start | bytes 1572872 | tf_op jit(solution)/shard_map/ppermute | solution.py:205
  18.1 5.9 %collective-permute-start.3 = (bf16[256,256]{1,0:T(8,128)(2,1)S(1)}, bf16[256,256]{1,0:T(8,128)(2,1)S(1)}, u32[]{:S(2)}, u32[]{:S(2)}) collective-permute-start(bf16[256,256]{1,0:T(8,128)(2,1)S(1)} %constant_dynamic-update-slice_fusion.refs_0_), channel_id=1, source_target_pairs={{0,8},{1,9},{2,10},{3,11},{4,12},{5,13},{6,14},{7,15},{8,0},{9,1},... | collective-permute-start | bytes 393224 | tf_op jit(solution)/shard_map/ppermute | solution.py:201
  18.1 5.9 %collective-permute-start.7 = (bf16[128,512]{1,0:T(8,128)(2,1)S(1)}, bf16[128,512]{1,0:T(8,128)(2,1)S(1)}, u32[]{:S(2)}, u32[]{:S(2)}) collective-permute-start(bf16[128,512]{1,0:T(8,128)(2,1)S(1)} %collective-permute-done.1.refs_0_), channel_id=1, source_target_pairs={{0,2},{1,3},{2,0},{3,1},{4,6},{5,7},{6,4},{7,5},{8,10},{9,11},{10,... | collective-permute-start | bytes 393224 | tf_op jit(solution)/shard_map/ppermute | solution.py:205
  19.9 9.0 %collective-permute-start.11 = (bf16[512,256]{1,0:T(8,128)(2,1)S(1)}, bf16[512,256]{1,0:T(8,128)(2,1)S(1)}, u32[]{:S(2)}, u32[]{:S(2)}) collective-permute-start(bf16[512,256]{1,0:T(8,128)(2,1)S(1)} %pad_maximum_fusion), channel_id=1, source_target_pairs={{0,4},{1,5},{2,6},{3,7},{4,0},{5,1},{6,2},{7,3},{8,12},{9,13},{10,... | collective-permute-start | bytes 786440 | tf_op jit(solution)/shard_map/ppermute | solution.py:201
  22.8 7.9 %collective-permute-start.6 = (bf16[128,1024]{1,0:T(8,128)(2,1)S(1)}, bf16[128,1024]{1,0:T(8,128)(2,1)S(1)}, u32[]{:S(2)}, u32[]{:S(2)}) collective-permute-start(bf16[128,1024]{1,0:T(8,128)(2,1)S(1)} %fusion.2), channel_id=1, source_target_pairs={{0,2},{1,3},{2,0},{3,1},{4,6},{5,7},{6,4},{7,5},{8,10},{9,11},{10,... | collective-permute-start | bytes 786440 | tf_op jit(solution)/shard_map/ppermute | solution.py:351
  23.1 1.4 %collective-permute-start.8 = (bf16[128,512]{1,0:T(8,128)(2,1)S(1)}, bf16[128,512]{1,0:T(8,128)(2,1)S(1)}, u32[]{:S(2)}, u32[]{:S(2)}) collective-permute-start(bf16[128,512]{1,0:T(8,128)(2,1)S(1)} %collective-permute-done.1.refs_0_), channel_id=1, source_target_pairs={{0,1},{1,0},{2,3},{3,2},{4,5},{5,4},{6,7},{7,6},{8,9},{9,8},{10,11... | collective-permute-start | bytes 393224 | tf_op jit(solution)/shard_map/ppermute | solution.py:205
  24.0 2.0 %collective-permute-start.10 = (bf16[128,512]{1,0:T(8,128)(2,1)S(1)}, bf16[128,512]{1,0:T(8,128)(2,1)S(1)}, u32[]{:S(2)}, u32[]{:S(2)}) collective-permute-start(bf16[128,512]{1,0:T(8,128)(2,1)S(1)} %collective-permute-done.2.refs_2_), channel_id=1, source_target_pairs={{0,1},{1,0},{2,3},{3,2},{4,5},{5,4},{6,7},{7,6},{8,9},{9,8},{10,11... | collective-permute-start | bytes 393224 | tf_op jit(solution)/shard_map/ppermute | solution.py:205
  24.1 1.9 %collective-permute-start.9 = (bf16[128,512]{1,0:T(8,128)(2,1)S(1)}, bf16[128,512]{1,0:T(8,128)(2,1)S(1)}, u32[]{:S(2)}, u32[]{:S(2)}) collective-permute-start(bf16[128,512]{1,0:T(8,128)(2,1)S(1)} %collective-permute-done.7.refs_1_), channel_id=1, source_target_pairs={{0,1},{1,0},{2,3},{3,2},{4,5},{5,4},{6,7},{7,6},{8,9},{9,8},{10,11... | collective-permute-start | bytes 393224 | tf_op jit(solution)/shard_map/ppermute | solution.py:205
  24.5 6.9 %collective-permute-start.4 = (bf16[256,256]{1,0:T(8,128)(2,1)S(1)}, bf16[256,256]{1,0:T(8,128)(2,1)S(1)}, u32[]{:S(2)}, u32[]{:S(2)}) collective-permute-start(bf16[256,256]{1,0:T(8,128)(2,1)S(1)} %collective-permute-done.3.refs_1_), channel_id=1, source_target_pairs={{0,4},{1,5},{2,6},{3,7},{4,0},{5,1},{6,2},{7,3},{8,12},{9,13},{10,... | collective-permute-start | bytes 393224 | tf_op jit(solution)/shard_map/ppermute | solution.py:201

commit v17 on v16

--- a/solution.py
+++ b/solution.py
@@ -17,7 +17,7 @@
 IN_HBM = pl.BlockSpec(memory_space=pltpu.HBM)
 ANYWHERE = pl.BlockSpec(memory_space=pl.ANY)
 IN_VMEM = pl.BlockSpec(memory_space=pltpu.VMEM)
-CHUNK = 512
+CHUNK = 256
 PARAMS = pltpu.CompilerParams(vmem_limit_bytes=24 * 1024 * 1024)
 WHOLE = pltpu.CompilerParams(vmem_limit_bytes=60 * 1024 * 1024)
 

time: 32.7 us -> 32.7 us (level)
  no operation moved by 1% of the time
where the time goes in v17:
time: 32.7 us; the launch traced here: 32.5 us
  starting transfers between devices  11.8 us (36%)
  Pallas kernels  10.5 us (32%)
  waiting for transfers between devices  6.21 us (19%)
  other arithmetic  1.99 us (6%)
  local copies, waits for them, and re-layouts  1.15 us (4%)
  between operations  0.77 us (2%)
    ppermute x6, starting transfers between devices, along_dp(): return lax.ppermute(array, ('dp', 'mp'), pairs)  9.18 us
    ppermute x6, waiting for transfers between devices, along_dp(): return lax.ppermute(array, ('dp', 'mp'), pairs)  5.27 us
    pallas_call x1, Pallas kernels, body(): pl.pallas_call(partials_kernel, in_specs=[IN_VMEM, IN_VMEM, IN_HBM], out_...  4.77 us
    pallas_call x1, Pallas kernels, body(): pl.pallas_call(attention_kernel, in_specs=[IN_HBM] * 4, out_specs=[IN_VME...  3.91 us
    ppermute x5, starting transfers between devices, along_mp(): return lax.ppermute(array, 'mp', [(m, m ^ bit) for m in range(groups)])  2.23 us
    add x1, other arithmetic, body(): total = kept.astype(F32) + came.astype(F32)  1.21 us
    dynamic_slice x1, local copies, waits for them, and re-layouts, block(): return lax.dynamic_slice(inputs, (0, (part ^ k) * width), (rows, width))  1.07 us
    pallas_call x1, Pallas kernels, summed_weights(): pl.pallas_call(functools.partial(last_kernel, parts), out_specs=ANYWHERE,...  1.03 us
  transfers between devices with their start and end apart: 12, of which 5 were waited for; matrix products, arithmetic and copies ran while one was open for 6% of the time, Pallas kernels for 29%

profile of v17, /device:TPU:0, one launch (start us, length us, event | category | flops | bytes accessed | tf_op | source)
XLA Modules:
  0.0 32.5 jit_solution(8167978675720953807)
XLA Ops:
  0.7 1.1 %constant_dynamic-slice_fusion.2 = (bf16[128,512]{1,0:T(8,128)(2,1)S(1)}, bf16[128,512]{1,0:T(8,128)(2,1)S(1)}) fusion(bf16[128,4096]{1,0:T(8,128)(2,1)} %refs_7_.1, s32[]{:T(128)S(6)} %select_n.10, s32[]{:T(128)S(6)} %select_n.9), kind=kLoop, calls=%fused_computation.10 | loop fusion | bytes 524296 | tf_op jit(solution)/shard_map/dynamic_slice | solution.py:214
  1.7 4.1 %collective-permute-start.1 = (bf16[128,512]{1,0:T(8,128)(2,1)S(1)}, bf16[128,512]{1,0:T(8,128)(2,1)S(1)}, u32[]{:S(2)}, u32[]{:S(2)}) collective-permute-start(bf16[128,512]{1,0:T(8,128)(2,1)S(1)} %get-tuple-element.36), channel_id=1, source_target_pairs={{0,16},{1,21},{2,26},{3,31},{4,20},{5,17},{6,30},{7,27},{8,24},{9,... | collective-permute-start | bytes 393224 | tf_op jit(solution)/shard_map/ppermute | solution.py:201
  5.8 1.6 %collective-permute-start.2 = (bf16[128,512]{1,0:T(8,128)(2,1)S(1)}, bf16[128,512]{1,0:T(8,128)(2,1)S(1)}, u32[]{:S(2)}, u32[]{:S(2)}) collective-permute-start(bf16[128,512]{1,0:T(8,128)(2,1)S(1)} %get-tuple-element.35), channel_id=1, source_target_pairs={{0,8},{1,13},{2,10},{3,15},{4,12},{5,9},{6,14},{7,11},{8,0},{9,5},... | collective-permute-start | bytes 393224 | tf_op jit(solution)/shard_map/ppermute | solution.py:201
  7.4 3.9 %shard_map.85 = (bf16[128,256]{1,0:T(8,128)(2,1)}, bf16[128,256]{1,0:T(8,128)(2,1)}, bf16[256,256]{1,0:T(8,128)(2,1)}, bf16[128,2048]{1,0:T(8,128)(2,1)}) custom-call(bf16[128,2048]{1,0:T(8,128)(2,1)} %q_hbm.1, bf16[128,256]{1,0:T(8,128)(2,1)} %k_hbm.1, bf16[128,256]{1,0:T(8,128)(2,1)} %v_hbm.1, bf16[128,2048]{1,0:T(8,128)(2,1)} %do_hbm.1), custom_call_target="tpu_custom_call" | custom-call | flops 335544320 | bytes 1572864 | tf_op jit(solution)/shard_map/pallas_call | solution.py:294
  11.3 0.0 copy-start.1
  11.3 0.4 %collective-permute-start = (bf16[128,256]{1,0:T(8,128)(2,1)}, bf16[128,256]{1,0:T(8,128)(2,1)S(1)}, u32[]{:S(2)}, u32[]{:S(2)}) collective-permute-start(bf16[128,256]{1,0:T(8,128)(2,1)} %get-tuple-element.19.gk_ref), channel_id=1, source_target_pairs={{0,16},{1,17},{2,18},{3,19},{4,20},{5,21},{6,22},{7,23},{8,24},{9,... | collective-permute-start | bytes 196616 | tf_op jit(solution)/shard_map/ppermute | solution.py:201
  11.7 4.8 %shard_map.86 = (bf16[2,128,1024]{2,1,0:T(8,128)(2,1)}, bf16[2,128,1024]{2,1,0:T(8,128)(2,1)}) custom-call(bf16[128,256]{1,0:T(8,128)(2,1)} %get-tuple-element.19.gk_ref, bf16[128,256]{1,0:T(8,128)(2,1)} %get-tuple-element.21.gv_ref, bf16[2,4096,256]{2,1,0:T(8,128)(2,1)} %p_hbm.1), custom_call_target="tpu_custom_call" | custom-call | flops 536870912 | bytes 4194304 | tf_op jit(solution)/shard_map/pallas_call | solution.py:312
  16.5 1.5 %collective-permute-done = bf16[128,256]{1,0:T(8,128)(2,1)S(1)} collective-permute-done((bf16[128,256]{1,0:T(8,128)(2,1)}, bf16[128,256]{1,0:T(8,128)(2,1)S(1)}, u32[]{:S(2)}, u32[]{:S(2)}) %collective-permute-start) | collective-permute-done | bytes 65568 | tf_op jit(solution)/shard_map/ppermute | solution.py:201
  18.0 0.0 collective-permute-start.5
  18.1 0.1 collective-permute-start.3
  18.1 1.8 %collective-permute-start.7 = (bf16[128,512]{1,0:T(8,128)(2,1)S(1)}, bf16[128,512]{1,0:T(8,128)(2,1)S(1)}, u32[]{:S(2)}, u32[]{:S(2)}) collective-permute-start(bf16[128,512]{1,0:T(8,128)(2,1)S(1)} %collective-permute-done.1.refs_0_), channel_id=1, source_target_pairs={{0,2},{1,3},{2,0},{3,1},{4,6},{5,7},{6,4},{7,5},{8,10},{9,11},{10,... | collective-permute-start | bytes 393224 | tf_op jit(solution)/shard_map/ppermute | solution.py:205
  19.9 1.5 %collective-permute-start.11 = (bf16[512,256]{1,0:T(8,128)(2,1)S(1)}, bf16[512,256]{1,0:T(8,128)(2,1)S(1)}, u32[]{:S(2)}, u32[]{:S(2)}) collective-permute-start(bf16[512,256]{1,0:T(8,128)(2,1)S(1)} %pad_maximum_fusion), channel_id=1, source_target_pairs={{0,4},{1,5},{2,6},{3,7},{4,0},{5,1},{6,2},{7,3},{8,12},{9,13},{10,... | collective-permute-start | bytes 786440 | tf_op jit(solution)/shard_map/ppermute | solution.py:201
  21.5 1.2 %convert_add_fusion = f32[2,128,1024]{2,1,0:T(8,128)S(1)} fusion(bf16[2,128,1024]{2,1,0:T(8,128)(2,1)S(1)} %collective-permute-done.5, bf16[2,128,1024]{2,1,0:T(8,128)(2,1)} %get-tuple-element.26), kind=kLoop, calls=%fused_computation | loop fusion | flops 786432 | bytes 2097152 | tf_op jit(solution)/shard_map/add | solution.py:347
  22.8 0.4 %collective-permute-start.6 = (bf16[128,1024]{1,0:T(8,128)(2,1)S(1)}, bf16[128,1024]{1,0:T(8,128)(2,1)S(1)}, u32[]{:S(2)}, u32[]{:S(2)}) collective-permute-start(bf16[128,1024]{1,0:T(8,128)(2,1)S(1)} %fusion.2), channel_id=1, source_target_pairs={{0,2},{1,3},{2,0},{3,1},{4,6},{5,7},{6,4},{7,5},{8,10},{9,11},{10,... | collective-permute-start | bytes 786440 | tf_op jit(solution)/shard_map/ppermute | solution.py:351
  23.1 0.9 %collective-permute-done.3.refs_1_ = bf16[256,256]{1,0:T(8,128)(2,1)S(1)} collective-permute-done((bf16[256,256]{1,0:T(8,128)(2,1)S(1)}, bf16[256,256]{1,0:T(8,128)(2,1)S(1)}, u32[]{:S(2)}, u32[]{:S(2)}) %collective-permute-start.3) | collective-permute-done | bytes 131104 | tf_op jit(solution)/shard_map/ppermute | solution.py:201
  24.0 0.1 collective-permute-done.7.refs_1_
  24.1 0.4 %collective-permute-start.9 = (bf16[128,512]{1,0:T(8,128)(2,1)S(1)}, bf16[128,512]{1,0:T(8,128)(2,1)S(1)}, u32[]{:S(2)}, u32[]{:S(2)}) collective-permute-start(bf16[128,512]{1,0:T(8,128)(2,1)S(1)} %collective-permute-done.7.refs_1_), channel_id=1, source_target_pairs={{0,1},{1,0},{2,3},{3,2},{4,5},{5,4},{6,7},{7,6},{8,9},{9,8},{10,11... | collective-permute-start | bytes 393224 | tf_op jit(solution)/shard_map/ppermute | solution.py:205
  24.5 1.5 %collective-permute-start.4 = (bf16[256,256]{1,0:T(8,128)(2,1)S(1)}, bf16[256,256]{1,0:T(8,128)(2,1)S(1)}, u32[]{:S(2)}, u32[]{:S(2)}) collective-permute-start(bf16[256,256]{1,0:T(8,128)(2,1)S(1)} %collective-permute-done.3.refs_1_), channel_id=1, source_target_pairs={{0,4},{1,5},{2,6},{3,7},{4,0},{5,1},{6,2},{7,3},{8,12},{9,13},{10,... | collective-permute-start | bytes 393224 | tf_op jit(solution)/shard_map/ppermute | solution.py:201
  26.0 2.9 %collective-permute-done.11.refs_6_.refs_2_ = bf16[512,256]{1,0:T(8,128)(2,1)S(1)} collective-permute-done((bf16[512,256]{1,0:T(8,128)(2,1)S(1)}, bf16[512,256]{1,0:T(8,128)(2,1)S(1)}, u32[]{:S(2)}, u32[]{:S(2)}) %collective-permute-start.11) | collective-permute-done | bytes 262176 | tf_op jit(solution)/shard_map/ppermute | solution.py:201
  29.0 0.5 %shard_map.87.x_ref = bf16[512,1024]{1,0:T(8,128)(2,1)S(1)} custom-call(bf16[128,512]{1,0:T(8,128)(2,1)S(1)} %collective-permute-done.1.refs_0_, bf16[128,512]{1,0:T(8,128)(2,1)S(1)} %collective-permute-done.7.refs_1_, bf16[128,512]{1,0:T(8,128)(2,1)S(1)} %collective-permute-done.2.refs_2_, bf16[128,512]{1,0:T(8,128)(2,1)S(1)} %collective-permute-done.8.refs_3_, ...), custom_call_target="tpu_custom_call" | custom-call | bytes 2097152 | tf_op jit(solution)/shard_map/pallas_call | solution.py:236
  29.4 0.4 %shard_map.88.sum_ref = f32[512,256]{1,0:T(8,128)S(1)} custom-call(bf16[512,1024]{1,0:T(8,128)(2,1)S(1)} %shard_map.87.x_ref, bf16[256,256]{1,0:T(8,128)(2,1)S(1)} %constant_dynamic-update-slice_fusion.refs_0_, bf16[256,256]{1,0:T(8,128)(2,1)S(1)} %collective-permute-done.3.refs_1_, bf16[512,256]{1,0:T(8,128)(2,1)S(1)} %collective-permute-done.11.refs_6_.refs_2_), custom_call_target="tpu_custom_call" | custom-call | flops 268435456 | bytes 1572864 | tf_op jit(solution)/shard_map/pallas_call | solution.py:250
  29.8 0.9 %collective-permute-done.6 = bf16[128,1024]{1,0:T(8,128)(2,1)S(1)} collective-permute-done((bf16[128,1024]{1,0:T(8,128)(2,1)S(1)}, bf16[128,1024]{1,0:T(8,128)(2,1)S(1)}, u32[]{:S(2)}, u32[]{:S(2)}) %collective-permute-start.6) | collective-permute-done | bytes 262176 | tf_op jit(solution)/shard_map/ppermute | solution.py:351
  30.7 0.8 %fusion.1 = bf16[128,1024]{1,0:T(8,128)(2,1)} fusion(f32[2,128,1024]{2,1,0:T(8,128)S(1)} %convert_add_fusion, bf16[128,1024]{1,0:T(8,128)(2,1)S(1)} %collective-permute-done.6), kind=kLoop, calls=%fused_computation.4 | loop fusion | flops 393216 | bytes 1048576 | tf_op jit(solution)/shard_map/convert_element_type | solution.py:352
  31.4 1.0 %shard_map.89 = f32[512,256]{1,0:T(8,128)} custom-call(bf16[512,1024]{1,0:T(8,128)(2,1)S(1)} %shard_map.87.x_ref, f32[512,256]{1,0:T(8,128)S(1)} %shard_map.88.sum_ref, bf16[256,256]{1,0:T(8,128)(2,1)S(1)} %collective-permute-done.4.key_ref), custom_call_target="tpu_custom_call" | custom-call | flops 67108864 | bytes 1048576 | tf_op jit(solution)/shard_map/pallas_call | solution.py:259
  (16 shorter events, 0.1 us)
Async XLA Ops:
  0.6 17.4 %copy-start = (bf16[128,4096]{1,0:T(8,128)(2,1)S(1)}, bf16[128,4096]{1,0:T(8,128)(2,1)}, u32[]{:S(2)}) copy-start(bf16[128,4096]{1,0:T(8,128)(2,1)} %refs_7_.1) | copy-start | bytes 3145732
  1.7 16.2 %collective-permute-start.1 = (bf16[128,512]{1,0:T(8,128)(2,1)S(1)}, bf16[128,512]{1,0:T(8,128)(2,1)S(1)}, u32[]{:S(2)}, u32[]{:S(2)}) collective-permute-start(bf16[128,512]{1,0:T(8,128)(2,1)S(1)} %get-tuple-element.36), channel_id=1, source_target_pairs={{0,16},{1,21},{2,26},{3,31},{4,20},{5,17},{6,30},{7,27},{8,24},{9,... | collective-permute-start | bytes 393224 | tf_op jit(solution)/shard_map/ppermute | solution.py:201
  5.8 12.1 %collective-permute-start.2 = (bf16[128,512]{1,0:T(8,128)(2,1)S(1)}, bf16[128,512]{1,0:T(8,128)(2,1)S(1)}, u32[]{:S(2)}, u32[]{:S(2)}) collective-permute-start(bf16[128,512]{1,0:T(8,128)(2,1)S(1)} %get-tuple-element.35), channel_id=1, source_target_pairs={{0,8},{1,13},{2,10},{3,15},{4,12},{5,9},{6,14},{7,11},{8,0},{9,5},... | collective-permute-start | bytes 393224 | tf_op jit(solution)/shard_map/ppermute | solution.py:201
  11.3 6.7 %copy-start.1 = (bf16[256,256]{1,0:T(8,128)(2,1)S(1)}, bf16[256,256]{1,0:T(8,128)(2,1)}, u32[]{:S(2)}) copy-start(bf16[256,256]{1,0:T(8,128)(2,1)} %get-tuple-element.24) | copy-start | bytes 393220
  11.3 6.6 %collective-permute-start = (bf16[128,256]{1,0:T(8,128)(2,1)}, bf16[128,256]{1,0:T(8,128)(2,1)S(1)}, u32[]{:S(2)}, u32[]{:S(2)}) collective-permute-start(bf16[128,256]{1,0:T(8,128)(2,1)} %get-tuple-element.19.gk_ref), channel_id=1, source_target_pairs={{0,16},{1,17},{2,18},{3,19},{4,20},{5,21},{6,22},{7,23},{8,24},{9,... | collective-permute-start | bytes 196616 | tf_op jit(solution)/shard_map/ppermute | solution.py:201
  18.0 3.5 %collective-permute-start.5 = (bf16[2,128,1024]{2,1,0:T(8,128)(2,1)}, bf16[2,128,1024]{2,1,0:T(8,128)(2,1)S(1)}, u32[]{:S(2)}, u32[]{:S(2)}) collective-permute-start(bf16[2,128,1024]{2,1,0:T(8,128)(2,1)} %get-tuple-element.27), channel_id=1, source_target_pairs={{0,1},{1,0},{2,3},{3,2},{4,5},{5,4},{6,7},{7,6},{8,9},{9,8},{10,11... | collective-permute-start | bytes 1572872 | tf_op jit(solution)/shard_map/ppermute | solution.py:205
  18.1 5.9 %collective-permute-start.3 = (bf16[256,256]{1,0:T(8,128)(2,1)S(1)}, bf16[256,256]{1,0:T(8,128)(2,1)S(1)}, u32[]{:S(2)}, u32[]{:S(2)}) collective-permute-start(bf16[256,256]{1,0:T(8,128)(2,1)S(1)} %constant_dynamic-update-slice_fusion.refs_0_), channel_id=1, source_target_pairs={{0,8},{1,9},{2,10},{3,11},{4,12},{5,13},{6,14},{7,15},{8,0},{9,1},... | collective-permute-start | bytes 393224 | tf_op jit(solution)/shard_map/ppermute | solution.py:201
  18.1 5.9 %collective-permute-start.7 = (bf16[128,512]{1,0:T(8,128)(2,1)S(1)}, bf16[128,512]{1,0:T(8,128)(2,1)S(1)}, u32[]{:S(2)}, u32[]{:S(2)}) collective-permute-start(bf16[128,512]{1,0:T(8,128)(2,1)S(1)} %collective-permute-done.1.refs_0_), channel_id=1, source_target_pairs={{0,2},{1,3},{2,0},{3,1},{4,6},{5,7},{6,4},{7,5},{8,10},{9,11},{10,... | collective-permute-start | bytes 393224 | tf_op jit(solution)/shard_map/ppermute | solution.py:205
  19.9 9.0 %collective-permute-start.11 = (bf16[512,256]{1,0:T(8,128)(2,1)S(1)}, bf16[512,256]{1,0:T(8,128)(2,1)S(1)}, u32[]{:S(2)}, u32[]{:S(2)}) collective-permute-start(bf16[512,256]{1,0:T(8,128)(2,1)S(1)} %pad_maximum_fusion), channel_id=1, source_target_pairs={{0,4},{1,5},{2,6},{3,7},{4,0},{5,1},{6,2},{7,3},{8,12},{9,13},{10,... | collective-permute-start | bytes 786440 | tf_op jit(solution)/shard_map/ppermute | solution.py:201
  22.8 7.9 %collective-permute-start.6 = (bf16[128,1024]{1,0:T(8,128)(2,1)S(1)}, bf16[128,1024]{1,0:T(8,128)(2,1)S(1)}, u32[]{:S(2)}, u32[]{:S(2)}) collective-permute-start(bf16[128,1024]{1,0:T(8,128)(2,1)S(1)} %fusion.2), channel_id=1, source_target_pairs={{0,2},{1,3},{2,0},{3,1},{4,6},{5,7},{6,4},{7,5},{8,10},{9,11},{10,... | collective-permute-start | bytes 786440 | tf_op jit(solution)/shard_map/ppermute | solution.py:351
  23.1 1.4 %collective-permute-start.8 = (bf16[128,512]{1,0:T(8,128)(2,1)S(1)}, bf16[128,512]{1,0:T(8,128)(2,1)S(1)}, u32[]{:S(2)}, u32[]{:S(2)}) collective-permute-start(bf16[128,512]{1,0:T(8,128)(2,1)S(1)} %collective-permute-done.1.refs_0_), channel_id=1, source_target_pairs={{0,1},{1,0},{2,3},{3,2},{4,5},{5,4},{6,7},{7,6},{8,9},{9,8},{10,11... | collective-permute-start | bytes 393224 | tf_op jit(solution)/shard_map/ppermute | solution.py:205
  24.0 2.0 %collective-permute-start.10 = (bf16[128,512]{1,0:T(8,128)(2,1)S(1)}, bf16[128,512]{1,0:T(8,128)(2,1)S(1)}, u32[]{:S(2)}, u32[]{:S(2)}) collective-permute-start(bf16[128,512]{1,0:T(8,128)(2,1)S(1)} %collective-permute-done.2.refs_2_), channel_id=1, source_target_pairs={{0,1},{1,0},{2,3},{3,2},{4,5},{5,4},{6,7},{7,6},{8,9},{9,8},{10,11... | collective-permute-start | bytes 393224 | tf_op jit(solution)/shard_map/ppermute | solution.py:205
  24.1 1.9 %collective-permute-start.9 = (bf16[128,512]{1,0:T(8,128)(2,1)S(1)}, bf16[128,512]{1,0:T(8,128)(2,1)S(1)}, u32[]{:S(2)}, u32[]{:S(2)}) collective-permute-start(bf16[128,512]{1,0:T(8,128)(2,1)S(1)} %collective-permute-done.7.refs_1_), channel_id=1, source_target_pairs={{0,1},{1,0},{2,3},{3,2},{4,5},{5,4},{6,7},{7,6},{8,9},{9,8},{10,11... | collective-permute-start | bytes 393224 | tf_op jit(solution)/shard_map/ppermute | solution.py:205
  24.5 6.9 %collective-permute-start.4 = (bf16[256,256]{1,0:T(8,128)(2,1)S(1)}, bf16[256,256]{1,0:T(8,128)(2,1)S(1)}, u32[]{:S(2)}, u32[]{:S(2)}) collective-permute-start(bf16[256,256]{1,0:T(8,128)(2,1)S(1)} %collective-permute-done.3.refs_1_), channel_id=1, source_target_pairs={{0,4},{1,5},{2,6},{3,7},{4,0},{5,1},{6,2},{7,3},{8,12},{9,13},{10,... | collective-permute-start | bytes 393224 | tf_op jit(solution)/shard_map/ppermute | solution.py:201

commit v18 on v16

--- a/solution.py
+++ b/solution.py
@@ -86,14 +86,13 @@
     for pair in large:
         for copy in pair:
             copy.start()
+    scale = 1.0 / math.sqrt(HEAD_SIZE)
     for copy in small:
         copy.wait()
     for g in range(kv_heads):
         for copy in large[g]:
             copy.wait()
         attention_scores(g, q, k, v, do, scores, grad_probs)
-    scale = 1.0 / math.sqrt(HEAD_SIZE)
-    for g in range(kv_heads):
         attention_softmax(g, scores, grad_probs, probs_b, ds)
         cols = slice(g * group, (g + 1) * group)
         head = slice(g * HEAD_SIZE, (g + 1) * HEAD_SIZE)

time: 32.7 us -> 32.9 us (level)
  transfers between devices with their start and end apart: 12 -> 12, of which waited for: 5 -> 5; matrix products, arithmetic and copies ran while one was open for 6% -> 6% of each run, Pallas kernels for 29% -> 30%
where the time goes in v18:
time: 32.9 us; the launch traced here: 32.7 us
  starting transfers between devices  11.8 us (36%)
  Pallas kernels  10.8 us (33%)
  waiting for transfers between devices  6.22 us (19%)
  other arithmetic  1.99 us (6%)
  local copies, waits for them, and re-layouts  1.15 us (3%)
  between operations  0.77 us (2%)
    ppermute x6, starting transfers between devices, along_dp(): return lax.ppermute(array, ('dp', 'mp'), pairs)  9.19 us
    ppermute x6, waiting for transfers between devices, along_dp(): return lax.ppermute(array, ('dp', 'mp'), pairs)  5.28 us
    pallas_call x1, Pallas kernels, body(): pl.pallas_call(partials_kernel, in_specs=[IN_VMEM, IN_VMEM, IN_HBM], out_...  4.76 us
    pallas_call x1, Pallas kernels, body(): pl.pallas_call(attention_kernel, in_specs=[IN_HBM] * 4, out_specs=[IN_VME...  4.14 us
    ppermute x5, starting transfers between devices, along_mp(): return lax.ppermute(array, 'mp', [(m, m ^ bit) for m in range(groups)])  2.23 us
    add x1, other arithmetic, body(): total = kept.astype(F32) + came.astype(F32)  1.21 us
    dynamic_slice x1, local copies, waits for them, and re-layouts, block(): return lax.dynamic_slice(inputs, (0, (part ^ k) * width), (rows, width))  1.07 us
    pallas_call x1, Pallas kernels, summed_weights(): pl.pallas_call(functools.partial(last_kernel, parts), out_specs=ANYWHERE,...  1.03 us
  transfers between devices with their start and end apart: 12, of which 5 were waited for; matrix products, arithmetic and copies ran while one was open for 6% of the time, Pallas kernels for 30%

profile of v18, /device:TPU:0, one launch (start us, length us, event | category | flops | bytes accessed | tf_op | source)
XLA Modules:
  0.0 32.7 jit_solution(13718129481416781818)
XLA Ops:
  0.7 1.1 %constant_dynamic-slice_fusion.2 = (bf16[128,512]{1,0:T(8,128)(2,1)S(1)}, bf16[128,512]{1,0:T(8,128)(2,1)S(1)}) fusion(bf16[128,4096]{1,0:T(8,128)(2,1)} %refs_7_.1, s32[]{:T(128)S(6)} %select_n.10, s32[]{:T(128)S(6)} %select_n.9), kind=kLoop, calls=%fused_computation.10 | loop fusion | bytes 524296 | tf_op jit(solution)/shard_map/dynamic_slice | solution.py:213
  1.7 4.1 %collective-permute-start.1 = (bf16[128,512]{1,0:T(8,128)(2,1)S(1)}, bf16[128,512]{1,0:T(8,128)(2,1)S(1)}, u32[]{:S(2)}, u32[]{:S(2)}) collective-permute-start(bf16[128,512]{1,0:T(8,128)(2,1)S(1)} %get-tuple-element.36), channel_id=1, source_target_pairs={{0,16},{1,21},{2,26},{3,31},{4,20},{5,17},{6,30},{7,27},{8,24},{9,... | collective-permute-start | bytes 393224 | tf_op jit(solution)/shard_map/ppermute | solution.py:200
  5.8 1.6 %collective-permute-start.2 = (bf16[128,512]{1,0:T(8,128)(2,1)S(1)}, bf16[128,512]{1,0:T(8,128)(2,1)S(1)}, u32[]{:S(2)}, u32[]{:S(2)}) collective-permute-start(bf16[128,512]{1,0:T(8,128)(2,1)S(1)} %get-tuple-element.35), channel_id=1, source_target_pairs={{0,8},{1,13},{2,10},{3,15},{4,12},{5,9},{6,14},{7,11},{8,0},{9,5},... | collective-permute-start | bytes 393224 | tf_op jit(solution)/shard_map/ppermute | solution.py:200
  7.4 4.1 %shard_map.85 = (bf16[128,256]{1,0:T(8,128)(2,1)}, bf16[128,256]{1,0:T(8,128)(2,1)}, bf16[256,256]{1,0:T(8,128)(2,1)}, bf16[128,2048]{1,0:T(8,128)(2,1)}) custom-call(bf16[128,2048]{1,0:T(8,128)(2,1)} %q_hbm.1, bf16[128,256]{1,0:T(8,128)(2,1)} %k_hbm.1, bf16[128,256]{1,0:T(8,128)(2,1)} %v_hbm.1, bf16[128,2048]{1,0:T(8,128)(2,1)} %do_hbm.1), custom_call_target="tpu_custom_call" | custom-call | flops 335544320 | bytes 1572864 | tf_op jit(solution)/shard_map/pallas_call | solution.py:293
  11.6 0.0 copy-start.1
  11.6 0.4 %collective-permute-start = (bf16[128,256]{1,0:T(8,128)(2,1)}, bf16[128,256]{1,0:T(8,128)(2,1)S(1)}, u32[]{:S(2)}, u32[]{:S(2)}) collective-permute-start(bf16[128,256]{1,0:T(8,128)(2,1)} %get-tuple-element.19.gk_ref), channel_id=1, source_target_pairs={{0,16},{1,17},{2,18},{3,19},{4,20},{5,21},{6,22},{7,23},{8,24},{9,... | collective-permute-start | bytes 196616 | tf_op jit(solution)/shard_map/ppermute | solution.py:200
  12.0 4.8 %shard_map.86 = (bf16[2,128,1024]{2,1,0:T(8,128)(2,1)}, bf16[2,128,1024]{2,1,0:T(8,128)(2,1)}) custom-call(bf16[128,256]{1,0:T(8,128)(2,1)} %get-tuple-element.19.gk_ref, bf16[128,256]{1,0:T(8,128)(2,1)} %get-tuple-element.21.gv_ref, bf16[2,4096,256]{2,1,0:T(8,128)(2,1)} %p_hbm.1), custom_call_target="tpu_custom_call" | custom-call | flops 536870912 | bytes 4194304 | tf_op jit(solution)/shard_map/pallas_call | solution.py:311
  16.8 1.5 %collective-permute-done = bf16[128,256]{1,0:T(8,128)(2,1)S(1)} collective-permute-done((bf16[128,256]{1,0:T(8,128)(2,1)}, bf16[128,256]{1,0:T(8,128)(2,1)S(1)}, u32[]{:S(2)}, u32[]{:S(2)}) %collective-permute-start) | collective-permute-done | bytes 65568 | tf_op jit(solution)/shard_map/ppermute | solution.py:200
  18.2 0.0 collective-permute-start.5
  18.3 0.1 collective-permute-start.3
  18.4 1.8 %collective-permute-start.7 = (bf16[128,512]{1,0:T(8,128)(2,1)S(1)}, bf16[128,512]{1,0:T(8,128)(2,1)S(1)}, u32[]{:S(2)}, u32[]{:S(2)}) collective-permute-start(bf16[128,512]{1,0:T(8,128)(2,1)S(1)} %collective-permute-done.1.refs_0_), channel_id=1, source_target_pairs={{0,2},{1,3},{2,0},{3,1},{4,6},{5,7},{6,4},{7,5},{8,10},{9,11},{10,... | collective-permute-start | bytes 393224 | tf_op jit(solution)/shard_map/ppermute | solution.py:204
  20.2 1.5 %collective-permute-start.11 = (bf16[512,256]{1,0:T(8,128)(2,1)S(1)}, bf16[512,256]{1,0:T(8,128)(2,1)S(1)}, u32[]{:S(2)}, u32[]{:S(2)}) collective-permute-start(bf16[512,256]{1,0:T(8,128)(2,1)S(1)} %pad_maximum_fusion), channel_id=1, source_target_pairs={{0,4},{1,5},{2,6},{3,7},{4,0},{5,1},{6,2},{7,3},{8,12},{9,13},{10,... | collective-permute-start | bytes 786440 | tf_op jit(solution)/shard_map/ppermute | solution.py:200
  21.7 1.2 %convert_add_fusion = f32[2,128,1024]{2,1,0:T(8,128)S(1)} fusion(bf16[2,128,1024]{2,1,0:T(8,128)(2,1)S(1)} %collective-permute-done.5, bf16[2,128,1024]{2,1,0:T(8,128)(2,1)} %get-tuple-element.26), kind=kLoop, calls=%fused_computation | loop fusion | flops 786432 | bytes 2097152 | tf_op jit(solution)/shard_map/add | solution.py:346
  23.0 0.4 %collective-permute-start.6 = (bf16[128,1024]{1,0:T(8,128)(2,1)S(1)}, bf16[128,1024]{1,0:T(8,128)(2,1)S(1)}, u32[]{:S(2)}, u32[]{:S(2)}) collective-permute-start(bf16[128,1024]{1,0:T(8,128)(2,1)S(1)} %fusion.2), channel_id=1, source_target_pairs={{0,2},{1,3},{2,0},{3,1},{4,6},{5,7},{6,4},{7,5},{8,10},{9,11},{10,... | collective-permute-start | bytes 786440 | tf_op jit(solution)/shard_map/ppermute | solution.py:350
  23.4 0.9 %collective-permute-done.3.refs_1_ = bf16[256,256]{1,0:T(8,128)(2,1)S(1)} collective-permute-done((bf16[256,256]{1,0:T(8,128)(2,1)S(1)}, bf16[256,256]{1,0:T(8,128)(2,1)S(1)}, u32[]{:S(2)}, u32[]{:S(2)}) %collective-permute-start.3) | collective-permute-done | bytes 131104 | tf_op jit(solution)/shard_map/ppermute | solution.py:200
  24.3 0.1 collective-permute-done.7.refs_1_
  24.3 0.4 %collective-permute-start.9 = (bf16[128,512]{1,0:T(8,128)(2,1)S(1)}, bf16[128,512]{1,0:T(8,128)(2,1)S(1)}, u32[]{:S(2)}, u32[]{:S(2)}) collective-permute-start(bf16[128,512]{1,0:T(8,128)(2,1)S(1)} %collective-permute-done.7.refs_1_), channel_id=1, source_target_pairs={{0,1},{1,0},{2,3},{3,2},{4,5},{5,4},{6,7},{7,6},{8,9},{9,8},{10,11... | collective-permute-start | bytes 393224 | tf_op jit(solution)/shard_map/ppermute | solution.py:204
  24.8 1.5 %collective-permute-start.4 = (bf16[256,256]{1,0:T(8,128)(2,1)S(1)}, bf16[256,256]{1,0:T(8,128)(2,1)S(1)}, u32[]{:S(2)}, u32[]{:S(2)}) collective-permute-start(bf16[256,256]{1,0:T(8,128)(2,1)S(1)} %collective-permute-done.3.refs_1_), channel_id=1, source_target_pairs={{0,4},{1,5},{2,6},{3,7},{4,0},{5,1},{6,2},{7,3},{8,12},{9,13},{10,... | collective-permute-start | bytes 393224 | tf_op jit(solution)/shard_map/ppermute | solution.py:200
  26.3 2.9 %collective-permute-done.11.refs_6_.refs_2_ = bf16[512,256]{1,0:T(8,128)(2,1)S(1)} collective-permute-done((bf16[512,256]{1,0:T(8,128)(2,1)S(1)}, bf16[512,256]{1,0:T(8,128)(2,1)S(1)}, u32[]{:S(2)}, u32[]{:S(2)}) %collective-permute-start.11) | collective-permute-done | bytes 262176 | tf_op jit(solution)/shard_map/ppermute | solution.py:200
  29.2 0.5 %shard_map.87.x_ref = bf16[512,1024]{1,0:T(8,128)(2,1)S(1)} custom-call(bf16[128,512]{1,0:T(8,128)(2,1)S(1)} %collective-permute-done.1.refs_0_, bf16[128,512]{1,0:T(8,128)(2,1)S(1)} %collective-permute-done.7.refs_1_, bf16[128,512]{1,0:T(8,128)(2,1)S(1)} %collective-permute-done.2.refs_2_, bf16[128,512]{1,0:T(8,128)(2,1)S(1)} %collective-permute-done.8.refs_3_, ...), custom_call_target="tpu_custom_call" | custom-call | bytes 2097152 | tf_op jit(solution)/shard_map/pallas_call | solution.py:235
  29.7 0.4 %shard_map.88.sum_ref = f32[512,256]{1,0:T(8,128)S(1)} custom-call(bf16[512,1024]{1,0:T(8,128)(2,1)S(1)} %shard_map.87.x_ref, bf16[256,256]{1,0:T(8,128)(2,1)S(1)} %constant_dynamic-update-slice_fusion.refs_0_, bf16[256,256]{1,0:T(8,128)(2,1)S(1)} %collective-permute-done.3.refs_1_, bf16[512,256]{1,0:T(8,128)(2,1)S(1)} %collective-permute-done.11.refs_6_.refs_2_), custom_call_target="tpu_custom_call" | custom-call | flops 268435456 | bytes 1572864 | tf_op jit(solution)/shard_map/pallas_call | solution.py:249
  30.1 0.9 %collective-permute-done.6 = bf16[128,1024]{1,0:T(8,128)(2,1)S(1)} collective-permute-done((bf16[128,1024]{1,0:T(8,128)(2,1)S(1)}, bf16[128,1024]{1,0:T(8,128)(2,1)S(1)}, u32[]{:S(2)}, u32[]{:S(2)}) %collective-permute-start.6) | collective-permute-done | bytes 262176 | tf_op jit(solution)/shard_map/ppermute | solution.py:350
  30.9 0.8 %fusion.1 = bf16[128,1024]{1,0:T(8,128)(2,1)} fusion(f32[2,128,1024]{2,1,0:T(8,128)S(1)} %convert_add_fusion, bf16[128,1024]{1,0:T(8,128)(2,1)S(1)} %collective-permute-done.6), kind=kLoop, calls=%fused_computation.4 | loop fusion | flops 393216 | bytes 1048576 | tf_op jit(solution)/shard_map/convert_element_type | solution.py:351
  31.7 1.0 %shard_map.89 = f32[512,256]{1,0:T(8,128)} custom-call(bf16[512,1024]{1,0:T(8,128)(2,1)S(1)} %shard_map.87.x_ref, f32[512,256]{1,0:T(8,128)S(1)} %shard_map.88.sum_ref, bf16[256,256]{1,0:T(8,128)(2,1)S(1)} %collective-permute-done.4.key_ref), custom_call_target="tpu_custom_call" | custom-call | flops 67108864 | bytes 1048576 | tf_op jit(solution)/shard_map/pallas_call | solution.py:258
  (16 shorter events, 0.1 us)
Async XLA Ops:
  0.6 17.6 %copy-start = (bf16[128,4096]{1,0:T(8,128)(2,1)S(1)}, bf16[128,4096]{1,0:T(8,128)(2,1)}, u32[]{:S(2)}) copy-start(bf16[128,4096]{1,0:T(8,128)(2,1)} %refs_7_.1) | copy-start | bytes 3145732
  1.7 16.5 %collective-permute-start.1 = (bf16[128,512]{1,0:T(8,128)(2,1)S(1)}, bf16[128,512]{1,0:T(8,128)(2,1)S(1)}, u32[]{:S(2)}, u32[]{:S(2)}) collective-permute-start(bf16[128,512]{1,0:T(8,128)(2,1)S(1)} %get-tuple-element.36), channel_id=1, source_target_pairs={{0,16},{1,21},{2,26},{3,31},{4,20},{5,17},{6,30},{7,27},{8,24},{9,... | collective-permute-start | bytes 393224 | tf_op jit(solution)/shard_map/ppermute | solution.py:200
  5.8 12.4 %collective-permute-start.2 = (bf16[128,512]{1,0:T(8,128)(2,1)S(1)}, bf16[128,512]{1,0:T(8,128)(2,1)S(1)}, u32[]{:S(2)}, u32[]{:S(2)}) collective-permute-start(bf16[128,512]{1,0:T(8,128)(2,1)S(1)} %get-tuple-element.35), channel_id=1, source_target_pairs={{0,8},{1,13},{2,10},{3,15},{4,12},{5,9},{6,14},{7,11},{8,0},{9,5},... | collective-permute-start | bytes 393224 | tf_op jit(solution)/shard_map/ppermute | solution.py:200
  11.6 6.7 %copy-start.1 = (bf16[256,256]{1,0:T(8,128)(2,1)S(1)}, bf16[256,256]{1,0:T(8,128)(2,1)}, u32[]{:S(2)}) copy-start(bf16[256,256]{1,0:T(8,128)(2,1)} %get-tuple-element.24) | copy-start | bytes 393220
  11.6 6.6 %collective-permute-start = (bf16[128,256]{1,0:T(8,128)(2,1)}, bf16[128,256]{1,0:T(8,128)(2,1)S(1)}, u32[]{:S(2)}, u32[]{:S(2)}) collective-permute-start(bf16[128,256]{1,0:T(8,128)(2,1)} %get-tuple-element.19.gk_ref), channel_id=1, source_target_pairs={{0,16},{1,17},{2,18},{3,19},{4,20},{5,21},{6,22},{7,23},{8,24},{9,... | collective-permute-start | bytes 196616 | tf_op jit(solution)/shard_map/ppermute | solution.py:200
  18.2 3.5 %collective-permute-start.5 = (bf16[2,128,1024]{2,1,0:T(8,128)(2,1)}, bf16[2,128,1024]{2,1,0:T(8,128)(2,1)S(1)}, u32[]{:S(2)}, u32[]{:S(2)}) collective-permute-start(bf16[2,128,1024]{2,1,0:T(8,128)(2,1)} %get-tuple-element.27), channel_id=1, source_target_pairs={{0,1},{1,0},{2,3},{3,2},{4,5},{5,4},{6,7},{7,6},{8,9},{9,8},{10,11... | collective-permute-start | bytes 1572872 | tf_op jit(solution)/shard_map/ppermute | solution.py:204
  18.3 5.9 %collective-permute-start.3 = (bf16[256,256]{1,0:T(8,128)(2,1)S(1)}, bf16[256,256]{1,0:T(8,128)(2,1)S(1)}, u32[]{:S(2)}, u32[]{:S(2)}) collective-permute-start(bf16[256,256]{1,0:T(8,128)(2,1)S(1)} %constant_dynamic-update-slice_fusion.refs_0_), channel_id=1, source_target_pairs={{0,8},{1,9},{2,10},{3,11},{4,12},{5,13},{6,14},{7,15},{8,0},{9,1},... | collective-permute-start | bytes 393224 | tf_op jit(solution)/shard_map/ppermute | solution.py:200
  18.4 5.9 %collective-permute-start.7 = (bf16[128,512]{1,0:T(8,128)(2,1)S(1)}, bf16[128,512]{1,0:T(8,128)(2,1)S(1)}, u32[]{:S(2)}, u32[]{:S(2)}) collective-permute-start(bf16[128,512]{1,0:T(8,128)(2,1)S(1)} %collective-permute-done.1.refs_0_), channel_id=1, source_target_pairs={{0,2},{1,3},{2,0},{3,1},{4,6},{5,7},{6,4},{7,5},{8,10},{9,11},{10,... | collective-permute-start | bytes 393224 | tf_op jit(solution)/shard_map/ppermute | solution.py:204
  20.2 9.0 %collective-permute-start.11 = (bf16[512,256]{1,0:T(8,128)(2,1)S(1)}, bf16[512,256]{1,0:T(8,128)(2,1)S(1)}, u32[]{:S(2)}, u32[]{:S(2)}) collective-permute-start(bf16[512,256]{1,0:T(8,128)(2,1)S(1)} %pad_maximum_fusion), channel_id=1, source_target_pairs={{0,4},{1,5},{2,6},{3,7},{4,0},{5,1},{6,2},{7,3},{8,12},{9,13},{10,... | collective-permute-start | bytes 786440 | tf_op jit(solution)/shard_map/ppermute | solution.py:200
  23.0 7.9 %collective-permute-start.6 = (bf16[128,1024]{1,0:T(8,128)(2,1)S(1)}, bf16[128,1024]{1,0:T(8,128)(2,1)S(1)}, u32[]{:S(2)}, u32[]{:S(2)}) collective-permute-start(bf16[128,1024]{1,0:T(8,128)(2,1)S(1)} %fusion.2), channel_id=1, source_target_pairs={{0,2},{1,3},{2,0},{3,1},{4,6},{5,7},{6,4},{7,5},{8,10},{9,11},{10,... | collective-permute-start | bytes 786440 | tf_op jit(solution)/shard_map/ppermute | solution.py:350
  23.4 1.4 %collective-permute-start.8 = (bf16[128,512]{1,0:T(8,128)(2,1)S(1)}, bf16[128,512]{1,0:T(8,128)(2,1)S(1)}, u32[]{:S(2)}, u32[]{:S(2)}) collective-permute-start(bf16[128,512]{1,0:T(8,128)(2,1)S(1)} %collective-permute-done.1.refs_0_), channel_id=1, source_target_pairs={{0,1},{1,0},{2,3},{3,2},{4,5},{5,4},{6,7},{7,6},{8,9},{9,8},{10,11... | collective-permute-start | bytes 393224 | tf_op jit(solution)/shard_map/ppermute | solution.py:204
  24.2 2.0 %collective-permute-start.10 = (bf16[128,512]{1,0:T(8,128)(2,1)S(1)}, bf16[128,512]{1,0:T(8,128)(2,1)S(1)}, u32[]{:S(2)}, u32[]{:S(2)}) collective-permute-start(bf16[128,512]{1,0:T(8,128)(2,1)S(1)} %collective-permute-done.2.refs_2_), channel_id=1, source_target_pairs={{0,1},{1,0},{2,3},{3,2},{4,5},{5,4},{6,7},{7,6},{8,9},{9,8},{10,11... | collective-permute-start | bytes 393224 | tf_op jit(solution)/shard_map/ppermute | solution.py:204
  24.3 1.9 %collective-permute-start.9 = (bf16[128,512]{1,0:T(8,128)(2,1)S(1)}, bf16[128,512]{1,0:T(8,128)(2,1)S(1)}, u32[]{:S(2)}, u32[]{:S(2)}) collective-permute-start(bf16[128,512]{1,0:T(8,128)(2,1)S(1)} %collective-permute-done.7.refs_1_), channel_id=1, source_target_pairs={{0,1},{1,0},{2,3},{3,2},{4,5},{5,4},{6,7},{7,6},{8,9},{9,8},{10,11... | collective-permute-start | bytes 393224 | tf_op jit(solution)/shard_map/ppermute | solution.py:204
  24.8 6.9 %collective-permute-start.4 = (bf16[256,256]{1,0:T(8,128)(2,1)S(1)}, bf16[256,256]{1,0:T(8,128)(2,1)S(1)}, u32[]{:S(2)}, u32[]{:S(2)}) collective-permute-start(bf16[256,256]{1,0:T(8,128)(2,1)S(1)} %collective-permute-done.3.refs_1_), channel_id=1, source_target_pairs={{0,4},{1,5},{2,6},{3,7},{4,0},{5,1},{6,2},{7,3},{8,12},{9,13},{10,... | collective-permute-start | bytes 393224 | tf_op jit(solution)/shard_map/ppermute | solution.py:200
